TPU v7x, 32 devices: a whole 2x2x4 slice. The times are simulated.
32 devices in a mesh: dp: 8 (over y, x, core), expert: 4 (over z).
Axes of the slice: x: 2, y: 2, z: 4, core: 2. Of those that a mesh axis runs over, the one named last changes fastest.
Arguments:
- tokens: bfloat16 [256, 4096], P(('dp', 'expert')), may hold values from -6 to 6
- expert_ids: int32 [256, 8], P(('dp', 'expert')), may hold values from 0 to 15, all different within a row; in each aligned block of 8 rows (0 to 7, 8 to 15, ...) at most 8 rows name the same one
- router: bfloat16 [16, 4096], replicated, may hold values from -0.09375 to 0.09375
- w_gate: bfloat16 [16, 1536, 4096], P('dp', 'expert'), may hold values from -0.09375 to 0.09375
- w_up: bfloat16 [16, 1536, 4096], P('dp', 'expert'), may hold values from -0.09375 to 0.09375
- w_down: bfloat16 [16, 1536, 4096], P('dp', 'expert'), may hold values from -0.15625 to 0.15625
Outputs:
- mixed: bfloat16 [256, 4096], P(('dp', 'expert'))
Inputs may be any that keep to these rules, and one draw needn't show every extreme that they name: `expert_ids`: each row names 8 different experts. Within the rows of one device (aligned blocks of 8 rows) no expert is named by more than 8 rows, and in some block one expert is named by exactly 8 rows.
All inputs are finite; a program needn't handle non-finite values.
Results may differ from a plain program's by a relative error of at most 0.0049.
Values may be sent and summed in bfloat16 or wider, within the bound.
No kernel may reach another device: no remote copies, remote signals or barrier semaphores. Data moves between devices by JAX's collectives and lax.ppermute only.
A program may use at most 192 MiB of HBM per device.

v0:
```python
import functools

import jax
import jax.numpy as jnp
from jax import lax
from jax.experimental import pallas as pl
from jax.experimental.pallas import tpu as pltpu
from jax.sharding import PartitionSpec as P

LANES = 128
ROWS = 256
TERMS = 3
VMEM_BYTES = 30 * 1024 * 1024
EXCHANGE_FLOPS = 20_000_000_000
IN_VMEM = pl.BlockSpec(memory_space=pltpu.VMEM)
ANYWHERE = pl.BlockSpec(memory_space=pl.ANY)


def times_rows(left, right):
    return lax.dot_general(
        left, right, (((1,), (1,)), ((), ())), preferred_element_type=jnp.float32
    )


def swap(value, axis, mask):
    count = lax.axis_size(axis)
    return lax.ppermute(value, axis, [(i, i ^ mask) for i in range(count)])


def send(value, step):
    return swap(value.astype(jnp.bfloat16), *step)


def wide(value):
    return value.astype(jnp.float32)


CORE = ("dp", 1)


def plane_steps():
    return [("dp", mask) for mask in range(lax.axis_size("dp") - 2, 0, -2)]


def cat(parts):
    return parts[0] if len(parts) == 1 else jnp.concatenate(parts)


def split(value, count):
    step = value.shape[0] // count
    return [value[start : start + step] for start in range(0, value.shape[0], step)]


def gather_rows(block, w_gate, w_up, w_down):
    depth = lax.axis_size("expert")
    column = [block] + [swap(block, "expert", mask) for mask in range(1, depth)]
    near, column = cat(column[: depth // 2]), column[depth // 2 :]
    near_rest = [swap(near, *step) for step in plane_steps()]
    far = cat(column)
    far_rest = [swap(far, *step) for step in plane_steps()]
    near = cat([near, *near_rest])
    near_there = swap(near, *CORE)
    far = cat([far, *far_rest])
    return [near, far, near_there, swap(far, *CORE)], [w_gate, w_up, w_down]


def scatter_sums(kept, away):
    steps, depth = plane_steps(), lax.axis_size("expert")
    sums = []
    for mine, other in reversed(list(zip(kept, away))):
        part, *rest = split(mine + wide(swap(other, *CORE)), len(steps) + 1)
        here = [send(other, step) for other, step in zip(rest, steps)]
        sums.append(sum([wide(other) for other in here], part))
    far, (total, *near) = split(sums[0], depth // 2), split(sums[1], depth // 2)
    far = [send(part, ("expert", mask + depth // 2)) for mask, part in enumerate(far)]
    near = [send(part, ("expert", mask + 1)) for mask, part in enumerate(near)]
    far = sum(wide(part) for part in far)
    far, *near = lax.optimization_barrier((far, *near))
    return sum([wide(part) for part in near], total + far).astype(jnp.bfloat16)


def pack_kernel(tokens_hbm, ids_hbm, router_hbm, packed_ref, tokens_ref, ids_ref, router_ref, done):
    pairs = [(tokens_hbm, tokens_ref), (ids_hbm, ids_ref), (router_hbm, router_ref)]
    copies = [
        pltpu.make_async_copy(source, target, done.at[index])
        for index, (source, target) in enumerate(pairs)
    ]
    for copy in copies:
        copy.start()
    for copy in copies:
        copy.wait()
    tokens = tokens_ref[...]
    width, expert_total = tokens.shape[1], router_ref.shape[0]
    logits = times_rows(tokens, router_ref[...])
    experts = lax.broadcasted_iota(jnp.int32, logits.shape, 1)
    ids = ids_ref[...]
    chosen = experts < 0
    for pick in range(ids.shape[1]):
        chosen = jnp.logical_or(chosen, ids[:, pick : pick + 1] == experts)
    scores = jnp.where(chosen, 1.0 / (1.0 + jnp.exp(-logits)), 0.0)
    rest = scores / jnp.sum(scores, axis=1, keepdims=True)
    place = (expert_total, packed_ref.shape[1] - width)
    source, lane = [lax.broadcasted_iota(jnp.int32, place, axis) for axis in (0, 1)]
    tags = 0.0
    for term in range(TERMS):
        part = rest.astype(jnp.bfloat16)
        rest = rest - part.astype(jnp.float32)
        moved = (lane == source + term * expert_total).astype(jnp.float32).astype(jnp.bfloat16)
        tags = tags + jnp.dot(part, moved, preferred_element_type=jnp.float32)
    packed_ref[:, :width] = tokens
    packed_ref[:, width:] = tags.astype(jnp.bfloat16)


def pack(tokens, expert_ids, router):
    rows, width = tokens.shape
    extra = -(-TERMS * router.shape[0] // LANES) * LANES
    return pl.pallas_call(
        pack_kernel,
        out_shape=pltpu.VMEM((rows, width + extra), tokens.dtype),
        in_specs=[ANYWHERE] * 3,
        out_specs=IN_VMEM,
        scratch_shapes=[
            *[pltpu.VMEM(value.shape, value.dtype) for value in (tokens, expert_ids, router)],
            pltpu.SemaphoreType.DMA((3,)),
        ],
        cost_estimate=pl.CostEstimate(
            flops=EXCHANGE_FLOPS, bytes_accessed=4 * router.size, transcendentals=0
        ),
    )(*[pltpu.with_memory_space_constraint(v, pltpu.HBM) for v in (tokens, expert_ids, router)])


def expert_kernel(exp_dev, expert_total, parts, *refs):
    pieces, (gate_ref, up_ref, down_ref, *results, rows_ref) = refs[:parts], refs[parts:]
    units, width = down_ref.shape[1:]
    start = 0
    for piece in pieces:
        rows_ref[start : start + piece.shape[0]] = piece[...]
        start += piece.shape[0]
    tags = rows_ref[:, width:].astype(jnp.float32)
    lane = lax.rem(lax.broadcasted_iota(jnp.int32, tags.shape, 1), expert_total)
    first_expert = lax.axis_index("dp") * exp_dev
    hidden, shares = [], []
    for local in range(exp_dev):
        weights = jnp.concatenate([gate_ref[local], up_ref[local]])
        both = times_rows(rows_ref[:, :width], weights)
        gate, up = both[:, :units], both[:, units:]
        hidden.append((gate / (1.0 + jnp.exp(-gate)) * up).astype(jnp.bfloat16))
        mine = jnp.where(lane == first_expert + local, tags, 0.0)
        shares.append(jnp.sum(mine, axis=1, keepdims=True))
    block = min(512, width)

    @pl.loop(0, width // block)
    def _(index):
        columns = pl.ds(pl.multiple_of(index * block, block), block)
        total = 0.0
        for local in range(exp_dev):
            out = jnp.dot(
                hidden[local],
                down_ref[local, :, columns],
                preferred_element_type=jnp.float32,
            )
            total = total + out * shares[local]
        start = 0
        for result in results:
            stop = start + result.shape[0]
            result[:, columns] = total[start:stop].astype(result.dtype)
            start = stop


def run_experts(pieces, kinds, expert_total, held):
    rows = sum(piece.shape[0] for piece in pieces)
    gate, up, down = held
    exp_dev, width = down.shape[0], down.shape[2]
    place = pltpu.VMEM if len(pieces) > 1 else jax.ShapeDtypeStruct
    return pl.pallas_call(
        functools.partial(expert_kernel, exp_dev, expert_total, len(pieces)),
        out_shape=[
            place((piece.shape[0], width), kind) for piece, kind in zip(pieces, kinds)
        ],
        in_specs=[IN_VMEM] * (len(pieces) + len(held)),
        out_specs=[IN_VMEM] * len(pieces),
        scratch_shapes=[pltpu.VMEM((rows, pieces[0].shape[1]), jnp.bfloat16)],
        compiler_params=pltpu.CompilerParams(vmem_limit_bytes=VMEM_BYTES),
        cost_estimate=pl.CostEstimate(
            flops=6 * rows * down.size, bytes_accessed=rows * width * 5, transcendentals=0
        ),
    )(*pieces, gate, up, down)


def body(tokens, expert_ids, router, w_gate, w_up, w_down):
    pieces, held = gather_rows(pack(tokens, expert_ids, router), w_gate, w_up, w_down)
    kinds = [jnp.float32] * 2 + [jnp.bfloat16] * 2
    operands = (router.shape[0], held)
    if sum(piece.shape[0] for piece in pieces) <= ROWS:
        results = run_experts(pieces, kinds, *operands)
    else:
        results = []
        for piece, kind in zip(pieces, kinds):
            chunks = [
                run_experts([piece[start : start + ROWS]], [kind], *operands)[0]
                for start in range(0, piece.shape[0], ROWS)
            ]
            results.append(cat(chunks))
    return scatter_sums(results[:2], results[2:])


def solution(mesh):
    in_specs = (
        P(("dp", "expert"), None),
        P(("dp", "expert"), None),
        P(),
        P("dp", "expert", None),
        P("dp", "expert", None),
        P("dp", "expert", None),
    )
    out_specs = P(("dp", "expert"), None)
    return jax.shard_map(body, mesh=mesh, in_specs=in_specs, out_specs=out_specs, check_vma=False)
```

profile of v0, /device:TPU:0, one launch (start us, length us, event | category | flops | bytes accessed | tf_op | source)
XLA Modules:
  0.0 67.9 jit_solution(6936527848353411031)
XLA Ops:
  0.0 1.4 %shard_map.64 = bf16[8,4224]{1,0:T(8,128)(2,1)S(1)} custom-call(bf16[8,4096]{1,0:T(8,128)(2,1)} %tokens_hbm.1, s32[8,8]{1,0:T(8,128)} %ids_hbm.1, bf16[16,4096]{1,0:T(8,128)(2,1)} %router_hbm.1), custom_call_target="tpu_custom_call" | custom-call | flops 20000000000 | bytes 262144 | tf_op jit(solution)/shard_map/pallas_call | solution.py:117
  1.4 5.1 %collective-permute-start.5 = (bf16[8,4224]{1,0:T(8,128)(2,1)S(1)}, bf16[8,4224]{1,0:T(8,128)(2,1)S(1)}, u32[]{:S(2)}, u32[]{:S(2)}) collective-permute-start(bf16[8,4224]{1,0:T(8,128)(2,1)S(1)} %shard_map.64), channel_id=1, source_target_pairs={{0,3},{1,2},{2,1},{3,0},{4,7},{5,6},{6,5},{7,4},{8,11},{9,10},{10,... | collective-permute-start | bytes 202760 | tf_op jit(solution)/shard_map/ppermute | solution.py:27
  6.5 0.0 collective-permute-start.4
  6.5 0.6 collective-permute-start
  7.2 3.7 %collective-permute-done = bf16[8,4224]{1,0:T(8,128)(2,1)S(1)} collective-permute-done((bf16[8,4224]{1,0:T(8,128)(2,1)S(1)}, bf16[8,4224]{1,0:T(8,128)(2,1)S(1)}, u32[]{:S(2)}, u32[]{:S(2)}) %collective-permute-start) | collective-permute-done | bytes 67616 | tf_op jit(solution)/shard_map/ppermute | solution.py:27
  10.9 1.6 %collective-permute-start.3 = (bf16[16,4224]{1,0:T(8,128)(2,1)S(1)}, bf16[16,4224]{1,0:T(8,128)(2,1)S(1)}, u32[]{:S(2)}, u32[]{:S(2)}) collective-permute-start(bf16[16,4224]{1,0:T(8,128)(2,1)S(1)} %pad_maximum_fusion), channel_id=1, source_target_pairs={{0,8},{4,12},{8,0},{12,4},{16,24},{20,28},{24,16},{28,20},{1,9},{5... | collective-permute-start | bytes 405512 | tf_op jit(solution)/shard_map/ppermute | solution.py:27
  12.5 1.5 %collective-permute-start.2 = (bf16[16,4224]{1,0:T(8,128)(2,1)S(1)}, bf16[16,4224]{1,0:T(8,128)(2,1)S(1)}, u32[]{:S(2)}, u32[]{:S(2)}) collective-permute-start(bf16[16,4224]{1,0:T(8,128)(2,1)S(1)} %pad_maximum_fusion), channel_id=1, source_target_pairs={{0,16},{4,20},{8,24},{12,28},{16,0},{20,4},{24,8},{28,12},{1,17},{... | collective-permute-start | bytes 405512 | tf_op jit(solution)/shard_map/ppermute | solution.py:27
  14.0 0.5 collective-permute-start.1
  14.5 0.0 collective-permute-done.4
  14.5 0.0 collective-permute-done.5
  14.5 1.6 %collective-permute-start.8 = (bf16[16,4224]{1,0:T(8,128)(2,1)S(1)}, bf16[16,4224]{1,0:T(8,128)(2,1)S(1)}, u32[]{:S(2)}, u32[]{:S(2)}) collective-permute-start(bf16[16,4224]{1,0:T(8,128)(2,1)S(1)} %get-tuple-element.29), channel_id=1, source_target_pairs={{0,8},{4,12},{8,0},{12,4},{16,24},{20,28},{24,16},{28,20},{1,9},{5... | collective-permute-start | bytes 405512 | tf_op jit(solution)/shard_map/ppermute | solution.py:27
  16.1 1.5 %collective-permute-start.7 = (bf16[16,4224]{1,0:T(8,128)(2,1)S(1)}, bf16[16,4224]{1,0:T(8,128)(2,1)S(1)}, u32[]{:S(2)}, u32[]{:S(2)}) collective-permute-start(bf16[16,4224]{1,0:T(8,128)(2,1)S(1)} %get-tuple-element.29), channel_id=1, source_target_pairs={{0,16},{4,20},{8,24},{12,28},{16,0},{20,4},{24,8},{28,12},{1,17},{... | collective-permute-start | bytes 405512 | tf_op jit(solution)/shard_map/ppermute | solution.py:27
  17.6 3.7 %collective-permute-done.1 = bf16[16,4224]{1,0:T(8,128)(2,1)S(1)} collective-permute-done((bf16[16,4224]{1,0:T(8,128)(2,1)S(1)}, bf16[16,4224]{1,0:T(8,128)(2,1)S(1)}, u32[]{:S(2)}, u32[]{:S(2)}) %collective-permute-start.1) | collective-permute-done | bytes 135200 | tf_op jit(solution)/shard_map/ppermute | solution.py:27
  21.3 0.9 %collective-permute-start.6 = (bf16[16,4224]{1,0:T(8,128)(2,1)S(1)}, bf16[16,4224]{1,0:T(8,128)(2,1)S(1)}, u32[]{:S(2)}, u32[]{:S(2)}) collective-permute-start(bf16[16,4224]{1,0:T(8,128)(2,1)S(1)} %get-tuple-element.29), channel_id=1, source_target_pairs={{0,24},{4,28},{8,16},{12,20},{16,8},{20,12},{24,0},{28,4},{1,25},{... | collective-permute-start | bytes 405512 | tf_op jit(solution)/shard_map/ppermute | solution.py:27
  22.3 0.0 collective-permute-done.2
  22.3 0.0 collective-permute-done.3
  22.3 0.1 collective-permute-start.9
  22.4 4.8 %collective-permute-done.6 = bf16[16,4224]{1,0:T(8,128)(2,1)S(1)} collective-permute-done((bf16[16,4224]{1,0:T(8,128)(2,1)S(1)}, bf16[16,4224]{1,0:T(8,128)(2,1)S(1)}, u32[]{:S(2)}, u32[]{:S(2)}) %collective-permute-start.6) | collective-permute-done | bytes 135200 | tf_op jit(solution)/shard_map/ppermute | solution.py:27
  27.3 0.0 collective-permute-done.7
  27.3 0.0 collective-permute-done.8
  27.3 0.1 collective-permute-start.10
  27.4 0.0 collective-permute-done.9.refs_2_
  27.4 1.9 %collective-permute-done.10.refs_3_ = bf16[64,4224]{1,0:T(8,128)(2,1)S(1)} collective-permute-done((bf16[64,4224]{1,0:T(8,128)(2,1)S(1)}, bf16[64,4224]{1,0:T(8,128)(2,1)S(1)}, u32[]{:S(2)}, u32[]{:S(2)}) %collective-permute-start.10) | collective-permute-done | bytes 540704 | tf_op jit(solution)/shard_map/ppermute | solution.py:27
  29.3 0.0 copy-start
  29.3 2.8 %copy-done = bf16[2,384,4096]{2,1,0:T(8,128)(2,1)S(1)} copy-done((bf16[2,384,4096]{2,1,0:T(8,128)(2,1)S(1)}, bf16[2,384,4096]{2,1,0:T(8,128)(2,1)}, u32[]{:S(2)}) %copy-start) | copy-done | bytes 6291480
  32.1 0.0 copy-start.1
  32.1 2.8 %copy-done.1 = bf16[2,384,4096]{2,1,0:T(8,128)(2,1)S(1)} copy-done((bf16[2,384,4096]{2,1,0:T(8,128)(2,1)S(1)}, bf16[2,384,4096]{2,1,0:T(8,128)(2,1)}, u32[]{:S(2)}) %copy-start.1) | copy-done | bytes 6291480
  34.9 0.0 copy-start.2
  34.9 2.8 %copy-done.2 = bf16[2,384,4096]{2,1,0:T(8,128)(2,1)S(1)} copy-done((bf16[2,384,4096]{2,1,0:T(8,128)(2,1)S(1)}, bf16[2,384,4096]{2,1,0:T(8,128)(2,1)}, u32[]{:S(2)}) %copy-start.2) | copy-done | bytes 6291480
  37.7 7.0 %shard_map.65 = (f32[64,4096]{1,0:T(8,128)S(1)}, f32[64,4096]{1,0:T(8,128)S(1)}, bf16[64,4096]{1,0:T(8,128)(2,1)S(1)}, bf16[64,4096]{1,0:T(8,128)(2,1)S(1)}) custom-call(bf16[64,4224]{1,0:T(8,128)(2,1)S(1)} %constant_dynamic-update-slice_fusion.refs_0_, bf16[64,4224]{1,0:T(8,128)(2,1)S(1)} %constant_dynamic-update-slice_fusion.7.refs_1_, ...), custom_call_target="tpu_custom_call" | custom-call | flops 4831838208 | bytes 5242880 | tf_op jit(solution)/shard_map/pallas_call | solution.py:175
  44.7 0.2 collective-permute-start.15
  44.9 0.4 collective-permute-start.11
  45.3 1.4 %collective-permute-done.15 = bf16[64,4096]{1,0:T(8,128)(2,1)S(1)} collective-permute-done((bf16[64,4096]{1,0:T(8,128)(2,1)S(1)}, bf16[64,4096]{1,0:T(8,128)(2,1)S(1)}, u32[]{:S(2)}, u32[]{:S(2)}) %collective-permute-start.15) | collective-permute-done | bytes 524320 | tf_op jit(solution)/shard_map/ppermute | solution.py:27
  46.7 0.1 fusion.8
  46.8 1.0 %collective-permute-start.16 = (bf16[16,4096]{1,0:T(8,128)(2,1)S(1)}, bf16[16,4096]{1,0:T(8,128)(2,1)S(1)}, u32[]{:S(2)}, u32[]{:S(2)}) collective-permute-start(bf16[16,4096]{1,0:T(8,128)(2,1)S(1)} %get-tuple-element.24), channel_id=1, source_target_pairs={{0,24},{4,28},{8,16},{12,20},{16,8},{20,12},{24,0},{28,4},{1,25},{... | collective-permute-start | bytes 393224 | tf_op jit(solution)/shard_map/ppermute | solution.py:27
  47.8 1.0 %collective-permute-start.18 = (bf16[16,4096]{1,0:T(8,128)(2,1)S(1)}, bf16[16,4096]{1,0:T(8,128)(2,1)S(1)}, u32[]{:S(2)}, u32[]{:S(2)}) collective-permute-start(bf16[16,4096]{1,0:T(8,128)(2,1)S(1)} %get-tuple-element.25), channel_id=1, source_target_pairs={{0,8},{4,12},{8,0},{12,4},{16,24},{20,28},{24,16},{28,20},{1,9},{5... | collective-permute-start | bytes 393224 | tf_op jit(solution)/shard_map/ppermute | solution.py:27
  48.9 1.5 %collective-permute-start.17 = (bf16[16,4096]{1,0:T(8,128)(2,1)S(1)}, bf16[16,4096]{1,0:T(8,128)(2,1)S(1)}, u32[]{:S(2)}, u32[]{:S(2)}) collective-permute-start(bf16[16,4096]{1,0:T(8,128)(2,1)S(1)} %get-tuple-element.26), channel_id=1, source_target_pairs={{0,16},{4,20},{8,24},{12,28},{16,0},{20,4},{24,8},{28,12},{1,17},{... | collective-permute-start | bytes 393224 | tf_op jit(solution)/shard_map/ppermute | solution.py:27
  50.4 0.0 collective-permute-done.11
  50.4 0.1 fusion.7
  50.6 1.0 %collective-permute-start.12 = (bf16[16,4096]{1,0:T(8,128)(2,1)S(1)}, bf16[16,4096]{1,0:T(8,128)(2,1)S(1)}, u32[]{:S(2)}, u32[]{:S(2)}) collective-permute-start(bf16[16,4096]{1,0:T(8,128)(2,1)S(1)} %get-tuple-element.21), channel_id=1, source_target_pairs={{0,24},{4,28},{8,16},{12,20},{16,8},{20,12},{24,0},{28,4},{1,25},{... | collective-permute-start | bytes 393224 | tf_op jit(solution)/shard_map/ppermute | solution.py:27
  51.6 1.0 %collective-permute-start.14 = (bf16[16,4096]{1,0:T(8,128)(2,1)S(1)}, bf16[16,4096]{1,0:T(8,128)(2,1)S(1)}, u32[]{:S(2)}, u32[]{:S(2)}) collective-permute-start(bf16[16,4096]{1,0:T(8,128)(2,1)S(1)} %get-tuple-element.22), channel_id=1, source_target_pairs={{0,8},{4,12},{8,0},{12,4},{16,24},{20,28},{24,16},{28,20},{1,9},{5... | collective-permute-start | bytes 393224 | tf_op jit(solution)/shard_map/ppermute | solution.py:27
  52.6 1.6 %collective-permute-done.16 = bf16[16,4096]{1,0:T(8,128)(2,1)S(1)} collective-permute-done((bf16[16,4096]{1,0:T(8,128)(2,1)S(1)}, bf16[16,4096]{1,0:T(8,128)(2,1)S(1)}, u32[]{:S(2)}, u32[]{:S(2)}) %collective-permute-start.16) | collective-permute-done | bytes 131104 | tf_op jit(solution)/shard_map/ppermute | solution.py:27
  54.1 0.5 collective-permute-start.13
  54.6 1.3 %collective-permute-done.18 = bf16[16,4096]{1,0:T(8,128)(2,1)S(1)} collective-permute-done((bf16[16,4096]{1,0:T(8,128)(2,1)S(1)}, bf16[16,4096]{1,0:T(8,128)(2,1)S(1)}, u32[]{:S(2)}, u32[]{:S(2)}) %collective-permute-start.18) | collective-permute-done | bytes 131104 | tf_op jit(solution)/shard_map/ppermute | solution.py:27
  56.0 1.1 %collective-permute-done.17 = bf16[16,4096]{1,0:T(8,128)(2,1)S(1)} collective-permute-done((bf16[16,4096]{1,0:T(8,128)(2,1)S(1)}, bf16[16,4096]{1,0:T(8,128)(2,1)S(1)}, u32[]{:S(2)}, u32[]{:S(2)}) %collective-permute-start.17) | collective-permute-done | bytes 131104 | tf_op jit(solution)/shard_map/ppermute | solution.py:27
  57.1 0.1 fusion.2
  57.1 2.8 %collective-permute-start.19 = (bf16[8,4096]{1,0:T(8,128)(2,1)S(1)}, bf16[8,4096]{1,0:T(8,128)(2,1)S(1)}, u32[]{:S(2)}, u32[]{:S(2)}) collective-permute-start(bf16[8,4096]{1,0:T(8,128)(2,1)S(1)} %get-tuple-element.27), channel_id=1, source_target_pairs={{0,2},{1,3},{2,0},{3,1},{4,6},{5,7},{6,4},{7,5},{8,10},{9,11},{10,... | collective-permute-start | bytes 196616 | tf_op jit(solution)/shard_map/ppermute | solution.py:27
  59.9 2.0 %collective-permute-start.20 = (bf16[8,4096]{1,0:T(8,128)(2,1)S(1)}, bf16[8,4096]{1,0:T(8,128)(2,1)S(1)}, u32[]{:S(2)}, u32[]{:S(2)}) collective-permute-start(bf16[8,4096]{1,0:T(8,128)(2,1)S(1)} %get-tuple-element.28), channel_id=1, source_target_pairs={{0,3},{1,2},{2,1},{3,0},{4,7},{5,6},{6,5},{7,4},{8,11},{9,10},{10,... | collective-permute-start | bytes 196616 | tf_op jit(solution)/shard_map/ppermute | solution.py:27
  62.0 0.0 collective-permute-done.12
  62.0 0.0 collective-permute-done.14
  62.0 0.0 collective-permute-done.13
  62.0 0.1 fusion.4
  62.1 2.3 %collective-permute-start.21 = (bf16[8,4096]{1,0:T(8,128)(2,1)S(1)}, bf16[8,4096]{1,0:T(8,128)(2,1)S(1)}, u32[]{:S(2)}, u32[]{:S(2)}) collective-permute-start(bf16[8,4096]{1,0:T(8,128)(2,1)S(1)} %slice.87), channel_id=1, source_target_pairs={{0,1},{1,0},{2,3},{3,2},{4,5},{5,4},{6,7},{7,6},{8,9},{9,8},{10,11... | collective-permute-start | bytes 196616 | tf_op jit(solution)/shard_map/ppermute | solution.py:27
  64.3 0.0 collective-permute-done.19
  64.3 1.8 %collective-permute-done.20 = bf16[8,4096]{1,0:T(8,128)(2,1)S(1)} collective-permute-done((bf16[8,4096]{1,0:T(8,128)(2,1)S(1)}, bf16[8,4096]{1,0:T(8,128)(2,1)S(1)}, u32[]{:S(2)}, u32[]{:S(2)}) %collective-permute-start.20) | collective-permute-done | bytes 65568 | tf_op jit(solution)/shard_map/ppermute | solution.py:27
  66.1 1.1 %collective-permute-done.21 = bf16[8,4096]{1,0:T(8,128)(2,1)S(1)} collective-permute-done((bf16[8,4096]{1,0:T(8,128)(2,1)S(1)}, bf16[8,4096]{1,0:T(8,128)(2,1)S(1)}, u32[]{:S(2)}, u32[]{:S(2)}) %collective-permute-start.21) | collective-permute-done | bytes 65568 | tf_op jit(solution)/shard_map/ppermute | solution.py:27
  67.2 0.6 fusion.6
  (16 shorter events, 0.2 us)
Async XLA Ops:
  1.4 13.1 %collective-permute-start.5 = (bf16[8,4224]{1,0:T(8,128)(2,1)S(1)}, bf16[8,4224]{1,0:T(8,128)(2,1)S(1)}, u32[]{:S(2)}, u32[]{:S(2)}) collective-permute-start(bf16[8,4224]{1,0:T(8,128)(2,1)S(1)} %shard_map.64), channel_id=1, source_target_pairs={{0,3},{1,2},{2,1},{3,0},{4,7},{5,6},{6,5},{7,4},{8,11},{9,10},{10,... | collective-permute-start | bytes 202760 | tf_op jit(solution)/shard_map/ppermute | solution.py:27
  6.5 8.0 %collective-permute-start.4 = (bf16[8,4224]{1,0:T(8,128)(2,1)S(1)}, bf16[8,4224]{1,0:T(8,128)(2,1)S(1)}, u32[]{:S(2)}, u32[]{:S(2)}) collective-permute-start(bf16[8,4224]{1,0:T(8,128)(2,1)S(1)} %shard_map.64), channel_id=1, source_target_pairs={{0,2},{1,3},{2,0},{3,1},{4,6},{5,7},{6,4},{7,5},{8,10},{9,11},{10,... | collective-permute-start | bytes 202760 | tf_op jit(solution)/shard_map/ppermute | solution.py:27
  6.5 4.4 %collective-permute-start = (bf16[8,4224]{1,0:T(8,128)(2,1)S(1)}, bf16[8,4224]{1,0:T(8,128)(2,1)S(1)}, u32[]{:S(2)}, u32[]{:S(2)}) collective-permute-start(bf16[8,4224]{1,0:T(8,128)(2,1)S(1)} %shard_map.64), channel_id=1, source_target_pairs={{0,1},{1,0},{2,3},{3,2},{4,5},{5,4},{6,7},{7,6},{8,9},{9,8},{10,11... | collective-permute-start | bytes 202760 | tf_op jit(solution)/shard_map/ppermute | solution.py:27
  10.9 11.4 %collective-permute-start.3 = (bf16[16,4224]{1,0:T(8,128)(2,1)S(1)}, bf16[16,4224]{1,0:T(8,128)(2,1)S(1)}, u32[]{:S(2)}, u32[]{:S(2)}) collective-permute-start(bf16[16,4224]{1,0:T(8,128)(2,1)S(1)} %pad_maximum_fusion), channel_id=1, source_target_pairs={{0,8},{4,12},{8,0},{12,4},{16,24},{20,28},{24,16},{28,20},{1,9},{5... | collective-permute-start | bytes 405512 | tf_op jit(solution)/shard_map/ppermute | solution.py:27
  12.5 9.8 %collective-permute-start.2 = (bf16[16,4224]{1,0:T(8,128)(2,1)S(1)}, bf16[16,4224]{1,0:T(8,128)(2,1)S(1)}, u32[]{:S(2)}, u32[]{:S(2)}) collective-permute-start(bf16[16,4224]{1,0:T(8,128)(2,1)S(1)} %pad_maximum_fusion), channel_id=1, source_target_pairs={{0,16},{4,20},{8,24},{12,28},{16,0},{20,4},{24,8},{28,12},{1,17},{... | collective-permute-start | bytes 405512 | tf_op jit(solution)/shard_map/ppermute | solution.py:27
  14.0 7.3 %collective-permute-start.1 = (bf16[16,4224]{1,0:T(8,128)(2,1)S(1)}, bf16[16,4224]{1,0:T(8,128)(2,1)S(1)}, u32[]{:S(2)}, u32[]{:S(2)}) collective-permute-start(bf16[16,4224]{1,0:T(8,128)(2,1)S(1)} %pad_maximum_fusion), channel_id=1, source_target_pairs={{0,24},{4,28},{8,16},{12,20},{16,8},{20,12},{24,0},{28,4},{1,25},{... | collective-permute-start | bytes 405512 | tf_op jit(solution)/shard_map/ppermute | solution.py:27
  14.5 12.8 %collective-permute-start.8 = (bf16[16,4224]{1,0:T(8,128)(2,1)S(1)}, bf16[16,4224]{1,0:T(8,128)(2,1)S(1)}, u32[]{:S(2)}, u32[]{:S(2)}) collective-permute-start(bf16[16,4224]{1,0:T(8,128)(2,1)S(1)} %get-tuple-element.29), channel_id=1, source_target_pairs={{0,8},{4,12},{8,0},{12,4},{16,24},{20,28},{24,16},{28,20},{1,9},{5... | collective-permute-start | bytes 405512 | tf_op jit(solution)/shard_map/ppermute | solution.py:27
  16.1 11.2 %collective-permute-start.7 = (bf16[16,4224]{1,0:T(8,128)(2,1)S(1)}, bf16[16,4224]{1,0:T(8,128)(2,1)S(1)}, u32[]{:S(2)}, u32[]{:S(2)}) collective-permute-start(bf16[16,4224]{1,0:T(8,128)(2,1)S(1)} %get-tuple-element.29), channel_id=1, source_target_pairs={{0,16},{4,20},{8,24},{12,28},{16,0},{20,4},{24,8},{28,12},{1,17},{... | collective-permute-start | bytes 405512 | tf_op jit(solution)/shard_map/ppermute | solution.py:27
  21.3 5.9 %collective-permute-start.6 = (bf16[16,4224]{1,0:T(8,128)(2,1)S(1)}, bf16[16,4224]{1,0:T(8,128)(2,1)S(1)}, u32[]{:S(2)}, u32[]{:S(2)}) collective-permute-start(bf16[16,4224]{1,0:T(8,128)(2,1)S(1)} %get-tuple-element.29), channel_id=1, source_target_pairs={{0,24},{4,28},{8,16},{12,20},{16,8},{20,12},{24,0},{28,4},{1,25},{... | collective-permute-start | bytes 405512 | tf_op jit(solution)/shard_map/ppermute | solution.py:27
  22.3 5.1 %collective-permute-start.9 = (bf16[64,4224]{1,0:T(8,128)(2,1)S(1)}, bf16[64,4224]{1,0:T(8,128)(2,1)S(1)}, u32[]{:S(2)}, u32[]{:S(2)}) collective-permute-start(bf16[64,4224]{1,0:T(8,128)(2,1)S(1)} %constant_dynamic-update-slice_fusion.refs_0_), channel_id=1, source_target_pairs={{0,4},{4,0},{8,12},{12,8},{16,20},{20,16},{24,28},{28,24},{1,5},{5... | collective-permute-start | bytes 1622024 | tf_op jit(solution)/shard_map/ppermute | solution.py:27
  27.3 2.0 %collective-permute-start.10 = (bf16[64,4224]{1,0:T(8,128)(2,1)S(1)}, bf16[64,4224]{1,0:T(8,128)(2,1)S(1)}, u32[]{:S(2)}, u32[]{:S(2)}) collective-permute-start(bf16[64,4224]{1,0:T(8,128)(2,1)S(1)} %constant_dynamic-update-slice_fusion.7.refs_1_), channel_id=1, source_target_pairs={{0,4},{4,0},{8,12},{12,8},{16,20},{20,16},{24,28},{28,24},{1,5},{5... | collective-permute-start | bytes 1622024 | tf_op jit(solution)/shard_map/ppermute | solution.py:27
  29.3 2.8 %copy-start = (bf16[2,384,4096]{2,1,0:T(8,128)(2,1)S(1)}, bf16[2,384,4096]{2,1,0:T(8,128)(2,1)}, u32[]{:S(2)}) copy-start(bf16[2,384,4096]{2,1,0:T(8,128)(2,1)} %refs_4_.1) | copy-start | bytes 18874372
  32.1 2.8 %copy-start.1 = (bf16[2,384,4096]{2,1,0:T(8,128)(2,1)S(1)}, bf16[2,384,4096]{2,1,0:T(8,128)(2,1)}, u32[]{:S(2)}) copy-start(bf16[2,384,4096]{2,1,0:T(8,128)(2,1)} %refs_5_.1) | copy-start | bytes 18874372
  34.9 2.8 %copy-start.2 = (bf16[2,384,4096]{2,1,0:T(8,128)(2,1)S(1)}, bf16[2,384,4096]{2,1,0:T(8,128)(2,1)}, u32[]{:S(2)}) copy-start(bf16[2,384,4096]{2,1,0:T(8,128)(2,1)} %refs_6_.1) | copy-start | bytes 18874372
  44.7 2.0 %collective-permute-start.15 = (bf16[64,4096]{1,0:T(8,128)(2,1)S(1)}, bf16[64,4096]{1,0:T(8,128)(2,1)S(1)}, u32[]{:S(2)}, u32[]{:S(2)}) collective-permute-start(bf16[64,4096]{1,0:T(8,128)(2,1)S(1)} %get-tuple-element.14), channel_id=1, source_target_pairs={{0,4},{4,0},{8,12},{12,8},{16,20},{20,16},{24,28},{28,24},{1,5},{5... | collective-permute-start | bytes 1572872 | tf_op jit(solution)/shard_map/ppermute | solution.py:27
  44.9 5.5 %collective-permute-start.11 = (bf16[64,4096]{1,0:T(8,128)(2,1)S(1)}, bf16[64,4096]{1,0:T(8,128)(2,1)S(1)}, u32[]{:S(2)}, u32[]{:S(2)}) collective-permute-start(bf16[64,4096]{1,0:T(8,128)(2,1)S(1)} %get-tuple-element.12), channel_id=1, source_target_pairs={{0,4},{4,0},{8,12},{12,8},{16,20},{20,16},{24,28},{28,24},{1,5},{5... | collective-permute-start | bytes 1572872 | tf_op jit(solution)/shard_map/ppermute | solution.py:27
  46.8 7.3 %collective-permute-start.16 = (bf16[16,4096]{1,0:T(8,128)(2,1)S(1)}, bf16[16,4096]{1,0:T(8,128)(2,1)S(1)}, u32[]{:S(2)}, u32[]{:S(2)}) collective-permute-start(bf16[16,4096]{1,0:T(8,128)(2,1)S(1)} %get-tuple-element.24), channel_id=1, source_target_pairs={{0,24},{4,28},{8,16},{12,20},{16,8},{20,12},{24,0},{28,4},{1,25},{... | collective-permute-start | bytes 393224 | tf_op jit(solution)/shard_map/ppermute | solution.py:27
  47.8 8.1 %collective-permute-start.18 = (bf16[16,4096]{1,0:T(8,128)(2,1)S(1)}, bf16[16,4096]{1,0:T(8,128)(2,1)S(1)}, u32[]{:S(2)}, u32[]{:S(2)}) collective-permute-start(bf16[16,4096]{1,0:T(8,128)(2,1)S(1)} %get-tuple-element.25), channel_id=1, source_target_pairs={{0,8},{4,12},{8,0},{12,4},{16,24},{20,28},{24,16},{28,20},{1,9},{5... | collective-permute-start | bytes 393224 | tf_op jit(solution)/shard_map/ppermute | solution.py:27
  48.9 8.2 %collective-permute-start.17 = (bf16[16,4096]{1,0:T(8,128)(2,1)S(1)}, bf16[16,4096]{1,0:T(8,128)(2,1)S(1)}, u32[]{:S(2)}, u32[]{:S(2)}) collective-permute-start(bf16[16,4096]{1,0:T(8,128)(2,1)S(1)} %get-tuple-element.26), channel_id=1, source_target_pairs={{0,16},{4,20},{8,24},{12,28},{16,0},{20,4},{24,8},{28,12},{1,17},{... | collective-permute-start | bytes 393224 | tf_op jit(solution)/shard_map/ppermute | solution.py:27
  50.6 11.4 %collective-permute-start.12 = (bf16[16,4096]{1,0:T(8,128)(2,1)S(1)}, bf16[16,4096]{1,0:T(8,128)(2,1)S(1)}, u32[]{:S(2)}, u32[]{:S(2)}) collective-permute-start(bf16[16,4096]{1,0:T(8,128)(2,1)S(1)} %get-tuple-element.21), channel_id=1, source_target_pairs={{0,24},{4,28},{8,16},{12,20},{16,8},{20,12},{24,0},{28,4},{1,25},{... | collective-permute-start | bytes 393224 | tf_op jit(solution)/shard_map/ppermute | solution.py:27
  51.6 10.4 %collective-permute-start.14 = (bf16[16,4096]{1,0:T(8,128)(2,1)S(1)}, bf16[16,4096]{1,0:T(8,128)(2,1)S(1)}, u32[]{:S(2)}, u32[]{:S(2)}) collective-permute-start(bf16[16,4096]{1,0:T(8,128)(2,1)S(1)} %get-tuple-element.22), channel_id=1, source_target_pairs={{0,8},{4,12},{8,0},{12,4},{16,24},{20,28},{24,16},{28,20},{1,9},{5... | collective-permute-start | bytes 393224 | tf_op jit(solution)/shard_map/ppermute | solution.py:27
  54.1 7.8 %collective-permute-start.13 = (bf16[16,4096]{1,0:T(8,128)(2,1)S(1)}, bf16[16,4096]{1,0:T(8,128)(2,1)S(1)}, u32[]{:S(2)}, u32[]{:S(2)}) collective-permute-start(bf16[16,4096]{1,0:T(8,128)(2,1)S(1)} %get-tuple-element.23), channel_id=1, source_target_pairs={{0,16},{4,20},{8,24},{12,28},{16,0},{20,4},{24,8},{28,12},{1,17},{... | collective-permute-start | bytes 393224 | tf_op jit(solution)/shard_map/ppermute | solution.py:27
  57.1 7.2 %collective-permute-start.19 = (bf16[8,4096]{1,0:T(8,128)(2,1)S(1)}, bf16[8,4096]{1,0:T(8,128)(2,1)S(1)}, u32[]{:S(2)}, u32[]{:S(2)}) collective-permute-start(bf16[8,4096]{1,0:T(8,128)(2,1)S(1)} %get-tuple-element.27), channel_id=1, source_target_pairs={{0,2},{1,3},{2,0},{3,1},{4,6},{5,7},{6,4},{7,5},{8,10},{9,11},{10,... | collective-permute-start | bytes 196616 | tf_op jit(solution)/shard_map/ppermute | solution.py:27
  59.9 6.2 %collective-permute-start.20 = (bf16[8,4096]{1,0:T(8,128)(2,1)S(1)}, bf16[8,4096]{1,0:T(8,128)(2,1)S(1)}, u32[]{:S(2)}, u32[]{:S(2)}) collective-permute-start(bf16[8,4096]{1,0:T(8,128)(2,1)S(1)} %get-tuple-element.28), channel_id=1, source_target_pairs={{0,3},{1,2},{2,1},{3,0},{4,7},{5,6},{6,5},{7,4},{8,11},{9,10},{10,... | collective-permute-start | bytes 196616 | tf_op jit(solution)/shard_map/ppermute | solution.py:27
  62.1 5.2 %collective-permute-start.21 = (bf16[8,4096]{1,0:T(8,128)(2,1)S(1)}, bf16[8,4096]{1,0:T(8,128)(2,1)S(1)}, u32[]{:S(2)}, u32[]{:S(2)}) collective-permute-start(bf16[8,4096]{1,0:T(8,128)(2,1)S(1)} %slice.87), channel_id=1, source_target_pairs={{0,1},{1,0},{2,3},{3,2},{4,5},{5,4},{6,7},{7,6},{8,9},{9,8},{10,11... | collective-permute-start | bytes 196616 | tf_op jit(solution)/shard_map/ppermute | solution.py:27
where the time goes:
time: 68.1 us; the launch traced here: 67.9 us
  starting transfers between devices  27.2 us (40%)
  waiting for transfers between devices  22.5 us (33%)
  local copies, waits for them, and re-layouts  8.58 us (13%)
  Pallas kernels  8.41 us (12%)
  other arithmetic  1.05 us (2%)
    ppermute x22, starting transfers between devices, swap(): return lax.ppermute(value, axis, [(i, i ^ mask) for i in range(count)])  27.2 us
    ppermute x22, waiting for transfers between devices, swap(): return lax.ppermute(value, axis, [(i, i ^ mask) for i in range(count)])  22.5 us
    unnamed x13, local copies, waits for them, and re-layouts  8.45 us
    pallas_call x1, Pallas kernels, run_experts(): pl.pallas_call(functools.partial(expert_kernel, exp_dev, expert_total, le...  7.01 us
    pallas_call x1, Pallas kernels, pack(): pl.pallas_call(pack_kernel, out_shape=pltpu.VMEM((rows, width + extra), t...  1.4 us
  transfers between devices with their start and end apart: 22, of which 10 were waited for; matrix products, arithmetic and copies ran while one was open for 1% of the time, Pallas kernels for 0%

commit v1 on v0

--- a/solution.py
+++ b/solution.py
@@ -10,7 +10,8 @@
 LANES = 128
 ROWS = 256
 TERMS = 3
-VMEM_BYTES = 30 * 1024 * 1024
+VMEM_BYTES = 24 * 1024 * 1024
+SMALL_BYTES = 2 * 1024 * 1024
 EXCHANGE_FLOPS = 20_000_000_000
 IN_VMEM = pl.BlockSpec(memory_space=pltpu.VMEM)
 ANYWHERE = pl.BlockSpec(memory_space=pl.ANY)
@@ -51,17 +52,17 @@
     return [value[start : start + step] for start in range(0, value.shape[0], step)]
 
 
-def gather_rows(block, w_gate, w_up, w_down):
+def gather_rows(block):
     depth = lax.axis_size("expert")
     column = [block] + [swap(block, "expert", mask) for mask in range(1, depth)]
-    near, column = cat(column[: depth // 2]), column[depth // 2 :]
+    near = join(column[: depth // 2])
     near_rest = [swap(near, *step) for step in plane_steps()]
-    far = cat(column)
+    far = cat(column[depth // 2 :])
     far_rest = [swap(far, *step) for step in plane_steps()]
     near = cat([near, *near_rest])
     near_there = swap(near, *CORE)
     far = cat([far, *far_rest])
-    return [near, far, near_there, swap(far, *CORE)], [w_gate, w_up, w_down]
+    return [near, far, near_there, swap(far, *CORE)]
 
 
 def scatter_sums(kept, away):
@@ -123,14 +124,38 @@
             *[pltpu.VMEM(value.shape, value.dtype) for value in (tokens, expert_ids, router)],
             pltpu.SemaphoreType.DMA((3,)),
         ],
+        compiler_params=pltpu.CompilerParams(vmem_limit_bytes=SMALL_BYTES),
         cost_estimate=pl.CostEstimate(
-            flops=EXCHANGE_FLOPS, bytes_accessed=4 * router.size, transcendentals=0
+            flops=2 * rows * router.size, bytes_accessed=4 * router.size, transcendentals=0
         ),
     )(*[pltpu.with_memory_space_constraint(v, pltpu.HBM) for v in (tokens, expert_ids, router)])
 
 
+def join_kernel(*refs):
+    *parts, joined_ref = refs
+    start = 0
+    for part in parts:
+        joined_ref[start : start + part.shape[0]] = part[...]
+        start += part.shape[0]
+
+
+def join(parts):
+    rows, width = sum(part.shape[0] for part in parts), parts[0].shape[1]
+    return pl.pallas_call(
+        join_kernel,
+        out_shape=pltpu.VMEM((rows, width), parts[0].dtype),
+        in_specs=[IN_VMEM] * len(parts),
+        out_specs=IN_VMEM,
+        compiler_params=pltpu.CompilerParams(vmem_limit_bytes=SMALL_BYTES),
+        cost_estimate=pl.CostEstimate(
+            flops=EXCHANGE_FLOPS, bytes_accessed=0, transcendentals=0
+        ),
+    )(*parts)
+
+
 def expert_kernel(exp_dev, expert_total, parts, *refs):
-    pieces, (gate_ref, up_ref, down_ref, *results, rows_ref) = refs[:parts], refs[parts:]
+    pieces, refs = refs[:parts], refs[parts:]
+    gate_ref, up_ref, down_ref, *results, rows_ref = refs
     units, width = down_ref.shape[1:]
     start = 0
     for piece in pieces:
@@ -167,30 +192,29 @@
             start = stop
 
 
-def run_experts(pieces, kinds, expert_total, held):
+def run_experts(pieces, kinds, expert_total, w_gate, w_up, w_down):
     rows = sum(piece.shape[0] for piece in pieces)
-    gate, up, down = held
-    exp_dev, width = down.shape[0], down.shape[2]
+    exp_dev, _, width = w_down.shape
     place = pltpu.VMEM if len(pieces) > 1 else jax.ShapeDtypeStruct
     return pl.pallas_call(
         functools.partial(expert_kernel, exp_dev, expert_total, len(pieces)),
         out_shape=[
             place((piece.shape[0], width), kind) for piece, kind in zip(pieces, kinds)
         ],
-        in_specs=[IN_VMEM] * (len(pieces) + len(held)),
+        in_specs=[IN_VMEM] * (len(pieces) + 3),
         out_specs=[IN_VMEM] * len(pieces),
         scratch_shapes=[pltpu.VMEM((rows, pieces[0].shape[1]), jnp.bfloat16)],
         compiler_params=pltpu.CompilerParams(vmem_limit_bytes=VMEM_BYTES),
         cost_estimate=pl.CostEstimate(
-            flops=6 * rows * down.size, bytes_accessed=rows * width * 5, transcendentals=0
+            flops=6 * rows * w_down.size, bytes_accessed=rows * width * 5, transcendentals=0
         ),
-    )(*pieces, gate, up, down)
+    )(*pieces, w_gate, w_up, w_down)
 
 
 def body(tokens, expert_ids, router, w_gate, w_up, w_down):
-    pieces, held = gather_rows(pack(tokens, expert_ids, router), w_gate, w_up, w_down)
+    pieces = gather_rows(pack(tokens, expert_ids, router))
     kinds = [jnp.float32] * 2 + [jnp.bfloat16] * 2
-    operands = (router.shape[0], held)
+    operands = (router.shape[0], w_gate, w_up, w_down)
     if sum(piece.shape[0] for piece in pieces) <= ROWS:
         results = run_experts(pieces, kinds, *operands)
     else:

time: 68.1 us -> 56 us (0.82)
  local copies, waits for them, and re-layouts: 8.58 us -> 0.19 us
  starting transfers between devices: 27.2 us -> 25.2 us
  waiting for transfers between devices: 22.5 us -> 20.6 us
    unnamed x13 -> x15, local copies, waits for them, and re-layouts: 8.45 us -> 0.08 us
    ppermute x22, starting transfers between devices: 27.2 us -> 25.2 us  [swap(): return lax.ppermute(value, axis, [(i, i ^ mask) for i in range(count)])]
    ppermute x22, waiting for transfers between devices: 22.5 us -> 20.6 us  [swap(): return lax.ppermute(value, axis, [(i, i ^ mask) for i in range(count)])]
where the time goes in v1:
time: 56 us; the launch traced here: 55.9 us
  starting transfers between devices  25.2 us (45%)
  waiting for transfers between devices  20.6 us (37%)
  Pallas kernels  8.56 us (15%)
  other arithmetic  1.08 us (2%)
    ppermute x22, starting transfers between devices, swap(): return lax.ppermute(value, axis, [(i, i ^ mask) for i in range(count)])  25.2 us
    ppermute x22, waiting for transfers between devices, swap(): return lax.ppermute(value, axis, [(i, i ^ mask) for i in range(count)])  20.6 us
    pallas_call x1, Pallas kernels, run_experts(): pl.pallas_call(functools.partial(expert_kernel, exp_dev, expert_total, le...  7.01 us
    pallas_call x1, Pallas kernels, pack(): pl.pallas_call(pack_kernel, out_shape=pltpu.VMEM((rows, width + extra), t...  1.54 us
  transfers between devices with their start and end apart: 22, of which 10 were waited for; matrix products, arithmetic and copies ran while one was open for 1% of the time, Pallas kernels for 0%

profile of v1, /device:TPU:0, one launch (start us, length us, event | category | flops | bytes accessed | tf_op | source)
XLA Modules:
  0.0 55.9 jit_solution(10817874742109993481)
XLA Ops:
  0.0 0.0 slice-start
  0.0 0.0 slice-start.2
  0.0 0.0 slice-start.4
  0.0 1.5 %shard_map.64.refs_0_ = bf16[8,4224]{1,0:T(8,128)(2,1)S(1)} custom-call(bf16[8,4096]{1,0:T(8,128)(2,1)} %tokens_hbm.1, s32[8,8]{1,0:T(8,128)} %ids_hbm.1, bf16[16,4096]{1,0:T(8,128)(2,1)} %router_hbm.1), custom_call_target="tpu_custom_call" | custom-call | flops 1048576 | bytes 262144 | tf_op jit(solution)/shard_map/pallas_call | solution.py:118
  1.6 0.0 slice-start.1
  1.6 0.0 slice-start.3
  1.6 0.0 slice-start.5
  1.6 3.1 %collective-permute-start = (bf16[8,4224]{1,0:T(8,128)(2,1)S(1)}, bf16[8,4224]{1,0:T(8,128)(2,1)S(1)}, u32[]{:S(2)}, u32[]{:S(2)}) collective-permute-start(bf16[8,4224]{1,0:T(8,128)(2,1)S(1)} %shard_map.64.refs_0_), channel_id=1, source_target_pairs={{0,1},{1,0},{2,3},{3,2},{4,5},{5,4},{6,7},{7,6},{8,9},{9,8},{10,11... | collective-permute-start | bytes 202760 | tf_op jit(solution)/shard_map/ppermute | solution.py:28
  4.7 2.5 %collective-permute-start.5 = (bf16[8,4224]{1,0:T(8,128)(2,1)S(1)}, bf16[8,4224]{1,0:T(8,128)(2,1)S(1)}, u32[]{:S(2)}, u32[]{:S(2)}) collective-permute-start(bf16[8,4224]{1,0:T(8,128)(2,1)S(1)} %shard_map.64.refs_0_), channel_id=1, source_target_pairs={{0,3},{1,2},{2,1},{3,0},{4,7},{5,6},{6,5},{7,4},{8,11},{9,10},{10,... | collective-permute-start | bytes 202760 | tf_op jit(solution)/shard_map/ppermute | solution.py:28
  7.2 0.1 collective-permute-start.4
  7.3 0.0 collective-permute-done.refs_1_
  7.3 1.7 %collective-permute-start.3 = (bf16[16,4224]{1,0:T(8,128)(2,1)S(1)}, bf16[16,4224]{1,0:T(8,128)(2,1)S(1)}, u32[]{:S(2)}, u32[]{:S(2)}) collective-permute-start(bf16[16,4224]{1,0:T(8,128)(2,1)S(1)} %shard_map.65), channel_id=1, source_target_pairs={{0,8},{4,12},{8,0},{12,4},{16,24},{20,28},{24,16},{28,20},{1,9},{5... | collective-permute-start | bytes 405512 | tf_op jit(solution)/shard_map/ppermute | solution.py:28
  9.0 1.5 %collective-permute-start.2 = (bf16[16,4224]{1,0:T(8,128)(2,1)S(1)}, bf16[16,4224]{1,0:T(8,128)(2,1)S(1)}, u32[]{:S(2)}, u32[]{:S(2)}) collective-permute-start(bf16[16,4224]{1,0:T(8,128)(2,1)S(1)} %shard_map.65), channel_id=1, source_target_pairs={{0,16},{4,20},{8,24},{12,28},{16,0},{20,4},{24,8},{28,12},{1,17},{... | collective-permute-start | bytes 405512 | tf_op jit(solution)/shard_map/ppermute | solution.py:28
  10.5 0.4 collective-permute-start.1
  10.9 2.9 %collective-permute-done.4 = bf16[8,4224]{1,0:T(8,128)(2,1)S(1)} collective-permute-done((bf16[8,4224]{1,0:T(8,128)(2,1)S(1)}, bf16[8,4224]{1,0:T(8,128)(2,1)S(1)}, u32[]{:S(2)}, u32[]{:S(2)}) %collective-permute-start.4) | collective-permute-done | bytes 67616 | tf_op jit(solution)/shard_map/ppermute | solution.py:28
  13.8 0.0 collective-permute-done.5
  13.8 1.6 %collective-permute-start.8 = (bf16[16,4224]{1,0:T(8,128)(2,1)S(1)}, bf16[16,4224]{1,0:T(8,128)(2,1)S(1)}, u32[]{:S(2)}, u32[]{:S(2)}) collective-permute-start(bf16[16,4224]{1,0:T(8,128)(2,1)S(1)} %get-tuple-element.29), channel_id=1, source_target_pairs={{0,8},{4,12},{8,0},{12,4},{16,24},{20,28},{24,16},{28,20},{1,9},{5... | collective-permute-start | bytes 405512 | tf_op jit(solution)/shard_map/ppermute | solution.py:28
  15.4 1.5 %collective-permute-start.7 = (bf16[16,4224]{1,0:T(8,128)(2,1)S(1)}, bf16[16,4224]{1,0:T(8,128)(2,1)S(1)}, u32[]{:S(2)}, u32[]{:S(2)}) collective-permute-start(bf16[16,4224]{1,0:T(8,128)(2,1)S(1)} %get-tuple-element.29), channel_id=1, source_target_pairs={{0,16},{4,20},{8,24},{12,28},{16,0},{20,4},{24,8},{28,12},{1,17},{... | collective-permute-start | bytes 405512 | tf_op jit(solution)/shard_map/ppermute | solution.py:28
  16.9 0.0 collective-permute-done.3
  16.9 0.5 collective-permute-start.6
  17.4 0.0 collective-permute-done.2
  17.4 0.0 collective-permute-done.1
  17.4 0.1 collective-permute-start.9
  17.5 5.8 %collective-permute-done.6 = bf16[16,4224]{1,0:T(8,128)(2,1)S(1)} collective-permute-done((bf16[16,4224]{1,0:T(8,128)(2,1)S(1)}, bf16[16,4224]{1,0:T(8,128)(2,1)S(1)}, u32[]{:S(2)}, u32[]{:S(2)}) %collective-permute-start.6) | collective-permute-done | bytes 135200 | tf_op jit(solution)/shard_map/ppermute | solution.py:28
  23.3 0.1 collective-permute-done.7
  23.4 0.0 collective-permute-done.8
  23.5 0.1 collective-permute-start.10
  23.6 0.0 collective-permute-done.9.refs_2_
  23.6 1.9 %collective-permute-done.10.refs_3_ = bf16[64,4224]{1,0:T(8,128)(2,1)S(1)} collective-permute-done((bf16[64,4224]{1,0:T(8,128)(2,1)S(1)}, bf16[64,4224]{1,0:T(8,128)(2,1)S(1)}, u32[]{:S(2)}, u32[]{:S(2)}) %collective-permute-start.10) | collective-permute-done | bytes 540704 | tf_op jit(solution)/shard_map/ppermute | solution.py:28
  25.5 0.0 slice-done
  25.5 0.0 slice-done.2
  25.5 0.0 slice-done.4
  25.5 0.0 slice-done.1
  25.5 0.0 slice-done.3
  25.5 0.0 slice-done.5
  25.5 7.0 %shard_map.66 = (f32[64,4096]{1,0:T(8,128)S(1)}, f32[64,4096]{1,0:T(8,128)S(1)}, bf16[64,4096]{1,0:T(8,128)(2,1)S(1)}, bf16[64,4096]{1,0:T(8,128)(2,1)S(1)}) custom-call(bf16[64,4224]{1,0:T(8,128)(2,1)S(1)} %pad_maximum_fusion.refs_0_, bf16[64,4224]{1,0:T(8,128)(2,1)S(1)} %constant_dynamic-update-slice_fusion.2.refs_1_, ...), custom_call_target="tpu_custom_call" | custom-call | flops 4831838208 | bytes 5242880 | tf_op jit(solution)/shard_map/pallas_call | solution.py:199
  32.6 0.2 collective-permute-start.15
  32.8 0.4 collective-permute-start.11
  33.1 1.4 %collective-permute-done.15 = bf16[64,4096]{1,0:T(8,128)(2,1)S(1)} collective-permute-done((bf16[64,4096]{1,0:T(8,128)(2,1)S(1)}, bf16[64,4096]{1,0:T(8,128)(2,1)S(1)}, u32[]{:S(2)}, u32[]{:S(2)}) %collective-permute-start.15) | collective-permute-done | bytes 524320 | tf_op jit(solution)/shard_map/ppermute | solution.py:28
  34.5 0.1 fusion.8
  34.7 1.6 %collective-permute-start.16 = (bf16[16,4096]{1,0:T(8,128)(2,1)S(1)}, bf16[16,4096]{1,0:T(8,128)(2,1)S(1)}, u32[]{:S(2)}, u32[]{:S(2)}) collective-permute-start(bf16[16,4096]{1,0:T(8,128)(2,1)S(1)} %get-tuple-element.24), channel_id=1, source_target_pairs={{0,24},{4,28},{8,16},{12,20},{16,8},{20,12},{24,0},{28,4},{1,25},{... | collective-permute-start | bytes 393224 | tf_op jit(solution)/shard_map/ppermute | solution.py:28
  36.3 1.5 %collective-permute-start.18 = (bf16[16,4096]{1,0:T(8,128)(2,1)S(1)}, bf16[16,4096]{1,0:T(8,128)(2,1)S(1)}, u32[]{:S(2)}, u32[]{:S(2)}) collective-permute-start(bf16[16,4096]{1,0:T(8,128)(2,1)S(1)} %get-tuple-element.25), channel_id=1, source_target_pairs={{0,8},{4,12},{8,0},{12,4},{16,24},{20,28},{24,16},{28,20},{1,9},{5... | collective-permute-start | bytes 393224 | tf_op jit(solution)/shard_map/ppermute | solution.py:28
  37.7 0.5 collective-permute-start.17
  38.3 0.0 collective-permute-done.11
  38.3 0.1 fusion.7
  38.4 1.6 %collective-permute-start.12 = (bf16[16,4096]{1,0:T(8,128)(2,1)S(1)}, bf16[16,4096]{1,0:T(8,128)(2,1)S(1)}, u32[]{:S(2)}, u32[]{:S(2)}) collective-permute-start(bf16[16,4096]{1,0:T(8,128)(2,1)S(1)} %get-tuple-element.21), channel_id=1, source_target_pairs={{0,24},{4,28},{8,16},{12,20},{16,8},{20,12},{24,0},{28,4},{1,25},{... | collective-permute-start | bytes 393224 | tf_op jit(solution)/shard_map/ppermute | solution.py:28
  40.0 1.5 %collective-permute-start.14 = (bf16[16,4096]{1,0:T(8,128)(2,1)S(1)}, bf16[16,4096]{1,0:T(8,128)(2,1)S(1)}, u32[]{:S(2)}, u32[]{:S(2)}) collective-permute-start(bf16[16,4096]{1,0:T(8,128)(2,1)S(1)} %get-tuple-element.22), channel_id=1, source_target_pairs={{0,8},{4,12},{8,0},{12,4},{16,24},{20,28},{24,16},{28,20},{1,9},{5... | collective-permute-start | bytes 393224 | tf_op jit(solution)/shard_map/ppermute | solution.py:28
  41.5 0.5 collective-permute-done.16
  42.0 1.5 %collective-permute-start.13 = (bf16[16,4096]{1,0:T(8,128)(2,1)S(1)}, bf16[16,4096]{1,0:T(8,128)(2,1)S(1)}, u32[]{:S(2)}, u32[]{:S(2)}) collective-permute-start(bf16[16,4096]{1,0:T(8,128)(2,1)S(1)} %get-tuple-element.23), channel_id=1, source_target_pairs={{0,16},{4,20},{8,24},{12,28},{16,0},{20,4},{24,8},{28,12},{1,17},{... | collective-permute-start | bytes 393224 | tf_op jit(solution)/shard_map/ppermute | solution.py:28
  43.5 1.3 %collective-permute-done.18 = bf16[16,4096]{1,0:T(8,128)(2,1)S(1)} collective-permute-done((bf16[16,4096]{1,0:T(8,128)(2,1)S(1)}, bf16[16,4096]{1,0:T(8,128)(2,1)S(1)}, u32[]{:S(2)}, u32[]{:S(2)}) %collective-permute-start.18) | collective-permute-done | bytes 131104 | tf_op jit(solution)/shard_map/ppermute | solution.py:28
  44.9 2.1 %collective-permute-done.17 = bf16[16,4096]{1,0:T(8,128)(2,1)S(1)} collective-permute-done((bf16[16,4096]{1,0:T(8,128)(2,1)S(1)}, bf16[16,4096]{1,0:T(8,128)(2,1)S(1)}, u32[]{:S(2)}, u32[]{:S(2)}) %collective-permute-start.17) | collective-permute-done | bytes 131104 | tf_op jit(solution)/shard_map/ppermute | solution.py:28
  47.0 0.1 fusion.2
  47.1 1.5 %collective-permute-start.19 = (bf16[8,4096]{1,0:T(8,128)(2,1)S(1)}, bf16[8,4096]{1,0:T(8,128)(2,1)S(1)}, u32[]{:S(2)}, u32[]{:S(2)}) collective-permute-start(bf16[8,4096]{1,0:T(8,128)(2,1)S(1)} %get-tuple-element.27), channel_id=1, source_target_pairs={{0,2},{1,3},{2,0},{3,1},{4,6},{5,7},{6,4},{7,5},{8,10},{9,11},{10,... | collective-permute-start | bytes 196616 | tf_op jit(solution)/shard_map/ppermute | solution.py:28
  48.6 1.1 %collective-permute-start.20 = (bf16[8,4096]{1,0:T(8,128)(2,1)S(1)}, bf16[8,4096]{1,0:T(8,128)(2,1)S(1)}, u32[]{:S(2)}, u32[]{:S(2)}) collective-permute-start(bf16[8,4096]{1,0:T(8,128)(2,1)S(1)} %get-tuple-element.28), channel_id=1, source_target_pairs={{0,3},{1,2},{2,1},{3,0},{4,7},{5,6},{6,5},{7,4},{8,11},{9,10},{10,... | collective-permute-start | bytes 196616 | tf_op jit(solution)/shard_map/ppermute | solution.py:28
  49.7 0.0 collective-permute-done.12
  49.7 0.0 collective-permute-done.14
  49.7 0.0 collective-permute-done.13
  49.7 0.1 fusion.4
  49.8 1.0 %collective-permute-start.21 = (bf16[8,4096]{1,0:T(8,128)(2,1)S(1)}, bf16[8,4096]{1,0:T(8,128)(2,1)S(1)}, u32[]{:S(2)}, u32[]{:S(2)}) collective-permute-start(bf16[8,4096]{1,0:T(8,128)(2,1)S(1)} %slice.87), channel_id=1, source_target_pairs={{0,1},{1,0},{2,3},{3,2},{4,5},{5,4},{6,7},{7,6},{8,9},{9,8},{10,11... | collective-permute-start | bytes 196616 | tf_op jit(solution)/shard_map/ppermute | solution.py:28
  50.8 2.3 %collective-permute-done.19 = bf16[8,4096]{1,0:T(8,128)(2,1)S(1)} collective-permute-done((bf16[8,4096]{1,0:T(8,128)(2,1)S(1)}, bf16[8,4096]{1,0:T(8,128)(2,1)S(1)}, u32[]{:S(2)}, u32[]{:S(2)}) %collective-permute-start.19) | collective-permute-done | bytes 65568 | tf_op jit(solution)/shard_map/ppermute | solution.py:28
  53.1 2.1 %collective-permute-done.20 = bf16[8,4096]{1,0:T(8,128)(2,1)S(1)} collective-permute-done((bf16[8,4096]{1,0:T(8,128)(2,1)S(1)}, bf16[8,4096]{1,0:T(8,128)(2,1)S(1)}, u32[]{:S(2)}, u32[]{:S(2)}) %collective-permute-start.20) | collective-permute-done | bytes 65568 | tf_op jit(solution)/shard_map/ppermute | solution.py:28
  55.2 0.0 collective-permute-done.21
  55.2 0.6 %fusion.6 = bf16[8,4096]{1,0:T(8,128)(2,1)} fusion(f32[8,4096]{1,0:T(8,128)S(1)} %convert_add_fusion.2, f32[16,4096]{1,0:T(8,128)S(1)} %fusion.4, bf16[8,4096]{1,0:T(8,128)(2,1)S(1)} %collective-permute-done.21), kind=kLoop, calls=%fused_computation.13 | loop fusion | flops 131072 | bytes 393216 | tf_op jit(solution)/shard_map/convert_element_type | solution.py:80
  (15 shorter events, 0.2 us)
Async XLA Ops:
  0.0 25.5 %slice-start = ((s8[6291456]{0:T(1024)(128)(4,1)}), s8[4194304]{0:T(1024)(128)(4,1)S(1)}, s32[]{:S(2)}) async-start(s8[6291456]{0:T(1024)(128)(4,1)} %bitcast), calls=%async_computation | async-start | bytes 8388608
  0.0 25.5 %slice-start.2 = ((s8[6291456]{0:T(1024)(128)(4,1)}), s8[4194304]{0:T(1024)(128)(4,1)S(1)}, s32[]{:S(2)}) async-start(s8[6291456]{0:T(1024)(128)(4,1)} %bitcast.2), calls=%async_computation.2 | async-start | bytes 8388608
  0.0 25.5 %slice-start.4 = ((s8[6291456]{0:T(1024)(128)(4,1)}), s8[4194304]{0:T(1024)(128)(4,1)S(1)}, s32[]{:S(2)}) async-start(s8[6291456]{0:T(1024)(128)(4,1)} %bitcast.4), calls=%async_computation.4 | async-start | bytes 8388608
  1.6 23.9 %slice-start.1 = ((s8[6291456]{0:T(1024)(128)(4,1)}), s8[2097152]{0:T(1024)(128)(4,1)S(1)}, s32[]{:S(2)}) async-start(s8[6291456]{0:T(1024)(128)(4,1)} %bitcast), calls=%async_computation.1 | async-start | bytes 4194304
  1.6 23.9 %slice-start.3 = ((s8[6291456]{0:T(1024)(128)(4,1)}), s8[2097152]{0:T(1024)(128)(4,1)S(1)}, s32[]{:S(2)}) async-start(s8[6291456]{0:T(1024)(128)(4,1)} %bitcast.2), calls=%async_computation.3 | async-start | bytes 4194304
  1.6 23.9 %slice-start.5 = ((s8[6291456]{0:T(1024)(128)(4,1)}), s8[2097152]{0:T(1024)(128)(4,1)S(1)}, s32[]{:S(2)}) async-start(s8[6291456]{0:T(1024)(128)(4,1)} %bitcast.4), calls=%async_computation.5 | async-start | bytes 4194304
  1.6 5.7 %collective-permute-start = (bf16[8,4224]{1,0:T(8,128)(2,1)S(1)}, bf16[8,4224]{1,0:T(8,128)(2,1)S(1)}, u32[]{:S(2)}, u32[]{:S(2)}) collective-permute-start(bf16[8,4224]{1,0:T(8,128)(2,1)S(1)} %shard_map.64.refs_0_), channel_id=1, source_target_pairs={{0,1},{1,0},{2,3},{3,2},{4,5},{5,4},{6,7},{7,6},{8,9},{9,8},{10,11... | collective-permute-start | bytes 202760 | tf_op jit(solution)/shard_map/ppermute | solution.py:28
  4.7 9.1 %collective-permute-start.5 = (bf16[8,4224]{1,0:T(8,128)(2,1)S(1)}, bf16[8,4224]{1,0:T(8,128)(2,1)S(1)}, u32[]{:S(2)}, u32[]{:S(2)}) collective-permute-start(bf16[8,4224]{1,0:T(8,128)(2,1)S(1)} %shard_map.64.refs_0_), channel_id=1, source_target_pairs={{0,3},{1,2},{2,1},{3,0},{4,7},{5,6},{6,5},{7,4},{8,11},{9,10},{10,... | collective-permute-start | bytes 202760 | tf_op jit(solution)/shard_map/ppermute | solution.py:28
  7.2 6.6 %collective-permute-start.4 = (bf16[8,4224]{1,0:T(8,128)(2,1)S(1)}, bf16[8,4224]{1,0:T(8,128)(2,1)S(1)}, u32[]{:S(2)}, u32[]{:S(2)}) collective-permute-start(bf16[8,4224]{1,0:T(8,128)(2,1)S(1)} %shard_map.64.refs_0_), channel_id=1, source_target_pairs={{0,2},{1,3},{2,0},{3,1},{4,6},{5,7},{6,4},{7,5},{8,10},{9,11},{10,... | collective-permute-start | bytes 202760 | tf_op jit(solution)/shard_map/ppermute | solution.py:28
  7.3 9.6 %collective-permute-start.3 = (bf16[16,4224]{1,0:T(8,128)(2,1)S(1)}, bf16[16,4224]{1,0:T(8,128)(2,1)S(1)}, u32[]{:S(2)}, u32[]{:S(2)}) collective-permute-start(bf16[16,4224]{1,0:T(8,128)(2,1)S(1)} %shard_map.65), channel_id=1, source_target_pairs={{0,8},{4,12},{8,0},{12,4},{16,24},{20,28},{24,16},{28,20},{1,9},{5... | collective-permute-start | bytes 405512 | tf_op jit(solution)/shard_map/ppermute | solution.py:28
  9.0 8.4 %collective-permute-start.2 = (bf16[16,4224]{1,0:T(8,128)(2,1)S(1)}, bf16[16,4224]{1,0:T(8,128)(2,1)S(1)}, u32[]{:S(2)}, u32[]{:S(2)}) collective-permute-start(bf16[16,4224]{1,0:T(8,128)(2,1)S(1)} %shard_map.65), channel_id=1, source_target_pairs={{0,16},{4,20},{8,24},{12,28},{16,0},{20,4},{24,8},{28,12},{1,17},{... | collective-permute-start | bytes 405512 | tf_op jit(solution)/shard_map/ppermute | solution.py:28
  10.5 6.9 %collective-permute-start.1 = (bf16[16,4224]{1,0:T(8,128)(2,1)S(1)}, bf16[16,4224]{1,0:T(8,128)(2,1)S(1)}, u32[]{:S(2)}, u32[]{:S(2)}) collective-permute-start(bf16[16,4224]{1,0:T(8,128)(2,1)S(1)} %shard_map.65), channel_id=1, source_target_pairs={{0,24},{4,28},{8,16},{12,20},{16,8},{20,12},{24,0},{28,4},{1,25},{... | collective-permute-start | bytes 405512 | tf_op jit(solution)/shard_map/ppermute | solution.py:28
  13.8 9.6 %collective-permute-start.8 = (bf16[16,4224]{1,0:T(8,128)(2,1)S(1)}, bf16[16,4224]{1,0:T(8,128)(2,1)S(1)}, u32[]{:S(2)}, u32[]{:S(2)}) collective-permute-start(bf16[16,4224]{1,0:T(8,128)(2,1)S(1)} %get-tuple-element.29), channel_id=1, source_target_pairs={{0,8},{4,12},{8,0},{12,4},{16,24},{20,28},{24,16},{28,20},{1,9},{5... | collective-permute-start | bytes 405512 | tf_op jit(solution)/shard_map/ppermute | solution.py:28
  15.4 8.1 %collective-permute-start.7 = (bf16[16,4224]{1,0:T(8,128)(2,1)S(1)}, bf16[16,4224]{1,0:T(8,128)(2,1)S(1)}, u32[]{:S(2)}, u32[]{:S(2)}) collective-permute-start(bf16[16,4224]{1,0:T(8,128)(2,1)S(1)} %get-tuple-element.29), channel_id=1, source_target_pairs={{0,16},{4,20},{8,24},{12,28},{16,0},{20,4},{24,8},{28,12},{1,17},{... | collective-permute-start | bytes 405512 | tf_op jit(solution)/shard_map/ppermute | solution.py:28
  16.9 6.4 %collective-permute-start.6 = (bf16[16,4224]{1,0:T(8,128)(2,1)S(1)}, bf16[16,4224]{1,0:T(8,128)(2,1)S(1)}, u32[]{:S(2)}, u32[]{:S(2)}) collective-permute-start(bf16[16,4224]{1,0:T(8,128)(2,1)S(1)} %get-tuple-element.29), channel_id=1, source_target_pairs={{0,24},{4,28},{8,16},{12,20},{16,8},{20,12},{24,0},{28,4},{1,25},{... | collective-permute-start | bytes 405512 | tf_op jit(solution)/shard_map/ppermute | solution.py:28
  17.4 6.1 %collective-permute-start.9 = (bf16[64,4224]{1,0:T(8,128)(2,1)S(1)}, bf16[64,4224]{1,0:T(8,128)(2,1)S(1)}, u32[]{:S(2)}, u32[]{:S(2)}) collective-permute-start(bf16[64,4224]{1,0:T(8,128)(2,1)S(1)} %pad_maximum_fusion.refs_0_), channel_id=1, source_target_pairs={{0,4},{4,0},{8,12},{12,8},{16,20},{20,16},{24,28},{28,24},{1,5},{5... | collective-permute-start | bytes 1622024 | tf_op jit(solution)/shard_map/ppermute | solution.py:28
  23.5 2.0 %collective-permute-start.10 = (bf16[64,4224]{1,0:T(8,128)(2,1)S(1)}, bf16[64,4224]{1,0:T(8,128)(2,1)S(1)}, u32[]{:S(2)}, u32[]{:S(2)}) collective-permute-start(bf16[64,4224]{1,0:T(8,128)(2,1)S(1)} %constant_dynamic-update-slice_fusion.2.refs_1_), channel_id=1, source_target_pairs={{0,4},{4,0},{8,12},{12,8},{16,20},{20,16},{24,28},{28,24},{1,5},{5... | collective-permute-start | bytes 1622024 | tf_op jit(solution)/shard_map/ppermute | solution.py:28
  32.6 2.0 %collective-permute-start.15 = (bf16[64,4096]{1,0:T(8,128)(2,1)S(1)}, bf16[64,4096]{1,0:T(8,128)(2,1)S(1)}, u32[]{:S(2)}, u32[]{:S(2)}) collective-permute-start(bf16[64,4096]{1,0:T(8,128)(2,1)S(1)} %get-tuple-element.14), channel_id=1, source_target_pairs={{0,4},{4,0},{8,12},{12,8},{16,20},{20,16},{24,28},{28,24},{1,5},{5... | collective-permute-start | bytes 1572872 | tf_op jit(solution)/shard_map/ppermute | solution.py:28
  32.8 5.5 %collective-permute-start.11 = (bf16[64,4096]{1,0:T(8,128)(2,1)S(1)}, bf16[64,4096]{1,0:T(8,128)(2,1)S(1)}, u32[]{:S(2)}, u32[]{:S(2)}) collective-permute-start(bf16[64,4096]{1,0:T(8,128)(2,1)S(1)} %get-tuple-element.12), channel_id=1, source_target_pairs={{0,4},{4,0},{8,12},{12,8},{16,20},{20,16},{24,28},{28,24},{1,5},{5... | collective-permute-start | bytes 1572872 | tf_op jit(solution)/shard_map/ppermute | solution.py:28
  34.7 7.3 %collective-permute-start.16 = (bf16[16,4096]{1,0:T(8,128)(2,1)S(1)}, bf16[16,4096]{1,0:T(8,128)(2,1)S(1)}, u32[]{:S(2)}, u32[]{:S(2)}) collective-permute-start(bf16[16,4096]{1,0:T(8,128)(2,1)S(1)} %get-tuple-element.24), channel_id=1, source_target_pairs={{0,24},{4,28},{8,16},{12,20},{16,8},{20,12},{24,0},{28,4},{1,25},{... | collective-permute-start | bytes 393224 | tf_op jit(solution)/shard_map/ppermute | solution.py:28
  36.3 8.6 %collective-permute-start.18 = (bf16[16,4096]{1,0:T(8,128)(2,1)S(1)}, bf16[16,4096]{1,0:T(8,128)(2,1)S(1)}, u32[]{:S(2)}, u32[]{:S(2)}) collective-permute-start(bf16[16,4096]{1,0:T(8,128)(2,1)S(1)} %get-tuple-element.25), channel_id=1, source_target_pairs={{0,8},{4,12},{8,0},{12,4},{16,24},{20,28},{24,16},{28,20},{1,9},{5... | collective-permute-start | bytes 393224 | tf_op jit(solution)/shard_map/ppermute | solution.py:28
  37.7 9.2 %collective-permute-start.17 = (bf16[16,4096]{1,0:T(8,128)(2,1)S(1)}, bf16[16,4096]{1,0:T(8,128)(2,1)S(1)}, u32[]{:S(2)}, u32[]{:S(2)}) collective-permute-start(bf16[16,4096]{1,0:T(8,128)(2,1)S(1)} %get-tuple-element.26), channel_id=1, source_target_pairs={{0,16},{4,20},{8,24},{12,28},{16,0},{20,4},{24,8},{28,12},{1,17},{... | collective-permute-start | bytes 393224 | tf_op jit(solution)/shard_map/ppermute | solution.py:28
  38.4 11.3 %collective-permute-start.12 = (bf16[16,4096]{1,0:T(8,128)(2,1)S(1)}, bf16[16,4096]{1,0:T(8,128)(2,1)S(1)}, u32[]{:S(2)}, u32[]{:S(2)}) collective-permute-start(bf16[16,4096]{1,0:T(8,128)(2,1)S(1)} %get-tuple-element.21), channel_id=1, source_target_pairs={{0,24},{4,28},{8,16},{12,20},{16,8},{20,12},{24,0},{28,4},{1,25},{... | collective-permute-start | bytes 393224 | tf_op jit(solution)/shard_map/ppermute | solution.py:28
  40.0 9.8 %collective-permute-start.14 = (bf16[16,4096]{1,0:T(8,128)(2,1)S(1)}, bf16[16,4096]{1,0:T(8,128)(2,1)S(1)}, u32[]{:S(2)}, u32[]{:S(2)}) collective-permute-start(bf16[16,4096]{1,0:T(8,128)(2,1)S(1)} %get-tuple-element.22), channel_id=1, source_target_pairs={{0,8},{4,12},{8,0},{12,4},{16,24},{20,28},{24,16},{28,20},{1,9},{5... | collective-permute-start | bytes 393224 | tf_op jit(solution)/shard_map/ppermute | solution.py:28
  42.0 7.7 %collective-permute-start.13 = (bf16[16,4096]{1,0:T(8,128)(2,1)S(1)}, bf16[16,4096]{1,0:T(8,128)(2,1)S(1)}, u32[]{:S(2)}, u32[]{:S(2)}) collective-permute-start(bf16[16,4096]{1,0:T(8,128)(2,1)S(1)} %get-tuple-element.23), channel_id=1, source_target_pairs={{0,16},{4,20},{8,24},{12,28},{16,0},{20,4},{24,8},{28,12},{1,17},{... | collective-permute-start | bytes 393224 | tf_op jit(solution)/shard_map/ppermute | solution.py:28
  47.1 6.0 %collective-permute-start.19 = (bf16[8,4096]{1,0:T(8,128)(2,1)S(1)}, bf16[8,4096]{1,0:T(8,128)(2,1)S(1)}, u32[]{:S(2)}, u32[]{:S(2)}) collective-permute-start(bf16[8,4096]{1,0:T(8,128)(2,1)S(1)} %get-tuple-element.27), channel_id=1, source_target_pairs={{0,2},{1,3},{2,0},{3,1},{4,6},{5,7},{6,4},{7,5},{8,10},{9,11},{10,... | collective-permute-start | bytes 196616 | tf_op jit(solution)/shard_map/ppermute | solution.py:28
  48.6 6.6 %collective-permute-start.20 = (bf16[8,4096]{1,0:T(8,128)(2,1)S(1)}, bf16[8,4096]{1,0:T(8,128)(2,1)S(1)}, u32[]{:S(2)}, u32[]{:S(2)}) collective-permute-start(bf16[8,4096]{1,0:T(8,128)(2,1)S(1)} %get-tuple-element.28), channel_id=1, source_target_pairs={{0,3},{1,2},{2,1},{3,0},{4,7},{5,6},{6,5},{7,4},{8,11},{9,10},{10,... | collective-permute-start | bytes 196616 | tf_op jit(solution)/shard_map/ppermute | solution.py:28
  49.8 5.4 %collective-permute-start.21 = (bf16[8,4096]{1,0:T(8,128)(2,1)S(1)}, bf16[8,4096]{1,0:T(8,128)(2,1)S(1)}, u32[]{:S(2)}, u32[]{:S(2)}) collective-permute-start(bf16[8,4096]{1,0:T(8,128)(2,1)S(1)} %slice.87), channel_id=1, source_target_pairs={{0,1},{1,0},{2,3},{3,2},{4,5},{5,4},{6,7},{7,6},{8,9},{9,8},{10,11... | collective-permute-start | bytes 196616 | tf_op jit(solution)/shard_map/ppermute | solution.py:28

commit v2 on v1

--- a/solution.py
+++ b/solution.py
@@ -52,32 +52,31 @@
     return [value[start : start + step] for start in range(0, value.shape[0], step)]
 
 
-def gather_rows(block):
-    depth = lax.axis_size("expert")
-    column = [block] + [swap(block, "expert", mask) for mask in range(1, depth)]
-    near = join(column[: depth // 2])
-    near_rest = [swap(near, *step) for step in plane_steps()]
-    far = cat(column[depth // 2 :])
-    far_rest = [swap(far, *step) for step in plane_steps()]
-    near = cat([near, *near_rest])
-    near_there = swap(near, *CORE)
-    far = cat([far, *far_rest])
-    return [near, far, near_there, swap(far, *CORE)]
-
-
-def scatter_sums(kept, away):
-    steps, depth = plane_steps(), lax.axis_size("expert")
-    sums = []
-    for mine, other in reversed(list(zip(kept, away))):
-        part, *rest = split(mine + wide(swap(other, *CORE)), len(steps) + 1)
-        here = [send(other, step) for other, step in zip(rest, steps)]
-        sums.append(sum([wide(other) for other in here], part))
-    far, (total, *near) = split(sums[0], depth // 2), split(sums[1], depth // 2)
-    far = [send(part, ("expert", mask + depth // 2)) for mask, part in enumerate(far)]
-    near = [send(part, ("expert", mask + 1)) for mask, part in enumerate(near)]
-    far = sum(wide(part) for part in far)
-    far, *near = lax.optimization_barrier((far, *near))
-    return sum([wide(part) for part in near], total + far).astype(jnp.bfloat16)
+def after(value, *others):
+    return lax.optimization_barrier((value, *others))[0]
+
+
+def gather_half(half, earlier):
+    rest = [swap(half, *step) for step in plane_steps()]
+    half = cat([half, after(rest[0], *earlier), *rest[1:]])
+    return half, swap(half, *CORE)
+
+
+def scatter_half(total):
+    steps = plane_steps()
+    part, *rest = split(total, len(steps) + 1)
+    here = [send(other, step) for other, step in zip(rest, steps)]
+    return sum([wide(other) for other in here], part)
+
+
+def scatter_sums(early, late):
+    count = lax.axis_size("expert") // 2
+    total, *early = split(scatter_half(early), count)
+    early = [send(part, ("expert", 2 * index + 2)) for index, part in enumerate(early)]
+    total = sum([wide(part) for part in early], total)
+    late = split(scatter_half(late), count)
+    late = [send(part, ("expert", 2 * index + 1)) for index, part in enumerate(late)]
+    return sum([wide(part) for part in late], total).astype(jnp.bfloat16)
 
 
 def pack_kernel(tokens_hbm, ids_hbm, router_hbm, packed_ref, tokens_ref, ids_ref, router_ref, done):
@@ -211,21 +210,30 @@
     )(*pieces, w_gate, w_up, w_down)
 
 
+def half_experts(here, there, *operands):
+    kinds = [jnp.float32, jnp.bfloat16]
+    if 2 * here.shape[0] <= ROWS:
+        return run_experts([here, there], kinds, *operands)
+    results = []
+    for piece, kind in zip((here, there), kinds):
+        chunks = [
+            run_experts([piece[start : start + ROWS]], [kind], *operands)[0]
+            for start in range(0, piece.shape[0], ROWS)
+        ]
+        results.append(cat(chunks))
+    return results
+
+
 def body(tokens, expert_ids, router, w_gate, w_up, w_down):
-    pieces = gather_rows(pack(tokens, expert_ids, router))
-    kinds = [jnp.float32] * 2 + [jnp.bfloat16] * 2
+    block = pack(tokens, expert_ids, router)
+    column = [block] + [swap(block, "expert", mask) for mask in range(1, lax.axis_size("expert"))]
     operands = (router.shape[0], w_gate, w_up, w_down)
-    if sum(piece.shape[0] for piece in pieces) <= ROWS:
-        results = run_experts(pieces, kinds, *operands)
-    else:
-        results = []
-        for piece, kind in zip(pieces, kinds):
-            chunks = [
-                run_experts([piece[start : start + ROWS]], [kind], *operands)[0]
-                for start in range(0, piece.shape[0], ROWS)
-            ]
-            results.append(cat(chunks))
-    return scatter_sums(results[:2], results[2:])
+    half = cat(column[1::2])
+    early = half_experts(*gather_half(join(column[0::2]), [half]), *operands)
+    early_total = early[0] + wide(swap(early[1], *CORE))
+    here, there = gather_half(half, early)
+    late = half_experts(here, after(there, early_total), *operands)
+    return scatter_sums(early_total, late[0] + wide(swap(late[1], *CORE)))
 
 
 def solution(mesh):

time: 56 us -> 64.2 us (1.15)
  Pallas kernels: 8.56 us -> 15 us
  starting transfers between devices: 25.2 us -> 26.2 us
  waiting for transfers between devices: 20.6 us -> 21.3 us
    pallas_call x1 -> x2, Pallas kernels: 7.01 us -> 13.5 us  [run_experts(): pl.pallas_call(functools.partial(expert_kernel, exp_dev, expert_total, le...]
    ppermute x22, starting transfers between devices: 25.2 us -> 26.2 us  [swap(): return lax.ppermute(value, axis, [(i, i ^ mask) for i in range(count)])]
    ppermute x22, waiting for transfers between devices: 20.6 us -> 21.3 us  [swap(): return lax.ppermute(value, axis, [(i, i ^ mask) for i in range(count)])]
  transfers between devices with their start and end apart: 22 -> 22, of which waited for: 10 -> 11; matrix products, arithmetic and copies ran while one was open for 1% -> 1% of each run, Pallas kernels for 0% -> 11%
where the time goes in v2:
time: 64.2 us; the launch traced here: 64 us
  starting transfers between devices  26.2 us (41%)
  waiting for transfers between devices  21.3 us (33%)
  Pallas kernels  15 us (23%)
  other arithmetic  1.06 us (2%)
    ppermute x22, starting transfers between devices, swap(): return lax.ppermute(value, axis, [(i, i ^ mask) for i in range(count)])  26.2 us
    ppermute x22, waiting for transfers between devices, swap(): return lax.ppermute(value, axis, [(i, i ^ mask) for i in range(count)])  21.3 us
    pallas_call x2, Pallas kernels, run_experts(): pl.pallas_call(functools.partial(expert_kernel, exp_dev, expert_total, le...  13.5 us
    pallas_call x1, Pallas kernels, pack(): pl.pallas_call(pack_kernel, out_shape=pltpu.VMEM((rows, width + extra), t...  1.54 us
  transfers between devices with their start and end apart: 22, of which 11 were waited for; matrix products, arithmetic and copies ran while one was open for 1% of the time, Pallas kernels for 11%

profile of v2, /device:TPU:0, one launch (start us, length us, event | category | flops | bytes accessed | tf_op | source)
XLA Modules:
  0.0 64.0 jit_solution(11823009062511490428)
XLA Ops:
  0.0 0.0 slice-start
  0.0 0.0 slice-start.2
  0.0 0.0 slice-start.4
  0.0 1.5 %shard_map.64.refs_0_ = bf16[8,4224]{1,0:T(8,128)(2,1)S(1)} custom-call(bf16[8,4096]{1,0:T(8,128)(2,1)} %tokens_hbm.1, s32[8,8]{1,0:T(8,128)} %ids_hbm.1, bf16[16,4096]{1,0:T(8,128)(2,1)} %router_hbm.1), custom_call_target="tpu_custom_call" | custom-call | flops 1048576 | bytes 262144 | tf_op jit(solution)/shard_map/pallas_call | solution.py:117
  1.6 0.0 slice-start.1
  1.6 0.0 slice-start.3
  1.6 0.0 slice-start.5
  1.6 4.1 %collective-permute-start = (bf16[8,4224]{1,0:T(8,128)(2,1)S(1)}, bf16[8,4224]{1,0:T(8,128)(2,1)S(1)}, u32[]{:S(2)}, u32[]{:S(2)}) collective-permute-start(bf16[8,4224]{1,0:T(8,128)(2,1)S(1)} %shard_map.64.refs_0_), channel_id=1, source_target_pairs={{0,2},{1,3},{2,0},{3,1},{4,6},{5,7},{6,4},{7,5},{8,10},{9,11},{10,... | collective-permute-start | bytes 202760 | tf_op jit(solution)/shard_map/ppermute | solution.py:28
  5.7 1.3 %collective-permute-start.3 = (bf16[8,4224]{1,0:T(8,128)(2,1)S(1)}, bf16[8,4224]{1,0:T(8,128)(2,1)S(1)}, u32[]{:S(2)}, u32[]{:S(2)}) collective-permute-start(bf16[8,4224]{1,0:T(8,128)(2,1)S(1)} %shard_map.64.refs_0_), channel_id=1, source_target_pairs={{0,3},{1,2},{2,1},{3,0},{4,7},{5,6},{6,5},{7,4},{8,11},{9,10},{10,... | collective-permute-start | bytes 202760 | tf_op jit(solution)/shard_map/ppermute | solution.py:28
  7.1 0.2 collective-permute-start.2
  7.3 2.2 %collective-permute-done.refs_1_ = bf16[8,4224]{1,0:T(8,128)(2,1)S(1)} collective-permute-done((bf16[8,4224]{1,0:T(8,128)(2,1)S(1)}, bf16[8,4224]{1,0:T(8,128)(2,1)S(1)}, u32[]{:S(2)}, u32[]{:S(2)}) %collective-permute-start) | collective-permute-done | bytes 67616 | tf_op jit(solution)/shard_map/ppermute | solution.py:28
  9.5 2.7 %collective-permute-start.5 = (bf16[16,4224]{1,0:T(8,128)(2,1)S(1)}, bf16[16,4224]{1,0:T(8,128)(2,1)S(1)}, u32[]{:S(2)}, u32[]{:S(2)}) collective-permute-start(bf16[16,4224]{1,0:T(8,128)(2,1)S(1)} %shard_map.65), channel_id=1, source_target_pairs={{0,8},{4,12},{8,0},{12,4},{16,24},{20,28},{24,16},{28,20},{1,9},{5... | collective-permute-start | bytes 405512 | tf_op jit(solution)/shard_map/ppermute | solution.py:28
  12.2 1.5 %collective-permute-start.4 = (bf16[16,4224]{1,0:T(8,128)(2,1)S(1)}, bf16[16,4224]{1,0:T(8,128)(2,1)S(1)}, u32[]{:S(2)}, u32[]{:S(2)}) collective-permute-start(bf16[16,4224]{1,0:T(8,128)(2,1)S(1)} %shard_map.65), channel_id=1, source_target_pairs={{0,16},{4,20},{8,24},{12,28},{16,0},{20,4},{24,8},{28,12},{1,17},{... | collective-permute-start | bytes 405512 | tf_op jit(solution)/shard_map/ppermute | solution.py:28
  13.7 0.0 collective-permute-start.1
  13.7 0.0 collective-permute-done.2
  13.8 0.0 collective-permute-done.3
  13.8 5.8 %collective-permute-done.1 = bf16[16,4224]{1,0:T(8,128)(2,1)S(1)} collective-permute-done((bf16[16,4224]{1,0:T(8,128)(2,1)S(1)}, bf16[16,4224]{1,0:T(8,128)(2,1)S(1)}, u32[]{:S(2)}, u32[]{:S(2)}) %collective-permute-start.1) | collective-permute-done | bytes 135200 | tf_op jit(solution)/shard_map/ppermute | solution.py:28
  19.6 0.0 collective-permute-done.5
  19.6 0.0 collective-permute-done.4
  19.7 0.1 collective-permute-start.6
  19.8 0.6 collective-permute-start.14
  20.4 0.5 collective-permute-start.13
  20.9 2.4 %collective-permute-start.12 = (bf16[16,4224]{1,0:T(8,128)(2,1)S(1)}, bf16[16,4224]{1,0:T(8,128)(2,1)S(1)}, u32[]{:S(2)}, u32[]{:S(2)}) collective-permute-start(bf16[16,4224]{1,0:T(8,128)(2,1)S(1)} %get-tuple-element.32), channel_id=1, source_target_pairs={{0,24},{4,28},{8,16},{12,20},{16,8},{20,12},{24,0},{28,4},{1,25},{... | collective-permute-start | bytes 405512 | tf_op jit(solution)/shard_map/ppermute | solution.py:28
  23.3 0.0 collective-permute-done.6.refs_1_
  23.3 0.0 slice-done
  23.3 0.0 slice-done.2
  23.3 0.0 slice-done.4
  23.3 0.0 slice-done.1
  23.3 0.0 slice-done.3
  23.3 0.0 slice-done.5
  23.4 6.7 %shard_map.66 = (f32[64,4096]{1,0:T(8,128)S(1)}, bf16[64,4096]{1,0:T(8,128)(2,1)S(1)}) custom-call(bf16[64,4224]{1,0:T(8,128)(2,1)S(1)} %pad_maximum_fusion.refs_0_, bf16[64,4224]{1,0:T(8,128)(2,1)S(1)} %collective-permute-done.6.refs_1_, bf16[2,384,4096]{2,1,0:T(8,128)(2,1)S(1)} %bitcast.1, bf16[2,384,4096]{2,1,0:T(8,128)(2,1)S(1)} %bitcast.3, ...), custom_call_target="tpu_custom_call" | custom-call | flops 2415919104 | bytes 2621440 | tf_op jit(solution)/shard_map/pallas_call | solution.py:198
  30.1 0.1 collective-permute-start.7
  30.2 0.0 collective-permute-done.12
  30.2 0.0 collective-permute-done.13
  30.3 0.0 collective-permute-done.14
  30.3 0.5 collective-permute-start.15
  30.8 1.3 %collective-permute-done.7 = bf16[64,4096]{1,0:T(8,128)(2,1)S(1)} collective-permute-done((bf16[64,4096]{1,0:T(8,128)(2,1)S(1)}, bf16[64,4096]{1,0:T(8,128)(2,1)S(1)}, u32[]{:S(2)}, u32[]{:S(2)}) %collective-permute-start.7) | collective-permute-done | bytes 524320 | tf_op jit(solution)/shard_map/ppermute | solution.py:28
  32.1 0.1 fusion.9
  32.2 0.6 %collective-permute-done.15.refs_1_ = bf16[64,4224]{1,0:T(8,128)(2,1)S(1)} collective-permute-done((bf16[64,4224]{1,0:T(8,128)(2,1)S(1)}, bf16[64,4224]{1,0:T(8,128)(2,1)S(1)}, u32[]{:S(2)}, u32[]{:S(2)}) %collective-permute-start.15) | collective-permute-done | bytes 540704 | tf_op jit(solution)/shard_map/ppermute | solution.py:28
  32.9 6.7 %shard_map.67 = (f32[64,4096]{1,0:T(8,128)S(1)}, bf16[64,4096]{1,0:T(8,128)(2,1)S(1)}) custom-call(bf16[64,4224]{1,0:T(8,128)(2,1)S(1)} %constant_dynamic-update-slice_fusion.2.refs_0_, bf16[64,4224]{1,0:T(8,128)(2,1)S(1)} %collective-permute-done.15.refs_1_, bf16[2,384,4096]{2,1,0:T(8,128)(2,1)S(1)} %bitcast.1, bf16[2,384,4096]{2,1,0:T(8,128)(2,1)S(1)} %bitcast.3, ...), custom_call_target="tpu_custom_call" | custom-call | flops 2415919104 | bytes 2621440 | tf_op jit(solution)/shard_map/pallas_call | solution.py:198
  39.6 0.2 collective-permute-start.16
  39.8 0.6 collective-permute-start.8
  40.4 1.5 %collective-permute-start.10 = (bf16[16,4096]{1,0:T(8,128)(2,1)S(1)}, bf16[16,4096]{1,0:T(8,128)(2,1)S(1)}, u32[]{:S(2)}, u32[]{:S(2)}) collective-permute-start(bf16[16,4096]{1,0:T(8,128)(2,1)S(1)} %get-tuple-element.27), channel_id=1, source_target_pairs={{0,8},{4,12},{8,0},{12,4},{16,24},{20,28},{24,16},{28,20},{1,9},{5... | collective-permute-start | bytes 393224 | tf_op jit(solution)/shard_map/ppermute | solution.py:28
  41.9 1.5 %collective-permute-start.9 = (bf16[16,4096]{1,0:T(8,128)(2,1)S(1)}, bf16[16,4096]{1,0:T(8,128)(2,1)S(1)}, u32[]{:S(2)}, u32[]{:S(2)}) collective-permute-start(bf16[16,4096]{1,0:T(8,128)(2,1)S(1)} %get-tuple-element.28), channel_id=1, source_target_pairs={{0,16},{4,20},{8,24},{12,28},{16,0},{20,4},{24,8},{28,12},{1,17},{... | collective-permute-start | bytes 393224 | tf_op jit(solution)/shard_map/ppermute | solution.py:28
  43.4 0.0 collective-permute-done.16
  43.4 0.1 fusion.8
  43.6 0.6 collective-permute-start.17
  44.2 1.5 %collective-permute-start.19 = (bf16[16,4096]{1,0:T(8,128)(2,1)S(1)}, bf16[16,4096]{1,0:T(8,128)(2,1)S(1)}, u32[]{:S(2)}, u32[]{:S(2)}) collective-permute-start(bf16[16,4096]{1,0:T(8,128)(2,1)S(1)} %get-tuple-element.24), channel_id=1, source_target_pairs={{0,8},{4,12},{8,0},{12,4},{16,24},{20,28},{24,16},{28,20},{1,9},{5... | collective-permute-start | bytes 393224 | tf_op jit(solution)/shard_map/ppermute | solution.py:28
  45.6 1.5 %collective-permute-done.8 = bf16[16,4096]{1,0:T(8,128)(2,1)S(1)} collective-permute-done((bf16[16,4096]{1,0:T(8,128)(2,1)S(1)}, bf16[16,4096]{1,0:T(8,128)(2,1)S(1)}, u32[]{:S(2)}, u32[]{:S(2)}) %collective-permute-start.8) | collective-permute-done | bytes 131104 | tf_op jit(solution)/shard_map/ppermute | solution.py:28
  47.2 0.5 collective-permute-start.18
  47.7 1.3 %collective-permute-done.10 = bf16[16,4096]{1,0:T(8,128)(2,1)S(1)} collective-permute-done((bf16[16,4096]{1,0:T(8,128)(2,1)S(1)}, bf16[16,4096]{1,0:T(8,128)(2,1)S(1)}, u32[]{:S(2)}, u32[]{:S(2)}) %collective-permute-start.10) | collective-permute-done | bytes 131104 | tf_op jit(solution)/shard_map/ppermute | solution.py:28
  49.0 1.0 %collective-permute-done.9 = bf16[16,4096]{1,0:T(8,128)(2,1)S(1)} collective-permute-done((bf16[16,4096]{1,0:T(8,128)(2,1)S(1)}, bf16[16,4096]{1,0:T(8,128)(2,1)S(1)}, u32[]{:S(2)}, u32[]{:S(2)}) %collective-permute-start.9) | collective-permute-done | bytes 131104 | tf_op jit(solution)/shard_map/ppermute | solution.py:28
  50.0 0.1 fusion.4
  50.1 1.0 %collective-permute-start.11 = (bf16[8,4096]{1,0:T(8,128)(2,1)S(1)}, bf16[8,4096]{1,0:T(8,128)(2,1)S(1)}, u32[]{:S(2)}, u32[]{:S(2)}) collective-permute-start(bf16[8,4096]{1,0:T(8,128)(2,1)S(1)} %slice.89), channel_id=1, source_target_pairs={{0,2},{1,3},{2,0},{3,1},{4,6},{5,7},{6,4},{7,5},{8,10},{9,11},{10,... | collective-permute-start | bytes 196616 | tf_op jit(solution)/shard_map/ppermute | solution.py:28
  51.2 1.7 %collective-permute-done.17 = bf16[16,4096]{1,0:T(8,128)(2,1)S(1)} collective-permute-done((bf16[16,4096]{1,0:T(8,128)(2,1)S(1)}, bf16[16,4096]{1,0:T(8,128)(2,1)S(1)}, u32[]{:S(2)}, u32[]{:S(2)}) %collective-permute-start.17) | collective-permute-done | bytes 131104 | tf_op jit(solution)/shard_map/ppermute | solution.py:28
  52.8 1.3 %collective-permute-done.19 = bf16[16,4096]{1,0:T(8,128)(2,1)S(1)} collective-permute-done((bf16[16,4096]{1,0:T(8,128)(2,1)S(1)}, bf16[16,4096]{1,0:T(8,128)(2,1)S(1)}, u32[]{:S(2)}, u32[]{:S(2)}) %collective-permute-start.19) | collective-permute-done | bytes 131104 | tf_op jit(solution)/shard_map/ppermute | solution.py:28
  54.1 0.9 %collective-permute-done.18 = bf16[16,4096]{1,0:T(8,128)(2,1)S(1)} collective-permute-done((bf16[16,4096]{1,0:T(8,128)(2,1)S(1)}, bf16[16,4096]{1,0:T(8,128)(2,1)S(1)}, u32[]{:S(2)}, u32[]{:S(2)}) %collective-permute-start.18) | collective-permute-done | bytes 131104 | tf_op jit(solution)/shard_map/ppermute | solution.py:28
  55.0 0.1 fusion.2
  55.1 1.5 %collective-permute-start.20 = (bf16[8,4096]{1,0:T(8,128)(2,1)S(1)}, bf16[8,4096]{1,0:T(8,128)(2,1)S(1)}, u32[]{:S(2)}, u32[]{:S(2)}) collective-permute-start(bf16[8,4096]{1,0:T(8,128)(2,1)S(1)} %get-tuple-element.29), channel_id=1, source_target_pairs={{0,1},{1,0},{2,3},{3,2},{4,5},{5,4},{6,7},{7,6},{8,9},{9,8},{10,11... | collective-permute-start | bytes 196616 | tf_op jit(solution)/shard_map/ppermute | solution.py:28
  56.6 3.1 %collective-permute-start.21 = (bf16[8,4096]{1,0:T(8,128)(2,1)S(1)}, bf16[8,4096]{1,0:T(8,128)(2,1)S(1)}, u32[]{:S(2)}, u32[]{:S(2)}) collective-permute-start(bf16[8,4096]{1,0:T(8,128)(2,1)S(1)} %get-tuple-element.30), channel_id=1, source_target_pairs={{0,3},{1,2},{2,1},{3,0},{4,7},{5,6},{6,5},{7,4},{8,11},{9,10},{10,... | collective-permute-start | bytes 196616 | tf_op jit(solution)/shard_map/ppermute | solution.py:28
  59.8 0.0 collective-permute-done.11
  59.8 0.0 collective-permute-done.20
  59.8 3.6 %collective-permute-done.21 = bf16[8,4096]{1,0:T(8,128)(2,1)S(1)} collective-permute-done((bf16[8,4096]{1,0:T(8,128)(2,1)S(1)}, bf16[8,4096]{1,0:T(8,128)(2,1)S(1)}, u32[]{:S(2)}, u32[]{:S(2)}) %collective-permute-start.21) | collective-permute-done | bytes 65568 | tf_op jit(solution)/shard_map/ppermute | solution.py:28
  63.4 0.7 %fusion.7 = bf16[8,4096]{1,0:T(8,128)(2,1)} fusion(f32[16,4096]{1,0:T(8,128)S(1)} %fusion.4, bf16[8,4096]{1,0:T(8,128)(2,1)S(1)} %collective-permute-done.21, bf16[8,4096]{1,0:T(8,128)(2,1)S(1)} %collective-permute-done.20, bf16[8,4096]{1,0:T(8,128)(2,1)S(1)} %collective-permute-done.11), kind=kLoop, calls=%fused_computation.14 | loop fusion | flops 229376 | bytes 393216 | tf_op jit(solution)/shard_map/convert_element_type | solution.py:79
  (14 shorter events, 0.2 us)
Async XLA Ops:
  0.0 23.3 %slice-start = ((s8[6291456]{0:T(1024)(128)(4,1)}), s8[4194304]{0:T(1024)(128)(4,1)S(1)}, s32[]{:S(2)}) async-start(s8[6291456]{0:T(1024)(128)(4,1)} %bitcast), calls=%async_computation | async-start | bytes 8388608
  0.0 23.3 %slice-start.2 = ((s8[6291456]{0:T(1024)(128)(4,1)}), s8[4194304]{0:T(1024)(128)(4,1)S(1)}, s32[]{:S(2)}) async-start(s8[6291456]{0:T(1024)(128)(4,1)} %bitcast.2), calls=%async_computation.2 | async-start | bytes 8388608
  0.0 23.3 %slice-start.4 = ((s8[6291456]{0:T(1024)(128)(4,1)}), s8[4194304]{0:T(1024)(128)(4,1)S(1)}, s32[]{:S(2)}) async-start(s8[6291456]{0:T(1024)(128)(4,1)} %bitcast.4), calls=%async_computation.4 | async-start | bytes 8388608
  1.6 21.8 %slice-start.1 = ((s8[6291456]{0:T(1024)(128)(4,1)}), s8[2097152]{0:T(1024)(128)(4,1)S(1)}, s32[]{:S(2)}) async-start(s8[6291456]{0:T(1024)(128)(4,1)} %bitcast), calls=%async_computation.1 | async-start | bytes 4194304
  1.6 21.8 %slice-start.3 = ((s8[6291456]{0:T(1024)(128)(4,1)}), s8[2097152]{0:T(1024)(128)(4,1)S(1)}, s32[]{:S(2)}) async-start(s8[6291456]{0:T(1024)(128)(4,1)} %bitcast.2), calls=%async_computation.3 | async-start | bytes 4194304
  1.6 21.8 %slice-start.5 = ((s8[6291456]{0:T(1024)(128)(4,1)}), s8[2097152]{0:T(1024)(128)(4,1)S(1)}, s32[]{:S(2)}) async-start(s8[6291456]{0:T(1024)(128)(4,1)} %bitcast.4), calls=%async_computation.5 | async-start | bytes 4194304
  1.6 7.9 %collective-permute-start = (bf16[8,4224]{1,0:T(8,128)(2,1)S(1)}, bf16[8,4224]{1,0:T(8,128)(2,1)S(1)}, u32[]{:S(2)}, u32[]{:S(2)}) collective-permute-start(bf16[8,4224]{1,0:T(8,128)(2,1)S(1)} %shard_map.64.refs_0_), channel_id=1, source_target_pairs={{0,2},{1,3},{2,0},{3,1},{4,6},{5,7},{6,4},{7,5},{8,10},{9,11},{10,... | collective-permute-start | bytes 202760 | tf_op jit(solution)/shard_map/ppermute | solution.py:28
  5.7 8.1 %collective-permute-start.3 = (bf16[8,4224]{1,0:T(8,128)(2,1)S(1)}, bf16[8,4224]{1,0:T(8,128)(2,1)S(1)}, u32[]{:S(2)}, u32[]{:S(2)}) collective-permute-start(bf16[8,4224]{1,0:T(8,128)(2,1)S(1)} %shard_map.64.refs_0_), channel_id=1, source_target_pairs={{0,3},{1,2},{2,1},{3,0},{4,7},{5,6},{6,5},{7,4},{8,11},{9,10},{10,... | collective-permute-start | bytes 202760 | tf_op jit(solution)/shard_map/ppermute | solution.py:28
  7.1 6.7 %collective-permute-start.2 = (bf16[8,4224]{1,0:T(8,128)(2,1)S(1)}, bf16[8,4224]{1,0:T(8,128)(2,1)S(1)}, u32[]{:S(2)}, u32[]{:S(2)}) collective-permute-start(bf16[8,4224]{1,0:T(8,128)(2,1)S(1)} %shard_map.64.refs_0_), channel_id=1, source_target_pairs={{0,1},{1,0},{2,3},{3,2},{4,5},{5,4},{6,7},{7,6},{8,9},{9,8},{10,11... | collective-permute-start | bytes 202760 | tf_op jit(solution)/shard_map/ppermute | solution.py:28
  9.5 10.1 %collective-permute-start.5 = (bf16[16,4224]{1,0:T(8,128)(2,1)S(1)}, bf16[16,4224]{1,0:T(8,128)(2,1)S(1)}, u32[]{:S(2)}, u32[]{:S(2)}) collective-permute-start(bf16[16,4224]{1,0:T(8,128)(2,1)S(1)} %shard_map.65), channel_id=1, source_target_pairs={{0,8},{4,12},{8,0},{12,4},{16,24},{20,28},{24,16},{28,20},{1,9},{5... | collective-permute-start | bytes 405512 | tf_op jit(solution)/shard_map/ppermute | solution.py:28
  12.2 7.4 %collective-permute-start.4 = (bf16[16,4224]{1,0:T(8,128)(2,1)S(1)}, bf16[16,4224]{1,0:T(8,128)(2,1)S(1)}, u32[]{:S(2)}, u32[]{:S(2)}) collective-permute-start(bf16[16,4224]{1,0:T(8,128)(2,1)S(1)} %shard_map.65), channel_id=1, source_target_pairs={{0,16},{4,20},{8,24},{12,28},{16,0},{20,4},{24,8},{28,12},{1,17},{... | collective-permute-start | bytes 405512 | tf_op jit(solution)/shard_map/ppermute | solution.py:28
  13.7 5.9 %collective-permute-start.1 = (bf16[16,4224]{1,0:T(8,128)(2,1)S(1)}, bf16[16,4224]{1,0:T(8,128)(2,1)S(1)}, u32[]{:S(2)}, u32[]{:S(2)}) collective-permute-start(bf16[16,4224]{1,0:T(8,128)(2,1)S(1)} %shard_map.65), channel_id=1, source_target_pairs={{0,24},{4,28},{8,16},{12,20},{16,8},{20,12},{24,0},{28,4},{1,25},{... | collective-permute-start | bytes 405512 | tf_op jit(solution)/shard_map/ppermute | solution.py:28
  19.7 3.6 %collective-permute-start.6 = (bf16[64,4224]{1,0:T(8,128)(2,1)S(1)}, bf16[64,4224]{1,0:T(8,128)(2,1)S(1)}, u32[]{:S(2)}, u32[]{:S(2)}) collective-permute-start(bf16[64,4224]{1,0:T(8,128)(2,1)S(1)} %pad_maximum_fusion.refs_0_), channel_id=1, source_target_pairs={{0,4},{4,0},{8,12},{12,8},{16,20},{20,16},{24,28},{28,24},{1,5},{5... | collective-permute-start | bytes 1622024 | tf_op jit(solution)/shard_map/ppermute | solution.py:28
  19.8 10.5 %collective-permute-start.14 = (bf16[16,4224]{1,0:T(8,128)(2,1)S(1)}, bf16[16,4224]{1,0:T(8,128)(2,1)S(1)}, u32[]{:S(2)}, u32[]{:S(2)}) collective-permute-start(bf16[16,4224]{1,0:T(8,128)(2,1)S(1)} %get-tuple-element.32), channel_id=1, source_target_pairs={{0,8},{4,12},{8,0},{12,4},{16,24},{20,28},{24,16},{28,20},{1,9},{5... | collective-permute-start | bytes 405512 | tf_op jit(solution)/shard_map/ppermute | solution.py:28
  20.4 9.9 %collective-permute-start.13 = (bf16[16,4224]{1,0:T(8,128)(2,1)S(1)}, bf16[16,4224]{1,0:T(8,128)(2,1)S(1)}, u32[]{:S(2)}, u32[]{:S(2)}) collective-permute-start(bf16[16,4224]{1,0:T(8,128)(2,1)S(1)} %get-tuple-element.32), channel_id=1, source_target_pairs={{0,16},{4,20},{8,24},{12,28},{16,0},{20,4},{24,8},{28,12},{1,17},{... | collective-permute-start | bytes 405512 | tf_op jit(solution)/shard_map/ppermute | solution.py:28
  20.9 9.3 %collective-permute-start.12 = (bf16[16,4224]{1,0:T(8,128)(2,1)S(1)}, bf16[16,4224]{1,0:T(8,128)(2,1)S(1)}, u32[]{:S(2)}, u32[]{:S(2)}) collective-permute-start(bf16[16,4224]{1,0:T(8,128)(2,1)S(1)} %get-tuple-element.32), channel_id=1, source_target_pairs={{0,24},{4,28},{8,16},{12,20},{16,8},{20,12},{24,0},{28,4},{1,25},{... | collective-permute-start | bytes 405512 | tf_op jit(solution)/shard_map/ppermute | solution.py:28
  30.1 2.0 %collective-permute-start.7 = (bf16[64,4096]{1,0:T(8,128)(2,1)S(1)}, bf16[64,4096]{1,0:T(8,128)(2,1)S(1)}, u32[]{:S(2)}, u32[]{:S(2)}) collective-permute-start(bf16[64,4096]{1,0:T(8,128)(2,1)S(1)} %get-tuple-element.14), channel_id=1, source_target_pairs={{0,4},{4,0},{8,12},{12,8},{16,20},{20,16},{24,28},{28,24},{1,5},{5... | collective-permute-start | bytes 1572872 | tf_op jit(solution)/shard_map/ppermute | solution.py:28
  30.3 2.6 %collective-permute-start.15 = (bf16[64,4224]{1,0:T(8,128)(2,1)S(1)}, bf16[64,4224]{1,0:T(8,128)(2,1)S(1)}, u32[]{:S(2)}, u32[]{:S(2)}) collective-permute-start(bf16[64,4224]{1,0:T(8,128)(2,1)S(1)} %constant_dynamic-update-slice_fusion.2.refs_0_), channel_id=1, source_target_pairs={{0,4},{4,0},{8,12},{12,8},{16,20},{20,16},{24,28},{28,24},{1,5},{5... | collective-permute-start | bytes 1622024 | tf_op jit(solution)/shard_map/ppermute | solution.py:28
  39.6 3.8 %collective-permute-start.16 = (bf16[64,4096]{1,0:T(8,128)(2,1)S(1)}, bf16[64,4096]{1,0:T(8,128)(2,1)S(1)}, u32[]{:S(2)}, u32[]{:S(2)}) collective-permute-start(bf16[64,4096]{1,0:T(8,128)(2,1)S(1)} %get-tuple-element.18), channel_id=1, source_target_pairs={{0,4},{4,0},{8,12},{12,8},{16,20},{20,16},{24,28},{28,24},{1,5},{5... | collective-permute-start | bytes 1572872 | tf_op jit(solution)/shard_map/ppermute | solution.py:28
  39.8 7.3 %collective-permute-start.8 = (bf16[16,4096]{1,0:T(8,128)(2,1)S(1)}, bf16[16,4096]{1,0:T(8,128)(2,1)S(1)}, u32[]{:S(2)}, u32[]{:S(2)}) collective-permute-start(bf16[16,4096]{1,0:T(8,128)(2,1)S(1)} %get-tuple-element.26), channel_id=1, source_target_pairs={{0,24},{4,28},{8,16},{12,20},{16,8},{20,12},{24,0},{28,4},{1,25},{... | collective-permute-start | bytes 393224 | tf_op jit(solution)/shard_map/ppermute | solution.py:28
  40.4 8.6 %collective-permute-start.10 = (bf16[16,4096]{1,0:T(8,128)(2,1)S(1)}, bf16[16,4096]{1,0:T(8,128)(2,1)S(1)}, u32[]{:S(2)}, u32[]{:S(2)}) collective-permute-start(bf16[16,4096]{1,0:T(8,128)(2,1)S(1)} %get-tuple-element.27), channel_id=1, source_target_pairs={{0,8},{4,12},{8,0},{12,4},{16,24},{20,28},{24,16},{28,20},{1,9},{5... | collective-permute-start | bytes 393224 | tf_op jit(solution)/shard_map/ppermute | solution.py:28
  41.9 8.1 %collective-permute-start.9 = (bf16[16,4096]{1,0:T(8,128)(2,1)S(1)}, bf16[16,4096]{1,0:T(8,128)(2,1)S(1)}, u32[]{:S(2)}, u32[]{:S(2)}) collective-permute-start(bf16[16,4096]{1,0:T(8,128)(2,1)S(1)} %get-tuple-element.28), channel_id=1, source_target_pairs={{0,16},{4,20},{8,24},{12,28},{16,0},{20,4},{24,8},{28,12},{1,17},{... | collective-permute-start | bytes 393224 | tf_op jit(solution)/shard_map/ppermute | solution.py:28
  43.6 9.2 %collective-permute-start.17 = (bf16[16,4096]{1,0:T(8,128)(2,1)S(1)}, bf16[16,4096]{1,0:T(8,128)(2,1)S(1)}, u32[]{:S(2)}, u32[]{:S(2)}) collective-permute-start(bf16[16,4096]{1,0:T(8,128)(2,1)S(1)} %get-tuple-element.23), channel_id=1, source_target_pairs={{0,24},{4,28},{8,16},{12,20},{16,8},{20,12},{24,0},{28,4},{1,25},{... | collective-permute-start | bytes 393224 | tf_op jit(solution)/shard_map/ppermute | solution.py:28
  44.2 10.0 %collective-permute-start.19 = (bf16[16,4096]{1,0:T(8,128)(2,1)S(1)}, bf16[16,4096]{1,0:T(8,128)(2,1)S(1)}, u32[]{:S(2)}, u32[]{:S(2)}) collective-permute-start(bf16[16,4096]{1,0:T(8,128)(2,1)S(1)} %get-tuple-element.24), channel_id=1, source_target_pairs={{0,8},{4,12},{8,0},{12,4},{16,24},{20,28},{24,16},{28,20},{1,9},{5... | collective-permute-start | bytes 393224 | tf_op jit(solution)/shard_map/ppermute | solution.py:28
  47.2 7.8 %collective-permute-start.18 = (bf16[16,4096]{1,0:T(8,128)(2,1)S(1)}, bf16[16,4096]{1,0:T(8,128)(2,1)S(1)}, u32[]{:S(2)}, u32[]{:S(2)}) collective-permute-start(bf16[16,4096]{1,0:T(8,128)(2,1)S(1)} %get-tuple-element.25), channel_id=1, source_target_pairs={{0,16},{4,20},{8,24},{12,28},{16,0},{20,4},{24,8},{28,12},{1,17},{... | collective-permute-start | bytes 393224 | tf_op jit(solution)/shard_map/ppermute | solution.py:28
  50.1 9.7 %collective-permute-start.11 = (bf16[8,4096]{1,0:T(8,128)(2,1)S(1)}, bf16[8,4096]{1,0:T(8,128)(2,1)S(1)}, u32[]{:S(2)}, u32[]{:S(2)}) collective-permute-start(bf16[8,4096]{1,0:T(8,128)(2,1)S(1)} %slice.89), channel_id=1, source_target_pairs={{0,2},{1,3},{2,0},{3,1},{4,6},{5,7},{6,4},{7,5},{8,10},{9,11},{10,... | collective-permute-start | bytes 196616 | tf_op jit(solution)/shard_map/ppermute | solution.py:28
  55.1 4.7 %collective-permute-start.20 = (bf16[8,4096]{1,0:T(8,128)(2,1)S(1)}, bf16[8,4096]{1,0:T(8,128)(2,1)S(1)}, u32[]{:S(2)}, u32[]{:S(2)}) collective-permute-start(bf16[8,4096]{1,0:T(8,128)(2,1)S(1)} %get-tuple-element.29), channel_id=1, source_target_pairs={{0,1},{1,0},{2,3},{3,2},{4,5},{5,4},{6,7},{7,6},{8,9},{9,8},{10,11... | collective-permute-start | bytes 196616 | tf_op jit(solution)/shard_map/ppermute | solution.py:28
  56.6 6.7 %collective-permute-start.21 = (bf16[8,4096]{1,0:T(8,128)(2,1)S(1)}, bf16[8,4096]{1,0:T(8,128)(2,1)S(1)}, u32[]{:S(2)}, u32[]{:S(2)}) collective-permute-start(bf16[8,4096]{1,0:T(8,128)(2,1)S(1)} %get-tuple-element.30), channel_id=1, source_target_pairs={{0,3},{1,2},{2,1},{3,0},{4,7},{5,6},{6,5},{7,4},{8,11},{9,10},{10,... | collective-permute-start | bytes 196616 | tf_op jit(solution)/shard_map/ppermute | solution.py:28

commit v3 on v1

--- a/solution.py
+++ b/solution.py
@@ -40,7 +40,7 @@
 
 
 def plane_steps():
-    return [("dp", mask) for mask in range(lax.axis_size("dp") - 2, 0, -2)]
+    return [("dp", mask) for mask in range(2, lax.axis_size("dp"), 2)]
 
 
 def cat(parts):
@@ -50,15 +50,20 @@
 def split(value, count):
     step = value.shape[0] // count
     return [value[start : start + step] for start in range(0, value.shape[0], step)]
+
+
+def after(value, *others):
+    return lax.optimization_barrier((value, *others))[0]
 
 
 def gather_rows(block):
     depth = lax.axis_size("expert")
     column = [block] + [swap(block, "expert", mask) for mask in range(1, depth)]
     near = join(column[: depth // 2])
-    near_rest = [swap(near, *step) for step in plane_steps()]
+    steps = plane_steps()
+    near_rest = [swap(near, *step) for step in steps]
     far = cat(column[depth // 2 :])
-    far_rest = [swap(far, *step) for step in plane_steps()]
+    far_rest = [swap(far, *step) for step in steps]
     near = cat([near, *near_rest])
     near_there = swap(near, *CORE)
     far = cat([far, *far_rest])
@@ -67,10 +72,13 @@
 
 def scatter_sums(kept, away):
     steps, depth = plane_steps(), lax.axis_size("expert")
-    sums = []
+    sums, here = [], []
     for mine, other in reversed(list(zip(kept, away))):
         part, *rest = split(mine + wide(swap(other, *CORE)), len(steps) + 1)
-        here = [send(other, step) for other, step in zip(rest, steps)]
+        rest = [other.astype(jnp.bfloat16) for other in rest[::-1]]
+        if here:
+            rest = [after(other, here[0]) for other in rest]
+        here = [send(other, step) for other, step in zip(rest, steps[::-1])]
         sums.append(sum([wide(other) for other in here], part))
     far, (total, *near) = split(sums[0], depth // 2), split(sums[1], depth // 2)
     far = [send(part, ("expert", mask + depth // 2)) for mask, part in enumerate(far)]

time: 56 us -> 55 us (0.982)
  starting transfers between devices: 25.2 us -> 23.3 us
  waiting for transfers between devices: 20.6 us -> 21.5 us
    ppermute x22, starting transfers between devices: 25.2 us -> 23.3 us  [swap(): return lax.ppermute(value, axis, [(i, i ^ mask) for i in range(count)])]
    ppermute x22, waiting for transfers between devices: 20.6 us -> 21.5 us  [swap(): return lax.ppermute(value, axis, [(i, i ^ mask) for i in range(count)])]
  transfers between devices with their start and end apart: 22 -> 22, of which waited for: 10 -> 11; matrix products, arithmetic and copies ran while one was open for 1% -> 1% of each run, Pallas kernels for 0% -> 0%
where the time goes in v3:
time: 55 us; the launch traced here: 54.8 us
  starting transfers between devices  23.3 us (42%)
  waiting for transfers between devices  21.5 us (39%)
  Pallas kernels  8.56 us (16%)
  other arithmetic  1.07 us (2%)
    ppermute x22, starting transfers between devices, swap(): return lax.ppermute(value, axis, [(i, i ^ mask) for i in range(count)])  23.3 us
    ppermute x22, waiting for transfers between devices, swap(): return lax.ppermute(value, axis, [(i, i ^ mask) for i in range(count)])  21.5 us
    pallas_call x1, Pallas kernels, run_experts(): pl.pallas_call(functools.partial(expert_kernel, exp_dev, expert_total, le...  7.01 us
    pallas_call x1, Pallas kernels, pack(): pl.pallas_call(pack_kernel, out_shape=pltpu.VMEM((rows, width + extra), t...  1.54 us
  transfers between devices with their start and end apart: 22, of which 11 were waited for; matrix products, arithmetic and copies ran while one was open for 1% of the time, Pallas kernels for 0%

profile of v3, /device:TPU:0, one launch (start us, length us, event | category | flops | bytes accessed | tf_op | source)
XLA Modules:
  0.0 54.8 jit_solution(3526619053362303092)
XLA Ops:
  0.0 0.0 slice-start
  0.0 0.0 slice-start.2
  0.0 0.0 slice-start.4
  0.0 1.5 %shard_map.64.refs_0_ = bf16[8,4224]{1,0:T(8,128)(2,1)S(1)} custom-call(bf16[8,4096]{1,0:T(8,128)(2,1)} %tokens_hbm.1, s32[8,8]{1,0:T(8,128)} %ids_hbm.1, bf16[16,4096]{1,0:T(8,128)(2,1)} %router_hbm.1), custom_call_target="tpu_custom_call" | custom-call | flops 1048576 | bytes 262144 | tf_op jit(solution)/shard_map/pallas_call | solution.py:126
  1.6 0.0 slice-start.1
  1.6 0.0 slice-start.3
  1.6 0.0 slice-start.5
  1.6 3.1 %collective-permute-start = (bf16[8,4224]{1,0:T(8,128)(2,1)S(1)}, bf16[8,4224]{1,0:T(8,128)(2,1)S(1)}, u32[]{:S(2)}, u32[]{:S(2)}) collective-permute-start(bf16[8,4224]{1,0:T(8,128)(2,1)S(1)} %shard_map.64.refs_0_), channel_id=1, source_target_pairs={{0,1},{1,0},{2,3},{3,2},{4,5},{5,4},{6,7},{7,6},{8,9},{9,8},{10,11... | collective-permute-start | bytes 202760 | tf_op jit(solution)/shard_map/ppermute | solution.py:28
  4.7 2.5 %collective-permute-start.5 = (bf16[8,4224]{1,0:T(8,128)(2,1)S(1)}, bf16[8,4224]{1,0:T(8,128)(2,1)S(1)}, u32[]{:S(2)}, u32[]{:S(2)}) collective-permute-start(bf16[8,4224]{1,0:T(8,128)(2,1)S(1)} %shard_map.64.refs_0_), channel_id=1, source_target_pairs={{0,3},{1,2},{2,1},{3,0},{4,7},{5,6},{6,5},{7,4},{8,11},{9,10},{10,... | collective-permute-start | bytes 202760 | tf_op jit(solution)/shard_map/ppermute | solution.py:28
  7.2 0.1 collective-permute-start.4
  7.3 0.0 collective-permute-done.refs_1_
  7.3 2.6 %collective-permute-start.3 = (bf16[16,4224]{1,0:T(8,128)(2,1)S(1)}, bf16[16,4224]{1,0:T(8,128)(2,1)S(1)}, u32[]{:S(2)}, u32[]{:S(2)}) collective-permute-start(bf16[16,4224]{1,0:T(8,128)(2,1)S(1)} %shard_map.65), channel_id=1, source_target_pairs={{0,24},{4,28},{8,16},{12,20},{16,8},{20,12},{24,0},{28,4},{1,25},{... | collective-permute-start | bytes 405512 | tf_op jit(solution)/shard_map/ppermute | solution.py:28
  9.9 0.5 collective-permute-start.2
  10.4 0.4 collective-permute-start.1
  10.9 2.9 %collective-permute-done.4 = bf16[8,4224]{1,0:T(8,128)(2,1)S(1)} collective-permute-done((bf16[8,4224]{1,0:T(8,128)(2,1)S(1)}, bf16[8,4224]{1,0:T(8,128)(2,1)S(1)}, u32[]{:S(2)}, u32[]{:S(2)}) %collective-permute-start.4) | collective-permute-done | bytes 67616 | tf_op jit(solution)/shard_map/ppermute | solution.py:28
  13.8 0.0 collective-permute-done.5
  13.8 2.5 %collective-permute-start.8 = (bf16[16,4224]{1,0:T(8,128)(2,1)S(1)}, bf16[16,4224]{1,0:T(8,128)(2,1)S(1)}, u32[]{:S(2)}, u32[]{:S(2)}) collective-permute-start(bf16[16,4224]{1,0:T(8,128)(2,1)S(1)} %get-tuple-element.35), channel_id=1, source_target_pairs={{0,24},{4,28},{8,16},{12,20},{16,8},{20,12},{24,0},{28,4},{1,25},{... | collective-permute-start | bytes 405512 | tf_op jit(solution)/shard_map/ppermute | solution.py:28
  16.3 0.5 collective-permute-start.7
  16.8 0.0 collective-permute-done.3
  16.8 0.5 collective-permute-start.6
  17.4 0.0 collective-permute-done.2
  17.4 0.0 collective-permute-done.1
  17.4 0.1 collective-permute-start.9
  17.5 5.7 %collective-permute-done.6 = bf16[16,4224]{1,0:T(8,128)(2,1)S(1)} collective-permute-done((bf16[16,4224]{1,0:T(8,128)(2,1)S(1)}, bf16[16,4224]{1,0:T(8,128)(2,1)S(1)}, u32[]{:S(2)}, u32[]{:S(2)}) %collective-permute-start.6) | collective-permute-done | bytes 135200 | tf_op jit(solution)/shard_map/ppermute | solution.py:28
  23.2 0.0 collective-permute-done.7
  23.2 0.0 collective-permute-done.8
  23.3 0.1 collective-permute-start.10
  23.3 0.0 collective-permute-done.9.refs_2_
  23.4 1.9 %collective-permute-done.10.refs_3_ = bf16[64,4224]{1,0:T(8,128)(2,1)S(1)} collective-permute-done((bf16[64,4224]{1,0:T(8,128)(2,1)S(1)}, bf16[64,4224]{1,0:T(8,128)(2,1)S(1)}, u32[]{:S(2)}, u32[]{:S(2)}) %collective-permute-start.10) | collective-permute-done | bytes 540704 | tf_op jit(solution)/shard_map/ppermute | solution.py:28
  25.3 0.0 slice-done
  25.3 0.0 slice-done.2
  25.3 0.0 slice-done.4
  25.3 0.0 slice-done.1
  25.3 0.0 slice-done.3
  25.3 0.0 slice-done.5
  25.3 7.0 %shard_map.66 = (f32[64,4096]{1,0:T(8,128)S(1)}, f32[64,4096]{1,0:T(8,128)S(1)}, bf16[64,4096]{1,0:T(8,128)(2,1)S(1)}, bf16[64,4096]{1,0:T(8,128)(2,1)S(1)}) custom-call(bf16[64,4224]{1,0:T(8,128)(2,1)S(1)} %pad_maximum_fusion.refs_0_, bf16[64,4224]{1,0:T(8,128)(2,1)S(1)} %constant_dynamic-update-slice_fusion.2.refs_1_, ...), custom_call_target="tpu_custom_call" | custom-call | flops 4831838208 | bytes 5242880 | tf_op jit(solution)/shard_map/pallas_call | solution.py:207
  32.3 0.2 collective-permute-start.12
  32.5 0.4 collective-permute-start.11
  32.9 1.4 %collective-permute-done.12 = bf16[64,4096]{1,0:T(8,128)(2,1)S(1)} collective-permute-done((bf16[64,4096]{1,0:T(8,128)(2,1)S(1)}, bf16[64,4096]{1,0:T(8,128)(2,1)S(1)}, u32[]{:S(2)}, u32[]{:S(2)}) %collective-permute-start.12) | collective-permute-done | bytes 524320 | tf_op jit(solution)/shard_map/ppermute | solution.py:28
  34.3 0.1 fusion.8
  34.5 1.7 %collective-permute-start.13 = (bf16[16,4096]{1,0:T(8,128)(2,1)S(1)}, bf16[16,4096]{1,0:T(8,128)(2,1)S(1)}, u32[]{:S(2)}, u32[]{:S(2)}) collective-permute-start(bf16[16,4096]{1,0:T(8,128)(2,1)S(1)} %get-tuple-element.30), channel_id=1, source_target_pairs={{0,24},{4,28},{8,16},{12,20},{16,8},{20,12},{24,0},{28,4},{1,25},{... | collective-permute-start | bytes 393224 | tf_op jit(solution)/shard_map/ppermute | solution.py:28
  36.2 1.2 %collective-permute-start.18 = (bf16[16,4096]{1,0:T(8,128)(2,1)S(1)}, bf16[16,4096]{1,0:T(8,128)(2,1)S(1)}, u32[]{:S(2)}, u32[]{:S(2)}) collective-permute-start(bf16[16,4096]{1,0:T(8,128)(2,1)S(1)} %get-tuple-element.31), channel_id=1, source_target_pairs={{0,8},{4,12},{8,0},{12,4},{16,24},{20,28},{24,16},{28,20},{1,9},{5... | collective-permute-start | bytes 393224 | tf_op jit(solution)/shard_map/ppermute | solution.py:28
  37.4 0.6 %collective-permute-start.17 = (bf16[16,4096]{1,0:T(8,128)(2,1)S(1)}, bf16[16,4096]{1,0:T(8,128)(2,1)S(1)}, u32[]{:S(2)}, u32[]{:S(2)}) collective-permute-start(bf16[16,4096]{1,0:T(8,128)(2,1)S(1)} %get-tuple-element.32), channel_id=1, source_target_pairs={{0,16},{4,20},{8,24},{12,28},{16,0},{20,4},{24,8},{28,12},{1,17},{... | collective-permute-start | bytes 393224 | tf_op jit(solution)/shard_map/ppermute | solution.py:28
  38.0 0.0 collective-permute-done.11
  38.0 0.1 fusion.7
  38.2 3.6 %collective-permute-done.13 = bf16[16,4096]{1,0:T(8,128)(2,1)S(1)} collective-permute-done((bf16[16,4096]{1,0:T(8,128)(2,1)S(1)}, bf16[16,4096]{1,0:T(8,128)(2,1)S(1)}, u32[]{:S(2)}, u32[]{:S(2)}) %collective-permute-start.13) | collective-permute-done | bytes 131104 | tf_op jit(solution)/shard_map/ppermute | solution.py:28
  41.8 1.6 %collective-permute-start.14 = (bf16[16,4096]{1,0:T(8,128)(2,1)S(1)}, bf16[16,4096]{1,0:T(8,128)(2,1)S(1)}, u32[]{:S(2)}, u32[]{:S(2)}) collective-permute-start(bf16[16,4096]{1,0:T(8,128)(2,1)S(1)} %get-tuple-element.18), channel_id=1, source_target_pairs={{0,24},{4,28},{8,16},{12,20},{16,8},{20,12},{24,0},{28,4},{1,25},{... | collective-permute-start | bytes 393224 | tf_op jit(solution)/shard_map/ppermute | solution.py:28
  43.4 1.3 %collective-permute-start.15 = (bf16[16,4096]{1,0:T(8,128)(2,1)S(1)}, bf16[16,4096]{1,0:T(8,128)(2,1)S(1)}, u32[]{:S(2)}, u32[]{:S(2)}) collective-permute-start(bf16[16,4096]{1,0:T(8,128)(2,1)S(1)} %get-tuple-element.19), channel_id=1, source_target_pairs={{0,16},{4,20},{8,24},{12,28},{16,0},{20,4},{24,8},{28,12},{1,17},{... | collective-permute-start | bytes 393224 | tf_op jit(solution)/shard_map/ppermute | solution.py:28
  44.8 0.5 collective-permute-start.16
  45.3 0.0 collective-permute-done.18
  45.3 0.0 collective-permute-done.17
  45.3 0.1 fusion.2
  45.4 1.5 %collective-permute-start.19 = (bf16[8,4096]{1,0:T(8,128)(2,1)S(1)}, bf16[8,4096]{1,0:T(8,128)(2,1)S(1)}, u32[]{:S(2)}, u32[]{:S(2)}) collective-permute-start(bf16[8,4096]{1,0:T(8,128)(2,1)S(1)} %get-tuple-element.33), channel_id=1, source_target_pairs={{0,2},{1,3},{2,0},{3,1},{4,6},{5,7},{6,4},{7,5},{8,10},{9,11},{10,... | collective-permute-start | bytes 196616 | tf_op jit(solution)/shard_map/ppermute | solution.py:28
  46.9 1.0 %collective-permute-start.20 = (bf16[8,4096]{1,0:T(8,128)(2,1)S(1)}, bf16[8,4096]{1,0:T(8,128)(2,1)S(1)}, u32[]{:S(2)}, u32[]{:S(2)}) collective-permute-start(bf16[8,4096]{1,0:T(8,128)(2,1)S(1)} %get-tuple-element.34), channel_id=1, source_target_pairs={{0,3},{1,2},{2,1},{3,0},{4,7},{5,6},{6,5},{7,4},{8,11},{9,10},{10,... | collective-permute-start | bytes 196616 | tf_op jit(solution)/shard_map/ppermute | solution.py:28
  47.9 0.4 collective-permute-done.14
  48.3 1.1 %collective-permute-done.15 = bf16[16,4096]{1,0:T(8,128)(2,1)S(1)} collective-permute-done((bf16[16,4096]{1,0:T(8,128)(2,1)S(1)}, bf16[16,4096]{1,0:T(8,128)(2,1)S(1)}, u32[]{:S(2)}, u32[]{:S(2)}) %collective-permute-start.15) | collective-permute-done | bytes 131104 | tf_op jit(solution)/shard_map/ppermute | solution.py:28
  49.4 0.3 collective-permute-done.16
  49.7 0.1 fusion.4
  49.8 0.2 collective-permute-start.21
  50.0 1.5 %collective-permute-done.19 = bf16[8,4096]{1,0:T(8,128)(2,1)S(1)} collective-permute-done((bf16[8,4096]{1,0:T(8,128)(2,1)S(1)}, bf16[8,4096]{1,0:T(8,128)(2,1)S(1)}, u32[]{:S(2)}, u32[]{:S(2)}) %collective-permute-start.19) | collective-permute-done | bytes 65568 | tf_op jit(solution)/shard_map/ppermute | solution.py:28
  51.5 1.5 %collective-permute-done.20 = bf16[8,4096]{1,0:T(8,128)(2,1)S(1)} collective-permute-done((bf16[8,4096]{1,0:T(8,128)(2,1)S(1)}, bf16[8,4096]{1,0:T(8,128)(2,1)S(1)}, u32[]{:S(2)}, u32[]{:S(2)}) %collective-permute-start.20) | collective-permute-done | bytes 65568 | tf_op jit(solution)/shard_map/ppermute | solution.py:28
  53.0 1.2 %collective-permute-done.21 = bf16[8,4096]{1,0:T(8,128)(2,1)S(1)} collective-permute-done((bf16[8,4096]{1,0:T(8,128)(2,1)S(1)}, bf16[8,4096]{1,0:T(8,128)(2,1)S(1)}, u32[]{:S(2)}, u32[]{:S(2)}) %collective-permute-start.21) | collective-permute-done | bytes 65568 | tf_op jit(solution)/shard_map/ppermute | solution.py:28
  54.2 0.6 %fusion.6 = bf16[8,4096]{1,0:T(8,128)(2,1)} fusion(f32[8,4096]{1,0:T(8,128)S(1)} %convert_add_fusion.2, f32[16,4096]{1,0:T(8,128)S(1)} %fusion.4, bf16[8,4096]{1,0:T(8,128)(2,1)S(1)} %collective-permute-done.21), kind=kLoop, calls=%fused_computation.13 | loop fusion | flops 131072 | bytes 393216 | tf_op jit(solution)/shard_map/convert_element_type | solution.py:88
  (15 shorter events, 0.2 us)
Async XLA Ops:
  0.0 25.3 %slice-start = ((s8[6291456]{0:T(1024)(128)(4,1)}), s8[4194304]{0:T(1024)(128)(4,1)S(1)}, s32[]{:S(2)}) async-start(s8[6291456]{0:T(1024)(128)(4,1)} %bitcast), calls=%async_computation | async-start | bytes 8388608
  0.0 25.3 %slice-start.2 = ((s8[6291456]{0:T(1024)(128)(4,1)}), s8[4194304]{0:T(1024)(128)(4,1)S(1)}, s32[]{:S(2)}) async-start(s8[6291456]{0:T(1024)(128)(4,1)} %bitcast.2), calls=%async_computation.2 | async-start | bytes 8388608
  0.0 25.3 %slice-start.4 = ((s8[6291456]{0:T(1024)(128)(4,1)}), s8[4194304]{0:T(1024)(128)(4,1)S(1)}, s32[]{:S(2)}) async-start(s8[6291456]{0:T(1024)(128)(4,1)} %bitcast.4), calls=%async_computation.4 | async-start | bytes 8388608
  1.6 23.7 %slice-start.1 = ((s8[6291456]{0:T(1024)(128)(4,1)}), s8[2097152]{0:T(1024)(128)(4,1)S(1)}, s32[]{:S(2)}) async-start(s8[6291456]{0:T(1024)(128)(4,1)} %bitcast), calls=%async_computation.1 | async-start | bytes 4194304
  1.6 23.7 %slice-start.3 = ((s8[6291456]{0:T(1024)(128)(4,1)}), s8[2097152]{0:T(1024)(128)(4,1)S(1)}, s32[]{:S(2)}) async-start(s8[6291456]{0:T(1024)(128)(4,1)} %bitcast.2), calls=%async_computation.3 | async-start | bytes 4194304
  1.6 23.7 %slice-start.5 = ((s8[6291456]{0:T(1024)(128)(4,1)}), s8[2097152]{0:T(1024)(128)(4,1)S(1)}, s32[]{:S(2)}) async-start(s8[6291456]{0:T(1024)(128)(4,1)} %bitcast.4), calls=%async_computation.5 | async-start | bytes 4194304
  1.6 5.7 %collective-permute-start = (bf16[8,4224]{1,0:T(8,128)(2,1)S(1)}, bf16[8,4224]{1,0:T(8,128)(2,1)S(1)}, u32[]{:S(2)}, u32[]{:S(2)}) collective-permute-start(bf16[8,4224]{1,0:T(8,128)(2,1)S(1)} %shard_map.64.refs_0_), channel_id=1, source_target_pairs={{0,1},{1,0},{2,3},{3,2},{4,5},{5,4},{6,7},{7,6},{8,9},{9,8},{10,11... | collective-permute-start | bytes 202760 | tf_op jit(solution)/shard_map/ppermute | solution.py:28
  4.7 9.1 %collective-permute-start.5 = (bf16[8,4224]{1,0:T(8,128)(2,1)S(1)}, bf16[8,4224]{1,0:T(8,128)(2,1)S(1)}, u32[]{:S(2)}, u32[]{:S(2)}) collective-permute-start(bf16[8,4224]{1,0:T(8,128)(2,1)S(1)} %shard_map.64.refs_0_), channel_id=1, source_target_pairs={{0,3},{1,2},{2,1},{3,0},{4,7},{5,6},{6,5},{7,4},{8,11},{9,10},{10,... | collective-permute-start | bytes 202760 | tf_op jit(solution)/shard_map/ppermute | solution.py:28
  7.2 6.6 %collective-permute-start.4 = (bf16[8,4224]{1,0:T(8,128)(2,1)S(1)}, bf16[8,4224]{1,0:T(8,128)(2,1)S(1)}, u32[]{:S(2)}, u32[]{:S(2)}) collective-permute-start(bf16[8,4224]{1,0:T(8,128)(2,1)S(1)} %shard_map.64.refs_0_), channel_id=1, source_target_pairs={{0,2},{1,3},{2,0},{3,1},{4,6},{5,7},{6,4},{7,5},{8,10},{9,11},{10,... | collective-permute-start | bytes 202760 | tf_op jit(solution)/shard_map/ppermute | solution.py:28
  7.3 9.5 %collective-permute-start.3 = (bf16[16,4224]{1,0:T(8,128)(2,1)S(1)}, bf16[16,4224]{1,0:T(8,128)(2,1)S(1)}, u32[]{:S(2)}, u32[]{:S(2)}) collective-permute-start(bf16[16,4224]{1,0:T(8,128)(2,1)S(1)} %shard_map.65), channel_id=1, source_target_pairs={{0,24},{4,28},{8,16},{12,20},{16,8},{20,12},{24,0},{28,4},{1,25},{... | collective-permute-start | bytes 405512 | tf_op jit(solution)/shard_map/ppermute | solution.py:28
  9.9 7.4 %collective-permute-start.2 = (bf16[16,4224]{1,0:T(8,128)(2,1)S(1)}, bf16[16,4224]{1,0:T(8,128)(2,1)S(1)}, u32[]{:S(2)}, u32[]{:S(2)}) collective-permute-start(bf16[16,4224]{1,0:T(8,128)(2,1)S(1)} %shard_map.65), channel_id=1, source_target_pairs={{0,16},{4,20},{8,24},{12,28},{16,0},{20,4},{24,8},{28,12},{1,17},{... | collective-permute-start | bytes 405512 | tf_op jit(solution)/shard_map/ppermute | solution.py:28
  10.4 6.9 %collective-permute-start.1 = (bf16[16,4224]{1,0:T(8,128)(2,1)S(1)}, bf16[16,4224]{1,0:T(8,128)(2,1)S(1)}, u32[]{:S(2)}, u32[]{:S(2)}) collective-permute-start(bf16[16,4224]{1,0:T(8,128)(2,1)S(1)} %shard_map.65), channel_id=1, source_target_pairs={{0,8},{4,12},{8,0},{12,4},{16,24},{20,28},{24,16},{28,20},{1,9},{5... | collective-permute-start | bytes 405512 | tf_op jit(solution)/shard_map/ppermute | solution.py:28
  13.8 9.4 %collective-permute-start.8 = (bf16[16,4224]{1,0:T(8,128)(2,1)S(1)}, bf16[16,4224]{1,0:T(8,128)(2,1)S(1)}, u32[]{:S(2)}, u32[]{:S(2)}) collective-permute-start(bf16[16,4224]{1,0:T(8,128)(2,1)S(1)} %get-tuple-element.35), channel_id=1, source_target_pairs={{0,24},{4,28},{8,16},{12,20},{16,8},{20,12},{24,0},{28,4},{1,25},{... | collective-permute-start | bytes 405512 | tf_op jit(solution)/shard_map/ppermute | solution.py:28
  16.3 6.9 %collective-permute-start.7 = (bf16[16,4224]{1,0:T(8,128)(2,1)S(1)}, bf16[16,4224]{1,0:T(8,128)(2,1)S(1)}, u32[]{:S(2)}, u32[]{:S(2)}) collective-permute-start(bf16[16,4224]{1,0:T(8,128)(2,1)S(1)} %get-tuple-element.35), channel_id=1, source_target_pairs={{0,16},{4,20},{8,24},{12,28},{16,0},{20,4},{24,8},{28,12},{1,17},{... | collective-permute-start | bytes 405512 | tf_op jit(solution)/shard_map/ppermute | solution.py:28
  16.8 6.4 %collective-permute-start.6 = (bf16[16,4224]{1,0:T(8,128)(2,1)S(1)}, bf16[16,4224]{1,0:T(8,128)(2,1)S(1)}, u32[]{:S(2)}, u32[]{:S(2)}) collective-permute-start(bf16[16,4224]{1,0:T(8,128)(2,1)S(1)} %get-tuple-element.35), channel_id=1, source_target_pairs={{0,8},{4,12},{8,0},{12,4},{16,24},{20,28},{24,16},{28,20},{1,9},{5... | collective-permute-start | bytes 405512 | tf_op jit(solution)/shard_map/ppermute | solution.py:28
  17.4 5.9 %collective-permute-start.9 = (bf16[64,4224]{1,0:T(8,128)(2,1)S(1)}, bf16[64,4224]{1,0:T(8,128)(2,1)S(1)}, u32[]{:S(2)}, u32[]{:S(2)}) collective-permute-start(bf16[64,4224]{1,0:T(8,128)(2,1)S(1)} %pad_maximum_fusion.refs_0_), channel_id=1, source_target_pairs={{0,4},{4,0},{8,12},{12,8},{16,20},{20,16},{24,28},{28,24},{1,5},{5... | collective-permute-start | bytes 1622024 | tf_op jit(solution)/shard_map/ppermute | solution.py:28
  23.3 2.0 %collective-permute-start.10 = (bf16[64,4224]{1,0:T(8,128)(2,1)S(1)}, bf16[64,4224]{1,0:T(8,128)(2,1)S(1)}, u32[]{:S(2)}, u32[]{:S(2)}) collective-permute-start(bf16[64,4224]{1,0:T(8,128)(2,1)S(1)} %constant_dynamic-update-slice_fusion.2.refs_1_), channel_id=1, source_target_pairs={{0,4},{4,0},{8,12},{12,8},{16,20},{20,16},{24,28},{28,24},{1,5},{5... | collective-permute-start | bytes 1622024 | tf_op jit(solution)/shard_map/ppermute | solution.py:28
  32.3 2.0 %collective-permute-start.12 = (bf16[64,4096]{1,0:T(8,128)(2,1)S(1)}, bf16[64,4096]{1,0:T(8,128)(2,1)S(1)}, u32[]{:S(2)}, u32[]{:S(2)}) collective-permute-start(bf16[64,4096]{1,0:T(8,128)(2,1)S(1)} %get-tuple-element.17), channel_id=1, source_target_pairs={{0,4},{4,0},{8,12},{12,8},{16,20},{20,16},{24,28},{28,24},{1,5},{5... | collective-permute-start | bytes 1572872 | tf_op jit(solution)/shard_map/ppermute | solution.py:28
  32.5 5.5 %collective-permute-start.11 = (bf16[64,4096]{1,0:T(8,128)(2,1)S(1)}, bf16[64,4096]{1,0:T(8,128)(2,1)S(1)}, u32[]{:S(2)}, u32[]{:S(2)}) collective-permute-start(bf16[64,4096]{1,0:T(8,128)(2,1)S(1)} %get-tuple-element.15), channel_id=1, source_target_pairs={{0,4},{4,0},{8,12},{12,8},{16,20},{20,16},{24,28},{28,24},{1,5},{5... | collective-permute-start | bytes 1572872 | tf_op jit(solution)/shard_map/ppermute | solution.py:28
  34.5 7.3 %collective-permute-start.13 = (bf16[16,4096]{1,0:T(8,128)(2,1)S(1)}, bf16[16,4096]{1,0:T(8,128)(2,1)S(1)}, u32[]{:S(2)}, u32[]{:S(2)}) collective-permute-start(bf16[16,4096]{1,0:T(8,128)(2,1)S(1)} %get-tuple-element.30), channel_id=1, source_target_pairs={{0,24},{4,28},{8,16},{12,20},{16,8},{20,12},{24,0},{28,4},{1,25},{... | collective-permute-start | bytes 393224 | tf_op jit(solution)/shard_map/ppermute | solution.py:28
  36.2 9.1 %collective-permute-start.18 = (bf16[16,4096]{1,0:T(8,128)(2,1)S(1)}, bf16[16,4096]{1,0:T(8,128)(2,1)S(1)}, u32[]{:S(2)}, u32[]{:S(2)}) collective-permute-start(bf16[16,4096]{1,0:T(8,128)(2,1)S(1)} %get-tuple-element.31), channel_id=1, source_target_pairs={{0,8},{4,12},{8,0},{12,4},{16,24},{20,28},{24,16},{28,20},{1,9},{5... | collective-permute-start | bytes 393224 | tf_op jit(solution)/shard_map/ppermute | solution.py:28
  37.4 7.9 %collective-permute-start.17 = (bf16[16,4096]{1,0:T(8,128)(2,1)S(1)}, bf16[16,4096]{1,0:T(8,128)(2,1)S(1)}, u32[]{:S(2)}, u32[]{:S(2)}) collective-permute-start(bf16[16,4096]{1,0:T(8,128)(2,1)S(1)} %get-tuple-element.32), channel_id=1, source_target_pairs={{0,16},{4,20},{8,24},{12,28},{16,0},{20,4},{24,8},{28,12},{1,17},{... | collective-permute-start | bytes 393224 | tf_op jit(solution)/shard_map/ppermute | solution.py:28
  41.8 6.5 %collective-permute-start.14 = (bf16[16,4096]{1,0:T(8,128)(2,1)S(1)}, bf16[16,4096]{1,0:T(8,128)(2,1)S(1)}, u32[]{:S(2)}, u32[]{:S(2)}) collective-permute-start(bf16[16,4096]{1,0:T(8,128)(2,1)S(1)} %get-tuple-element.18), channel_id=1, source_target_pairs={{0,24},{4,28},{8,16},{12,20},{16,8},{20,12},{24,0},{28,4},{1,25},{... | collective-permute-start | bytes 393224 | tf_op jit(solution)/shard_map/ppermute | solution.py:28
  43.4 6.0 %collective-permute-start.15 = (bf16[16,4096]{1,0:T(8,128)(2,1)S(1)}, bf16[16,4096]{1,0:T(8,128)(2,1)S(1)}, u32[]{:S(2)}, u32[]{:S(2)}) collective-permute-start(bf16[16,4096]{1,0:T(8,128)(2,1)S(1)} %get-tuple-element.19), channel_id=1, source_target_pairs={{0,16},{4,20},{8,24},{12,28},{16,0},{20,4},{24,8},{28,12},{1,17},{... | collective-permute-start | bytes 393224 | tf_op jit(solution)/shard_map/ppermute | solution.py:28
  44.8 5.0 %collective-permute-start.16 = (bf16[16,4096]{1,0:T(8,128)(2,1)S(1)}, bf16[16,4096]{1,0:T(8,128)(2,1)S(1)}, u32[]{:S(2)}, u32[]{:S(2)}) collective-permute-start(bf16[16,4096]{1,0:T(8,128)(2,1)S(1)} %get-tuple-element.20), channel_id=1, source_target_pairs={{0,8},{4,12},{8,0},{12,4},{16,24},{20,28},{24,16},{28,20},{1,9},{5... | collective-permute-start | bytes 393224 | tf_op jit(solution)/shard_map/ppermute | solution.py:28
  45.4 6.1 %collective-permute-start.19 = (bf16[8,4096]{1,0:T(8,128)(2,1)S(1)}, bf16[8,4096]{1,0:T(8,128)(2,1)S(1)}, u32[]{:S(2)}, u32[]{:S(2)}) collective-permute-start(bf16[8,4096]{1,0:T(8,128)(2,1)S(1)} %get-tuple-element.33), channel_id=1, source_target_pairs={{0,2},{1,3},{2,0},{3,1},{4,6},{5,7},{6,4},{7,5},{8,10},{9,11},{10,... | collective-permute-start | bytes 196616 | tf_op jit(solution)/shard_map/ppermute | solution.py:28
  46.9 6.1 %collective-permute-start.20 = (bf16[8,4096]{1,0:T(8,128)(2,1)S(1)}, bf16[8,4096]{1,0:T(8,128)(2,1)S(1)}, u32[]{:S(2)}, u32[]{:S(2)}) collective-permute-start(bf16[8,4096]{1,0:T(8,128)(2,1)S(1)} %get-tuple-element.34), channel_id=1, source_target_pairs={{0,3},{1,2},{2,1},{3,0},{4,7},{5,6},{6,5},{7,4},{8,11},{9,10},{10,... | collective-permute-start | bytes 196616 | tf_op jit(solution)/shard_map/ppermute | solution.py:28
  49.8 4.3 %collective-permute-start.21 = (bf16[8,4096]{1,0:T(8,128)(2,1)S(1)}, bf16[8,4096]{1,0:T(8,128)(2,1)S(1)}, u32[]{:S(2)}, u32[]{:S(2)}) collective-permute-start(bf16[8,4096]{1,0:T(8,128)(2,1)S(1)} %slice.87), channel_id=1, source_target_pairs={{0,1},{1,0},{2,3},{3,2},{4,5},{5,4},{6,7},{7,6},{8,9},{9,8},{10,11... | collective-permute-start | bytes 196616 | tf_op jit(solution)/shard_map/ppermute | solution.py:28

commit v4 on v3

--- a/solution.py
+++ b/solution.py
@@ -56,13 +56,22 @@
     return lax.optimization_barrier((value, *others))[0]
 
 
+def gather_near(near, steps):
+    if len(steps) != 3:
+        return [swap(near, *step) for step in steps]
+    x, y, _ = steps
+    near_x, near_y = swap(near, *x), swap(near, *y)
+    over_y, over_x = swap(split(near_x, 2)[0], *y), swap(split(near_y, 2)[1], *x)
+    return [near_x, near_y, over_y, over_x]
+
+
 def gather_rows(block):
     depth = lax.axis_size("expert")
     column = [block] + [swap(block, "expert", mask) for mask in range(1, depth)]
     near = join(column[: depth // 2])
     steps = plane_steps()
-    near_rest = [swap(near, *step) for step in steps]
-    far = cat(column[depth // 2 :])
+    near_rest = gather_near(near, steps)
+    far = cat([after(column[depth // 2], *near_rest[:2]), *column[depth // 2 + 1 :]])
     far_rest = [swap(far, *step) for step in steps]
     near = cat([near, *near_rest])
     near_there = swap(near, *CORE)
@@ -72,14 +81,20 @@
 
 def scatter_sums(kept, away):
     steps, depth = plane_steps(), lax.axis_size("expert")
-    sums, here = [], []
-    for mine, other in reversed(list(zip(kept, away))):
-        part, *rest = split(mine + wide(swap(other, *CORE)), len(steps) + 1)
-        rest = [other.astype(jnp.bfloat16) for other in rest[::-1]]
-        if here:
-            rest = [after(other, here[0]) for other in rest]
-        here = [send(other, step) for other, step in zip(rest, steps[::-1])]
-        sums.append(sum([wide(other) for other in here], part))
+    near, far = [mine + wide(swap(other, *CORE)) for mine, other in zip(kept, away)]
+    far, *rest = split(far, len(steps) + 1)
+    far_here = [send(other, step) for other, step in zip(rest[::-1], steps[::-1])]
+    far = sum([wide(other) for other in far_here], far)
+    near, *rest = split(near, len(steps) + 1)
+    if len(steps) == 3:
+        x, y, _ = steps
+        (x_first, x_last), (y_first, y_last), (over_y, over_x) = [split(part, 2) for part in rest]
+        x_first = x_first + wide(send(over_y, y))
+        y_last = y_last + wide(send(over_x, x))
+        rest, steps = [cat([x_first, x_last]), cat([y_first, y_last])], [x, y]
+    rest = [after(other.astype(jnp.bfloat16), far_here[0]) for other in rest[::-1]]
+    near_here = [send(other, step) for other, step in zip(rest, steps[::-1])]
+    sums = [far, sum([wide(other) for other in near_here], near)]
     far, (total, *near) = split(sums[0], depth // 2), split(sums[1], depth // 2)
     far = [send(part, ("expert", mask + depth // 2)) for mask, part in enumerate(far)]
     near = [send(part, ("expert", mask + 1)) for mask, part in enumerate(near)]

time: 55 us -> 58 us (1.055)
  starting transfers between devices: 23.3 us -> 26.4 us
    ppermute x22 -> x24, starting transfers between devices: 23.3 us -> 26.4 us  [swap(): return lax.ppermute(value, axis, [(i, i ^ mask) for i in range(count)])]
    ppermute x22 -> x24, waiting for transfers between devices: 21.5 us -> 21.4 us  [swap(): return lax.ppermute(value, axis, [(i, i ^ mask) for i in range(count)])]
  transfers between devices with their start and end apart: 22 -> 24, of which waited for: 11 -> 15; matrix products, arithmetic and copies ran while one was open for 1% -> 1% of each run, Pallas kernels for 0% -> 0%
where the time goes in v4:
time: 58 us; the launch traced here: 57.9 us
  starting transfers between devices  26.4 us (46%)
  waiting for transfers between devices  21.4 us (37%)
  Pallas kernels  8.56 us (15%)
  other arithmetic  1.06 us (2%)
    ppermute x24, starting transfers between devices, swap(): return lax.ppermute(value, axis, [(i, i ^ mask) for i in range(count)])  26.4 us
    ppermute x24, waiting for transfers between devices, swap(): return lax.ppermute(value, axis, [(i, i ^ mask) for i in range(count)])  21.4 us
    pallas_call x1, Pallas kernels, run_experts(): pl.pallas_call(functools.partial(expert_kernel, exp_dev, expert_total, le...  7.01 us
    pallas_call x1, Pallas kernels, pack(): pl.pallas_call(pack_kernel, out_shape=pltpu.VMEM((rows, width + extra), t...  1.54 us
  transfers between devices with their start and end apart: 24, of which 15 were waited for; matrix products, arithmetic and copies ran while one was open for 1% of the time, Pallas kernels for 0%

profile of v4, /device:TPU:0, one launch (start us, length us, event | category | flops | bytes accessed | tf_op | source)
XLA Modules:
  0.0 57.9 jit_solution(16156679528279934737)
XLA Ops:
  0.0 0.0 slice-start
  0.0 1.5 %shard_map.64.refs_0_ = bf16[8,4224]{1,0:T(8,128)(2,1)S(1)} custom-call(bf16[8,4096]{1,0:T(8,128)(2,1)} %tokens_hbm.1, s32[8,8]{1,0:T(8,128)} %ids_hbm.1, bf16[16,4096]{1,0:T(8,128)(2,1)} %router_hbm.1), custom_call_target="tpu_custom_call" | custom-call | flops 1048576 | bytes 262144 | tf_op jit(solution)/shard_map/pallas_call | solution.py:141
  1.6 0.0 slice-start.1
  1.6 0.0 slice-start.3
  1.6 0.0 slice-start.5
  1.6 3.1 %collective-permute-start = (bf16[8,4224]{1,0:T(8,128)(2,1)S(1)}, bf16[8,4224]{1,0:T(8,128)(2,1)S(1)}, u32[]{:S(2)}, u32[]{:S(2)}) collective-permute-start(bf16[8,4224]{1,0:T(8,128)(2,1)S(1)} %shard_map.64.refs_0_), channel_id=1, source_target_pairs={{0,1},{1,0},{2,3},{3,2},{4,5},{5,4},{6,7},{7,6},{8,9},{9,8},{10,11... | collective-permute-start | bytes 202760 | tf_op jit(solution)/shard_map/ppermute | solution.py:28
  4.7 2.5 %collective-permute-start.6 = (bf16[8,4224]{1,0:T(8,128)(2,1)S(1)}, bf16[8,4224]{1,0:T(8,128)(2,1)S(1)}, u32[]{:S(2)}, u32[]{:S(2)}) collective-permute-start(bf16[8,4224]{1,0:T(8,128)(2,1)S(1)} %shard_map.64.refs_0_), channel_id=1, source_target_pairs={{0,3},{1,2},{2,1},{3,0},{4,7},{5,6},{6,5},{7,4},{8,11},{9,10},{10,... | collective-permute-start | bytes 202760 | tf_op jit(solution)/shard_map/ppermute | solution.py:28
  7.2 0.1 collective-permute-start.5
  7.3 0.0 collective-permute-done.refs_1_
  7.3 1.7 %collective-permute-start.2 = (bf16[16,4224]{1,0:T(8,128)(2,1)S(1)}, bf16[16,4224]{1,0:T(8,128)(2,1)S(1)}, u32[]{:S(2)}, u32[]{:S(2)}) collective-permute-start(bf16[16,4224]{1,0:T(8,128)(2,1)S(1)} %shard_map.65), channel_id=1, source_target_pairs={{0,16},{4,20},{8,24},{12,28},{16,0},{20,4},{24,8},{28,12},{1,17},{... | collective-permute-start | bytes 405512 | tf_op jit(solution)/shard_map/ppermute | solution.py:28
  9.0 1.5 %collective-permute-start.1 = (bf16[16,4224]{1,0:T(8,128)(2,1)S(1)}, bf16[16,4224]{1,0:T(8,128)(2,1)S(1)}, u32[]{:S(2)}, u32[]{:S(2)}) collective-permute-start(bf16[16,4224]{1,0:T(8,128)(2,1)S(1)} %shard_map.65), channel_id=1, source_target_pairs={{0,8},{4,12},{8,0},{12,4},{16,24},{20,28},{24,16},{28,20},{1,9},{5... | collective-permute-start | bytes 405512 | tf_op jit(solution)/shard_map/ppermute | solution.py:28
  10.5 3.3 %collective-permute-done.5 = bf16[8,4224]{1,0:T(8,128)(2,1)S(1)} collective-permute-done((bf16[8,4224]{1,0:T(8,128)(2,1)S(1)}, bf16[8,4224]{1,0:T(8,128)(2,1)S(1)}, u32[]{:S(2)}, u32[]{:S(2)}) %collective-permute-start.5) | collective-permute-done | bytes 67616 | tf_op jit(solution)/shard_map/ppermute | solution.py:28
  13.8 0.0 collective-permute-done.2
  13.8 0.2 collective-permute-done.1
  14.0 0.0 collective-permute-done.6
  14.1 2.3 %collective-permute-start.9 = (bf16[16,4224]{1,0:T(8,128)(2,1)S(1)}, bf16[16,4224]{1,0:T(8,128)(2,1)S(1)}, u32[]{:S(2)}, u32[]{:S(2)}) collective-permute-start(bf16[16,4224]{1,0:T(8,128)(2,1)S(1)} %get-tuple-element.38), channel_id=1, source_target_pairs={{0,24},{4,28},{8,16},{12,20},{16,8},{20,12},{24,0},{28,4},{1,25},{... | collective-permute-start | bytes 405512 | tf_op jit(solution)/shard_map/ppermute | solution.py:28
  16.3 0.7 %collective-permute-start.8 = (bf16[16,4224]{1,0:T(8,128)(2,1)S(1)}, bf16[16,4224]{1,0:T(8,128)(2,1)S(1)}, u32[]{:S(2)}, u32[]{:S(2)}) collective-permute-start(bf16[16,4224]{1,0:T(8,128)(2,1)S(1)} %get-tuple-element.38), channel_id=1, source_target_pairs={{0,16},{4,20},{8,24},{12,28},{16,0},{20,4},{24,8},{28,12},{1,17},{... | collective-permute-start | bytes 405512 | tf_op jit(solution)/shard_map/ppermute | solution.py:28
  17.1 0.5 collective-permute-start.7
  17.6 1.5 %collective-permute-start.4 = (bf16[8,4224]{1,0:T(8,128)(2,1)S(1)}, bf16[8,4224]{1,0:T(8,128)(2,1)S(1)}, u32[]{:S(2)}, u32[]{:S(2)}) collective-permute-start(bf16[8,4224]{1,0:T(8,128)(2,1)S(1)} %slice.88), channel_id=1, source_target_pairs={{0,8},{4,12},{8,0},{12,4},{16,24},{20,28},{24,16},{28,20},{1,9},{5... | collective-permute-start | bytes 202760 | tf_op jit(solution)/shard_map/ppermute | solution.py:28
  19.1 1.3 %collective-permute-start.3 = (bf16[8,4224]{1,0:T(8,128)(2,1)S(1)}, bf16[8,4224]{1,0:T(8,128)(2,1)S(1)}, u32[]{:S(2)}, u32[]{:S(2)}) collective-permute-start(bf16[8,4224]{1,0:T(8,128)(2,1)S(1)} %slice.87), channel_id=1, source_target_pairs={{0,16},{4,20},{8,24},{12,28},{16,0},{20,4},{24,8},{28,12},{1,17},{... | collective-permute-start | bytes 202760 | tf_op jit(solution)/shard_map/ppermute | solution.py:28
  20.4 4.1 %collective-permute-done.3 = bf16[8,4224]{1,0:T(8,128)(2,1)S(1)} collective-permute-done((bf16[8,4224]{1,0:T(8,128)(2,1)S(1)}, bf16[8,4224]{1,0:T(8,128)(2,1)S(1)}, u32[]{:S(2)}, u32[]{:S(2)}) %collective-permute-start.3) | collective-permute-done | bytes 67616 | tf_op jit(solution)/shard_map/ppermute | solution.py:28
  24.6 0.1 collective-permute-done.4
  24.7 0.1 collective-permute-start.10
  24.7 0.0 collective-permute-done.7
  24.8 0.0 collective-permute-done.8
  24.8 0.0 collective-permute-done.9
  24.8 0.5 collective-permute-start.11
  25.4 1.3 %collective-permute-done.10.refs_2_ = bf16[64,4224]{1,0:T(8,128)(2,1)S(1)} collective-permute-done((bf16[64,4224]{1,0:T(8,128)(2,1)S(1)}, bf16[64,4224]{1,0:T(8,128)(2,1)S(1)}, u32[]{:S(2)}, u32[]{:S(2)}) %collective-permute-start.10) | collective-permute-done | bytes 540704 | tf_op jit(solution)/shard_map/ppermute | solution.py:28
  26.6 0.8 %collective-permute-done.11.refs_3_ = bf16[64,4224]{1,0:T(8,128)(2,1)S(1)} collective-permute-done((bf16[64,4224]{1,0:T(8,128)(2,1)S(1)}, bf16[64,4224]{1,0:T(8,128)(2,1)S(1)}, u32[]{:S(2)}, u32[]{:S(2)}) %collective-permute-start.11) | collective-permute-done | bytes 540704 | tf_op jit(solution)/shard_map/ppermute | solution.py:28
  27.4 0.0 slice-done
  27.4 0.0 slice-done.2
  27.4 0.0 slice-done.4
  27.4 0.0 slice-done.1
  27.4 0.0 slice-done.3
  27.5 0.0 slice-done.5
  27.5 7.0 %shard_map.66 = (f32[64,4096]{1,0:T(8,128)S(1)}, f32[64,4096]{1,0:T(8,128)S(1)}, bf16[64,4096]{1,0:T(8,128)(2,1)S(1)}, bf16[64,4096]{1,0:T(8,128)(2,1)S(1)}) custom-call(bf16[64,4224]{1,0:T(8,128)(2,1)S(1)} %constant_dynamic-update-slice_fusion.refs_0_, bf16[64,4224]{1,0:T(8,128)(2,1)S(1)} %constant_dynamic-update-slice_fusion.7.refs_1_, ...), custom_call_target="tpu_custom_call" | custom-call | flops 4831838208 | bytes 5242880 | tf_op jit(solution)/shard_map/pallas_call | solution.py:222
  34.5 0.2 collective-permute-start.12
  34.7 0.4 collective-permute-start.14
  35.1 1.4 %collective-permute-done.12 = bf16[64,4096]{1,0:T(8,128)(2,1)S(1)} collective-permute-done((bf16[64,4096]{1,0:T(8,128)(2,1)S(1)}, bf16[64,4096]{1,0:T(8,128)(2,1)S(1)}, u32[]{:S(2)}, u32[]{:S(2)}) %collective-permute-start.12) | collective-permute-done | bytes 524320 | tf_op jit(solution)/shard_map/ppermute | solution.py:28
  36.5 0.1 fusion.8
  36.6 1.6 %collective-permute-start.17 = (bf16[8,4096]{1,0:T(8,128)(2,1)S(1)}, bf16[8,4096]{1,0:T(8,128)(2,1)S(1)}, u32[]{:S(2)}, u32[]{:S(2)}) collective-permute-start(bf16[8,4096]{1,0:T(8,128)(2,1)S(1)} %get-tuple-element.31), channel_id=1, source_target_pairs={{0,16},{4,20},{8,24},{12,28},{16,0},{20,4},{24,8},{28,12},{1,17},{... | collective-permute-start | bytes 196616 | tf_op jit(solution)/shard_map/ppermute | solution.py:28
  38.2 0.8 %collective-permute-start.13 = (bf16[8,4096]{1,0:T(8,128)(2,1)S(1)}, bf16[8,4096]{1,0:T(8,128)(2,1)S(1)}, u32[]{:S(2)}, u32[]{:S(2)}) collective-permute-start(bf16[8,4096]{1,0:T(8,128)(2,1)S(1)} %get-tuple-element.32), channel_id=1, source_target_pairs={{0,8},{4,12},{8,0},{12,4},{16,24},{20,28},{24,16},{28,20},{1,9},{5... | collective-permute-start | bytes 196616 | tf_op jit(solution)/shard_map/ppermute | solution.py:28
  39.0 0.0 collective-permute-done.14
  39.0 0.1 fusion.9
  39.1 1.3 %collective-permute-start.15 = (bf16[16,4096]{1,0:T(8,128)(2,1)S(1)}, bf16[16,4096]{1,0:T(8,128)(2,1)S(1)}, u32[]{:S(2)}, u32[]{:S(2)}) collective-permute-start(bf16[16,4096]{1,0:T(8,128)(2,1)S(1)} %get-tuple-element.33), channel_id=1, source_target_pairs={{0,24},{4,28},{8,16},{12,20},{16,8},{20,12},{24,0},{28,4},{1,25},{... | collective-permute-start | bytes 393224 | tf_op jit(solution)/shard_map/ppermute | solution.py:28
  40.4 1.5 %collective-permute-start.20 = (bf16[16,4096]{1,0:T(8,128)(2,1)S(1)}, bf16[16,4096]{1,0:T(8,128)(2,1)S(1)}, u32[]{:S(2)}, u32[]{:S(2)}) collective-permute-start(bf16[16,4096]{1,0:T(8,128)(2,1)S(1)} %get-tuple-element.34), channel_id=1, source_target_pairs={{0,8},{4,12},{8,0},{12,4},{16,24},{20,28},{24,16},{28,20},{1,9},{5... | collective-permute-start | bytes 393224 | tf_op jit(solution)/shard_map/ppermute | solution.py:28
  42.0 0.7 %collective-permute-start.19 = (bf16[16,4096]{1,0:T(8,128)(2,1)S(1)}, bf16[16,4096]{1,0:T(8,128)(2,1)S(1)}, u32[]{:S(2)}, u32[]{:S(2)}) collective-permute-start(bf16[16,4096]{1,0:T(8,128)(2,1)S(1)} %get-tuple-element.35), channel_id=1, source_target_pairs={{0,16},{4,20},{8,24},{12,28},{16,0},{20,4},{24,8},{28,12},{1,17},{... | collective-permute-start | bytes 393224 | tf_op jit(solution)/shard_map/ppermute | solution.py:28
  42.7 0.0 collective-permute-done.17
  42.7 0.1 collective-permute-done.13
  42.9 3.7 %collective-permute-done.15 = bf16[16,4096]{1,0:T(8,128)(2,1)S(1)} collective-permute-done((bf16[16,4096]{1,0:T(8,128)(2,1)S(1)}, bf16[16,4096]{1,0:T(8,128)(2,1)S(1)}, u32[]{:S(2)}, u32[]{:S(2)}) %collective-permute-start.15) | collective-permute-done | bytes 131104 | tf_op jit(solution)/shard_map/ppermute | solution.py:28
  46.5 1.3 %collective-permute-start.16 = (bf16[16,4096]{1,0:T(8,128)(2,1)S(1)}, bf16[16,4096]{1,0:T(8,128)(2,1)S(1)}, u32[]{:S(2)}, u32[]{:S(2)}) collective-permute-start(bf16[16,4096]{1,0:T(8,128)(2,1)S(1)} %get-tuple-element.19), channel_id=1, source_target_pairs={{0,16},{4,20},{8,24},{12,28},{16,0},{20,4},{24,8},{28,12},{1,17},{... | collective-permute-start | bytes 393224 | tf_op jit(solution)/shard_map/ppermute | solution.py:28
  47.8 0.5 collective-permute-start.18
  48.3 0.0 collective-permute-done.20
  48.3 0.6 collective-permute-done.19
  48.9 0.1 fusion.2
  49.0 1.5 %collective-permute-start.21 = (bf16[8,4096]{1,0:T(8,128)(2,1)S(1)}, bf16[8,4096]{1,0:T(8,128)(2,1)S(1)}, u32[]{:S(2)}, u32[]{:S(2)}) collective-permute-start(bf16[8,4096]{1,0:T(8,128)(2,1)S(1)} %get-tuple-element.36), channel_id=1, source_target_pairs={{0,2},{1,3},{2,0},{3,1},{4,6},{5,7},{6,4},{7,5},{8,10},{9,11},{10,... | collective-permute-start | bytes 196616 | tf_op jit(solution)/shard_map/ppermute | solution.py:28
  50.5 0.8 %collective-permute-start.22 = (bf16[8,4096]{1,0:T(8,128)(2,1)S(1)}, bf16[8,4096]{1,0:T(8,128)(2,1)S(1)}, u32[]{:S(2)}, u32[]{:S(2)}) collective-permute-start(bf16[8,4096]{1,0:T(8,128)(2,1)S(1)} %get-tuple-element.37), channel_id=1, source_target_pairs={{0,3},{1,2},{2,1},{3,0},{4,7},{5,6},{6,5},{7,4},{8,11},{9,10},{10,... | collective-permute-start | bytes 196616 | tf_op jit(solution)/shard_map/ppermute | solution.py:28
  51.3 0.2 collective-permute-done.16
  51.5 1.3 %collective-permute-done.18 = bf16[16,4096]{1,0:T(8,128)(2,1)S(1)} collective-permute-done((bf16[16,4096]{1,0:T(8,128)(2,1)S(1)}, bf16[16,4096]{1,0:T(8,128)(2,1)S(1)}, u32[]{:S(2)}, u32[]{:S(2)}) %collective-permute-start.18) | collective-permute-done | bytes 131104 | tf_op jit(solution)/shard_map/ppermute | solution.py:28
  52.8 0.1 collective-permute-start.23
  52.9 2.0 %collective-permute-done.21 = bf16[8,4096]{1,0:T(8,128)(2,1)S(1)} collective-permute-done((bf16[8,4096]{1,0:T(8,128)(2,1)S(1)}, bf16[8,4096]{1,0:T(8,128)(2,1)S(1)}, u32[]{:S(2)}, u32[]{:S(2)}) %collective-permute-start.21) | collective-permute-done | bytes 65568 | tf_op jit(solution)/shard_map/ppermute | solution.py:28
  54.9 1.6 %collective-permute-done.22 = bf16[8,4096]{1,0:T(8,128)(2,1)S(1)} collective-permute-done((bf16[8,4096]{1,0:T(8,128)(2,1)S(1)}, bf16[8,4096]{1,0:T(8,128)(2,1)S(1)}, u32[]{:S(2)}, u32[]{:S(2)}) %collective-permute-start.22) | collective-permute-done | bytes 65568 | tf_op jit(solution)/shard_map/ppermute | solution.py:28
  56.6 0.7 %collective-permute-done.23 = bf16[8,4096]{1,0:T(8,128)(2,1)S(1)} collective-permute-done((bf16[8,4096]{1,0:T(8,128)(2,1)S(1)}, bf16[8,4096]{1,0:T(8,128)(2,1)S(1)}, u32[]{:S(2)}, u32[]{:S(2)}) %collective-permute-start.23) | collective-permute-done | bytes 65568 | tf_op jit(solution)/shard_map/ppermute | solution.py:28
  57.2 0.6 %fusion.5 = bf16[8,4096]{1,0:T(8,128)(2,1)} fusion(f32[8,4096]{1,0:T(8,128)S(1)} %convert_add_fusion.2, f32[16,4096]{1,0:T(8,128)S(1)} %fusion.3, bf16[8,4096]{1,0:T(8,128)(2,1)S(1)} %collective-permute-done.23), kind=kLoop, calls=%fused_computation.11 | loop fusion | flops 131072 | bytes 393216 | tf_op jit(solution)/shard_map/convert_element_type | solution.py:103
  (26 shorter events, 0.3 us)
Async XLA Ops:
  0.0 27.4 %slice-start = ((s8[6291456]{0:T(1024)(128)(4,1)}), s8[4194304]{0:T(1024)(128)(4,1)S(1)}, s32[]{:S(2)}) async-start(s8[6291456]{0:T(1024)(128)(4,1)} %bitcast), calls=%async_computation | async-start | bytes 8388608
  0.0 27.4 %slice-start.2 = ((s8[6291456]{0:T(1024)(128)(4,1)}), s8[4194304]{0:T(1024)(128)(4,1)S(1)}, s32[]{:S(2)}) async-start(s8[6291456]{0:T(1024)(128)(4,1)} %bitcast.2), calls=%async_computation.2 | async-start | bytes 8388608
  0.0 27.4 %slice-start.4 = ((s8[6291456]{0:T(1024)(128)(4,1)}), s8[4194304]{0:T(1024)(128)(4,1)S(1)}, s32[]{:S(2)}) async-start(s8[6291456]{0:T(1024)(128)(4,1)} %bitcast.4), calls=%async_computation.4 | async-start | bytes 8388608
  1.6 25.9 %slice-start.1 = ((s8[6291456]{0:T(1024)(128)(4,1)}), s8[2097152]{0:T(1024)(128)(4,1)S(1)}, s32[]{:S(2)}) async-start(s8[6291456]{0:T(1024)(128)(4,1)} %bitcast), calls=%async_computation.1 | async-start | bytes 4194304
  1.6 25.9 %slice-start.3 = ((s8[6291456]{0:T(1024)(128)(4,1)}), s8[2097152]{0:T(1024)(128)(4,1)S(1)}, s32[]{:S(2)}) async-start(s8[6291456]{0:T(1024)(128)(4,1)} %bitcast.2), calls=%async_computation.3 | async-start | bytes 4194304
  1.6 25.9 %slice-start.5 = ((s8[6291456]{0:T(1024)(128)(4,1)}), s8[2097152]{0:T(1024)(128)(4,1)S(1)}, s32[]{:S(2)}) async-start(s8[6291456]{0:T(1024)(128)(4,1)} %bitcast.4), calls=%async_computation.5 | async-start | bytes 4194304
  1.6 5.7 %collective-permute-start = (bf16[8,4224]{1,0:T(8,128)(2,1)S(1)}, bf16[8,4224]{1,0:T(8,128)(2,1)S(1)}, u32[]{:S(2)}, u32[]{:S(2)}) collective-permute-start(bf16[8,4224]{1,0:T(8,128)(2,1)S(1)} %shard_map.64.refs_0_), channel_id=1, source_target_pairs={{0,1},{1,0},{2,3},{3,2},{4,5},{5,4},{6,7},{7,6},{8,9},{9,8},{10,11... | collective-permute-start | bytes 202760 | tf_op jit(solution)/shard_map/ppermute | solution.py:28
  4.7 9.3 %collective-permute-start.6 = (bf16[8,4224]{1,0:T(8,128)(2,1)S(1)}, bf16[8,4224]{1,0:T(8,128)(2,1)S(1)}, u32[]{:S(2)}, u32[]{:S(2)}) collective-permute-start(bf16[8,4224]{1,0:T(8,128)(2,1)S(1)} %shard_map.64.refs_0_), channel_id=1, source_target_pairs={{0,3},{1,2},{2,1},{3,0},{4,7},{5,6},{6,5},{7,4},{8,11},{9,10},{10,... | collective-permute-start | bytes 202760 | tf_op jit(solution)/shard_map/ppermute | solution.py:28
  7.2 6.6 %collective-permute-start.5 = (bf16[8,4224]{1,0:T(8,128)(2,1)S(1)}, bf16[8,4224]{1,0:T(8,128)(2,1)S(1)}, u32[]{:S(2)}, u32[]{:S(2)}) collective-permute-start(bf16[8,4224]{1,0:T(8,128)(2,1)S(1)} %shard_map.64.refs_0_), channel_id=1, source_target_pairs={{0,2},{1,3},{2,0},{3,1},{4,6},{5,7},{6,4},{7,5},{8,10},{9,11},{10,... | collective-permute-start | bytes 202760 | tf_op jit(solution)/shard_map/ppermute | solution.py:28
  7.3 6.5 %collective-permute-start.2 = (bf16[16,4224]{1,0:T(8,128)(2,1)S(1)}, bf16[16,4224]{1,0:T(8,128)(2,1)S(1)}, u32[]{:S(2)}, u32[]{:S(2)}) collective-permute-start(bf16[16,4224]{1,0:T(8,128)(2,1)S(1)} %shard_map.65), channel_id=1, source_target_pairs={{0,16},{4,20},{8,24},{12,28},{16,0},{20,4},{24,8},{28,12},{1,17},{... | collective-permute-start | bytes 405512 | tf_op jit(solution)/shard_map/ppermute | solution.py:28
  9.0 5.0 %collective-permute-start.1 = (bf16[16,4224]{1,0:T(8,128)(2,1)S(1)}, bf16[16,4224]{1,0:T(8,128)(2,1)S(1)}, u32[]{:S(2)}, u32[]{:S(2)}) collective-permute-start(bf16[16,4224]{1,0:T(8,128)(2,1)S(1)} %shard_map.65), channel_id=1, source_target_pairs={{0,8},{4,12},{8,0},{12,4},{16,24},{20,28},{24,16},{28,20},{1,9},{5... | collective-permute-start | bytes 405512 | tf_op jit(solution)/shard_map/ppermute | solution.py:28
  14.1 10.7 %collective-permute-start.9 = (bf16[16,4224]{1,0:T(8,128)(2,1)S(1)}, bf16[16,4224]{1,0:T(8,128)(2,1)S(1)}, u32[]{:S(2)}, u32[]{:S(2)}) collective-permute-start(bf16[16,4224]{1,0:T(8,128)(2,1)S(1)} %get-tuple-element.38), channel_id=1, source_target_pairs={{0,24},{4,28},{8,16},{12,20},{16,8},{20,12},{24,0},{28,4},{1,25},{... | collective-permute-start | bytes 405512 | tf_op jit(solution)/shard_map/ppermute | solution.py:28
  16.3 8.4 %collective-permute-start.8 = (bf16[16,4224]{1,0:T(8,128)(2,1)S(1)}, bf16[16,4224]{1,0:T(8,128)(2,1)S(1)}, u32[]{:S(2)}, u32[]{:S(2)}) collective-permute-start(bf16[16,4224]{1,0:T(8,128)(2,1)S(1)} %get-tuple-element.38), channel_id=1, source_target_pairs={{0,16},{4,20},{8,24},{12,28},{16,0},{20,4},{24,8},{28,12},{1,17},{... | collective-permute-start | bytes 405512 | tf_op jit(solution)/shard_map/ppermute | solution.py:28
  17.1 7.7 %collective-permute-start.7 = (bf16[16,4224]{1,0:T(8,128)(2,1)S(1)}, bf16[16,4224]{1,0:T(8,128)(2,1)S(1)}, u32[]{:S(2)}, u32[]{:S(2)}) collective-permute-start(bf16[16,4224]{1,0:T(8,128)(2,1)S(1)} %get-tuple-element.38), channel_id=1, source_target_pairs={{0,8},{4,12},{8,0},{12,4},{16,24},{20,28},{24,16},{28,20},{1,9},{5... | collective-permute-start | bytes 405512 | tf_op jit(solution)/shard_map/ppermute | solution.py:28
  17.6 7.0 %collective-permute-start.4 = (bf16[8,4224]{1,0:T(8,128)(2,1)S(1)}, bf16[8,4224]{1,0:T(8,128)(2,1)S(1)}, u32[]{:S(2)}, u32[]{:S(2)}) collective-permute-start(bf16[8,4224]{1,0:T(8,128)(2,1)S(1)} %slice.88), channel_id=1, source_target_pairs={{0,8},{4,12},{8,0},{12,4},{16,24},{20,28},{24,16},{28,20},{1,9},{5... | collective-permute-start | bytes 202760 | tf_op jit(solution)/shard_map/ppermute | solution.py:28
  19.1 5.5 %collective-permute-start.3 = (bf16[8,4224]{1,0:T(8,128)(2,1)S(1)}, bf16[8,4224]{1,0:T(8,128)(2,1)S(1)}, u32[]{:S(2)}, u32[]{:S(2)}) collective-permute-start(bf16[8,4224]{1,0:T(8,128)(2,1)S(1)} %slice.87), channel_id=1, source_target_pairs={{0,16},{4,20},{8,24},{12,28},{16,0},{20,4},{24,8},{28,12},{1,17},{... | collective-permute-start | bytes 202760 | tf_op jit(solution)/shard_map/ppermute | solution.py:28
  24.7 2.0 %collective-permute-start.10 = (bf16[64,4224]{1,0:T(8,128)(2,1)S(1)}, bf16[64,4224]{1,0:T(8,128)(2,1)S(1)}, u32[]{:S(2)}, u32[]{:S(2)}) collective-permute-start(bf16[64,4224]{1,0:T(8,128)(2,1)S(1)} %constant_dynamic-update-slice_fusion.refs_0_), channel_id=1, source_target_pairs={{0,4},{4,0},{8,12},{12,8},{16,20},{20,16},{24,28},{28,24},{1,5},{5... | collective-permute-start | bytes 1622024 | tf_op jit(solution)/shard_map/ppermute | solution.py:28
  24.8 2.6 %collective-permute-start.11 = (bf16[64,4224]{1,0:T(8,128)(2,1)S(1)}, bf16[64,4224]{1,0:T(8,128)(2,1)S(1)}, u32[]{:S(2)}, u32[]{:S(2)}) collective-permute-start(bf16[64,4224]{1,0:T(8,128)(2,1)S(1)} %constant_dynamic-update-slice_fusion.7.refs_1_), channel_id=1, source_target_pairs={{0,4},{4,0},{8,12},{12,8},{16,20},{20,16},{24,28},{28,24},{1,5},{5... | collective-permute-start | bytes 1622024 | tf_op jit(solution)/shard_map/ppermute | solution.py:28
  34.5 2.0 %collective-permute-start.12 = (bf16[64,4096]{1,0:T(8,128)(2,1)S(1)}, bf16[64,4096]{1,0:T(8,128)(2,1)S(1)}, u32[]{:S(2)}, u32[]{:S(2)}) collective-permute-start(bf16[64,4096]{1,0:T(8,128)(2,1)S(1)} %get-tuple-element.16), channel_id=1, source_target_pairs={{0,4},{4,0},{8,12},{12,8},{16,20},{20,16},{24,28},{28,24},{1,5},{5... | collective-permute-start | bytes 1572872 | tf_op jit(solution)/shard_map/ppermute | solution.py:28
  34.7 4.3 %collective-permute-start.14 = (bf16[64,4096]{1,0:T(8,128)(2,1)S(1)}, bf16[64,4096]{1,0:T(8,128)(2,1)S(1)}, u32[]{:S(2)}, u32[]{:S(2)}) collective-permute-start(bf16[64,4096]{1,0:T(8,128)(2,1)S(1)} %get-tuple-element.18), channel_id=1, source_target_pairs={{0,4},{4,0},{8,12},{12,8},{16,20},{20,16},{24,28},{28,24},{1,5},{5... | collective-permute-start | bytes 1572872 | tf_op jit(solution)/shard_map/ppermute | solution.py:28
  36.6 6.1 %collective-permute-start.17 = (bf16[8,4096]{1,0:T(8,128)(2,1)S(1)}, bf16[8,4096]{1,0:T(8,128)(2,1)S(1)}, u32[]{:S(2)}, u32[]{:S(2)}) collective-permute-start(bf16[8,4096]{1,0:T(8,128)(2,1)S(1)} %get-tuple-element.31), channel_id=1, source_target_pairs={{0,16},{4,20},{8,24},{12,28},{16,0},{20,4},{24,8},{28,12},{1,17},{... | collective-permute-start | bytes 196616 | tf_op jit(solution)/shard_map/ppermute | solution.py:28
  38.2 4.6 %collective-permute-start.13 = (bf16[8,4096]{1,0:T(8,128)(2,1)S(1)}, bf16[8,4096]{1,0:T(8,128)(2,1)S(1)}, u32[]{:S(2)}, u32[]{:S(2)}) collective-permute-start(bf16[8,4096]{1,0:T(8,128)(2,1)S(1)} %get-tuple-element.32), channel_id=1, source_target_pairs={{0,8},{4,12},{8,0},{12,4},{16,24},{20,28},{24,16},{28,20},{1,9},{5... | collective-permute-start | bytes 196616 | tf_op jit(solution)/shard_map/ppermute | solution.py:28
  39.1 7.4 %collective-permute-start.15 = (bf16[16,4096]{1,0:T(8,128)(2,1)S(1)}, bf16[16,4096]{1,0:T(8,128)(2,1)S(1)}, u32[]{:S(2)}, u32[]{:S(2)}) collective-permute-start(bf16[16,4096]{1,0:T(8,128)(2,1)S(1)} %get-tuple-element.33), channel_id=1, source_target_pairs={{0,24},{4,28},{8,16},{12,20},{16,8},{20,12},{24,0},{28,4},{1,25},{... | collective-permute-start | bytes 393224 | tf_op jit(solution)/shard_map/ppermute | solution.py:28
  40.4 7.9 %collective-permute-start.20 = (bf16[16,4096]{1,0:T(8,128)(2,1)S(1)}, bf16[16,4096]{1,0:T(8,128)(2,1)S(1)}, u32[]{:S(2)}, u32[]{:S(2)}) collective-permute-start(bf16[16,4096]{1,0:T(8,128)(2,1)S(1)} %get-tuple-element.34), channel_id=1, source_target_pairs={{0,8},{4,12},{8,0},{12,4},{16,24},{20,28},{24,16},{28,20},{1,9},{5... | collective-permute-start | bytes 393224 | tf_op jit(solution)/shard_map/ppermute | solution.py:28
  42.0 6.9 %collective-permute-start.19 = (bf16[16,4096]{1,0:T(8,128)(2,1)S(1)}, bf16[16,4096]{1,0:T(8,128)(2,1)S(1)}, u32[]{:S(2)}, u32[]{:S(2)}) collective-permute-start(bf16[16,4096]{1,0:T(8,128)(2,1)S(1)} %get-tuple-element.35), channel_id=1, source_target_pairs={{0,16},{4,20},{8,24},{12,28},{16,0},{20,4},{24,8},{28,12},{1,17},{... | collective-permute-start | bytes 393224 | tf_op jit(solution)/shard_map/ppermute | solution.py:28
  46.5 5.0 %collective-permute-start.16 = (bf16[16,4096]{1,0:T(8,128)(2,1)S(1)}, bf16[16,4096]{1,0:T(8,128)(2,1)S(1)}, u32[]{:S(2)}, u32[]{:S(2)}) collective-permute-start(bf16[16,4096]{1,0:T(8,128)(2,1)S(1)} %get-tuple-element.19), channel_id=1, source_target_pairs={{0,16},{4,20},{8,24},{12,28},{16,0},{20,4},{24,8},{28,12},{1,17},{... | collective-permute-start | bytes 393224 | tf_op jit(solution)/shard_map/ppermute | solution.py:28
  47.8 5.0 %collective-permute-start.18 = (bf16[16,4096]{1,0:T(8,128)(2,1)S(1)}, bf16[16,4096]{1,0:T(8,128)(2,1)S(1)}, u32[]{:S(2)}, u32[]{:S(2)}) collective-permute-start(bf16[16,4096]{1,0:T(8,128)(2,1)S(1)} %get-tuple-element.20), channel_id=1, source_target_pairs={{0,8},{4,12},{8,0},{12,4},{16,24},{20,28},{24,16},{28,20},{1,9},{5... | collective-permute-start | bytes 393224 | tf_op jit(solution)/shard_map/ppermute | solution.py:28
  49.0 5.9 %collective-permute-start.21 = (bf16[8,4096]{1,0:T(8,128)(2,1)S(1)}, bf16[8,4096]{1,0:T(8,128)(2,1)S(1)}, u32[]{:S(2)}, u32[]{:S(2)}) collective-permute-start(bf16[8,4096]{1,0:T(8,128)(2,1)S(1)} %get-tuple-element.36), channel_id=1, source_target_pairs={{0,2},{1,3},{2,0},{3,1},{4,6},{5,7},{6,4},{7,5},{8,10},{9,11},{10,... | collective-permute-start | bytes 196616 | tf_op jit(solution)/shard_map/ppermute | solution.py:28
  50.5 6.1 %collective-permute-start.22 = (bf16[8,4096]{1,0:T(8,128)(2,1)S(1)}, bf16[8,4096]{1,0:T(8,128)(2,1)S(1)}, u32[]{:S(2)}, u32[]{:S(2)}) collective-permute-start(bf16[8,4096]{1,0:T(8,128)(2,1)S(1)} %get-tuple-element.37), channel_id=1, source_target_pairs={{0,3},{1,2},{2,1},{3,0},{4,7},{5,6},{6,5},{7,4},{8,11},{9,10},{10,... | collective-permute-start | bytes 196616 | tf_op jit(solution)/shard_map/ppermute | solution.py:28
  52.8 4.4 %collective-permute-start.23 = (bf16[8,4096]{1,0:T(8,128)(2,1)S(1)}, bf16[8,4096]{1,0:T(8,128)(2,1)S(1)}, u32[]{:S(2)}, u32[]{:S(2)}) collective-permute-start(bf16[8,4096]{1,0:T(8,128)(2,1)S(1)} %slice.126), channel_id=1, source_target_pairs={{0,1},{1,0},{2,3},{3,2},{4,5},{5,4},{6,7},{7,6},{8,9},{9,8},{10,11... | collective-permute-start | bytes 196616 | tf_op jit(solution)/shard_map/ppermute | solution.py:28

commit v5 on v3

--- a/solution.py
+++ b/solution.py
@@ -180,23 +180,20 @@
         hidden.append((gate / (1.0 + jnp.exp(-gate)) * up).astype(jnp.bfloat16))
         mine = jnp.where(lane == first_expert + local, tags, 0.0)
         shares.append(jnp.sum(mine, axis=1, keepdims=True))
-    block = min(512, width)
-
-    @pl.loop(0, width // block)
-    def _(index):
-        columns = pl.ds(pl.multiple_of(index * block, block), block)
+    block = min(1024, width)
+    for first in range(0, width, block):
         total = 0.0
         for local in range(exp_dev):
             out = jnp.dot(
                 hidden[local],
-                down_ref[local, :, columns],
+                down_ref[local, :, first : first + block],
                 preferred_element_type=jnp.float32,
             )
             total = total + out * shares[local]
         start = 0
         for result in results:
             stop = start + result.shape[0]
-            result[:, columns] = total[start:stop].astype(result.dtype)
+            result[:, first : first + block] = total[start:stop].astype(result.dtype)
             start = stop
 
 

time: 55 us -> 53.6 us (0.975)
  Pallas kernels: 8.56 us -> 7.24 us
    pallas_call x1, Pallas kernels: 7.01 us -> 5.69 us  [run_experts(): pl.pallas_call(functools.partial(expert_kernel, exp_dev, expert_total, le...]
where the time goes in v5:
time: 53.6 us; the launch traced here: 53.5 us
  starting transfers between devices  23.3 us (43%)
  waiting for transfers between devices  21.5 us (40%)
  Pallas kernels  7.24 us (14%)
  other arithmetic  1.07 us (2%)
    ppermute x22, starting transfers between devices, swap(): return lax.ppermute(value, axis, [(i, i ^ mask) for i in range(count)])  23.3 us
    ppermute x22, waiting for transfers between devices, swap(): return lax.ppermute(value, axis, [(i, i ^ mask) for i in range(count)])  21.5 us
    pallas_call x1, Pallas kernels, run_experts(): pl.pallas_call(functools.partial(expert_kernel, exp_dev, expert_total, le...  5.69 us
    pallas_call x1, Pallas kernels, pack(): pl.pallas_call(pack_kernel, out_shape=pltpu.VMEM((rows, width + extra), t...  1.54 us
  transfers between devices with their start and end apart: 22, of which 11 were waited for; matrix products, arithmetic and copies ran while one was open for 1% of the time, Pallas kernels for 0%

profile of v5, /device:TPU:0, one launch (start us, length us, event | category | flops | bytes accessed | tf_op | source)
XLA Modules:
  0.0 53.5 jit_solution(6870995863964880820)
XLA Ops:
  0.0 0.0 slice-start
  0.0 0.0 slice-start.2
  0.0 0.0 slice-start.4
  0.0 1.5 %shard_map.64.refs_0_ = bf16[8,4224]{1,0:T(8,128)(2,1)S(1)} custom-call(bf16[8,4096]{1,0:T(8,128)(2,1)} %tokens_hbm.1, s32[8,8]{1,0:T(8,128)} %ids_hbm.1, bf16[16,4096]{1,0:T(8,128)(2,1)} %router_hbm.1), custom_call_target="tpu_custom_call" | custom-call | flops 1048576 | bytes 262144 | tf_op jit(solution)/shard_map/pallas_call | solution.py:126
  1.6 0.0 slice-start.1
  1.6 0.0 slice-start.3
  1.6 0.0 slice-start.5
  1.6 3.1 %collective-permute-start = (bf16[8,4224]{1,0:T(8,128)(2,1)S(1)}, bf16[8,4224]{1,0:T(8,128)(2,1)S(1)}, u32[]{:S(2)}, u32[]{:S(2)}) collective-permute-start(bf16[8,4224]{1,0:T(8,128)(2,1)S(1)} %shard_map.64.refs_0_), channel_id=1, source_target_pairs={{0,1},{1,0},{2,3},{3,2},{4,5},{5,4},{6,7},{7,6},{8,9},{9,8},{10,11... | collective-permute-start | bytes 202760 | tf_op jit(solution)/shard_map/ppermute | solution.py:28
  4.7 2.5 %collective-permute-start.5 = (bf16[8,4224]{1,0:T(8,128)(2,1)S(1)}, bf16[8,4224]{1,0:T(8,128)(2,1)S(1)}, u32[]{:S(2)}, u32[]{:S(2)}) collective-permute-start(bf16[8,4224]{1,0:T(8,128)(2,1)S(1)} %shard_map.64.refs_0_), channel_id=1, source_target_pairs={{0,3},{1,2},{2,1},{3,0},{4,7},{5,6},{6,5},{7,4},{8,11},{9,10},{10,... | collective-permute-start | bytes 202760 | tf_op jit(solution)/shard_map/ppermute | solution.py:28
  7.2 0.1 collective-permute-start.4
  7.3 0.0 collective-permute-done.refs_1_
  7.3 2.6 %collective-permute-start.3 = (bf16[16,4224]{1,0:T(8,128)(2,1)S(1)}, bf16[16,4224]{1,0:T(8,128)(2,1)S(1)}, u32[]{:S(2)}, u32[]{:S(2)}) collective-permute-start(bf16[16,4224]{1,0:T(8,128)(2,1)S(1)} %shard_map.65), channel_id=1, source_target_pairs={{0,24},{4,28},{8,16},{12,20},{16,8},{20,12},{24,0},{28,4},{1,25},{... | collective-permute-start | bytes 405512 | tf_op jit(solution)/shard_map/ppermute | solution.py:28
  9.9 0.5 collective-permute-start.2
  10.4 0.4 collective-permute-start.1
  10.9 2.9 %collective-permute-done.4 = bf16[8,4224]{1,0:T(8,128)(2,1)S(1)} collective-permute-done((bf16[8,4224]{1,0:T(8,128)(2,1)S(1)}, bf16[8,4224]{1,0:T(8,128)(2,1)S(1)}, u32[]{:S(2)}, u32[]{:S(2)}) %collective-permute-start.4) | collective-permute-done | bytes 67616 | tf_op jit(solution)/shard_map/ppermute | solution.py:28
  13.8 0.0 collective-permute-done.5
  13.8 2.5 %collective-permute-start.8 = (bf16[16,4224]{1,0:T(8,128)(2,1)S(1)}, bf16[16,4224]{1,0:T(8,128)(2,1)S(1)}, u32[]{:S(2)}, u32[]{:S(2)}) collective-permute-start(bf16[16,4224]{1,0:T(8,128)(2,1)S(1)} %get-tuple-element.35), channel_id=1, source_target_pairs={{0,24},{4,28},{8,16},{12,20},{16,8},{20,12},{24,0},{28,4},{1,25},{... | collective-permute-start | bytes 405512 | tf_op jit(solution)/shard_map/ppermute | solution.py:28
  16.3 0.5 collective-permute-start.7
  16.8 0.0 collective-permute-done.3
  16.8 0.5 %collective-permute-start.6 = (bf16[16,4224]{1,0:T(8,128)(2,1)S(1)}, bf16[16,4224]{1,0:T(8,128)(2,1)S(1)}, u32[]{:S(2)}, u32[]{:S(2)}) collective-permute-start(bf16[16,4224]{1,0:T(8,128)(2,1)S(1)} %get-tuple-element.35), channel_id=1, source_target_pairs={{0,8},{4,12},{8,0},{12,4},{16,24},{20,28},{24,16},{28,20},{1,9},{5... | collective-permute-start | bytes 405512 | tf_op jit(solution)/shard_map/ppermute | solution.py:28
  17.4 0.0 collective-permute-done.2
  17.4 0.0 collective-permute-done.1
  17.4 0.1 collective-permute-start.9
  17.5 5.7 %collective-permute-done.6 = bf16[16,4224]{1,0:T(8,128)(2,1)S(1)} collective-permute-done((bf16[16,4224]{1,0:T(8,128)(2,1)S(1)}, bf16[16,4224]{1,0:T(8,128)(2,1)S(1)}, u32[]{:S(2)}, u32[]{:S(2)}) %collective-permute-start.6) | collective-permute-done | bytes 135200 | tf_op jit(solution)/shard_map/ppermute | solution.py:28
  23.2 0.0 collective-permute-done.7
  23.2 0.0 collective-permute-done.8
  23.3 0.1 collective-permute-start.10
  23.3 0.0 collective-permute-done.9.refs_2_
  23.4 1.9 %collective-permute-done.10.refs_3_ = bf16[64,4224]{1,0:T(8,128)(2,1)S(1)} collective-permute-done((bf16[64,4224]{1,0:T(8,128)(2,1)S(1)}, bf16[64,4224]{1,0:T(8,128)(2,1)S(1)}, u32[]{:S(2)}, u32[]{:S(2)}) %collective-permute-start.10) | collective-permute-done | bytes 540704 | tf_op jit(solution)/shard_map/ppermute | solution.py:28
  25.3 0.0 slice-done
  25.3 0.0 slice-done.2
  25.3 0.0 slice-done.4
  25.3 0.0 slice-done.1
  25.3 0.0 slice-done.3
  25.3 0.0 slice-done.5
  25.3 5.7 %shard_map.66 = (f32[64,4096]{1,0:T(8,128)S(1)}, f32[64,4096]{1,0:T(8,128)S(1)}, bf16[64,4096]{1,0:T(8,128)(2,1)S(1)}, bf16[64,4096]{1,0:T(8,128)(2,1)S(1)}) custom-call(bf16[64,4224]{1,0:T(8,128)(2,1)S(1)} %pad_maximum_fusion.refs_0_, bf16[64,4224]{1,0:T(8,128)(2,1)S(1)} %constant_dynamic-update-slice_fusion.2.refs_1_, ...), custom_call_target="tpu_custom_call" | custom-call | flops 4831838208 | bytes 5242880 | tf_op jit(solution)/shard_map/pallas_call | solution.py:204
  31.0 0.2 collective-permute-start.12
  31.2 0.4 collective-permute-start.11
  31.6 1.4 %collective-permute-done.12 = bf16[64,4096]{1,0:T(8,128)(2,1)S(1)} collective-permute-done((bf16[64,4096]{1,0:T(8,128)(2,1)S(1)}, bf16[64,4096]{1,0:T(8,128)(2,1)S(1)}, u32[]{:S(2)}, u32[]{:S(2)}) %collective-permute-start.12) | collective-permute-done | bytes 524320 | tf_op jit(solution)/shard_map/ppermute | solution.py:28
  33.0 0.1 fusion.8
  33.2 1.7 %collective-permute-start.13 = (bf16[16,4096]{1,0:T(8,128)(2,1)S(1)}, bf16[16,4096]{1,0:T(8,128)(2,1)S(1)}, u32[]{:S(2)}, u32[]{:S(2)}) collective-permute-start(bf16[16,4096]{1,0:T(8,128)(2,1)S(1)} %get-tuple-element.30), channel_id=1, source_target_pairs={{0,24},{4,28},{8,16},{12,20},{16,8},{20,12},{24,0},{28,4},{1,25},{... | collective-permute-start | bytes 393224 | tf_op jit(solution)/shard_map/ppermute | solution.py:28
  34.9 1.2 %collective-permute-start.18 = (bf16[16,4096]{1,0:T(8,128)(2,1)S(1)}, bf16[16,4096]{1,0:T(8,128)(2,1)S(1)}, u32[]{:S(2)}, u32[]{:S(2)}) collective-permute-start(bf16[16,4096]{1,0:T(8,128)(2,1)S(1)} %get-tuple-element.31), channel_id=1, source_target_pairs={{0,8},{4,12},{8,0},{12,4},{16,24},{20,28},{24,16},{28,20},{1,9},{5... | collective-permute-start | bytes 393224 | tf_op jit(solution)/shard_map/ppermute | solution.py:28
  36.1 0.6 %collective-permute-start.17 = (bf16[16,4096]{1,0:T(8,128)(2,1)S(1)}, bf16[16,4096]{1,0:T(8,128)(2,1)S(1)}, u32[]{:S(2)}, u32[]{:S(2)}) collective-permute-start(bf16[16,4096]{1,0:T(8,128)(2,1)S(1)} %get-tuple-element.32), channel_id=1, source_target_pairs={{0,16},{4,20},{8,24},{12,28},{16,0},{20,4},{24,8},{28,12},{1,17},{... | collective-permute-start | bytes 393224 | tf_op jit(solution)/shard_map/ppermute | solution.py:28
  36.7 0.0 collective-permute-done.11
  36.7 0.1 fusion.7
  36.9 3.6 %collective-permute-done.13 = bf16[16,4096]{1,0:T(8,128)(2,1)S(1)} collective-permute-done((bf16[16,4096]{1,0:T(8,128)(2,1)S(1)}, bf16[16,4096]{1,0:T(8,128)(2,1)S(1)}, u32[]{:S(2)}, u32[]{:S(2)}) %collective-permute-start.13) | collective-permute-done | bytes 131104 | tf_op jit(solution)/shard_map/ppermute | solution.py:28
  40.5 1.6 %collective-permute-start.14 = (bf16[16,4096]{1,0:T(8,128)(2,1)S(1)}, bf16[16,4096]{1,0:T(8,128)(2,1)S(1)}, u32[]{:S(2)}, u32[]{:S(2)}) collective-permute-start(bf16[16,4096]{1,0:T(8,128)(2,1)S(1)} %get-tuple-element.18), channel_id=1, source_target_pairs={{0,24},{4,28},{8,16},{12,20},{16,8},{20,12},{24,0},{28,4},{1,25},{... | collective-permute-start | bytes 393224 | tf_op jit(solution)/shard_map/ppermute | solution.py:28
  42.1 1.3 %collective-permute-start.15 = (bf16[16,4096]{1,0:T(8,128)(2,1)S(1)}, bf16[16,4096]{1,0:T(8,128)(2,1)S(1)}, u32[]{:S(2)}, u32[]{:S(2)}) collective-permute-start(bf16[16,4096]{1,0:T(8,128)(2,1)S(1)} %get-tuple-element.19), channel_id=1, source_target_pairs={{0,16},{4,20},{8,24},{12,28},{16,0},{20,4},{24,8},{28,12},{1,17},{... | collective-permute-start | bytes 393224 | tf_op jit(solution)/shard_map/ppermute | solution.py:28
  43.5 0.5 collective-permute-start.16
  44.0 0.0 collective-permute-done.18
  44.0 0.0 collective-permute-done.17
  44.0 0.1 fusion.2
  44.1 1.5 %collective-permute-start.19 = (bf16[8,4096]{1,0:T(8,128)(2,1)S(1)}, bf16[8,4096]{1,0:T(8,128)(2,1)S(1)}, u32[]{:S(2)}, u32[]{:S(2)}) collective-permute-start(bf16[8,4096]{1,0:T(8,128)(2,1)S(1)} %get-tuple-element.33), channel_id=1, source_target_pairs={{0,2},{1,3},{2,0},{3,1},{4,6},{5,7},{6,4},{7,5},{8,10},{9,11},{10,... | collective-permute-start | bytes 196616 | tf_op jit(solution)/shard_map/ppermute | solution.py:28
  45.6 1.0 %collective-permute-start.20 = (bf16[8,4096]{1,0:T(8,128)(2,1)S(1)}, bf16[8,4096]{1,0:T(8,128)(2,1)S(1)}, u32[]{:S(2)}, u32[]{:S(2)}) collective-permute-start(bf16[8,4096]{1,0:T(8,128)(2,1)S(1)} %get-tuple-element.34), channel_id=1, source_target_pairs={{0,3},{1,2},{2,1},{3,0},{4,7},{5,6},{6,5},{7,4},{8,11},{9,10},{10,... | collective-permute-start | bytes 196616 | tf_op jit(solution)/shard_map/ppermute | solution.py:28
  46.6 0.4 collective-permute-done.14
  47.0 1.1 %collective-permute-done.15 = bf16[16,4096]{1,0:T(8,128)(2,1)S(1)} collective-permute-done((bf16[16,4096]{1,0:T(8,128)(2,1)S(1)}, bf16[16,4096]{1,0:T(8,128)(2,1)S(1)}, u32[]{:S(2)}, u32[]{:S(2)}) %collective-permute-start.15) | collective-permute-done | bytes 131104 | tf_op jit(solution)/shard_map/ppermute | solution.py:28
  48.1 0.3 collective-permute-done.16
  48.4 0.1 fusion.4
  48.5 0.2 collective-permute-start.21
  48.7 1.5 %collective-permute-done.19 = bf16[8,4096]{1,0:T(8,128)(2,1)S(1)} collective-permute-done((bf16[8,4096]{1,0:T(8,128)(2,1)S(1)}, bf16[8,4096]{1,0:T(8,128)(2,1)S(1)}, u32[]{:S(2)}, u32[]{:S(2)}) %collective-permute-start.19) | collective-permute-done | bytes 65568 | tf_op jit(solution)/shard_map/ppermute | solution.py:28
  50.2 1.4 %collective-permute-done.20 = bf16[8,4096]{1,0:T(8,128)(2,1)S(1)} collective-permute-done((bf16[8,4096]{1,0:T(8,128)(2,1)S(1)}, bf16[8,4096]{1,0:T(8,128)(2,1)S(1)}, u32[]{:S(2)}, u32[]{:S(2)}) %collective-permute-start.20) | collective-permute-done | bytes 65568 | tf_op jit(solution)/shard_map/ppermute | solution.py:28
  51.6 1.2 %collective-permute-done.21 = bf16[8,4096]{1,0:T(8,128)(2,1)S(1)} collective-permute-done((bf16[8,4096]{1,0:T(8,128)(2,1)S(1)}, bf16[8,4096]{1,0:T(8,128)(2,1)S(1)}, u32[]{:S(2)}, u32[]{:S(2)}) %collective-permute-start.21) | collective-permute-done | bytes 65568 | tf_op jit(solution)/shard_map/ppermute | solution.py:28
  52.8 0.6 %fusion.6 = bf16[8,4096]{1,0:T(8,128)(2,1)} fusion(f32[8,4096]{1,0:T(8,128)S(1)} %convert_add_fusion.2, f32[16,4096]{1,0:T(8,128)S(1)} %fusion.4, bf16[8,4096]{1,0:T(8,128)(2,1)S(1)} %collective-permute-done.21), kind=kLoop, calls=%fused_computation.13 | loop fusion | flops 131072 | bytes 393216 | tf_op jit(solution)/shard_map/convert_element_type | solution.py:88
  (15 shorter events, 0.2 us)
Async XLA Ops:
  0.0 25.3 %slice-start = ((s8[6291456]{0:T(1024)(128)(4,1)}), s8[4194304]{0:T(1024)(128)(4,1)S(1)}, s32[]{:S(2)}) async-start(s8[6291456]{0:T(1024)(128)(4,1)} %bitcast), calls=%async_computation | async-start | bytes 8388608
  0.0 25.3 %slice-start.2 = ((s8[6291456]{0:T(1024)(128)(4,1)}), s8[4194304]{0:T(1024)(128)(4,1)S(1)}, s32[]{:S(2)}) async-start(s8[6291456]{0:T(1024)(128)(4,1)} %bitcast.2), calls=%async_computation.2 | async-start | bytes 8388608
  0.0 25.3 %slice-start.4 = ((s8[6291456]{0:T(1024)(128)(4,1)}), s8[4194304]{0:T(1024)(128)(4,1)S(1)}, s32[]{:S(2)}) async-start(s8[6291456]{0:T(1024)(128)(4,1)} %bitcast.4), calls=%async_computation.4 | async-start | bytes 8388608
  1.6 23.7 %slice-start.1 = ((s8[6291456]{0:T(1024)(128)(4,1)}), s8[2097152]{0:T(1024)(128)(4,1)S(1)}, s32[]{:S(2)}) async-start(s8[6291456]{0:T(1024)(128)(4,1)} %bitcast), calls=%async_computation.1 | async-start | bytes 4194304
  1.6 23.7 %slice-start.3 = ((s8[6291456]{0:T(1024)(128)(4,1)}), s8[2097152]{0:T(1024)(128)(4,1)S(1)}, s32[]{:S(2)}) async-start(s8[6291456]{0:T(1024)(128)(4,1)} %bitcast.2), calls=%async_computation.3 | async-start | bytes 4194304
  1.6 23.7 %slice-start.5 = ((s8[6291456]{0:T(1024)(128)(4,1)}), s8[2097152]{0:T(1024)(128)(4,1)S(1)}, s32[]{:S(2)}) async-start(s8[6291456]{0:T(1024)(128)(4,1)} %bitcast.4), calls=%async_computation.5 | async-start | bytes 4194304
  1.6 5.7 %collective-permute-start = (bf16[8,4224]{1,0:T(8,128)(2,1)S(1)}, bf16[8,4224]{1,0:T(8,128)(2,1)S(1)}, u32[]{:S(2)}, u32[]{:S(2)}) collective-permute-start(bf16[8,4224]{1,0:T(8,128)(2,1)S(1)} %shard_map.64.refs_0_), channel_id=1, source_target_pairs={{0,1},{1,0},{2,3},{3,2},{4,5},{5,4},{6,7},{7,6},{8,9},{9,8},{10,11... | collective-permute-start | bytes 202760 | tf_op jit(solution)/shard_map/ppermute | solution.py:28
  4.7 9.1 %collective-permute-start.5 = (bf16[8,4224]{1,0:T(8,128)(2,1)S(1)}, bf16[8,4224]{1,0:T(8,128)(2,1)S(1)}, u32[]{:S(2)}, u32[]{:S(2)}) collective-permute-start(bf16[8,4224]{1,0:T(8,128)(2,1)S(1)} %shard_map.64.refs_0_), channel_id=1, source_target_pairs={{0,3},{1,2},{2,1},{3,0},{4,7},{5,6},{6,5},{7,4},{8,11},{9,10},{10,... | collective-permute-start | bytes 202760 | tf_op jit(solution)/shard_map/ppermute | solution.py:28
  7.2 6.6 %collective-permute-start.4 = (bf16[8,4224]{1,0:T(8,128)(2,1)S(1)}, bf16[8,4224]{1,0:T(8,128)(2,1)S(1)}, u32[]{:S(2)}, u32[]{:S(2)}) collective-permute-start(bf16[8,4224]{1,0:T(8,128)(2,1)S(1)} %shard_map.64.refs_0_), channel_id=1, source_target_pairs={{0,2},{1,3},{2,0},{3,1},{4,6},{5,7},{6,4},{7,5},{8,10},{9,11},{10,... | collective-permute-start | bytes 202760 | tf_op jit(solution)/shard_map/ppermute | solution.py:28
  7.3 9.5 %collective-permute-start.3 = (bf16[16,4224]{1,0:T(8,128)(2,1)S(1)}, bf16[16,4224]{1,0:T(8,128)(2,1)S(1)}, u32[]{:S(2)}, u32[]{:S(2)}) collective-permute-start(bf16[16,4224]{1,0:T(8,128)(2,1)S(1)} %shard_map.65), channel_id=1, source_target_pairs={{0,24},{4,28},{8,16},{12,20},{16,8},{20,12},{24,0},{28,4},{1,25},{... | collective-permute-start | bytes 405512 | tf_op jit(solution)/shard_map/ppermute | solution.py:28
  9.9 7.4 %collective-permute-start.2 = (bf16[16,4224]{1,0:T(8,128)(2,1)S(1)}, bf16[16,4224]{1,0:T(8,128)(2,1)S(1)}, u32[]{:S(2)}, u32[]{:S(2)}) collective-permute-start(bf16[16,4224]{1,0:T(8,128)(2,1)S(1)} %shard_map.65), channel_id=1, source_target_pairs={{0,16},{4,20},{8,24},{12,28},{16,0},{20,4},{24,8},{28,12},{1,17},{... | collective-permute-start | bytes 405512 | tf_op jit(solution)/shard_map/ppermute | solution.py:28
  10.4 6.9 %collective-permute-start.1 = (bf16[16,4224]{1,0:T(8,128)(2,1)S(1)}, bf16[16,4224]{1,0:T(8,128)(2,1)S(1)}, u32[]{:S(2)}, u32[]{:S(2)}) collective-permute-start(bf16[16,4224]{1,0:T(8,128)(2,1)S(1)} %shard_map.65), channel_id=1, source_target_pairs={{0,8},{4,12},{8,0},{12,4},{16,24},{20,28},{24,16},{28,20},{1,9},{5... | collective-permute-start | bytes 405512 | tf_op jit(solution)/shard_map/ppermute | solution.py:28
  13.8 9.4 %collective-permute-start.8 = (bf16[16,4224]{1,0:T(8,128)(2,1)S(1)}, bf16[16,4224]{1,0:T(8,128)(2,1)S(1)}, u32[]{:S(2)}, u32[]{:S(2)}) collective-permute-start(bf16[16,4224]{1,0:T(8,128)(2,1)S(1)} %get-tuple-element.35), channel_id=1, source_target_pairs={{0,24},{4,28},{8,16},{12,20},{16,8},{20,12},{24,0},{28,4},{1,25},{... | collective-permute-start | bytes 405512 | tf_op jit(solution)/shard_map/ppermute | solution.py:28
  16.3 6.9 %collective-permute-start.7 = (bf16[16,4224]{1,0:T(8,128)(2,1)S(1)}, bf16[16,4224]{1,0:T(8,128)(2,1)S(1)}, u32[]{:S(2)}, u32[]{:S(2)}) collective-permute-start(bf16[16,4224]{1,0:T(8,128)(2,1)S(1)} %get-tuple-element.35), channel_id=1, source_target_pairs={{0,16},{4,20},{8,24},{12,28},{16,0},{20,4},{24,8},{28,12},{1,17},{... | collective-permute-start | bytes 405512 | tf_op jit(solution)/shard_map/ppermute | solution.py:28
  16.8 6.4 %collective-permute-start.6 = (bf16[16,4224]{1,0:T(8,128)(2,1)S(1)}, bf16[16,4224]{1,0:T(8,128)(2,1)S(1)}, u32[]{:S(2)}, u32[]{:S(2)}) collective-permute-start(bf16[16,4224]{1,0:T(8,128)(2,1)S(1)} %get-tuple-element.35), channel_id=1, source_target_pairs={{0,8},{4,12},{8,0},{12,4},{16,24},{20,28},{24,16},{28,20},{1,9},{5... | collective-permute-start | bytes 405512 | tf_op jit(solution)/shard_map/ppermute | solution.py:28
  17.4 5.9 %collective-permute-start.9 = (bf16[64,4224]{1,0:T(8,128)(2,1)S(1)}, bf16[64,4224]{1,0:T(8,128)(2,1)S(1)}, u32[]{:S(2)}, u32[]{:S(2)}) collective-permute-start(bf16[64,4224]{1,0:T(8,128)(2,1)S(1)} %pad_maximum_fusion.refs_0_), channel_id=1, source_target_pairs={{0,4},{4,0},{8,12},{12,8},{16,20},{20,16},{24,28},{28,24},{1,5},{5... | collective-permute-start | bytes 1622024 | tf_op jit(solution)/shard_map/ppermute | solution.py:28
  23.3 2.0 %collective-permute-start.10 = (bf16[64,4224]{1,0:T(8,128)(2,1)S(1)}, bf16[64,4224]{1,0:T(8,128)(2,1)S(1)}, u32[]{:S(2)}, u32[]{:S(2)}) collective-permute-start(bf16[64,4224]{1,0:T(8,128)(2,1)S(1)} %constant_dynamic-update-slice_fusion.2.refs_1_), channel_id=1, source_target_pairs={{0,4},{4,0},{8,12},{12,8},{16,20},{20,16},{24,28},{28,24},{1,5},{5... | collective-permute-start | bytes 1622024 | tf_op jit(solution)/shard_map/ppermute | solution.py:28
  31.0 2.0 %collective-permute-start.12 = (bf16[64,4096]{1,0:T(8,128)(2,1)S(1)}, bf16[64,4096]{1,0:T(8,128)(2,1)S(1)}, u32[]{:S(2)}, u32[]{:S(2)}) collective-permute-start(bf16[64,4096]{1,0:T(8,128)(2,1)S(1)} %get-tuple-element.17), channel_id=1, source_target_pairs={{0,4},{4,0},{8,12},{12,8},{16,20},{20,16},{24,28},{28,24},{1,5},{5... | collective-permute-start | bytes 1572872 | tf_op jit(solution)/shard_map/ppermute | solution.py:28
  31.2 5.5 %collective-permute-start.11 = (bf16[64,4096]{1,0:T(8,128)(2,1)S(1)}, bf16[64,4096]{1,0:T(8,128)(2,1)S(1)}, u32[]{:S(2)}, u32[]{:S(2)}) collective-permute-start(bf16[64,4096]{1,0:T(8,128)(2,1)S(1)} %get-tuple-element.15), channel_id=1, source_target_pairs={{0,4},{4,0},{8,12},{12,8},{16,20},{20,16},{24,28},{28,24},{1,5},{5... | collective-permute-start | bytes 1572872 | tf_op jit(solution)/shard_map/ppermute | solution.py:28
  33.2 7.3 %collective-permute-start.13 = (bf16[16,4096]{1,0:T(8,128)(2,1)S(1)}, bf16[16,4096]{1,0:T(8,128)(2,1)S(1)}, u32[]{:S(2)}, u32[]{:S(2)}) collective-permute-start(bf16[16,4096]{1,0:T(8,128)(2,1)S(1)} %get-tuple-element.30), channel_id=1, source_target_pairs={{0,24},{4,28},{8,16},{12,20},{16,8},{20,12},{24,0},{28,4},{1,25},{... | collective-permute-start | bytes 393224 | tf_op jit(solution)/shard_map/ppermute | solution.py:28
  34.9 9.1 %collective-permute-start.18 = (bf16[16,4096]{1,0:T(8,128)(2,1)S(1)}, bf16[16,4096]{1,0:T(8,128)(2,1)S(1)}, u32[]{:S(2)}, u32[]{:S(2)}) collective-permute-start(bf16[16,4096]{1,0:T(8,128)(2,1)S(1)} %get-tuple-element.31), channel_id=1, source_target_pairs={{0,8},{4,12},{8,0},{12,4},{16,24},{20,28},{24,16},{28,20},{1,9},{5... | collective-permute-start | bytes 393224 | tf_op jit(solution)/shard_map/ppermute | solution.py:28
  36.1 7.9 %collective-permute-start.17 = (bf16[16,4096]{1,0:T(8,128)(2,1)S(1)}, bf16[16,4096]{1,0:T(8,128)(2,1)S(1)}, u32[]{:S(2)}, u32[]{:S(2)}) collective-permute-start(bf16[16,4096]{1,0:T(8,128)(2,1)S(1)} %get-tuple-element.32), channel_id=1, source_target_pairs={{0,16},{4,20},{8,24},{12,28},{16,0},{20,4},{24,8},{28,12},{1,17},{... | collective-permute-start | bytes 393224 | tf_op jit(solution)/shard_map/ppermute | solution.py:28
  40.5 6.5 %collective-permute-start.14 = (bf16[16,4096]{1,0:T(8,128)(2,1)S(1)}, bf16[16,4096]{1,0:T(8,128)(2,1)S(1)}, u32[]{:S(2)}, u32[]{:S(2)}) collective-permute-start(bf16[16,4096]{1,0:T(8,128)(2,1)S(1)} %get-tuple-element.18), channel_id=1, source_target_pairs={{0,24},{4,28},{8,16},{12,20},{16,8},{20,12},{24,0},{28,4},{1,25},{... | collective-permute-start | bytes 393224 | tf_op jit(solution)/shard_map/ppermute | solution.py:28
  42.1 6.0 %collective-permute-start.15 = (bf16[16,4096]{1,0:T(8,128)(2,1)S(1)}, bf16[16,4096]{1,0:T(8,128)(2,1)S(1)}, u32[]{:S(2)}, u32[]{:S(2)}) collective-permute-start(bf16[16,4096]{1,0:T(8,128)(2,1)S(1)} %get-tuple-element.19), channel_id=1, source_target_pairs={{0,16},{4,20},{8,24},{12,28},{16,0},{20,4},{24,8},{28,12},{1,17},{... | collective-permute-start | bytes 393224 | tf_op jit(solution)/shard_map/ppermute | solution.py:28
  43.5 5.0 %collective-permute-start.16 = (bf16[16,4096]{1,0:T(8,128)(2,1)S(1)}, bf16[16,4096]{1,0:T(8,128)(2,1)S(1)}, u32[]{:S(2)}, u32[]{:S(2)}) collective-permute-start(bf16[16,4096]{1,0:T(8,128)(2,1)S(1)} %get-tuple-element.20), channel_id=1, source_target_pairs={{0,8},{4,12},{8,0},{12,4},{16,24},{20,28},{24,16},{28,20},{1,9},{5... | collective-permute-start | bytes 393224 | tf_op jit(solution)/shard_map/ppermute | solution.py:28
  44.1 6.1 %collective-permute-start.19 = (bf16[8,4096]{1,0:T(8,128)(2,1)S(1)}, bf16[8,4096]{1,0:T(8,128)(2,1)S(1)}, u32[]{:S(2)}, u32[]{:S(2)}) collective-permute-start(bf16[8,4096]{1,0:T(8,128)(2,1)S(1)} %get-tuple-element.33), channel_id=1, source_target_pairs={{0,2},{1,3},{2,0},{3,1},{4,6},{5,7},{6,4},{7,5},{8,10},{9,11},{10,... | collective-permute-start | bytes 196616 | tf_op jit(solution)/shard_map/ppermute | solution.py:28
  45.6 6.1 %collective-permute-start.20 = (bf16[8,4096]{1,0:T(8,128)(2,1)S(1)}, bf16[8,4096]{1,0:T(8,128)(2,1)S(1)}, u32[]{:S(2)}, u32[]{:S(2)}) collective-permute-start(bf16[8,4096]{1,0:T(8,128)(2,1)S(1)} %get-tuple-element.34), channel_id=1, source_target_pairs={{0,3},{1,2},{2,1},{3,0},{4,7},{5,6},{6,5},{7,4},{8,11},{9,10},{10,... | collective-permute-start | bytes 196616 | tf_op jit(solution)/shard_map/ppermute | solution.py:28
  48.5 4.3 %collective-permute-start.21 = (bf16[8,4096]{1,0:T(8,128)(2,1)S(1)}, bf16[8,4096]{1,0:T(8,128)(2,1)S(1)}, u32[]{:S(2)}, u32[]{:S(2)}) collective-permute-start(bf16[8,4096]{1,0:T(8,128)(2,1)S(1)} %slice.87), channel_id=1, source_target_pairs={{0,1},{1,0},{2,3},{3,2},{4,5},{5,4},{6,7},{7,6},{8,9},{9,8},{10,11... | collective-permute-start | bytes 196616 | tf_op jit(solution)/shard_map/ppermute | solution.py:28

commit v6 on v5

--- a/solution.py
+++ b/solution.py
@@ -163,24 +163,22 @@
 
 def expert_kernel(exp_dev, expert_total, parts, *refs):
     pieces, refs = refs[:parts], refs[parts:]
-    gate_ref, up_ref, down_ref, *results, rows_ref = refs
+    gate_ref, up_ref, down_ref, *results = refs
     units, width = down_ref.shape[1:]
-    start = 0
-    for piece in pieces:
-        rows_ref[start : start + piece.shape[0]] = piece[...]
-        start += piece.shape[0]
-    tags = rows_ref[:, width:].astype(jnp.float32)
+    rows = jnp.concatenate([piece[...] for piece in pieces])
+    tags = rows[:, width:].astype(jnp.float32)
     lane = lax.rem(lax.broadcasted_iota(jnp.int32, tags.shape, 1), expert_total)
     first_expert = lax.axis_index("dp") * exp_dev
+    weights = [ref[local] for local in range(exp_dev) for ref in (gate_ref, up_ref)]
+    both = times_rows(rows[:, :width], jnp.concatenate(weights))
     hidden, shares = [], []
     for local in range(exp_dev):
-        weights = jnp.concatenate([gate_ref[local], up_ref[local]])
-        both = times_rows(rows_ref[:, :width], weights)
-        gate, up = both[:, :units], both[:, units:]
+        middle = (2 * local + 1) * units
+        gate, up = both[:, middle - units : middle], both[:, middle : middle + units]
         hidden.append((gate / (1.0 + jnp.exp(-gate)) * up).astype(jnp.bfloat16))
         mine = jnp.where(lane == first_expert + local, tags, 0.0)
         shares.append(jnp.sum(mine, axis=1, keepdims=True))
-    block = min(1024, width)
+    block = min(2048, width)
     for first in range(0, width, block):
         total = 0.0
         for local in range(exp_dev):
@@ -208,7 +206,6 @@
         ],
         in_specs=[IN_VMEM] * (len(pieces) + 3),
         out_specs=[IN_VMEM] * len(pieces),
-        scratch_shapes=[pltpu.VMEM((rows, pieces[0].shape[1]), jnp.bfloat16)],
         compiler_params=pltpu.CompilerParams(vmem_limit_bytes=VMEM_BYTES),
         cost_estimate=pl.CostEstimate(
             flops=6 * rows * w_down.size, bytes_accessed=rows * width * 5, transcendentals=0

time: 53.6 us -> 53.6 us (level)
  no operation moved by 1% of the time
where the time goes in v6:
time: 53.6 us; the launch traced here: 53.5 us
  starting transfers between devices  23.3 us (43%)
  waiting for transfers between devices  21.5 us (40%)
  Pallas kernels  7.22 us (13%)
  other arithmetic  1.07 us (2%)
    ppermute x22, starting transfers between devices, swap(): return lax.ppermute(value, axis, [(i, i ^ mask) for i in range(count)])  23.3 us
    ppermute x22, waiting for transfers between devices, swap(): return lax.ppermute(value, axis, [(i, i ^ mask) for i in range(count)])  21.5 us
    pallas_call x1, Pallas kernels, run_experts(): pl.pallas_call(functools.partial(expert_kernel, exp_dev, expert_total, le...  5.67 us
    pallas_call x1, Pallas kernels, pack(): pl.pallas_call(pack_kernel, out_shape=pltpu.VMEM((rows, width + extra), t...  1.54 us
  transfers between devices with their start and end apart: 22, of which 11 were waited for; matrix products, arithmetic and copies ran while one was open for 1% of the time, Pallas kernels for 0%

profile of v6, /device:TPU:0, one launch (start us, length us, event | category | flops | bytes accessed | tf_op | source)
XLA Modules:
  0.0 53.5 jit_solution(9196181442762904102)
XLA Ops:
  0.0 0.0 slice-start
  0.0 0.0 slice-start.2
  0.0 0.0 slice-start.4
  0.0 1.5 %shard_map.64.refs_0_ = bf16[8,4224]{1,0:T(8,128)(2,1)S(1)} custom-call(bf16[8,4096]{1,0:T(8,128)(2,1)} %tokens_hbm.1, s32[8,8]{1,0:T(8,128)} %ids_hbm.1, bf16[16,4096]{1,0:T(8,128)(2,1)} %router_hbm.1), custom_call_target="tpu_custom_call" | custom-call | flops 1048576 | bytes 262144 | tf_op jit(solution)/shard_map/pallas_call | solution.py:126
  1.6 0.0 slice-start.1
  1.6 0.0 slice-start.3
  1.6 0.0 slice-start.5
  1.6 3.1 %collective-permute-start = (bf16[8,4224]{1,0:T(8,128)(2,1)S(1)}, bf16[8,4224]{1,0:T(8,128)(2,1)S(1)}, u32[]{:S(2)}, u32[]{:S(2)}) collective-permute-start(bf16[8,4224]{1,0:T(8,128)(2,1)S(1)} %shard_map.64.refs_0_), channel_id=1, source_target_pairs={{0,1},{1,0},{2,3},{3,2},{4,5},{5,4},{6,7},{7,6},{8,9},{9,8},{10,11... | collective-permute-start | bytes 202760 | tf_op jit(solution)/shard_map/ppermute | solution.py:28
  4.7 2.5 %collective-permute-start.5 = (bf16[8,4224]{1,0:T(8,128)(2,1)S(1)}, bf16[8,4224]{1,0:T(8,128)(2,1)S(1)}, u32[]{:S(2)}, u32[]{:S(2)}) collective-permute-start(bf16[8,4224]{1,0:T(8,128)(2,1)S(1)} %shard_map.64.refs_0_), channel_id=1, source_target_pairs={{0,3},{1,2},{2,1},{3,0},{4,7},{5,6},{6,5},{7,4},{8,11},{9,10},{10,... | collective-permute-start | bytes 202760 | tf_op jit(solution)/shard_map/ppermute | solution.py:28
  7.2 0.1 collective-permute-start.4
  7.3 0.0 collective-permute-done.refs_1_
  7.3 2.6 %collective-permute-start.3 = (bf16[16,4224]{1,0:T(8,128)(2,1)S(1)}, bf16[16,4224]{1,0:T(8,128)(2,1)S(1)}, u32[]{:S(2)}, u32[]{:S(2)}) collective-permute-start(bf16[16,4224]{1,0:T(8,128)(2,1)S(1)} %shard_map.65), channel_id=1, source_target_pairs={{0,24},{4,28},{8,16},{12,20},{16,8},{20,12},{24,0},{28,4},{1,25},{... | collective-permute-start | bytes 405512 | tf_op jit(solution)/shard_map/ppermute | solution.py:28
  9.9 0.5 collective-permute-start.2
  10.4 0.4 collective-permute-start.1
  10.9 2.9 %collective-permute-done.4 = bf16[8,4224]{1,0:T(8,128)(2,1)S(1)} collective-permute-done((bf16[8,4224]{1,0:T(8,128)(2,1)S(1)}, bf16[8,4224]{1,0:T(8,128)(2,1)S(1)}, u32[]{:S(2)}, u32[]{:S(2)}) %collective-permute-start.4) | collective-permute-done | bytes 67616 | tf_op jit(solution)/shard_map/ppermute | solution.py:28
  13.8 0.0 collective-permute-done.5
  13.8 2.5 %collective-permute-start.8 = (bf16[16,4224]{1,0:T(8,128)(2,1)S(1)}, bf16[16,4224]{1,0:T(8,128)(2,1)S(1)}, u32[]{:S(2)}, u32[]{:S(2)}) collective-permute-start(bf16[16,4224]{1,0:T(8,128)(2,1)S(1)} %get-tuple-element.35), channel_id=1, source_target_pairs={{0,24},{4,28},{8,16},{12,20},{16,8},{20,12},{24,0},{28,4},{1,25},{... | collective-permute-start | bytes 405512 | tf_op jit(solution)/shard_map/ppermute | solution.py:28
  16.3 0.5 collective-permute-start.7
  16.8 0.0 collective-permute-done.3
  16.8 0.5 %collective-permute-start.6 = (bf16[16,4224]{1,0:T(8,128)(2,1)S(1)}, bf16[16,4224]{1,0:T(8,128)(2,1)S(1)}, u32[]{:S(2)}, u32[]{:S(2)}) collective-permute-start(bf16[16,4224]{1,0:T(8,128)(2,1)S(1)} %get-tuple-element.35), channel_id=1, source_target_pairs={{0,8},{4,12},{8,0},{12,4},{16,24},{20,28},{24,16},{28,20},{1,9},{5... | collective-permute-start | bytes 405512 | tf_op jit(solution)/shard_map/ppermute | solution.py:28
  17.4 0.0 collective-permute-done.2
  17.4 0.0 collective-permute-done.1
  17.4 0.1 collective-permute-start.9
  17.5 5.7 %collective-permute-done.6 = bf16[16,4224]{1,0:T(8,128)(2,1)S(1)} collective-permute-done((bf16[16,4224]{1,0:T(8,128)(2,1)S(1)}, bf16[16,4224]{1,0:T(8,128)(2,1)S(1)}, u32[]{:S(2)}, u32[]{:S(2)}) %collective-permute-start.6) | collective-permute-done | bytes 135200 | tf_op jit(solution)/shard_map/ppermute | solution.py:28
  23.2 0.0 collective-permute-done.7
  23.2 0.0 collective-permute-done.8
  23.3 0.1 collective-permute-start.10
  23.3 0.0 collective-permute-done.9.refs_2_
  23.4 1.9 %collective-permute-done.10.refs_3_ = bf16[64,4224]{1,0:T(8,128)(2,1)S(1)} collective-permute-done((bf16[64,4224]{1,0:T(8,128)(2,1)S(1)}, bf16[64,4224]{1,0:T(8,128)(2,1)S(1)}, u32[]{:S(2)}, u32[]{:S(2)}) %collective-permute-start.10) | collective-permute-done | bytes 540704 | tf_op jit(solution)/shard_map/ppermute | solution.py:28
  25.3 0.0 slice-done
  25.3 0.0 slice-done.2
  25.3 0.0 slice-done.4
  25.3 0.0 slice-done.1
  25.3 0.0 slice-done.3
  25.3 0.0 slice-done.5
  25.3 5.7 %shard_map.66 = (f32[64,4096]{1,0:T(8,128)S(1)}, f32[64,4096]{1,0:T(8,128)S(1)}, bf16[64,4096]{1,0:T(8,128)(2,1)S(1)}, bf16[64,4096]{1,0:T(8,128)(2,1)S(1)}) custom-call(bf16[64,4224]{1,0:T(8,128)(2,1)S(1)} %pad_maximum_fusion.refs_0_, bf16[64,4224]{1,0:T(8,128)(2,1)S(1)} %constant_dynamic-update-slice_fusion.2.refs_1_, ...), custom_call_target="tpu_custom_call" | custom-call | flops 4831838208 | bytes 5242880 | tf_op jit(solution)/shard_map/pallas_call | solution.py:202
  31.0 0.2 collective-permute-start.12
  31.2 0.4 collective-permute-start.11
  31.6 1.4 %collective-permute-done.12 = bf16[64,4096]{1,0:T(8,128)(2,1)S(1)} collective-permute-done((bf16[64,4096]{1,0:T(8,128)(2,1)S(1)}, bf16[64,4096]{1,0:T(8,128)(2,1)S(1)}, u32[]{:S(2)}, u32[]{:S(2)}) %collective-permute-start.12) | collective-permute-done | bytes 524320 | tf_op jit(solution)/shard_map/ppermute | solution.py:28
  33.0 0.1 fusion.8
  33.2 1.7 %collective-permute-start.13 = (bf16[16,4096]{1,0:T(8,128)(2,1)S(1)}, bf16[16,4096]{1,0:T(8,128)(2,1)S(1)}, u32[]{:S(2)}, u32[]{:S(2)}) collective-permute-start(bf16[16,4096]{1,0:T(8,128)(2,1)S(1)} %get-tuple-element.30), channel_id=1, source_target_pairs={{0,24},{4,28},{8,16},{12,20},{16,8},{20,12},{24,0},{28,4},{1,25},{... | collective-permute-start | bytes 393224 | tf_op jit(solution)/shard_map/ppermute | solution.py:28
  34.9 1.2 %collective-permute-start.18 = (bf16[16,4096]{1,0:T(8,128)(2,1)S(1)}, bf16[16,4096]{1,0:T(8,128)(2,1)S(1)}, u32[]{:S(2)}, u32[]{:S(2)}) collective-permute-start(bf16[16,4096]{1,0:T(8,128)(2,1)S(1)} %get-tuple-element.31), channel_id=1, source_target_pairs={{0,8},{4,12},{8,0},{12,4},{16,24},{20,28},{24,16},{28,20},{1,9},{5... | collective-permute-start | bytes 393224 | tf_op jit(solution)/shard_map/ppermute | solution.py:28
  36.1 0.6 %collective-permute-start.17 = (bf16[16,4096]{1,0:T(8,128)(2,1)S(1)}, bf16[16,4096]{1,0:T(8,128)(2,1)S(1)}, u32[]{:S(2)}, u32[]{:S(2)}) collective-permute-start(bf16[16,4096]{1,0:T(8,128)(2,1)S(1)} %get-tuple-element.32), channel_id=1, source_target_pairs={{0,16},{4,20},{8,24},{12,28},{16,0},{20,4},{24,8},{28,12},{1,17},{... | collective-permute-start | bytes 393224 | tf_op jit(solution)/shard_map/ppermute | solution.py:28
  36.7 0.0 collective-permute-done.11
  36.7 0.1 fusion.7
  36.9 3.6 %collective-permute-done.13 = bf16[16,4096]{1,0:T(8,128)(2,1)S(1)} collective-permute-done((bf16[16,4096]{1,0:T(8,128)(2,1)S(1)}, bf16[16,4096]{1,0:T(8,128)(2,1)S(1)}, u32[]{:S(2)}, u32[]{:S(2)}) %collective-permute-start.13) | collective-permute-done | bytes 131104 | tf_op jit(solution)/shard_map/ppermute | solution.py:28
  40.5 1.6 %collective-permute-start.14 = (bf16[16,4096]{1,0:T(8,128)(2,1)S(1)}, bf16[16,4096]{1,0:T(8,128)(2,1)S(1)}, u32[]{:S(2)}, u32[]{:S(2)}) collective-permute-start(bf16[16,4096]{1,0:T(8,128)(2,1)S(1)} %get-tuple-element.18), channel_id=1, source_target_pairs={{0,24},{4,28},{8,16},{12,20},{16,8},{20,12},{24,0},{28,4},{1,25},{... | collective-permute-start | bytes 393224 | tf_op jit(solution)/shard_map/ppermute | solution.py:28
  42.1 1.3 %collective-permute-start.15 = (bf16[16,4096]{1,0:T(8,128)(2,1)S(1)}, bf16[16,4096]{1,0:T(8,128)(2,1)S(1)}, u32[]{:S(2)}, u32[]{:S(2)}) collective-permute-start(bf16[16,4096]{1,0:T(8,128)(2,1)S(1)} %get-tuple-element.19), channel_id=1, source_target_pairs={{0,16},{4,20},{8,24},{12,28},{16,0},{20,4},{24,8},{28,12},{1,17},{... | collective-permute-start | bytes 393224 | tf_op jit(solution)/shard_map/ppermute | solution.py:28
  43.4 0.5 collective-permute-start.16
  43.9 0.0 collective-permute-done.18
  44.0 0.0 collective-permute-done.17
  44.0 0.1 fusion.2
  44.0 1.5 %collective-permute-start.19 = (bf16[8,4096]{1,0:T(8,128)(2,1)S(1)}, bf16[8,4096]{1,0:T(8,128)(2,1)S(1)}, u32[]{:S(2)}, u32[]{:S(2)}) collective-permute-start(bf16[8,4096]{1,0:T(8,128)(2,1)S(1)} %get-tuple-element.33), channel_id=1, source_target_pairs={{0,2},{1,3},{2,0},{3,1},{4,6},{5,7},{6,4},{7,5},{8,10},{9,11},{10,... | collective-permute-start | bytes 196616 | tf_op jit(solution)/shard_map/ppermute | solution.py:28
  45.5 1.0 %collective-permute-start.20 = (bf16[8,4096]{1,0:T(8,128)(2,1)S(1)}, bf16[8,4096]{1,0:T(8,128)(2,1)S(1)}, u32[]{:S(2)}, u32[]{:S(2)}) collective-permute-start(bf16[8,4096]{1,0:T(8,128)(2,1)S(1)} %get-tuple-element.34), channel_id=1, source_target_pairs={{0,3},{1,2},{2,1},{3,0},{4,7},{5,6},{6,5},{7,4},{8,11},{9,10},{10,... | collective-permute-start | bytes 196616 | tf_op jit(solution)/shard_map/ppermute | solution.py:28
  46.6 0.4 collective-permute-done.14
  47.0 1.1 %collective-permute-done.15 = bf16[16,4096]{1,0:T(8,128)(2,1)S(1)} collective-permute-done((bf16[16,4096]{1,0:T(8,128)(2,1)S(1)}, bf16[16,4096]{1,0:T(8,128)(2,1)S(1)}, u32[]{:S(2)}, u32[]{:S(2)}) %collective-permute-start.15) | collective-permute-done | bytes 131104 | tf_op jit(solution)/shard_map/ppermute | solution.py:28
  48.1 0.3 collective-permute-done.16
  48.4 0.1 fusion.4
  48.5 0.2 collective-permute-start.21
  48.7 1.5 %collective-permute-done.19 = bf16[8,4096]{1,0:T(8,128)(2,1)S(1)} collective-permute-done((bf16[8,4096]{1,0:T(8,128)(2,1)S(1)}, bf16[8,4096]{1,0:T(8,128)(2,1)S(1)}, u32[]{:S(2)}, u32[]{:S(2)}) %collective-permute-start.19) | collective-permute-done | bytes 65568 | tf_op jit(solution)/shard_map/ppermute | solution.py:28
  50.1 1.4 %collective-permute-done.20 = bf16[8,4096]{1,0:T(8,128)(2,1)S(1)} collective-permute-done((bf16[8,4096]{1,0:T(8,128)(2,1)S(1)}, bf16[8,4096]{1,0:T(8,128)(2,1)S(1)}, u32[]{:S(2)}, u32[]{:S(2)}) %collective-permute-start.20) | collective-permute-done | bytes 65568 | tf_op jit(solution)/shard_map/ppermute | solution.py:28
  51.6 1.2 %collective-permute-done.21 = bf16[8,4096]{1,0:T(8,128)(2,1)S(1)} collective-permute-done((bf16[8,4096]{1,0:T(8,128)(2,1)S(1)}, bf16[8,4096]{1,0:T(8,128)(2,1)S(1)}, u32[]{:S(2)}, u32[]{:S(2)}) %collective-permute-start.21) | collective-permute-done | bytes 65568 | tf_op jit(solution)/shard_map/ppermute | solution.py:28
  52.8 0.6 %fusion.6 = bf16[8,4096]{1,0:T(8,128)(2,1)} fusion(f32[8,4096]{1,0:T(8,128)S(1)} %convert_add_fusion.2, f32[16,4096]{1,0:T(8,128)S(1)} %fusion.4, bf16[8,4096]{1,0:T(8,128)(2,1)S(1)} %collective-permute-done.21), kind=kLoop, calls=%fused_computation.13 | loop fusion | flops 131072 | bytes 393216 | tf_op jit(solution)/shard_map/convert_element_type | solution.py:88
  (15 shorter events, 0.2 us)
Async XLA Ops:
  0.0 25.3 %slice-start = ((s8[6291456]{0:T(1024)(128)(4,1)}), s8[4194304]{0:T(1024)(128)(4,1)S(1)}, s32[]{:S(2)}) async-start(s8[6291456]{0:T(1024)(128)(4,1)} %bitcast), calls=%async_computation | async-start | bytes 8388608
  0.0 25.3 %slice-start.2 = ((s8[6291456]{0:T(1024)(128)(4,1)}), s8[4194304]{0:T(1024)(128)(4,1)S(1)}, s32[]{:S(2)}) async-start(s8[6291456]{0:T(1024)(128)(4,1)} %bitcast.2), calls=%async_computation.2 | async-start | bytes 8388608
  0.0 25.3 %slice-start.4 = ((s8[6291456]{0:T(1024)(128)(4,1)}), s8[4194304]{0:T(1024)(128)(4,1)S(1)}, s32[]{:S(2)}) async-start(s8[6291456]{0:T(1024)(128)(4,1)} %bitcast.4), calls=%async_computation.4 | async-start | bytes 8388608
  1.6 23.7 %slice-start.1 = ((s8[6291456]{0:T(1024)(128)(4,1)}), s8[2097152]{0:T(1024)(128)(4,1)S(1)}, s32[]{:S(2)}) async-start(s8[6291456]{0:T(1024)(128)(4,1)} %bitcast), calls=%async_computation.1 | async-start | bytes 4194304
  1.6 23.7 %slice-start.3 = ((s8[6291456]{0:T(1024)(128)(4,1)}), s8[2097152]{0:T(1024)(128)(4,1)S(1)}, s32[]{:S(2)}) async-start(s8[6291456]{0:T(1024)(128)(4,1)} %bitcast.2), calls=%async_computation.3 | async-start | bytes 4194304
  1.6 23.7 %slice-start.5 = ((s8[6291456]{0:T(1024)(128)(4,1)}), s8[2097152]{0:T(1024)(128)(4,1)S(1)}, s32[]{:S(2)}) async-start(s8[6291456]{0:T(1024)(128)(4,1)} %bitcast.4), calls=%async_computation.5 | async-start | bytes 4194304
  1.6 5.7 %collective-permute-start = (bf16[8,4224]{1,0:T(8,128)(2,1)S(1)}, bf16[8,4224]{1,0:T(8,128)(2,1)S(1)}, u32[]{:S(2)}, u32[]{:S(2)}) collective-permute-start(bf16[8,4224]{1,0:T(8,128)(2,1)S(1)} %shard_map.64.refs_0_), channel_id=1, source_target_pairs={{0,1},{1,0},{2,3},{3,2},{4,5},{5,4},{6,7},{7,6},{8,9},{9,8},{10,11... | collective-permute-start | bytes 202760 | tf_op jit(solution)/shard_map/ppermute | solution.py:28
  4.7 9.1 %collective-permute-start.5 = (bf16[8,4224]{1,0:T(8,128)(2,1)S(1)}, bf16[8,4224]{1,0:T(8,128)(2,1)S(1)}, u32[]{:S(2)}, u32[]{:S(2)}) collective-permute-start(bf16[8,4224]{1,0:T(8,128)(2,1)S(1)} %shard_map.64.refs_0_), channel_id=1, source_target_pairs={{0,3},{1,2},{2,1},{3,0},{4,7},{5,6},{6,5},{7,4},{8,11},{9,10},{10,... | collective-permute-start | bytes 202760 | tf_op jit(solution)/shard_map/ppermute | solution.py:28
  7.2 6.6 %collective-permute-start.4 = (bf16[8,4224]{1,0:T(8,128)(2,1)S(1)}, bf16[8,4224]{1,0:T(8,128)(2,1)S(1)}, u32[]{:S(2)}, u32[]{:S(2)}) collective-permute-start(bf16[8,4224]{1,0:T(8,128)(2,1)S(1)} %shard_map.64.refs_0_), channel_id=1, source_target_pairs={{0,2},{1,3},{2,0},{3,1},{4,6},{5,7},{6,4},{7,5},{8,10},{9,11},{10,... | collective-permute-start | bytes 202760 | tf_op jit(solution)/shard_map/ppermute | solution.py:28
  7.3 9.5 %collective-permute-start.3 = (bf16[16,4224]{1,0:T(8,128)(2,1)S(1)}, bf16[16,4224]{1,0:T(8,128)(2,1)S(1)}, u32[]{:S(2)}, u32[]{:S(2)}) collective-permute-start(bf16[16,4224]{1,0:T(8,128)(2,1)S(1)} %shard_map.65), channel_id=1, source_target_pairs={{0,24},{4,28},{8,16},{12,20},{16,8},{20,12},{24,0},{28,4},{1,25},{... | collective-permute-start | bytes 405512 | tf_op jit(solution)/shard_map/ppermute | solution.py:28
  9.9 7.4 %collective-permute-start.2 = (bf16[16,4224]{1,0:T(8,128)(2,1)S(1)}, bf16[16,4224]{1,0:T(8,128)(2,1)S(1)}, u32[]{:S(2)}, u32[]{:S(2)}) collective-permute-start(bf16[16,4224]{1,0:T(8,128)(2,1)S(1)} %shard_map.65), channel_id=1, source_target_pairs={{0,16},{4,20},{8,24},{12,28},{16,0},{20,4},{24,8},{28,12},{1,17},{... | collective-permute-start | bytes 405512 | tf_op jit(solution)/shard_map/ppermute | solution.py:28
  10.4 6.9 %collective-permute-start.1 = (bf16[16,4224]{1,0:T(8,128)(2,1)S(1)}, bf16[16,4224]{1,0:T(8,128)(2,1)S(1)}, u32[]{:S(2)}, u32[]{:S(2)}) collective-permute-start(bf16[16,4224]{1,0:T(8,128)(2,1)S(1)} %shard_map.65), channel_id=1, source_target_pairs={{0,8},{4,12},{8,0},{12,4},{16,24},{20,28},{24,16},{28,20},{1,9},{5... | collective-permute-start | bytes 405512 | tf_op jit(solution)/shard_map/ppermute | solution.py:28
  13.8 9.4 %collective-permute-start.8 = (bf16[16,4224]{1,0:T(8,128)(2,1)S(1)}, bf16[16,4224]{1,0:T(8,128)(2,1)S(1)}, u32[]{:S(2)}, u32[]{:S(2)}) collective-permute-start(bf16[16,4224]{1,0:T(8,128)(2,1)S(1)} %get-tuple-element.35), channel_id=1, source_target_pairs={{0,24},{4,28},{8,16},{12,20},{16,8},{20,12},{24,0},{28,4},{1,25},{... | collective-permute-start | bytes 405512 | tf_op jit(solution)/shard_map/ppermute | solution.py:28
  16.3 6.9 %collective-permute-start.7 = (bf16[16,4224]{1,0:T(8,128)(2,1)S(1)}, bf16[16,4224]{1,0:T(8,128)(2,1)S(1)}, u32[]{:S(2)}, u32[]{:S(2)}) collective-permute-start(bf16[16,4224]{1,0:T(8,128)(2,1)S(1)} %get-tuple-element.35), channel_id=1, source_target_pairs={{0,16},{4,20},{8,24},{12,28},{16,0},{20,4},{24,8},{28,12},{1,17},{... | collective-permute-start | bytes 405512 | tf_op jit(solution)/shard_map/ppermute | solution.py:28
  16.8 6.4 %collective-permute-start.6 = (bf16[16,4224]{1,0:T(8,128)(2,1)S(1)}, bf16[16,4224]{1,0:T(8,128)(2,1)S(1)}, u32[]{:S(2)}, u32[]{:S(2)}) collective-permute-start(bf16[16,4224]{1,0:T(8,128)(2,1)S(1)} %get-tuple-element.35), channel_id=1, source_target_pairs={{0,8},{4,12},{8,0},{12,4},{16,24},{20,28},{24,16},{28,20},{1,9},{5... | collective-permute-start | bytes 405512 | tf_op jit(solution)/shard_map/ppermute | solution.py:28
  17.4 5.9 %collective-permute-start.9 = (bf16[64,4224]{1,0:T(8,128)(2,1)S(1)}, bf16[64,4224]{1,0:T(8,128)(2,1)S(1)}, u32[]{:S(2)}, u32[]{:S(2)}) collective-permute-start(bf16[64,4224]{1,0:T(8,128)(2,1)S(1)} %pad_maximum_fusion.refs_0_), channel_id=1, source_target_pairs={{0,4},{4,0},{8,12},{12,8},{16,20},{20,16},{24,28},{28,24},{1,5},{5... | collective-permute-start | bytes 1622024 | tf_op jit(solution)/shard_map/ppermute | solution.py:28
  23.3 2.0 %collective-permute-start.10 = (bf16[64,4224]{1,0:T(8,128)(2,1)S(1)}, bf16[64,4224]{1,0:T(8,128)(2,1)S(1)}, u32[]{:S(2)}, u32[]{:S(2)}) collective-permute-start(bf16[64,4224]{1,0:T(8,128)(2,1)S(1)} %constant_dynamic-update-slice_fusion.2.refs_1_), channel_id=1, source_target_pairs={{0,4},{4,0},{8,12},{12,8},{16,20},{20,16},{24,28},{28,24},{1,5},{5... | collective-permute-start | bytes 1622024 | tf_op jit(solution)/shard_map/ppermute | solution.py:28
  31.0 2.0 %collective-permute-start.12 = (bf16[64,4096]{1,0:T(8,128)(2,1)S(1)}, bf16[64,4096]{1,0:T(8,128)(2,1)S(1)}, u32[]{:S(2)}, u32[]{:S(2)}) collective-permute-start(bf16[64,4096]{1,0:T(8,128)(2,1)S(1)} %get-tuple-element.17), channel_id=1, source_target_pairs={{0,4},{4,0},{8,12},{12,8},{16,20},{20,16},{24,28},{28,24},{1,5},{5... | collective-permute-start | bytes 1572872 | tf_op jit(solution)/shard_map/ppermute | solution.py:28
  31.2 5.5 %collective-permute-start.11 = (bf16[64,4096]{1,0:T(8,128)(2,1)S(1)}, bf16[64,4096]{1,0:T(8,128)(2,1)S(1)}, u32[]{:S(2)}, u32[]{:S(2)}) collective-permute-start(bf16[64,4096]{1,0:T(8,128)(2,1)S(1)} %get-tuple-element.15), channel_id=1, source_target_pairs={{0,4},{4,0},{8,12},{12,8},{16,20},{20,16},{24,28},{28,24},{1,5},{5... | collective-permute-start | bytes 1572872 | tf_op jit(solution)/shard_map/ppermute | solution.py:28
  33.2 7.3 %collective-permute-start.13 = (bf16[16,4096]{1,0:T(8,128)(2,1)S(1)}, bf16[16,4096]{1,0:T(8,128)(2,1)S(1)}, u32[]{:S(2)}, u32[]{:S(2)}) collective-permute-start(bf16[16,4096]{1,0:T(8,128)(2,1)S(1)} %get-tuple-element.30), channel_id=1, source_target_pairs={{0,24},{4,28},{8,16},{12,20},{16,8},{20,12},{24,0},{28,4},{1,25},{... | collective-permute-start | bytes 393224 | tf_op jit(solution)/shard_map/ppermute | solution.py:28
  34.9 9.1 %collective-permute-start.18 = (bf16[16,4096]{1,0:T(8,128)(2,1)S(1)}, bf16[16,4096]{1,0:T(8,128)(2,1)S(1)}, u32[]{:S(2)}, u32[]{:S(2)}) collective-permute-start(bf16[16,4096]{1,0:T(8,128)(2,1)S(1)} %get-tuple-element.31), channel_id=1, source_target_pairs={{0,8},{4,12},{8,0},{12,4},{16,24},{20,28},{24,16},{28,20},{1,9},{5... | collective-permute-start | bytes 393224 | tf_op jit(solution)/shard_map/ppermute | solution.py:28
  36.1 7.9 %collective-permute-start.17 = (bf16[16,4096]{1,0:T(8,128)(2,1)S(1)}, bf16[16,4096]{1,0:T(8,128)(2,1)S(1)}, u32[]{:S(2)}, u32[]{:S(2)}) collective-permute-start(bf16[16,4096]{1,0:T(8,128)(2,1)S(1)} %get-tuple-element.32), channel_id=1, source_target_pairs={{0,16},{4,20},{8,24},{12,28},{16,0},{20,4},{24,8},{28,12},{1,17},{... | collective-permute-start | bytes 393224 | tf_op jit(solution)/shard_map/ppermute | solution.py:28
  40.5 6.5 %collective-permute-start.14 = (bf16[16,4096]{1,0:T(8,128)(2,1)S(1)}, bf16[16,4096]{1,0:T(8,128)(2,1)S(1)}, u32[]{:S(2)}, u32[]{:S(2)}) collective-permute-start(bf16[16,4096]{1,0:T(8,128)(2,1)S(1)} %get-tuple-element.18), channel_id=1, source_target_pairs={{0,24},{4,28},{8,16},{12,20},{16,8},{20,12},{24,0},{28,4},{1,25},{... | collective-permute-start | bytes 393224 | tf_op jit(solution)/shard_map/ppermute | solution.py:28
  42.1 6.0 %collective-permute-start.15 = (bf16[16,4096]{1,0:T(8,128)(2,1)S(1)}, bf16[16,4096]{1,0:T(8,128)(2,1)S(1)}, u32[]{:S(2)}, u32[]{:S(2)}) collective-permute-start(bf16[16,4096]{1,0:T(8,128)(2,1)S(1)} %get-tuple-element.19), channel_id=1, source_target_pairs={{0,16},{4,20},{8,24},{12,28},{16,0},{20,4},{24,8},{28,12},{1,17},{... | collective-permute-start | bytes 393224 | tf_op jit(solution)/shard_map/ppermute | solution.py:28
  43.4 5.0 %collective-permute-start.16 = (bf16[16,4096]{1,0:T(8,128)(2,1)S(1)}, bf16[16,4096]{1,0:T(8,128)(2,1)S(1)}, u32[]{:S(2)}, u32[]{:S(2)}) collective-permute-start(bf16[16,4096]{1,0:T(8,128)(2,1)S(1)} %get-tuple-element.20), channel_id=1, source_target_pairs={{0,8},{4,12},{8,0},{12,4},{16,24},{20,28},{24,16},{28,20},{1,9},{5... | collective-permute-start | bytes 393224 | tf_op jit(solution)/shard_map/ppermute | solution.py:28
  44.0 6.1 %collective-permute-start.19 = (bf16[8,4096]{1,0:T(8,128)(2,1)S(1)}, bf16[8,4096]{1,0:T(8,128)(2,1)S(1)}, u32[]{:S(2)}, u32[]{:S(2)}) collective-permute-start(bf16[8,4096]{1,0:T(8,128)(2,1)S(1)} %get-tuple-element.33), channel_id=1, source_target_pairs={{0,2},{1,3},{2,0},{3,1},{4,6},{5,7},{6,4},{7,5},{8,10},{9,11},{10,... | collective-permute-start | bytes 196616 | tf_op jit(solution)/shard_map/ppermute | solution.py:28
  45.5 6.1 %collective-permute-start.20 = (bf16[8,4096]{1,0:T(8,128)(2,1)S(1)}, bf16[8,4096]{1,0:T(8,128)(2,1)S(1)}, u32[]{:S(2)}, u32[]{:S(2)}) collective-permute-start(bf16[8,4096]{1,0:T(8,128)(2,1)S(1)} %get-tuple-element.34), channel_id=1, source_target_pairs={{0,3},{1,2},{2,1},{3,0},{4,7},{5,6},{6,5},{7,4},{8,11},{9,10},{10,... | collective-permute-start | bytes 196616 | tf_op jit(solution)/shard_map/ppermute | solution.py:28
  48.5 4.3 %collective-permute-start.21 = (bf16[8,4096]{1,0:T(8,128)(2,1)S(1)}, bf16[8,4096]{1,0:T(8,128)(2,1)S(1)}, u32[]{:S(2)}, u32[]{:S(2)}) collective-permute-start(bf16[8,4096]{1,0:T(8,128)(2,1)S(1)} %slice.87), channel_id=1, source_target_pairs={{0,1},{1,0},{2,3},{3,2},{4,5},{5,4},{6,7},{7,6},{8,9},{9,8},{10,11... | collective-permute-start | bytes 196616 | tf_op jit(solution)/shard_map/ppermute | solution.py:28

commit v7 on v6

--- a/solution.py
+++ b/solution.py
@@ -77,7 +77,7 @@
         part, *rest = split(mine + wide(swap(other, *CORE)), len(steps) + 1)
         rest = [other.astype(jnp.bfloat16) for other in rest[::-1]]
         if here:
-            rest = [after(other, here[0]) for other in rest]
+            rest = rest[:1] + [after(other, here[0]) for other in rest[1:]]
         here = [send(other, step) for other, step in zip(rest, steps[::-1])]
         sums.append(sum([wide(other) for other in here], part))
     far, (total, *near) = split(sums[0], depth // 2), split(sums[1], depth // 2)

time: 53.6 us -> 54 us (level)
  starting transfers between devices: 23.3 us -> 24.5 us
  waiting for transfers between devices: 21.5 us -> 20.6 us
    ppermute x22, starting transfers between devices: 23.3 us -> 24.5 us  [swap(): return lax.ppermute(value, axis, [(i, i ^ mask) for i in range(count)])]
    ppermute x22, waiting for transfers between devices: 21.5 us -> 20.6 us  [swap(): return lax.ppermute(value, axis, [(i, i ^ mask) for i in range(count)])]
where the time goes in v7:
time: 54 us; the launch traced here: 53.9 us
  starting transfers between devices  24.5 us (45%)
  waiting for transfers between devices  20.6 us (38%)
  Pallas kernels  7.22 us (13%)
  other arithmetic  1.07 us (2%)
    ppermute x22, starting transfers between devices, swap(): return lax.ppermute(value, axis, [(i, i ^ mask) for i in range(count)])  24.5 us
    ppermute x22, waiting for transfers between devices, swap(): return lax.ppermute(value, axis, [(i, i ^ mask) for i in range(count)])  20.6 us
    pallas_call x1, Pallas kernels, run_experts(): pl.pallas_call(functools.partial(expert_kernel, exp_dev, expert_total, le...  5.67 us
    pallas_call x1, Pallas kernels, pack(): pl.pallas_call(pack_kernel, out_shape=pltpu.VMEM((rows, width + extra), t...  1.54 us
  transfers between devices with their start and end apart: 22, of which 11 were waited for; matrix products, arithmetic and copies ran while one was open for 1% of the time, Pallas kernels for 0%

profile of v7, /device:TPU:0, one launch (start us, length us, event | category | flops | bytes accessed | tf_op | source)
XLA Modules:
  0.0 53.9 jit_solution(6061524362337743265)
XLA Ops:
  0.0 0.0 slice-start
  0.0 0.0 slice-start.2
  0.0 0.0 slice-start.4
  0.0 1.5 %shard_map.64.refs_0_ = bf16[8,4224]{1,0:T(8,128)(2,1)S(1)} custom-call(bf16[8,4096]{1,0:T(8,128)(2,1)} %tokens_hbm.1, s32[8,8]{1,0:T(8,128)} %ids_hbm.1, bf16[16,4096]{1,0:T(8,128)(2,1)} %router_hbm.1), custom_call_target="tpu_custom_call" | custom-call | flops 1048576 | bytes 262144 | tf_op jit(solution)/shard_map/pallas_call | solution.py:126
  1.6 0.0 slice-start.1
  1.6 0.0 slice-start.3
  1.6 0.0 slice-start.5
  1.6 3.1 %collective-permute-start = (bf16[8,4224]{1,0:T(8,128)(2,1)S(1)}, bf16[8,4224]{1,0:T(8,128)(2,1)S(1)}, u32[]{:S(2)}, u32[]{:S(2)}) collective-permute-start(bf16[8,4224]{1,0:T(8,128)(2,1)S(1)} %shard_map.64.refs_0_), channel_id=1, source_target_pairs={{0,1},{1,0},{2,3},{3,2},{4,5},{5,4},{6,7},{7,6},{8,9},{9,8},{10,11... | collective-permute-start | bytes 202760 | tf_op jit(solution)/shard_map/ppermute | solution.py:28
  4.7 2.5 %collective-permute-start.5 = (bf16[8,4224]{1,0:T(8,128)(2,1)S(1)}, bf16[8,4224]{1,0:T(8,128)(2,1)S(1)}, u32[]{:S(2)}, u32[]{:S(2)}) collective-permute-start(bf16[8,4224]{1,0:T(8,128)(2,1)S(1)} %shard_map.64.refs_0_), channel_id=1, source_target_pairs={{0,3},{1,2},{2,1},{3,0},{4,7},{5,6},{6,5},{7,4},{8,11},{9,10},{10,... | collective-permute-start | bytes 202760 | tf_op jit(solution)/shard_map/ppermute | solution.py:28
  7.2 0.1 collective-permute-start.4
  7.3 0.0 collective-permute-done.refs_1_
  7.3 2.6 %collective-permute-start.3 = (bf16[16,4224]{1,0:T(8,128)(2,1)S(1)}, bf16[16,4224]{1,0:T(8,128)(2,1)S(1)}, u32[]{:S(2)}, u32[]{:S(2)}) collective-permute-start(bf16[16,4224]{1,0:T(8,128)(2,1)S(1)} %shard_map.65), channel_id=1, source_target_pairs={{0,24},{4,28},{8,16},{12,20},{16,8},{20,12},{24,0},{28,4},{1,25},{... | collective-permute-start | bytes 405512 | tf_op jit(solution)/shard_map/ppermute | solution.py:28
  9.9 0.5 collective-permute-start.2
  10.4 0.4 collective-permute-start.1
  10.9 2.9 %collective-permute-done.4 = bf16[8,4224]{1,0:T(8,128)(2,1)S(1)} collective-permute-done((bf16[8,4224]{1,0:T(8,128)(2,1)S(1)}, bf16[8,4224]{1,0:T(8,128)(2,1)S(1)}, u32[]{:S(2)}, u32[]{:S(2)}) %collective-permute-start.4) | collective-permute-done | bytes 67616 | tf_op jit(solution)/shard_map/ppermute | solution.py:28
  13.8 0.0 collective-permute-done.5
  13.8 2.5 %collective-permute-start.8 = (bf16[16,4224]{1,0:T(8,128)(2,1)S(1)}, bf16[16,4224]{1,0:T(8,128)(2,1)S(1)}, u32[]{:S(2)}, u32[]{:S(2)}) collective-permute-start(bf16[16,4224]{1,0:T(8,128)(2,1)S(1)} %get-tuple-element.33), channel_id=1, source_target_pairs={{0,24},{4,28},{8,16},{12,20},{16,8},{20,12},{24,0},{28,4},{1,25},{... | collective-permute-start | bytes 405512 | tf_op jit(solution)/shard_map/ppermute | solution.py:28
  16.3 0.5 collective-permute-start.7
  16.8 0.0 collective-permute-done.3
  16.8 0.5 %collective-permute-start.6 = (bf16[16,4224]{1,0:T(8,128)(2,1)S(1)}, bf16[16,4224]{1,0:T(8,128)(2,1)S(1)}, u32[]{:S(2)}, u32[]{:S(2)}) collective-permute-start(bf16[16,4224]{1,0:T(8,128)(2,1)S(1)} %get-tuple-element.33), channel_id=1, source_target_pairs={{0,8},{4,12},{8,0},{12,4},{16,24},{20,28},{24,16},{28,20},{1,9},{5... | collective-permute-start | bytes 405512 | tf_op jit(solution)/shard_map/ppermute | solution.py:28
  17.4 0.0 collective-permute-done.2
  17.4 0.0 collective-permute-done.1
  17.4 0.1 collective-permute-start.9
  17.5 5.7 %collective-permute-done.6 = bf16[16,4224]{1,0:T(8,128)(2,1)S(1)} collective-permute-done((bf16[16,4224]{1,0:T(8,128)(2,1)S(1)}, bf16[16,4224]{1,0:T(8,128)(2,1)S(1)}, u32[]{:S(2)}, u32[]{:S(2)}) %collective-permute-start.6) | collective-permute-done | bytes 135200 | tf_op jit(solution)/shard_map/ppermute | solution.py:28
  23.2 0.0 collective-permute-done.7
  23.2 0.0 collective-permute-done.8
  23.3 0.1 collective-permute-start.10
  23.3 0.0 collective-permute-done.9.refs_2_
  23.4 1.9 %collective-permute-done.10.refs_3_ = bf16[64,4224]{1,0:T(8,128)(2,1)S(1)} collective-permute-done((bf16[64,4224]{1,0:T(8,128)(2,1)S(1)}, bf16[64,4224]{1,0:T(8,128)(2,1)S(1)}, u32[]{:S(2)}, u32[]{:S(2)}) %collective-permute-start.10) | collective-permute-done | bytes 540704 | tf_op jit(solution)/shard_map/ppermute | solution.py:28
  25.3 0.0 slice-done
  25.3 0.0 slice-done.2
  25.3 0.0 slice-done.4
  25.3 0.0 slice-done.1
  25.3 0.0 slice-done.3
  25.3 0.0 slice-done.5
  25.3 5.7 %shard_map.66 = (f32[64,4096]{1,0:T(8,128)S(1)}, f32[64,4096]{1,0:T(8,128)S(1)}, bf16[64,4096]{1,0:T(8,128)(2,1)S(1)}, bf16[64,4096]{1,0:T(8,128)(2,1)S(1)}) custom-call(bf16[64,4224]{1,0:T(8,128)(2,1)S(1)} %pad_maximum_fusion.refs_0_, bf16[64,4224]{1,0:T(8,128)(2,1)S(1)} %constant_dynamic-update-slice_fusion.2.refs_1_, ...), custom_call_target="tpu_custom_call" | custom-call | flops 4831838208 | bytes 5242880 | tf_op jit(solution)/shard_map/pallas_call | solution.py:202
  31.0 0.2 collective-permute-start.13
  31.2 0.4 collective-permute-start.11
  31.6 1.4 %collective-permute-done.13 = bf16[64,4096]{1,0:T(8,128)(2,1)S(1)} collective-permute-done((bf16[64,4096]{1,0:T(8,128)(2,1)S(1)}, bf16[64,4096]{1,0:T(8,128)(2,1)S(1)}, u32[]{:S(2)}, u32[]{:S(2)}) %collective-permute-start.13) | collective-permute-done | bytes 524320 | tf_op jit(solution)/shard_map/ppermute | solution.py:28
  33.0 0.1 fusion.8
  33.2 1.7 %collective-permute-start.14 = (bf16[16,4096]{1,0:T(8,128)(2,1)S(1)}, bf16[16,4096]{1,0:T(8,128)(2,1)S(1)}, u32[]{:S(2)}, u32[]{:S(2)}) collective-permute-start(bf16[16,4096]{1,0:T(8,128)(2,1)S(1)} %get-tuple-element.28), channel_id=1, source_target_pairs={{0,24},{4,28},{8,16},{12,20},{16,8},{20,12},{24,0},{28,4},{1,25},{... | collective-permute-start | bytes 393224 | tf_op jit(solution)/shard_map/ppermute | solution.py:28
  34.9 1.2 %collective-permute-start.18 = (bf16[16,4096]{1,0:T(8,128)(2,1)S(1)}, bf16[16,4096]{1,0:T(8,128)(2,1)S(1)}, u32[]{:S(2)}, u32[]{:S(2)}) collective-permute-start(bf16[16,4096]{1,0:T(8,128)(2,1)S(1)} %get-tuple-element.29), channel_id=1, source_target_pairs={{0,8},{4,12},{8,0},{12,4},{16,24},{20,28},{24,16},{28,20},{1,9},{5... | collective-permute-start | bytes 393224 | tf_op jit(solution)/shard_map/ppermute | solution.py:28
  36.1 0.6 %collective-permute-start.17 = (bf16[16,4096]{1,0:T(8,128)(2,1)S(1)}, bf16[16,4096]{1,0:T(8,128)(2,1)S(1)}, u32[]{:S(2)}, u32[]{:S(2)}) collective-permute-start(bf16[16,4096]{1,0:T(8,128)(2,1)S(1)} %get-tuple-element.30), channel_id=1, source_target_pairs={{0,16},{4,20},{8,24},{12,28},{16,0},{20,4},{24,8},{28,12},{1,17},{... | collective-permute-start | bytes 393224 | tf_op jit(solution)/shard_map/ppermute | solution.py:28
  36.7 0.0 collective-permute-done.11
  36.7 0.1 fusion.7
  36.9 1.7 %collective-permute-start.12 = (bf16[16,4096]{1,0:T(8,128)(2,1)S(1)}, bf16[16,4096]{1,0:T(8,128)(2,1)S(1)}, u32[]{:S(2)}, u32[]{:S(2)}) collective-permute-start(bf16[16,4096]{1,0:T(8,128)(2,1)S(1)} %get-tuple-element.25), channel_id=1, source_target_pairs={{0,24},{4,28},{8,16},{12,20},{16,8},{20,12},{24,0},{28,4},{1,25},{... | collective-permute-start | bytes 393224 | tf_op jit(solution)/shard_map/ppermute | solution.py:28
  38.6 1.9 %collective-permute-done.14 = bf16[16,4096]{1,0:T(8,128)(2,1)S(1)} collective-permute-done((bf16[16,4096]{1,0:T(8,128)(2,1)S(1)}, bf16[16,4096]{1,0:T(8,128)(2,1)S(1)}, u32[]{:S(2)}, u32[]{:S(2)}) %collective-permute-start.14) | collective-permute-done | bytes 131104 | tf_op jit(solution)/shard_map/ppermute | solution.py:28
  40.5 1.4 %collective-permute-start.15 = (bf16[16,4096]{1,0:T(8,128)(2,1)S(1)}, bf16[16,4096]{1,0:T(8,128)(2,1)S(1)}, u32[]{:S(2)}, u32[]{:S(2)}) collective-permute-start(bf16[16,4096]{1,0:T(8,128)(2,1)S(1)} %get-tuple-element.17), channel_id=1, source_target_pairs={{0,16},{4,20},{8,24},{12,28},{16,0},{20,4},{24,8},{28,12},{1,17},{... | collective-permute-start | bytes 393224 | tf_op jit(solution)/shard_map/ppermute | solution.py:28
  41.9 0.8 %collective-permute-start.16 = (bf16[16,4096]{1,0:T(8,128)(2,1)S(1)}, bf16[16,4096]{1,0:T(8,128)(2,1)S(1)}, u32[]{:S(2)}, u32[]{:S(2)}) collective-permute-start(bf16[16,4096]{1,0:T(8,128)(2,1)S(1)} %get-tuple-element.18), channel_id=1, source_target_pairs={{0,8},{4,12},{8,0},{12,4},{16,24},{20,28},{24,16},{28,20},{1,9},{5... | collective-permute-start | bytes 393224 | tf_op jit(solution)/shard_map/ppermute | solution.py:28
  42.7 0.6 %collective-permute-done.18 = bf16[16,4096]{1,0:T(8,128)(2,1)S(1)} collective-permute-done((bf16[16,4096]{1,0:T(8,128)(2,1)S(1)}, bf16[16,4096]{1,0:T(8,128)(2,1)S(1)}, u32[]{:S(2)}, u32[]{:S(2)}) %collective-permute-start.18) | collective-permute-done | bytes 131104 | tf_op jit(solution)/shard_map/ppermute | solution.py:28
  43.2 2.1 %collective-permute-done.17 = bf16[16,4096]{1,0:T(8,128)(2,1)S(1)} collective-permute-done((bf16[16,4096]{1,0:T(8,128)(2,1)S(1)}, bf16[16,4096]{1,0:T(8,128)(2,1)S(1)}, u32[]{:S(2)}, u32[]{:S(2)}) %collective-permute-start.17) | collective-permute-done | bytes 131104 | tf_op jit(solution)/shard_map/ppermute | solution.py:28
  45.3 0.1 fusion.2
  45.4 1.2 %collective-permute-start.19 = (bf16[8,4096]{1,0:T(8,128)(2,1)S(1)}, bf16[8,4096]{1,0:T(8,128)(2,1)S(1)}, u32[]{:S(2)}, u32[]{:S(2)}) collective-permute-start(bf16[8,4096]{1,0:T(8,128)(2,1)S(1)} %get-tuple-element.31), channel_id=1, source_target_pairs={{0,2},{1,3},{2,0},{3,1},{4,6},{5,7},{6,4},{7,5},{8,10},{9,11},{10,... | collective-permute-start | bytes 196616 | tf_op jit(solution)/shard_map/ppermute | solution.py:28
  46.6 1.4 %collective-permute-start.20 = (bf16[8,4096]{1,0:T(8,128)(2,1)S(1)}, bf16[8,4096]{1,0:T(8,128)(2,1)S(1)}, u32[]{:S(2)}, u32[]{:S(2)}) collective-permute-start(bf16[8,4096]{1,0:T(8,128)(2,1)S(1)} %get-tuple-element.32), channel_id=1, source_target_pairs={{0,3},{1,2},{2,1},{3,0},{4,7},{5,6},{6,5},{7,4},{8,11},{9,10},{10,... | collective-permute-start | bytes 196616 | tf_op jit(solution)/shard_map/ppermute | solution.py:28
  48.0 0.0 collective-permute-done.12
  48.0 0.1 collective-permute-done.15
  48.1 0.0 collective-permute-done.16
  48.1 0.1 fusion.4
  48.2 1.0 %collective-permute-start.21 = (bf16[8,4096]{1,0:T(8,128)(2,1)S(1)}, bf16[8,4096]{1,0:T(8,128)(2,1)S(1)}, u32[]{:S(2)}, u32[]{:S(2)}) collective-permute-start(bf16[8,4096]{1,0:T(8,128)(2,1)S(1)} %slice.87), channel_id=1, source_target_pairs={{0,1},{1,0},{2,3},{3,2},{4,5},{5,4},{6,7},{7,6},{8,9},{9,8},{10,11... | collective-permute-start | bytes 196616 | tf_op jit(solution)/shard_map/ppermute | solution.py:28
  49.1 1.8 %collective-permute-done.19 = bf16[8,4096]{1,0:T(8,128)(2,1)S(1)} collective-permute-done((bf16[8,4096]{1,0:T(8,128)(2,1)S(1)}, bf16[8,4096]{1,0:T(8,128)(2,1)S(1)}, u32[]{:S(2)}, u32[]{:S(2)}) %collective-permute-start.19) | collective-permute-done | bytes 65568 | tf_op jit(solution)/shard_map/ppermute | solution.py:28
  50.9 2.0 %collective-permute-done.20 = bf16[8,4096]{1,0:T(8,128)(2,1)S(1)} collective-permute-done((bf16[8,4096]{1,0:T(8,128)(2,1)S(1)}, bf16[8,4096]{1,0:T(8,128)(2,1)S(1)}, u32[]{:S(2)}, u32[]{:S(2)}) %collective-permute-start.20) | collective-permute-done | bytes 65568 | tf_op jit(solution)/shard_map/ppermute | solution.py:28
  53.0 0.2 collective-permute-done.21
  53.2 0.6 %fusion.6 = bf16[8,4096]{1,0:T(8,128)(2,1)} fusion(f32[8,4096]{1,0:T(8,128)S(1)} %convert_add_fusion.2, f32[16,4096]{1,0:T(8,128)S(1)} %fusion.4, bf16[8,4096]{1,0:T(8,128)(2,1)S(1)} %collective-permute-done.21), kind=kLoop, calls=%fused_computation.13 | loop fusion | flops 131072 | bytes 393216 | tf_op jit(solution)/shard_map/convert_element_type | solution.py:88
  (15 shorter events, 0.2 us)
Async XLA Ops:
  0.0 25.3 %slice-start = ((s8[6291456]{0:T(1024)(128)(4,1)}), s8[4194304]{0:T(1024)(128)(4,1)S(1)}, s32[]{:S(2)}) async-start(s8[6291456]{0:T(1024)(128)(4,1)} %bitcast), calls=%async_computation | async-start | bytes 8388608
  0.0 25.3 %slice-start.2 = ((s8[6291456]{0:T(1024)(128)(4,1)}), s8[4194304]{0:T(1024)(128)(4,1)S(1)}, s32[]{:S(2)}) async-start(s8[6291456]{0:T(1024)(128)(4,1)} %bitcast.2), calls=%async_computation.2 | async-start | bytes 8388608
  0.0 25.3 %slice-start.4 = ((s8[6291456]{0:T(1024)(128)(4,1)}), s8[4194304]{0:T(1024)(128)(4,1)S(1)}, s32[]{:S(2)}) async-start(s8[6291456]{0:T(1024)(128)(4,1)} %bitcast.4), calls=%async_computation.4 | async-start | bytes 8388608
  1.6 23.7 %slice-start.1 = ((s8[6291456]{0:T(1024)(128)(4,1)}), s8[2097152]{0:T(1024)(128)(4,1)S(1)}, s32[]{:S(2)}) async-start(s8[6291456]{0:T(1024)(128)(4,1)} %bitcast), calls=%async_computation.1 | async-start | bytes 4194304
  1.6 23.7 %slice-start.3 = ((s8[6291456]{0:T(1024)(128)(4,1)}), s8[2097152]{0:T(1024)(128)(4,1)S(1)}, s32[]{:S(2)}) async-start(s8[6291456]{0:T(1024)(128)(4,1)} %bitcast.2), calls=%async_computation.3 | async-start | bytes 4194304
  1.6 23.7 %slice-start.5 = ((s8[6291456]{0:T(1024)(128)(4,1)}), s8[2097152]{0:T(1024)(128)(4,1)S(1)}, s32[]{:S(2)}) async-start(s8[6291456]{0:T(1024)(128)(4,1)} %bitcast.4), calls=%async_computation.5 | async-start | bytes 4194304
  1.6 5.7 %collective-permute-start = (bf16[8,4224]{1,0:T(8,128)(2,1)S(1)}, bf16[8,4224]{1,0:T(8,128)(2,1)S(1)}, u32[]{:S(2)}, u32[]{:S(2)}) collective-permute-start(bf16[8,4224]{1,0:T(8,128)(2,1)S(1)} %shard_map.64.refs_0_), channel_id=1, source_target_pairs={{0,1},{1,0},{2,3},{3,2},{4,5},{5,4},{6,7},{7,6},{8,9},{9,8},{10,11... | collective-permute-start | bytes 202760 | tf_op jit(solution)/shard_map/ppermute | solution.py:28
  4.7 9.1 %collective-permute-start.5 = (bf16[8,4224]{1,0:T(8,128)(2,1)S(1)}, bf16[8,4224]{1,0:T(8,128)(2,1)S(1)}, u32[]{:S(2)}, u32[]{:S(2)}) collective-permute-start(bf16[8,4224]{1,0:T(8,128)(2,1)S(1)} %shard_map.64.refs_0_), channel_id=1, source_target_pairs={{0,3},{1,2},{2,1},{3,0},{4,7},{5,6},{6,5},{7,4},{8,11},{9,10},{10,... | collective-permute-start | bytes 202760 | tf_op jit(solution)/shard_map/ppermute | solution.py:28
  7.2 6.6 %collective-permute-start.4 = (bf16[8,4224]{1,0:T(8,128)(2,1)S(1)}, bf16[8,4224]{1,0:T(8,128)(2,1)S(1)}, u32[]{:S(2)}, u32[]{:S(2)}) collective-permute-start(bf16[8,4224]{1,0:T(8,128)(2,1)S(1)} %shard_map.64.refs_0_), channel_id=1, source_target_pairs={{0,2},{1,3},{2,0},{3,1},{4,6},{5,7},{6,4},{7,5},{8,10},{9,11},{10,... | collective-permute-start | bytes 202760 | tf_op jit(solution)/shard_map/ppermute | solution.py:28
  7.3 9.5 %collective-permute-start.3 = (bf16[16,4224]{1,0:T(8,128)(2,1)S(1)}, bf16[16,4224]{1,0:T(8,128)(2,1)S(1)}, u32[]{:S(2)}, u32[]{:S(2)}) collective-permute-start(bf16[16,4224]{1,0:T(8,128)(2,1)S(1)} %shard_map.65), channel_id=1, source_target_pairs={{0,24},{4,28},{8,16},{12,20},{16,8},{20,12},{24,0},{28,4},{1,25},{... | collective-permute-start | bytes 405512 | tf_op jit(solution)/shard_map/ppermute | solution.py:28
  9.9 7.4 %collective-permute-start.2 = (bf16[16,4224]{1,0:T(8,128)(2,1)S(1)}, bf16[16,4224]{1,0:T(8,128)(2,1)S(1)}, u32[]{:S(2)}, u32[]{:S(2)}) collective-permute-start(bf16[16,4224]{1,0:T(8,128)(2,1)S(1)} %shard_map.65), channel_id=1, source_target_pairs={{0,16},{4,20},{8,24},{12,28},{16,0},{20,4},{24,8},{28,12},{1,17},{... | collective-permute-start | bytes 405512 | tf_op jit(solution)/shard_map/ppermute | solution.py:28
  10.4 6.9 %collective-permute-start.1 = (bf16[16,4224]{1,0:T(8,128)(2,1)S(1)}, bf16[16,4224]{1,0:T(8,128)(2,1)S(1)}, u32[]{:S(2)}, u32[]{:S(2)}) collective-permute-start(bf16[16,4224]{1,0:T(8,128)(2,1)S(1)} %shard_map.65), channel_id=1, source_target_pairs={{0,8},{4,12},{8,0},{12,4},{16,24},{20,28},{24,16},{28,20},{1,9},{5... | collective-permute-start | bytes 405512 | tf_op jit(solution)/shard_map/ppermute | solution.py:28
  13.8 9.4 %collective-permute-start.8 = (bf16[16,4224]{1,0:T(8,128)(2,1)S(1)}, bf16[16,4224]{1,0:T(8,128)(2,1)S(1)}, u32[]{:S(2)}, u32[]{:S(2)}) collective-permute-start(bf16[16,4224]{1,0:T(8,128)(2,1)S(1)} %get-tuple-element.33), channel_id=1, source_target_pairs={{0,24},{4,28},{8,16},{12,20},{16,8},{20,12},{24,0},{28,4},{1,25},{... | collective-permute-start | bytes 405512 | tf_op jit(solution)/shard_map/ppermute | solution.py:28
  16.3 6.9 %collective-permute-start.7 = (bf16[16,4224]{1,0:T(8,128)(2,1)S(1)}, bf16[16,4224]{1,0:T(8,128)(2,1)S(1)}, u32[]{:S(2)}, u32[]{:S(2)}) collective-permute-start(bf16[16,4224]{1,0:T(8,128)(2,1)S(1)} %get-tuple-element.33), channel_id=1, source_target_pairs={{0,16},{4,20},{8,24},{12,28},{16,0},{20,4},{24,8},{28,12},{1,17},{... | collective-permute-start | bytes 405512 | tf_op jit(solution)/shard_map/ppermute | solution.py:28
  16.8 6.4 %collective-permute-start.6 = (bf16[16,4224]{1,0:T(8,128)(2,1)S(1)}, bf16[16,4224]{1,0:T(8,128)(2,1)S(1)}, u32[]{:S(2)}, u32[]{:S(2)}) collective-permute-start(bf16[16,4224]{1,0:T(8,128)(2,1)S(1)} %get-tuple-element.33), channel_id=1, source_target_pairs={{0,8},{4,12},{8,0},{12,4},{16,24},{20,28},{24,16},{28,20},{1,9},{5... | collective-permute-start | bytes 405512 | tf_op jit(solution)/shard_map/ppermute | solution.py:28
  17.4 5.9 %collective-permute-start.9 = (bf16[64,4224]{1,0:T(8,128)(2,1)S(1)}, bf16[64,4224]{1,0:T(8,128)(2,1)S(1)}, u32[]{:S(2)}, u32[]{:S(2)}) collective-permute-start(bf16[64,4224]{1,0:T(8,128)(2,1)S(1)} %pad_maximum_fusion.refs_0_), channel_id=1, source_target_pairs={{0,4},{4,0},{8,12},{12,8},{16,20},{20,16},{24,28},{28,24},{1,5},{5... | collective-permute-start | bytes 1622024 | tf_op jit(solution)/shard_map/ppermute | solution.py:28
  23.3 2.0 %collective-permute-start.10 = (bf16[64,4224]{1,0:T(8,128)(2,1)S(1)}, bf16[64,4224]{1,0:T(8,128)(2,1)S(1)}, u32[]{:S(2)}, u32[]{:S(2)}) collective-permute-start(bf16[64,4224]{1,0:T(8,128)(2,1)S(1)} %constant_dynamic-update-slice_fusion.2.refs_1_), channel_id=1, source_target_pairs={{0,4},{4,0},{8,12},{12,8},{16,20},{20,16},{24,28},{28,24},{1,5},{5... | collective-permute-start | bytes 1622024 | tf_op jit(solution)/shard_map/ppermute | solution.py:28
  31.0 2.0 %collective-permute-start.13 = (bf16[64,4096]{1,0:T(8,128)(2,1)S(1)}, bf16[64,4096]{1,0:T(8,128)(2,1)S(1)}, u32[]{:S(2)}, u32[]{:S(2)}) collective-permute-start(bf16[64,4096]{1,0:T(8,128)(2,1)S(1)} %get-tuple-element.16), channel_id=1, source_target_pairs={{0,4},{4,0},{8,12},{12,8},{16,20},{20,16},{24,28},{28,24},{1,5},{5... | collective-permute-start | bytes 1572872 | tf_op jit(solution)/shard_map/ppermute | solution.py:28
  31.2 5.5 %collective-permute-start.11 = (bf16[64,4096]{1,0:T(8,128)(2,1)S(1)}, bf16[64,4096]{1,0:T(8,128)(2,1)S(1)}, u32[]{:S(2)}, u32[]{:S(2)}) collective-permute-start(bf16[64,4096]{1,0:T(8,128)(2,1)S(1)} %get-tuple-element.14), channel_id=1, source_target_pairs={{0,4},{4,0},{8,12},{12,8},{16,20},{20,16},{24,28},{28,24},{1,5},{5... | collective-permute-start | bytes 1572872 | tf_op jit(solution)/shard_map/ppermute | solution.py:28
  33.2 7.3 %collective-permute-start.14 = (bf16[16,4096]{1,0:T(8,128)(2,1)S(1)}, bf16[16,4096]{1,0:T(8,128)(2,1)S(1)}, u32[]{:S(2)}, u32[]{:S(2)}) collective-permute-start(bf16[16,4096]{1,0:T(8,128)(2,1)S(1)} %get-tuple-element.28), channel_id=1, source_target_pairs={{0,24},{4,28},{8,16},{12,20},{16,8},{20,12},{24,0},{28,4},{1,25},{... | collective-permute-start | bytes 393224 | tf_op jit(solution)/shard_map/ppermute | solution.py:28
  34.9 8.4 %collective-permute-start.18 = (bf16[16,4096]{1,0:T(8,128)(2,1)S(1)}, bf16[16,4096]{1,0:T(8,128)(2,1)S(1)}, u32[]{:S(2)}, u32[]{:S(2)}) collective-permute-start(bf16[16,4096]{1,0:T(8,128)(2,1)S(1)} %get-tuple-element.29), channel_id=1, source_target_pairs={{0,8},{4,12},{8,0},{12,4},{16,24},{20,28},{24,16},{28,20},{1,9},{5... | collective-permute-start | bytes 393224 | tf_op jit(solution)/shard_map/ppermute | solution.py:28
  36.1 9.2 %collective-permute-start.17 = (bf16[16,4096]{1,0:T(8,128)(2,1)S(1)}, bf16[16,4096]{1,0:T(8,128)(2,1)S(1)}, u32[]{:S(2)}, u32[]{:S(2)}) collective-permute-start(bf16[16,4096]{1,0:T(8,128)(2,1)S(1)} %get-tuple-element.30), channel_id=1, source_target_pairs={{0,16},{4,20},{8,24},{12,28},{16,0},{20,4},{24,8},{28,12},{1,17},{... | collective-permute-start | bytes 393224 | tf_op jit(solution)/shard_map/ppermute | solution.py:28
  36.9 11.1 %collective-permute-start.12 = (bf16[16,4096]{1,0:T(8,128)(2,1)S(1)}, bf16[16,4096]{1,0:T(8,128)(2,1)S(1)}, u32[]{:S(2)}, u32[]{:S(2)}) collective-permute-start(bf16[16,4096]{1,0:T(8,128)(2,1)S(1)} %get-tuple-element.25), channel_id=1, source_target_pairs={{0,24},{4,28},{8,16},{12,20},{16,8},{20,12},{24,0},{28,4},{1,25},{... | collective-permute-start | bytes 393224 | tf_op jit(solution)/shard_map/ppermute | solution.py:28
  40.5 7.6 %collective-permute-start.15 = (bf16[16,4096]{1,0:T(8,128)(2,1)S(1)}, bf16[16,4096]{1,0:T(8,128)(2,1)S(1)}, u32[]{:S(2)}, u32[]{:S(2)}) collective-permute-start(bf16[16,4096]{1,0:T(8,128)(2,1)S(1)} %get-tuple-element.17), channel_id=1, source_target_pairs={{0,16},{4,20},{8,24},{12,28},{16,0},{20,4},{24,8},{28,12},{1,17},{... | collective-permute-start | bytes 393224 | tf_op jit(solution)/shard_map/ppermute | solution.py:28
  41.9 6.2 %collective-permute-start.16 = (bf16[16,4096]{1,0:T(8,128)(2,1)S(1)}, bf16[16,4096]{1,0:T(8,128)(2,1)S(1)}, u32[]{:S(2)}, u32[]{:S(2)}) collective-permute-start(bf16[16,4096]{1,0:T(8,128)(2,1)S(1)} %get-tuple-element.18), channel_id=1, source_target_pairs={{0,8},{4,12},{8,0},{12,4},{16,24},{20,28},{24,16},{28,20},{1,9},{5... | collective-permute-start | bytes 393224 | tf_op jit(solution)/shard_map/ppermute | solution.py:28
  45.4 5.5 %collective-permute-start.19 = (bf16[8,4096]{1,0:T(8,128)(2,1)S(1)}, bf16[8,4096]{1,0:T(8,128)(2,1)S(1)}, u32[]{:S(2)}, u32[]{:S(2)}) collective-permute-start(bf16[8,4096]{1,0:T(8,128)(2,1)S(1)} %get-tuple-element.31), channel_id=1, source_target_pairs={{0,2},{1,3},{2,0},{3,1},{4,6},{5,7},{6,4},{7,5},{8,10},{9,11},{10,... | collective-permute-start | bytes 196616 | tf_op jit(solution)/shard_map/ppermute | solution.py:28
  46.6 6.4 %collective-permute-start.20 = (bf16[8,4096]{1,0:T(8,128)(2,1)S(1)}, bf16[8,4096]{1,0:T(8,128)(2,1)S(1)}, u32[]{:S(2)}, u32[]{:S(2)}) collective-permute-start(bf16[8,4096]{1,0:T(8,128)(2,1)S(1)} %get-tuple-element.32), channel_id=1, source_target_pairs={{0,3},{1,2},{2,1},{3,0},{4,7},{5,6},{6,5},{7,4},{8,11},{9,10},{10,... | collective-permute-start | bytes 196616 | tf_op jit(solution)/shard_map/ppermute | solution.py:28
  48.2 5.0 %collective-permute-start.21 = (bf16[8,4096]{1,0:T(8,128)(2,1)S(1)}, bf16[8,4096]{1,0:T(8,128)(2,1)S(1)}, u32[]{:S(2)}, u32[]{:S(2)}) collective-permute-start(bf16[8,4096]{1,0:T(8,128)(2,1)S(1)} %slice.87), channel_id=1, source_target_pairs={{0,1},{1,0},{2,3},{3,2},{4,5},{5,4},{6,7},{7,6},{8,9},{9,8},{10,11... | collective-permute-start | bytes 196616 | tf_op jit(solution)/shard_map/ppermute | solution.py:28

commit v8 on v7

--- a/solution.py
+++ b/solution.py
@@ -70,16 +70,23 @@
     return [near, far, near_there, swap(far, *CORE)]
 
 
-def scatter_sums(kept, away):
+def kept_and_away(unit, count):
+    sizes = [unit * (count + 1), unit * count, unit]
+    return [(size, kind) for kind in (jnp.float32, jnp.bfloat16) for size in sizes]
+
+
+def scatter_sums(*results):
     steps, depth = plane_steps(), lax.axis_size("expert")
-    sums, here = [], []
-    for mine, other in reversed(list(zip(kept, away))):
-        part, *rest = split(mine + wide(swap(other, *CORE)), len(steps) + 1)
-        rest = [other.astype(jnp.bfloat16) for other in rest[::-1]]
-        if here:
-            rest = rest[:1] + [after(other, here[0]) for other in rest[1:]]
-        here = [send(other, step) for other, step in zip(rest, steps[::-1])]
-        sums.append(sum([wide(other) for other in here], part))
+    joined = [mine + wide(swap(other, *CORE)) for mine, other in zip(results[2::-1], results[:2:-1])]
+    diagonal, (far, *rest), (near, *others) = [
+        split(total, count) for total, count in zip(joined, (1, len(steps), len(steps) + 1))
+    ]
+    here = [send(other, step) for other, step in zip(diagonal + rest[::-1], steps[::-1])]
+    others = [other.astype(jnp.bfloat16) for other in others[::-1]]
+    here[0] = after(here[0], *others)
+    others = [after(other, here[0]) for other in others]
+    near_here = [send(other, step) for other, step in zip(others, steps[::-1])]
+    sums = [sum([wide(other) for other in here], far), sum([wide(other) for other in near_here], near)]
     far, (total, *near) = split(sums[0], depth // 2), split(sums[1], depth // 2)
     far = [send(part, ("expert", mask + depth // 2)) for mask, part in enumerate(far)]
     near = [send(part, ("expert", mask + 1)) for mask, part in enumerate(near)]
@@ -195,17 +202,15 @@
             start = stop
 
 
-def run_experts(pieces, kinds, expert_total, w_gate, w_up, w_down):
+def run_experts(pieces, results, expert_total, w_gate, w_up, w_down):
     rows = sum(piece.shape[0] for piece in pieces)
     exp_dev, _, width = w_down.shape
-    place = pltpu.VMEM if len(pieces) > 1 else jax.ShapeDtypeStruct
+    place = pltpu.VMEM if len(results) > 1 else jax.ShapeDtypeStruct
     return pl.pallas_call(
         functools.partial(expert_kernel, exp_dev, expert_total, len(pieces)),
-        out_shape=[
-            place((piece.shape[0], width), kind) for piece, kind in zip(pieces, kinds)
-        ],
+        out_shape=[place((size, width), kind) for size, kind in results],
         in_specs=[IN_VMEM] * (len(pieces) + 3),
-        out_specs=[IN_VMEM] * len(pieces),
+        out_specs=[IN_VMEM] * len(results),
         compiler_params=pltpu.CompilerParams(vmem_limit_bytes=VMEM_BYTES),
         cost_estimate=pl.CostEstimate(
             flops=6 * rows * w_down.size, bytes_accessed=rows * width * 5, transcendentals=0
@@ -215,19 +220,22 @@
 
 def body(tokens, expert_ids, router, w_gate, w_up, w_down):
     pieces = gather_rows(pack(tokens, expert_ids, router))
-    kinds = [jnp.float32] * 2 + [jnp.bfloat16] * 2
+    count = len(plane_steps())
+    results = kept_and_away(pieces[0].shape[0] // (count + 1), count)
     operands = (router.shape[0], w_gate, w_up, w_down)
-    if sum(piece.shape[0] for piece in pieces) <= ROWS:
-        results = run_experts(pieces, kinds, *operands)
-    else:
-        results = []
-        for piece, kind in zip(pieces, kinds):
-            chunks = [
-                run_experts([piece[start : start + ROWS]], [kind], *operands)[0]
-                for start in range(0, piece.shape[0], ROWS)
-            ]
-            results.append(cat(chunks))
-    return scatter_sums(results[:2], results[2:])
+    rows = sum(piece.shape[0] for piece in pieces)
+    if rows <= ROWS:
+        return scatter_sums(*run_experts(pieces, results, *operands))
+    pieces = cat(pieces)
+    outputs = cat([
+        run_experts([pieces[first : first + ROWS]], [(ROWS, jnp.float32)], *operands)[0]
+        for first in range(0, rows, ROWS)
+    ])
+    parts, start = [], 0
+    for size, kind in results:
+        parts.append(outputs[start : start + size].astype(kind))
+        start += size
+    return scatter_sums(*parts)
 
 
 def solution(mesh):

time: 54 us -> 52.9 us (0.980)
  starting transfers between devices: 24.5 us -> 23.5 us
    ppermute x22 -> x23, starting transfers between devices: 24.5 us -> 23.5 us  [swap(): return lax.ppermute(value, axis, [(i, i ^ mask) for i in range(count)])]
    ppermute x22 -> x23, waiting for transfers between devices: 20.6 us -> 20.6 us  [swap(): return lax.ppermute(value, axis, [(i, i ^ mask) for i in range(count)])]
  transfers between devices with their start and end apart: 22 -> 23, of which waited for: 11 -> 11; matrix products, arithmetic and copies ran while one was open for 1% -> 1% of each run, Pallas kernels for 0% -> 0%
where the time goes in v8:
time: 52.9 us; the launch traced here: 52.8 us
  starting transfers between devices  23.5 us (44%)
  waiting for transfers between devices  20.6 us (39%)
  Pallas kernels  7.23 us (14%)
  other arithmetic  1.05 us (2%)
    ppermute x23, starting transfers between devices, swap(): return lax.ppermute(value, axis, [(i, i ^ mask) for i in range(count)])  23.5 us
    ppermute x23, waiting for transfers between devices, swap(): return lax.ppermute(value, axis, [(i, i ^ mask) for i in range(count)])  20.6 us
    pallas_call x1, Pallas kernels, run_experts(): pl.pallas_call(functools.partial(expert_kernel, exp_dev, expert_total, le...  5.67 us
    pallas_call x1, Pallas kernels, pack(): pl.pallas_call(pack_kernel, out_shape=pltpu.VMEM((rows, width + extra), t...  1.54 us
  transfers between devices with their start and end apart: 23, of which 11 were waited for; matrix products, arithmetic and copies ran while one was open for 1% of the time, Pallas kernels for 0%

profile of v8, /device:TPU:0, one launch (start us, length us, event | category | flops | bytes accessed | tf_op | source)
XLA Modules:
  0.0 52.8 jit_solution(6158383301603525702)
XLA Ops:
  0.0 0.0 slice-start
  0.0 0.0 slice-start.2
  0.0 1.5 %shard_map.64.refs_0_ = bf16[8,4224]{1,0:T(8,128)(2,1)S(1)} custom-call(bf16[8,4096]{1,0:T(8,128)(2,1)} %tokens_hbm.1, s32[8,8]{1,0:T(8,128)} %ids_hbm.1, bf16[16,4096]{1,0:T(8,128)(2,1)} %router_hbm.1), custom_call_target="tpu_custom_call" | custom-call | flops 1048576 | bytes 262144 | tf_op jit(solution)/shard_map/pallas_call | solution.py:133
  1.6 0.0 slice-start.1
  1.6 0.0 slice-start.3
  1.6 0.0 slice-start.5
  1.6 3.1 %collective-permute-start = (bf16[8,4224]{1,0:T(8,128)(2,1)S(1)}, bf16[8,4224]{1,0:T(8,128)(2,1)S(1)}, u32[]{:S(2)}, u32[]{:S(2)}) collective-permute-start(bf16[8,4224]{1,0:T(8,128)(2,1)S(1)} %shard_map.64.refs_0_), channel_id=1, source_target_pairs={{0,1},{1,0},{2,3},{3,2},{4,5},{5,4},{6,7},{7,6},{8,9},{9,8},{10,11... | collective-permute-start | bytes 202760 | tf_op jit(solution)/shard_map/ppermute | solution.py:28
  4.7 2.5 %collective-permute-start.5 = (bf16[8,4224]{1,0:T(8,128)(2,1)S(1)}, bf16[8,4224]{1,0:T(8,128)(2,1)S(1)}, u32[]{:S(2)}, u32[]{:S(2)}) collective-permute-start(bf16[8,4224]{1,0:T(8,128)(2,1)S(1)} %shard_map.64.refs_0_), channel_id=1, source_target_pairs={{0,3},{1,2},{2,1},{3,0},{4,7},{5,6},{6,5},{7,4},{8,11},{9,10},{10,... | collective-permute-start | bytes 202760 | tf_op jit(solution)/shard_map/ppermute | solution.py:28
  7.2 0.1 collective-permute-start.4
  7.3 0.0 collective-permute-done.refs_1_
  7.3 2.6 %collective-permute-start.3 = (bf16[16,4224]{1,0:T(8,128)(2,1)S(1)}, bf16[16,4224]{1,0:T(8,128)(2,1)S(1)}, u32[]{:S(2)}, u32[]{:S(2)}) collective-permute-start(bf16[16,4224]{1,0:T(8,128)(2,1)S(1)} %shard_map.65), channel_id=1, source_target_pairs={{0,24},{4,28},{8,16},{12,20},{16,8},{20,12},{24,0},{28,4},{1,25},{... | collective-permute-start | bytes 405512 | tf_op jit(solution)/shard_map/ppermute | solution.py:28
  9.9 0.5 collective-permute-start.2
  10.4 0.4 collective-permute-start.1
  10.9 2.9 %collective-permute-done.4 = bf16[8,4224]{1,0:T(8,128)(2,1)S(1)} collective-permute-done((bf16[8,4224]{1,0:T(8,128)(2,1)S(1)}, bf16[8,4224]{1,0:T(8,128)(2,1)S(1)}, u32[]{:S(2)}, u32[]{:S(2)}) %collective-permute-start.4) | collective-permute-done | bytes 67616 | tf_op jit(solution)/shard_map/ppermute | solution.py:28
  13.8 0.0 collective-permute-done.5
  13.8 2.5 %collective-permute-start.8 = (bf16[16,4224]{1,0:T(8,128)(2,1)S(1)}, bf16[16,4224]{1,0:T(8,128)(2,1)S(1)}, u32[]{:S(2)}, u32[]{:S(2)}) collective-permute-start(bf16[16,4224]{1,0:T(8,128)(2,1)S(1)} %get-tuple-element.40), channel_id=1, source_target_pairs={{0,24},{4,28},{8,16},{12,20},{16,8},{20,12},{24,0},{28,4},{1,25},{... | collective-permute-start | bytes 405512 | tf_op jit(solution)/shard_map/ppermute | solution.py:28
  16.3 0.5 collective-permute-start.7
  16.8 0.0 collective-permute-done.3
  16.8 0.5 %collective-permute-start.6 = (bf16[16,4224]{1,0:T(8,128)(2,1)S(1)}, bf16[16,4224]{1,0:T(8,128)(2,1)S(1)}, u32[]{:S(2)}, u32[]{:S(2)}) collective-permute-start(bf16[16,4224]{1,0:T(8,128)(2,1)S(1)} %get-tuple-element.40), channel_id=1, source_target_pairs={{0,8},{4,12},{8,0},{12,4},{16,24},{20,28},{24,16},{28,20},{1,9},{5... | collective-permute-start | bytes 405512 | tf_op jit(solution)/shard_map/ppermute | solution.py:28
  17.4 0.0 collective-permute-done.2
  17.4 0.0 collective-permute-done.1
  17.4 0.1 collective-permute-start.9
  17.5 5.7 %collective-permute-done.6 = bf16[16,4224]{1,0:T(8,128)(2,1)S(1)} collective-permute-done((bf16[16,4224]{1,0:T(8,128)(2,1)S(1)}, bf16[16,4224]{1,0:T(8,128)(2,1)S(1)}, u32[]{:S(2)}, u32[]{:S(2)}) %collective-permute-start.6) | collective-permute-done | bytes 135200 | tf_op jit(solution)/shard_map/ppermute | solution.py:28
  23.2 0.0 collective-permute-done.7
  23.2 0.0 collective-permute-done.8
  23.3 0.1 collective-permute-start.10
  23.3 0.0 collective-permute-done.9.refs_2_
  23.4 1.9 %collective-permute-done.10.refs_3_ = bf16[64,4224]{1,0:T(8,128)(2,1)S(1)} collective-permute-done((bf16[64,4224]{1,0:T(8,128)(2,1)S(1)}, bf16[64,4224]{1,0:T(8,128)(2,1)S(1)}, u32[]{:S(2)}, u32[]{:S(2)}) %collective-permute-start.10) | collective-permute-done | bytes 540704 | tf_op jit(solution)/shard_map/ppermute | solution.py:28
  25.3 0.0 slice-done
  25.3 0.0 slice-done.2
  25.3 0.0 slice-done.4
  25.3 0.0 slice-done.1
  25.3 0.0 slice-done.3
  25.3 0.0 slice-done.5
  25.3 5.7 %shard_map.66 = (f32[64,4096]{1,0:T(8,128)S(1)}, f32[48,4096]{1,0:T(8,128)S(1)}, f32[16,4096]{1,0:T(8,128)S(1)}, bf16[64,4096]{1,0:T(8,128)(2,1)S(1)}, bf16[48,4...) custom-call(bf16[64,4224]{1,0:T(8,128)(2,1)S(1)} %pad_maximum_fusion.refs_0_, ...), custom_call_target="tpu_custom_call" | custom-call | flops 4831838208 | bytes 5242880 | tf_op jit(solution)/shard_map/pallas_call | solution.py:209
  31.0 0.2 collective-permute-start.12
  31.2 0.4 collective-permute-start.17
  31.6 0.1 collective-permute-start.11
  31.7 0.7 %collective-permute-done.12 = bf16[16,4096]{1,0:T(8,128)(2,1)S(1)} collective-permute-done((bf16[16,4096]{1,0:T(8,128)(2,1)S(1)}, bf16[16,4096]{1,0:T(8,128)(2,1)S(1)}, u32[]{:S(2)}, u32[]{:S(2)}) %collective-permute-start.12) | collective-permute-done | bytes 131104 | tf_op jit(solution)/shard_map/ppermute | solution.py:28
  32.5 1.7 %collective-permute-start.13 = (bf16[16,4096]{1,0:T(8,128)(2,1)S(1)}, bf16[16,4096]{1,0:T(8,128)(2,1)S(1)}, u32[]{:S(2)}, u32[]{:S(2)}) collective-permute-start(bf16[16,4096]{1,0:T(8,128)(2,1)S(1)} %add_convert_fusion), channel_id=1, source_target_pairs={{0,24},{4,28},{8,16},{12,20},{16,8},{20,12},{24,0},{28,4},{1,25},{... | collective-permute-start | bytes 393224 | tf_op jit(solution)/shard_map/ppermute | solution.py:28
  34.2 0.0 collective-permute-done.17
  34.2 0.1 fusion.8
  34.3 1.4 %collective-permute-start.18 = (bf16[16,4096]{1,0:T(8,128)(2,1)S(1)}, bf16[16,4096]{1,0:T(8,128)(2,1)S(1)}, u32[]{:S(2)}, u32[]{:S(2)}) collective-permute-start(bf16[16,4096]{1,0:T(8,128)(2,1)S(1)} %get-tuple-element.36), channel_id=1, source_target_pairs={{0,16},{4,20},{8,24},{12,28},{16,0},{20,4},{24,8},{28,12},{1,17},{... | collective-permute-start | bytes 393224 | tf_op jit(solution)/shard_map/ppermute | solution.py:28
  35.7 0.5 collective-permute-start.19
  36.2 0.0 collective-permute-done.11
  36.2 0.1 fusion.7
  36.4 3.4 %collective-permute-done.13 = bf16[16,4096]{1,0:T(8,128)(2,1)S(1)} collective-permute-done((bf16[16,4096]{1,0:T(8,128)(2,1)S(1)}, bf16[16,4096]{1,0:T(8,128)(2,1)S(1)}, u32[]{:S(2)}, u32[]{:S(2)}) %collective-permute-start.13) | collective-permute-done | bytes 131104 | tf_op jit(solution)/shard_map/ppermute | solution.py:28
  39.8 1.7 %collective-permute-start.14 = (bf16[16,4096]{1,0:T(8,128)(2,1)S(1)}, bf16[16,4096]{1,0:T(8,128)(2,1)S(1)}, u32[]{:S(2)}, u32[]{:S(2)}) collective-permute-start(bf16[16,4096]{1,0:T(8,128)(2,1)S(1)} %get-tuple-element.22), channel_id=1, source_target_pairs={{0,24},{4,28},{8,16},{12,20},{16,8},{20,12},{24,0},{28,4},{1,25},{... | collective-permute-start | bytes 393224 | tf_op jit(solution)/shard_map/ppermute | solution.py:28
  41.4 1.3 %collective-permute-start.15 = (bf16[16,4096]{1,0:T(8,128)(2,1)S(1)}, bf16[16,4096]{1,0:T(8,128)(2,1)S(1)}, u32[]{:S(2)}, u32[]{:S(2)}) collective-permute-start(bf16[16,4096]{1,0:T(8,128)(2,1)S(1)} %get-tuple-element.23), channel_id=1, source_target_pairs={{0,16},{4,20},{8,24},{12,28},{16,0},{20,4},{24,8},{28,12},{1,17},{... | collective-permute-start | bytes 393224 | tf_op jit(solution)/shard_map/ppermute | solution.py:28
  42.8 0.5 collective-permute-start.16
  43.3 0.0 collective-permute-done.18
  43.3 0.0 collective-permute-done.19
  43.3 0.1 fusion.2
  43.3 1.5 %collective-permute-start.20 = (bf16[8,4096]{1,0:T(8,128)(2,1)S(1)}, bf16[8,4096]{1,0:T(8,128)(2,1)S(1)}, u32[]{:S(2)}, u32[]{:S(2)}) collective-permute-start(bf16[8,4096]{1,0:T(8,128)(2,1)S(1)} %get-tuple-element.38), channel_id=1, source_target_pairs={{0,2},{1,3},{2,0},{3,1},{4,6},{5,7},{6,4},{7,5},{8,10},{9,11},{10,... | collective-permute-start | bytes 196616 | tf_op jit(solution)/shard_map/ppermute | solution.py:28
  44.9 1.0 %collective-permute-start.21 = (bf16[8,4096]{1,0:T(8,128)(2,1)S(1)}, bf16[8,4096]{1,0:T(8,128)(2,1)S(1)}, u32[]{:S(2)}, u32[]{:S(2)}) collective-permute-start(bf16[8,4096]{1,0:T(8,128)(2,1)S(1)} %get-tuple-element.39), channel_id=1, source_target_pairs={{0,3},{1,2},{2,1},{3,0},{4,7},{5,6},{6,5},{7,4},{8,11},{9,10},{10,... | collective-permute-start | bytes 196616 | tf_op jit(solution)/shard_map/ppermute | solution.py:28
  45.9 0.5 collective-permute-done.14
  46.3 1.1 %collective-permute-done.15 = bf16[16,4096]{1,0:T(8,128)(2,1)S(1)} collective-permute-done((bf16[16,4096]{1,0:T(8,128)(2,1)S(1)}, bf16[16,4096]{1,0:T(8,128)(2,1)S(1)}, u32[]{:S(2)}, u32[]{:S(2)}) %collective-permute-start.15) | collective-permute-done | bytes 131104 | tf_op jit(solution)/shard_map/ppermute | solution.py:28
  47.4 0.3 collective-permute-done.16
  47.7 0.1 fusion.4
  47.8 0.2 collective-permute-start.22
  48.0 1.6 %collective-permute-done.20 = bf16[8,4096]{1,0:T(8,128)(2,1)S(1)} collective-permute-done((bf16[8,4096]{1,0:T(8,128)(2,1)S(1)}, bf16[8,4096]{1,0:T(8,128)(2,1)S(1)}, u32[]{:S(2)}, u32[]{:S(2)}) %collective-permute-start.20) | collective-permute-done | bytes 65568 | tf_op jit(solution)/shard_map/ppermute | solution.py:28
  49.6 1.4 %collective-permute-done.21 = bf16[8,4096]{1,0:T(8,128)(2,1)S(1)} collective-permute-done((bf16[8,4096]{1,0:T(8,128)(2,1)S(1)}, bf16[8,4096]{1,0:T(8,128)(2,1)S(1)}, u32[]{:S(2)}, u32[]{:S(2)}) %collective-permute-start.21) | collective-permute-done | bytes 65568 | tf_op jit(solution)/shard_map/ppermute | solution.py:28
  50.9 1.2 %collective-permute-done.22 = bf16[8,4096]{1,0:T(8,128)(2,1)S(1)} collective-permute-done((bf16[8,4096]{1,0:T(8,128)(2,1)S(1)}, bf16[8,4096]{1,0:T(8,128)(2,1)S(1)}, u32[]{:S(2)}, u32[]{:S(2)}) %collective-permute-start.22) | collective-permute-done | bytes 65568 | tf_op jit(solution)/shard_map/ppermute | solution.py:28
  52.1 0.6 %fusion.6 = bf16[8,4096]{1,0:T(8,128)(2,1)} fusion(f32[8,4096]{1,0:T(8,128)S(1)} %convert_add_fusion.2, f32[16,4096]{1,0:T(8,128)S(1)} %fusion.4, bf16[8,4096]{1,0:T(8,128)(2,1)S(1)} %collective-permute-done.22), kind=kLoop, calls=%fused_computation.14 | loop fusion | flops 131072 | bytes 393216 | tf_op jit(solution)/shard_map/convert_element_type | solution.py:95
  (17 shorter events, 0.2 us)
Async XLA Ops:
  0.0 25.3 %slice-start = ((s8[6291456]{0:T(1024)(128)(4,1)}), s8[4194304]{0:T(1024)(128)(4,1)S(1)}, s32[]{:S(2)}) async-start(s8[6291456]{0:T(1024)(128)(4,1)} %bitcast), calls=%async_computation | async-start | bytes 8388608
  0.0 25.3 %slice-start.2 = ((s8[6291456]{0:T(1024)(128)(4,1)}), s8[4194304]{0:T(1024)(128)(4,1)S(1)}, s32[]{:S(2)}) async-start(s8[6291456]{0:T(1024)(128)(4,1)} %bitcast.2), calls=%async_computation.2 | async-start | bytes 8388608
  0.0 25.3 %slice-start.4 = ((s8[6291456]{0:T(1024)(128)(4,1)}), s8[4194304]{0:T(1024)(128)(4,1)S(1)}, s32[]{:S(2)}) async-start(s8[6291456]{0:T(1024)(128)(4,1)} %bitcast.4), calls=%async_computation.4 | async-start | bytes 8388608
  1.6 23.7 %slice-start.1 = ((s8[6291456]{0:T(1024)(128)(4,1)}), s8[2097152]{0:T(1024)(128)(4,1)S(1)}, s32[]{:S(2)}) async-start(s8[6291456]{0:T(1024)(128)(4,1)} %bitcast), calls=%async_computation.1 | async-start | bytes 4194304
  1.6 23.7 %slice-start.3 = ((s8[6291456]{0:T(1024)(128)(4,1)}), s8[2097152]{0:T(1024)(128)(4,1)S(1)}, s32[]{:S(2)}) async-start(s8[6291456]{0:T(1024)(128)(4,1)} %bitcast.2), calls=%async_computation.3 | async-start | bytes 4194304
  1.6 23.7 %slice-start.5 = ((s8[6291456]{0:T(1024)(128)(4,1)}), s8[2097152]{0:T(1024)(128)(4,1)S(1)}, s32[]{:S(2)}) async-start(s8[6291456]{0:T(1024)(128)(4,1)} %bitcast.4), calls=%async_computation.5 | async-start | bytes 4194304
  1.6 5.7 %collective-permute-start = (bf16[8,4224]{1,0:T(8,128)(2,1)S(1)}, bf16[8,4224]{1,0:T(8,128)(2,1)S(1)}, u32[]{:S(2)}, u32[]{:S(2)}) collective-permute-start(bf16[8,4224]{1,0:T(8,128)(2,1)S(1)} %shard_map.64.refs_0_), channel_id=1, source_target_pairs={{0,1},{1,0},{2,3},{3,2},{4,5},{5,4},{6,7},{7,6},{8,9},{9,8},{10,11... | collective-permute-start | bytes 202760 | tf_op jit(solution)/shard_map/ppermute | solution.py:28
  4.7 9.1 %collective-permute-start.5 = (bf16[8,4224]{1,0:T(8,128)(2,1)S(1)}, bf16[8,4224]{1,0:T(8,128)(2,1)S(1)}, u32[]{:S(2)}, u32[]{:S(2)}) collective-permute-start(bf16[8,4224]{1,0:T(8,128)(2,1)S(1)} %shard_map.64.refs_0_), channel_id=1, source_target_pairs={{0,3},{1,2},{2,1},{3,0},{4,7},{5,6},{6,5},{7,4},{8,11},{9,10},{10,... | collective-permute-start | bytes 202760 | tf_op jit(solution)/shard_map/ppermute | solution.py:28
  7.2 6.6 %collective-permute-start.4 = (bf16[8,4224]{1,0:T(8,128)(2,1)S(1)}, bf16[8,4224]{1,0:T(8,128)(2,1)S(1)}, u32[]{:S(2)}, u32[]{:S(2)}) collective-permute-start(bf16[8,4224]{1,0:T(8,128)(2,1)S(1)} %shard_map.64.refs_0_), channel_id=1, source_target_pairs={{0,2},{1,3},{2,0},{3,1},{4,6},{5,7},{6,4},{7,5},{8,10},{9,11},{10,... | collective-permute-start | bytes 202760 | tf_op jit(solution)/shard_map/ppermute | solution.py:28
  7.3 9.5 %collective-permute-start.3 = (bf16[16,4224]{1,0:T(8,128)(2,1)S(1)}, bf16[16,4224]{1,0:T(8,128)(2,1)S(1)}, u32[]{:S(2)}, u32[]{:S(2)}) collective-permute-start(bf16[16,4224]{1,0:T(8,128)(2,1)S(1)} %shard_map.65), channel_id=1, source_target_pairs={{0,24},{4,28},{8,16},{12,20},{16,8},{20,12},{24,0},{28,4},{1,25},{... | collective-permute-start | bytes 405512 | tf_op jit(solution)/shard_map/ppermute | solution.py:28
  9.9 7.4 %collective-permute-start.2 = (bf16[16,4224]{1,0:T(8,128)(2,1)S(1)}, bf16[16,4224]{1,0:T(8,128)(2,1)S(1)}, u32[]{:S(2)}, u32[]{:S(2)}) collective-permute-start(bf16[16,4224]{1,0:T(8,128)(2,1)S(1)} %shard_map.65), channel_id=1, source_target_pairs={{0,16},{4,20},{8,24},{12,28},{16,0},{20,4},{24,8},{28,12},{1,17},{... | collective-permute-start | bytes 405512 | tf_op jit(solution)/shard_map/ppermute | solution.py:28
  10.4 6.9 %collective-permute-start.1 = (bf16[16,4224]{1,0:T(8,128)(2,1)S(1)}, bf16[16,4224]{1,0:T(8,128)(2,1)S(1)}, u32[]{:S(2)}, u32[]{:S(2)}) collective-permute-start(bf16[16,4224]{1,0:T(8,128)(2,1)S(1)} %shard_map.65), channel_id=1, source_target_pairs={{0,8},{4,12},{8,0},{12,4},{16,24},{20,28},{24,16},{28,20},{1,9},{5... | collective-permute-start | bytes 405512 | tf_op jit(solution)/shard_map/ppermute | solution.py:28
  13.8 9.4 %collective-permute-start.8 = (bf16[16,4224]{1,0:T(8,128)(2,1)S(1)}, bf16[16,4224]{1,0:T(8,128)(2,1)S(1)}, u32[]{:S(2)}, u32[]{:S(2)}) collective-permute-start(bf16[16,4224]{1,0:T(8,128)(2,1)S(1)} %get-tuple-element.40), channel_id=1, source_target_pairs={{0,24},{4,28},{8,16},{12,20},{16,8},{20,12},{24,0},{28,4},{1,25},{... | collective-permute-start | bytes 405512 | tf_op jit(solution)/shard_map/ppermute | solution.py:28
  16.3 6.9 %collective-permute-start.7 = (bf16[16,4224]{1,0:T(8,128)(2,1)S(1)}, bf16[16,4224]{1,0:T(8,128)(2,1)S(1)}, u32[]{:S(2)}, u32[]{:S(2)}) collective-permute-start(bf16[16,4224]{1,0:T(8,128)(2,1)S(1)} %get-tuple-element.40), channel_id=1, source_target_pairs={{0,16},{4,20},{8,24},{12,28},{16,0},{20,4},{24,8},{28,12},{1,17},{... | collective-permute-start | bytes 405512 | tf_op jit(solution)/shard_map/ppermute | solution.py:28
  16.8 6.4 %collective-permute-start.6 = (bf16[16,4224]{1,0:T(8,128)(2,1)S(1)}, bf16[16,4224]{1,0:T(8,128)(2,1)S(1)}, u32[]{:S(2)}, u32[]{:S(2)}) collective-permute-start(bf16[16,4224]{1,0:T(8,128)(2,1)S(1)} %get-tuple-element.40), channel_id=1, source_target_pairs={{0,8},{4,12},{8,0},{12,4},{16,24},{20,28},{24,16},{28,20},{1,9},{5... | collective-permute-start | bytes 405512 | tf_op jit(solution)/shard_map/ppermute | solution.py:28
  17.4 5.9 %collective-permute-start.9 = (bf16[64,4224]{1,0:T(8,128)(2,1)S(1)}, bf16[64,4224]{1,0:T(8,128)(2,1)S(1)}, u32[]{:S(2)}, u32[]{:S(2)}) collective-permute-start(bf16[64,4224]{1,0:T(8,128)(2,1)S(1)} %pad_maximum_fusion.refs_0_), channel_id=1, source_target_pairs={{0,4},{4,0},{8,12},{12,8},{16,20},{20,16},{24,28},{28,24},{1,5},{5... | collective-permute-start | bytes 1622024 | tf_op jit(solution)/shard_map/ppermute | solution.py:28
  23.3 2.0 %collective-permute-start.10 = (bf16[64,4224]{1,0:T(8,128)(2,1)S(1)}, bf16[64,4224]{1,0:T(8,128)(2,1)S(1)}, u32[]{:S(2)}, u32[]{:S(2)}) collective-permute-start(bf16[64,4224]{1,0:T(8,128)(2,1)S(1)} %constant_dynamic-update-slice_fusion.2.refs_1_), channel_id=1, source_target_pairs={{0,4},{4,0},{8,12},{12,8},{16,20},{20,16},{24,28},{28,24},{1,5},{5... | collective-permute-start | bytes 1622024 | tf_op jit(solution)/shard_map/ppermute | solution.py:28
  31.0 1.4 %collective-permute-start.12 = (bf16[16,4096]{1,0:T(8,128)(2,1)S(1)}, bf16[16,4096]{1,0:T(8,128)(2,1)S(1)}, u32[]{:S(2)}, u32[]{:S(2)}) collective-permute-start(bf16[16,4096]{1,0:T(8,128)(2,1)S(1)} %get-tuple-element.20), channel_id=1, source_target_pairs={{0,4},{4,0},{8,12},{12,8},{16,20},{20,16},{24,28},{28,24},{1,5},{5... | collective-permute-start | bytes 393224 | tf_op jit(solution)/shard_map/ppermute | solution.py:28
  31.2 3.0 %collective-permute-start.17 = (bf16[48,4096]{1,0:T(8,128)(2,1)S(1)}, bf16[48,4096]{1,0:T(8,128)(2,1)S(1)}, u32[]{:S(2)}, u32[]{:S(2)}) collective-permute-start(bf16[48,4096]{1,0:T(8,128)(2,1)S(1)} %get-tuple-element.26), channel_id=1, source_target_pairs={{0,4},{4,0},{8,12},{12,8},{16,20},{20,16},{24,28},{28,24},{1,5},{5... | collective-permute-start | bytes 1179656 | tf_op jit(solution)/shard_map/ppermute | solution.py:28
  31.6 4.6 %collective-permute-start.11 = (bf16[64,4096]{1,0:T(8,128)(2,1)S(1)}, bf16[64,4096]{1,0:T(8,128)(2,1)S(1)}, u32[]{:S(2)}, u32[]{:S(2)}) collective-permute-start(bf16[64,4096]{1,0:T(8,128)(2,1)S(1)} %get-tuple-element.18), channel_id=1, source_target_pairs={{0,4},{4,0},{8,12},{12,8},{16,20},{20,16},{24,28},{28,24},{1,5},{5... | collective-permute-start | bytes 1572872 | tf_op jit(solution)/shard_map/ppermute | solution.py:28
  32.5 7.3 %collective-permute-start.13 = (bf16[16,4096]{1,0:T(8,128)(2,1)S(1)}, bf16[16,4096]{1,0:T(8,128)(2,1)S(1)}, u32[]{:S(2)}, u32[]{:S(2)}) collective-permute-start(bf16[16,4096]{1,0:T(8,128)(2,1)S(1)} %add_convert_fusion), channel_id=1, source_target_pairs={{0,24},{4,28},{8,16},{12,20},{16,8},{20,12},{24,0},{28,4},{1,25},{... | collective-permute-start | bytes 393224 | tf_op jit(solution)/shard_map/ppermute | solution.py:28
  34.3 9.0 %collective-permute-start.18 = (bf16[16,4096]{1,0:T(8,128)(2,1)S(1)}, bf16[16,4096]{1,0:T(8,128)(2,1)S(1)}, u32[]{:S(2)}, u32[]{:S(2)}) collective-permute-start(bf16[16,4096]{1,0:T(8,128)(2,1)S(1)} %get-tuple-element.36), channel_id=1, source_target_pairs={{0,16},{4,20},{8,24},{12,28},{16,0},{20,4},{24,8},{28,12},{1,17},{... | collective-permute-start | bytes 393224 | tf_op jit(solution)/shard_map/ppermute | solution.py:28
  35.7 7.6 %collective-permute-start.19 = (bf16[16,4096]{1,0:T(8,128)(2,1)S(1)}, bf16[16,4096]{1,0:T(8,128)(2,1)S(1)}, u32[]{:S(2)}, u32[]{:S(2)}) collective-permute-start(bf16[16,4096]{1,0:T(8,128)(2,1)S(1)} %get-tuple-element.37), channel_id=1, source_target_pairs={{0,8},{4,12},{8,0},{12,4},{16,24},{20,28},{24,16},{28,20},{1,9},{5... | collective-permute-start | bytes 393224 | tf_op jit(solution)/shard_map/ppermute | solution.py:28
  39.8 6.6 %collective-permute-start.14 = (bf16[16,4096]{1,0:T(8,128)(2,1)S(1)}, bf16[16,4096]{1,0:T(8,128)(2,1)S(1)}, u32[]{:S(2)}, u32[]{:S(2)}) collective-permute-start(bf16[16,4096]{1,0:T(8,128)(2,1)S(1)} %get-tuple-element.22), channel_id=1, source_target_pairs={{0,24},{4,28},{8,16},{12,20},{16,8},{20,12},{24,0},{28,4},{1,25},{... | collective-permute-start | bytes 393224 | tf_op jit(solution)/shard_map/ppermute | solution.py:28
  41.4 6.0 %collective-permute-start.15 = (bf16[16,4096]{1,0:T(8,128)(2,1)S(1)}, bf16[16,4096]{1,0:T(8,128)(2,1)S(1)}, u32[]{:S(2)}, u32[]{:S(2)}) collective-permute-start(bf16[16,4096]{1,0:T(8,128)(2,1)S(1)} %get-tuple-element.23), channel_id=1, source_target_pairs={{0,16},{4,20},{8,24},{12,28},{16,0},{20,4},{24,8},{28,12},{1,17},{... | collective-permute-start | bytes 393224 | tf_op jit(solution)/shard_map/ppermute | solution.py:28
  42.8 5.0 %collective-permute-start.16 = (bf16[16,4096]{1,0:T(8,128)(2,1)S(1)}, bf16[16,4096]{1,0:T(8,128)(2,1)S(1)}, u32[]{:S(2)}, u32[]{:S(2)}) collective-permute-start(bf16[16,4096]{1,0:T(8,128)(2,1)S(1)} %get-tuple-element.24), channel_id=1, source_target_pairs={{0,8},{4,12},{8,0},{12,4},{16,24},{20,28},{24,16},{28,20},{1,9},{5... | collective-permute-start | bytes 393224 | tf_op jit(solution)/shard_map/ppermute | solution.py:28
  43.3 6.2 %collective-permute-start.20 = (bf16[8,4096]{1,0:T(8,128)(2,1)S(1)}, bf16[8,4096]{1,0:T(8,128)(2,1)S(1)}, u32[]{:S(2)}, u32[]{:S(2)}) collective-permute-start(bf16[8,4096]{1,0:T(8,128)(2,1)S(1)} %get-tuple-element.38), channel_id=1, source_target_pairs={{0,2},{1,3},{2,0},{3,1},{4,6},{5,7},{6,4},{7,5},{8,10},{9,11},{10,... | collective-permute-start | bytes 196616 | tf_op jit(solution)/shard_map/ppermute | solution.py:28
  44.9 6.1 %collective-permute-start.21 = (bf16[8,4096]{1,0:T(8,128)(2,1)S(1)}, bf16[8,4096]{1,0:T(8,128)(2,1)S(1)}, u32[]{:S(2)}, u32[]{:S(2)}) collective-permute-start(bf16[8,4096]{1,0:T(8,128)(2,1)S(1)} %get-tuple-element.39), channel_id=1, source_target_pairs={{0,3},{1,2},{2,1},{3,0},{4,7},{5,6},{6,5},{7,4},{8,11},{9,10},{10,... | collective-permute-start | bytes 196616 | tf_op jit(solution)/shard_map/ppermute | solution.py:28
  47.8 4.3 %collective-permute-start.22 = (bf16[8,4096]{1,0:T(8,128)(2,1)S(1)}, bf16[8,4096]{1,0:T(8,128)(2,1)S(1)}, u32[]{:S(2)}, u32[]{:S(2)}) collective-permute-start(bf16[8,4096]{1,0:T(8,128)(2,1)S(1)} %slice.81), channel_id=1, source_target_pairs={{0,1},{1,0},{2,3},{3,2},{4,5},{5,4},{6,7},{7,6},{8,9},{9,8},{10,11... | collective-permute-start | bytes 196616 | tf_op jit(solution)/shard_map/ppermute | solution.py:28

commit v9 on v8

--- a/solution.py
+++ b/solution.py
@@ -178,23 +178,18 @@
     first_expert = lax.axis_index("dp") * exp_dev
     weights = [ref[local] for local in range(exp_dev) for ref in (gate_ref, up_ref)]
     both = times_rows(rows[:, :width], jnp.concatenate(weights))
-    hidden, shares = [], []
+    hidden = []
     for local in range(exp_dev):
         middle = (2 * local + 1) * units
         gate, up = both[:, middle - units : middle], both[:, middle : middle + units]
-        hidden.append((gate / (1.0 + jnp.exp(-gate)) * up).astype(jnp.bfloat16))
         mine = jnp.where(lane == first_expert + local, tags, 0.0)
-        shares.append(jnp.sum(mine, axis=1, keepdims=True))
+        share = jnp.sum(mine, axis=1, keepdims=True)
+        hidden.append((gate / (1.0 + jnp.exp(-gate)) * up * share).astype(jnp.bfloat16))
+    hidden = jnp.concatenate(hidden, axis=1)
     block = min(2048, width)
     for first in range(0, width, block):
-        total = 0.0
-        for local in range(exp_dev):
-            out = jnp.dot(
-                hidden[local],
-                down_ref[local, :, first : first + block],
-                preferred_element_type=jnp.float32,
-            )
-            total = total + out * shares[local]
+        down = down_ref[:, :, first : first + block].reshape(exp_dev * units, block)
+        total = jnp.dot(hidden, down, preferred_element_type=jnp.float32)
         start = 0
         for result in results:
             stop = start + result.shape[0]

time: 52.9 us -> 52.3 us (0.989)
  Pallas kernels: 7.23 us -> 6.63 us
    pallas_call x1, Pallas kernels: 5.67 us -> 5.07 us  [run_experts(): pl.pallas_call(functools.partial(expert_kernel, exp_dev, expert_total, le...]
where the time goes in v9:
time: 52.3 us; the launch traced here: 52.2 us
  starting transfers between devices  23.5 us (45%)
  waiting for transfers between devices  20.6 us (39%)
  Pallas kernels  6.63 us (13%)
  other arithmetic  1.05 us (2%)
    ppermute x23, starting transfers between devices, swap(): return lax.ppermute(value, axis, [(i, i ^ mask) for i in range(count)])  23.5 us
    ppermute x23, waiting for transfers between devices, swap(): return lax.ppermute(value, axis, [(i, i ^ mask) for i in range(count)])  20.6 us
    pallas_call x1, Pallas kernels, run_experts(): pl.pallas_call(functools.partial(expert_kernel, exp_dev, expert_total, le...  5.07 us
    pallas_call x1, Pallas kernels, pack(): pl.pallas_call(pack_kernel, out_shape=pltpu.VMEM((rows, width + extra), t...  1.54 us
  transfers between devices with their start and end apart: 23, of which 11 were waited for; matrix products, arithmetic and copies ran while one was open for 1% of the time, Pallas kernels for 0%

profile of v9, /device:TPU:0, one launch (start us, length us, event | category | flops | bytes accessed | tf_op | source)
XLA Modules:
  0.0 52.2 jit_solution(8457006977866188724)
XLA Ops:
  0.0 0.0 slice-start
  0.0 0.0 slice-start.2
  0.0 1.5 %shard_map.64.refs_0_ = bf16[8,4224]{1,0:T(8,128)(2,1)S(1)} custom-call(bf16[8,4096]{1,0:T(8,128)(2,1)} %tokens_hbm.1, s32[8,8]{1,0:T(8,128)} %ids_hbm.1, bf16[16,4096]{1,0:T(8,128)(2,1)} %router_hbm.1), custom_call_target="tpu_custom_call" | custom-call | flops 1048576 | bytes 262144 | tf_op jit(solution)/shard_map/pallas_call | solution.py:133
  1.6 0.0 slice-start.1
  1.6 0.0 slice-start.3
  1.6 0.0 slice-start.5
  1.6 3.1 %collective-permute-start = (bf16[8,4224]{1,0:T(8,128)(2,1)S(1)}, bf16[8,4224]{1,0:T(8,128)(2,1)S(1)}, u32[]{:S(2)}, u32[]{:S(2)}) collective-permute-start(bf16[8,4224]{1,0:T(8,128)(2,1)S(1)} %shard_map.64.refs_0_), channel_id=1, source_target_pairs={{0,1},{1,0},{2,3},{3,2},{4,5},{5,4},{6,7},{7,6},{8,9},{9,8},{10,11... | collective-permute-start | bytes 202760 | tf_op jit(solution)/shard_map/ppermute | solution.py:28
  4.7 2.5 %collective-permute-start.5 = (bf16[8,4224]{1,0:T(8,128)(2,1)S(1)}, bf16[8,4224]{1,0:T(8,128)(2,1)S(1)}, u32[]{:S(2)}, u32[]{:S(2)}) collective-permute-start(bf16[8,4224]{1,0:T(8,128)(2,1)S(1)} %shard_map.64.refs_0_), channel_id=1, source_target_pairs={{0,3},{1,2},{2,1},{3,0},{4,7},{5,6},{6,5},{7,4},{8,11},{9,10},{10,... | collective-permute-start | bytes 202760 | tf_op jit(solution)/shard_map/ppermute | solution.py:28
  7.2 0.1 collective-permute-start.4
  7.3 0.0 collective-permute-done.refs_1_
  7.3 2.6 %collective-permute-start.3 = (bf16[16,4224]{1,0:T(8,128)(2,1)S(1)}, bf16[16,4224]{1,0:T(8,128)(2,1)S(1)}, u32[]{:S(2)}, u32[]{:S(2)}) collective-permute-start(bf16[16,4224]{1,0:T(8,128)(2,1)S(1)} %shard_map.65), channel_id=1, source_target_pairs={{0,24},{4,28},{8,16},{12,20},{16,8},{20,12},{24,0},{28,4},{1,25},{... | collective-permute-start | bytes 405512 | tf_op jit(solution)/shard_map/ppermute | solution.py:28
  9.9 0.5 collective-permute-start.2
  10.4 0.4 collective-permute-start.1
  10.9 2.9 %collective-permute-done.4 = bf16[8,4224]{1,0:T(8,128)(2,1)S(1)} collective-permute-done((bf16[8,4224]{1,0:T(8,128)(2,1)S(1)}, bf16[8,4224]{1,0:T(8,128)(2,1)S(1)}, u32[]{:S(2)}, u32[]{:S(2)}) %collective-permute-start.4) | collective-permute-done | bytes 67616 | tf_op jit(solution)/shard_map/ppermute | solution.py:28
  13.8 0.0 collective-permute-done.5
  13.8 2.5 %collective-permute-start.8 = (bf16[16,4224]{1,0:T(8,128)(2,1)S(1)}, bf16[16,4224]{1,0:T(8,128)(2,1)S(1)}, u32[]{:S(2)}, u32[]{:S(2)}) collective-permute-start(bf16[16,4224]{1,0:T(8,128)(2,1)S(1)} %get-tuple-element.40), channel_id=1, source_target_pairs={{0,24},{4,28},{8,16},{12,20},{16,8},{20,12},{24,0},{28,4},{1,25},{... | collective-permute-start | bytes 405512 | tf_op jit(solution)/shard_map/ppermute | solution.py:28
  16.3 0.5 collective-permute-start.7
  16.8 0.0 collective-permute-done.3
  16.8 0.5 %collective-permute-start.6 = (bf16[16,4224]{1,0:T(8,128)(2,1)S(1)}, bf16[16,4224]{1,0:T(8,128)(2,1)S(1)}, u32[]{:S(2)}, u32[]{:S(2)}) collective-permute-start(bf16[16,4224]{1,0:T(8,128)(2,1)S(1)} %get-tuple-element.40), channel_id=1, source_target_pairs={{0,8},{4,12},{8,0},{12,4},{16,24},{20,28},{24,16},{28,20},{1,9},{5... | collective-permute-start | bytes 405512 | tf_op jit(solution)/shard_map/ppermute | solution.py:28
  17.4 0.0 collective-permute-done.2
  17.4 0.0 collective-permute-done.1
  17.4 0.1 collective-permute-start.9
  17.5 5.7 %collective-permute-done.6 = bf16[16,4224]{1,0:T(8,128)(2,1)S(1)} collective-permute-done((bf16[16,4224]{1,0:T(8,128)(2,1)S(1)}, bf16[16,4224]{1,0:T(8,128)(2,1)S(1)}, u32[]{:S(2)}, u32[]{:S(2)}) %collective-permute-start.6) | collective-permute-done | bytes 135200 | tf_op jit(solution)/shard_map/ppermute | solution.py:28
  23.2 0.0 collective-permute-done.7
  23.2 0.0 collective-permute-done.8
  23.3 0.1 collective-permute-start.10
  23.3 0.0 collective-permute-done.9.refs_2_
  23.4 1.9 %collective-permute-done.10.refs_3_ = bf16[64,4224]{1,0:T(8,128)(2,1)S(1)} collective-permute-done((bf16[64,4224]{1,0:T(8,128)(2,1)S(1)}, bf16[64,4224]{1,0:T(8,128)(2,1)S(1)}, u32[]{:S(2)}, u32[]{:S(2)}) %collective-permute-start.10) | collective-permute-done | bytes 540704 | tf_op jit(solution)/shard_map/ppermute | solution.py:28
  25.3 0.0 slice-done
  25.3 0.0 slice-done.2
  25.3 0.0 slice-done.4
  25.3 0.0 slice-done.1
  25.3 0.0 slice-done.3
  25.3 0.0 slice-done.5
  25.3 5.1 %shard_map.66 = (f32[64,4096]{1,0:T(8,128)S(1)}, f32[48,4096]{1,0:T(8,128)S(1)}, f32[16,4096]{1,0:T(8,128)S(1)}, bf16[64,4096]{1,0:T(8,128)(2,1)S(1)}, bf16[48,4...) custom-call(bf16[64,4224]{1,0:T(8,128)(2,1)S(1)} %pad_maximum_fusion.refs_0_, ...), custom_call_target="tpu_custom_call" | custom-call | flops 4831838208 | bytes 5242880 | tf_op jit(solution)/shard_map/pallas_call | solution.py:204
  30.4 0.2 collective-permute-start.12
  30.6 0.4 collective-permute-start.17
  31.0 0.1 collective-permute-start.11
  31.1 0.7 %collective-permute-done.12 = bf16[16,4096]{1,0:T(8,128)(2,1)S(1)} collective-permute-done((bf16[16,4096]{1,0:T(8,128)(2,1)S(1)}, bf16[16,4096]{1,0:T(8,128)(2,1)S(1)}, u32[]{:S(2)}, u32[]{:S(2)}) %collective-permute-start.12) | collective-permute-done | bytes 131104 | tf_op jit(solution)/shard_map/ppermute | solution.py:28
  31.9 1.7 %collective-permute-start.13 = (bf16[16,4096]{1,0:T(8,128)(2,1)S(1)}, bf16[16,4096]{1,0:T(8,128)(2,1)S(1)}, u32[]{:S(2)}, u32[]{:S(2)}) collective-permute-start(bf16[16,4096]{1,0:T(8,128)(2,1)S(1)} %add_convert_fusion), channel_id=1, source_target_pairs={{0,24},{4,28},{8,16},{12,20},{16,8},{20,12},{24,0},{28,4},{1,25},{... | collective-permute-start | bytes 393224 | tf_op jit(solution)/shard_map/ppermute | solution.py:28
  33.6 0.0 collective-permute-done.17
  33.6 0.1 fusion.8
  33.7 1.4 %collective-permute-start.18 = (bf16[16,4096]{1,0:T(8,128)(2,1)S(1)}, bf16[16,4096]{1,0:T(8,128)(2,1)S(1)}, u32[]{:S(2)}, u32[]{:S(2)}) collective-permute-start(bf16[16,4096]{1,0:T(8,128)(2,1)S(1)} %get-tuple-element.36), channel_id=1, source_target_pairs={{0,16},{4,20},{8,24},{12,28},{16,0},{20,4},{24,8},{28,12},{1,17},{... | collective-permute-start | bytes 393224 | tf_op jit(solution)/shard_map/ppermute | solution.py:28
  35.1 0.5 collective-permute-start.19
  35.6 0.0 collective-permute-done.11
  35.6 0.1 fusion.7
  35.8 3.4 %collective-permute-done.13 = bf16[16,4096]{1,0:T(8,128)(2,1)S(1)} collective-permute-done((bf16[16,4096]{1,0:T(8,128)(2,1)S(1)}, bf16[16,4096]{1,0:T(8,128)(2,1)S(1)}, u32[]{:S(2)}, u32[]{:S(2)}) %collective-permute-start.13) | collective-permute-done | bytes 131104 | tf_op jit(solution)/shard_map/ppermute | solution.py:28
  39.2 1.7 %collective-permute-start.14 = (bf16[16,4096]{1,0:T(8,128)(2,1)S(1)}, bf16[16,4096]{1,0:T(8,128)(2,1)S(1)}, u32[]{:S(2)}, u32[]{:S(2)}) collective-permute-start(bf16[16,4096]{1,0:T(8,128)(2,1)S(1)} %get-tuple-element.22), channel_id=1, source_target_pairs={{0,24},{4,28},{8,16},{12,20},{16,8},{20,12},{24,0},{28,4},{1,25},{... | collective-permute-start | bytes 393224 | tf_op jit(solution)/shard_map/ppermute | solution.py:28
  40.8 1.3 %collective-permute-start.15 = (bf16[16,4096]{1,0:T(8,128)(2,1)S(1)}, bf16[16,4096]{1,0:T(8,128)(2,1)S(1)}, u32[]{:S(2)}, u32[]{:S(2)}) collective-permute-start(bf16[16,4096]{1,0:T(8,128)(2,1)S(1)} %get-tuple-element.23), channel_id=1, source_target_pairs={{0,16},{4,20},{8,24},{12,28},{16,0},{20,4},{24,8},{28,12},{1,17},{... | collective-permute-start | bytes 393224 | tf_op jit(solution)/shard_map/ppermute | solution.py:28
  42.2 0.5 collective-permute-start.16
  42.7 0.0 collective-permute-done.18
  42.7 0.0 collective-permute-done.19
  42.7 0.1 fusion.2
  42.7 1.5 %collective-permute-start.20 = (bf16[8,4096]{1,0:T(8,128)(2,1)S(1)}, bf16[8,4096]{1,0:T(8,128)(2,1)S(1)}, u32[]{:S(2)}, u32[]{:S(2)}) collective-permute-start(bf16[8,4096]{1,0:T(8,128)(2,1)S(1)} %get-tuple-element.38), channel_id=1, source_target_pairs={{0,2},{1,3},{2,0},{3,1},{4,6},{5,7},{6,4},{7,5},{8,10},{9,11},{10,... | collective-permute-start | bytes 196616 | tf_op jit(solution)/shard_map/ppermute | solution.py:28
  44.3 1.0 %collective-permute-start.21 = (bf16[8,4096]{1,0:T(8,128)(2,1)S(1)}, bf16[8,4096]{1,0:T(8,128)(2,1)S(1)}, u32[]{:S(2)}, u32[]{:S(2)}) collective-permute-start(bf16[8,4096]{1,0:T(8,128)(2,1)S(1)} %get-tuple-element.39), channel_id=1, source_target_pairs={{0,3},{1,2},{2,1},{3,0},{4,7},{5,6},{6,5},{7,4},{8,11},{9,10},{10,... | collective-permute-start | bytes 196616 | tf_op jit(solution)/shard_map/ppermute | solution.py:28
  45.3 0.5 collective-permute-done.14
  45.7 1.1 %collective-permute-done.15 = bf16[16,4096]{1,0:T(8,128)(2,1)S(1)} collective-permute-done((bf16[16,4096]{1,0:T(8,128)(2,1)S(1)}, bf16[16,4096]{1,0:T(8,128)(2,1)S(1)}, u32[]{:S(2)}, u32[]{:S(2)}) %collective-permute-start.15) | collective-permute-done | bytes 131104 | tf_op jit(solution)/shard_map/ppermute | solution.py:28
  46.8 0.3 collective-permute-done.16
  47.1 0.1 fusion.4
  47.2 0.2 collective-permute-start.22
  47.4 1.6 %collective-permute-done.20 = bf16[8,4096]{1,0:T(8,128)(2,1)S(1)} collective-permute-done((bf16[8,4096]{1,0:T(8,128)(2,1)S(1)}, bf16[8,4096]{1,0:T(8,128)(2,1)S(1)}, u32[]{:S(2)}, u32[]{:S(2)}) %collective-permute-start.20) | collective-permute-done | bytes 65568 | tf_op jit(solution)/shard_map/ppermute | solution.py:28
  49.0 1.4 %collective-permute-done.21 = bf16[8,4096]{1,0:T(8,128)(2,1)S(1)} collective-permute-done((bf16[8,4096]{1,0:T(8,128)(2,1)S(1)}, bf16[8,4096]{1,0:T(8,128)(2,1)S(1)}, u32[]{:S(2)}, u32[]{:S(2)}) %collective-permute-start.21) | collective-permute-done | bytes 65568 | tf_op jit(solution)/shard_map/ppermute | solution.py:28
  50.3 1.2 %collective-permute-done.22 = bf16[8,4096]{1,0:T(8,128)(2,1)S(1)} collective-permute-done((bf16[8,4096]{1,0:T(8,128)(2,1)S(1)}, bf16[8,4096]{1,0:T(8,128)(2,1)S(1)}, u32[]{:S(2)}, u32[]{:S(2)}) %collective-permute-start.22) | collective-permute-done | bytes 65568 | tf_op jit(solution)/shard_map/ppermute | solution.py:28
  51.5 0.6 %fusion.6 = bf16[8,4096]{1,0:T(8,128)(2,1)} fusion(f32[8,4096]{1,0:T(8,128)S(1)} %convert_add_fusion.2, f32[16,4096]{1,0:T(8,128)S(1)} %fusion.4, bf16[8,4096]{1,0:T(8,128)(2,1)S(1)} %collective-permute-done.22), kind=kLoop, calls=%fused_computation.14 | loop fusion | flops 131072 | bytes 393216 | tf_op jit(solution)/shard_map/convert_element_type | solution.py:95
  (17 shorter events, 0.2 us)
Async XLA Ops:
  0.0 25.3 %slice-start = ((s8[6291456]{0:T(1024)(128)(4,1)}), s8[4194304]{0:T(1024)(128)(4,1)S(1)}, s32[]{:S(2)}) async-start(s8[6291456]{0:T(1024)(128)(4,1)} %bitcast), calls=%async_computation | async-start | bytes 8388608
  0.0 25.3 %slice-start.2 = ((s8[6291456]{0:T(1024)(128)(4,1)}), s8[4194304]{0:T(1024)(128)(4,1)S(1)}, s32[]{:S(2)}) async-start(s8[6291456]{0:T(1024)(128)(4,1)} %bitcast.2), calls=%async_computation.2 | async-start | bytes 8388608
  0.0 25.3 %slice-start.4 = ((s8[6291456]{0:T(1024)(128)(4,1)}), s8[4194304]{0:T(1024)(128)(4,1)S(1)}, s32[]{:S(2)}) async-start(s8[6291456]{0:T(1024)(128)(4,1)} %bitcast.4), calls=%async_computation.4 | async-start | bytes 8388608
  1.6 23.7 %slice-start.1 = ((s8[6291456]{0:T(1024)(128)(4,1)}), s8[2097152]{0:T(1024)(128)(4,1)S(1)}, s32[]{:S(2)}) async-start(s8[6291456]{0:T(1024)(128)(4,1)} %bitcast), calls=%async_computation.1 | async-start | bytes 4194304
  1.6 23.7 %slice-start.3 = ((s8[6291456]{0:T(1024)(128)(4,1)}), s8[2097152]{0:T(1024)(128)(4,1)S(1)}, s32[]{:S(2)}) async-start(s8[6291456]{0:T(1024)(128)(4,1)} %bitcast.2), calls=%async_computation.3 | async-start | bytes 4194304
  1.6 23.7 %slice-start.5 = ((s8[6291456]{0:T(1024)(128)(4,1)}), s8[2097152]{0:T(1024)(128)(4,1)S(1)}, s32[]{:S(2)}) async-start(s8[6291456]{0:T(1024)(128)(4,1)} %bitcast.4), calls=%async_computation.5 | async-start | bytes 4194304
  1.6 5.7 %collective-permute-start = (bf16[8,4224]{1,0:T(8,128)(2,1)S(1)}, bf16[8,4224]{1,0:T(8,128)(2,1)S(1)}, u32[]{:S(2)}, u32[]{:S(2)}) collective-permute-start(bf16[8,4224]{1,0:T(8,128)(2,1)S(1)} %shard_map.64.refs_0_), channel_id=1, source_target_pairs={{0,1},{1,0},{2,3},{3,2},{4,5},{5,4},{6,7},{7,6},{8,9},{9,8},{10,11... | collective-permute-start | bytes 202760 | tf_op jit(solution)/shard_map/ppermute | solution.py:28
  4.7 9.1 %collective-permute-start.5 = (bf16[8,4224]{1,0:T(8,128)(2,1)S(1)}, bf16[8,4224]{1,0:T(8,128)(2,1)S(1)}, u32[]{:S(2)}, u32[]{:S(2)}) collective-permute-start(bf16[8,4224]{1,0:T(8,128)(2,1)S(1)} %shard_map.64.refs_0_), channel_id=1, source_target_pairs={{0,3},{1,2},{2,1},{3,0},{4,7},{5,6},{6,5},{7,4},{8,11},{9,10},{10,... | collective-permute-start | bytes 202760 | tf_op jit(solution)/shard_map/ppermute | solution.py:28
  7.2 6.6 %collective-permute-start.4 = (bf16[8,4224]{1,0:T(8,128)(2,1)S(1)}, bf16[8,4224]{1,0:T(8,128)(2,1)S(1)}, u32[]{:S(2)}, u32[]{:S(2)}) collective-permute-start(bf16[8,4224]{1,0:T(8,128)(2,1)S(1)} %shard_map.64.refs_0_), channel_id=1, source_target_pairs={{0,2},{1,3},{2,0},{3,1},{4,6},{5,7},{6,4},{7,5},{8,10},{9,11},{10,... | collective-permute-start | bytes 202760 | tf_op jit(solution)/shard_map/ppermute | solution.py:28
  7.3 9.5 %collective-permute-start.3 = (bf16[16,4224]{1,0:T(8,128)(2,1)S(1)}, bf16[16,4224]{1,0:T(8,128)(2,1)S(1)}, u32[]{:S(2)}, u32[]{:S(2)}) collective-permute-start(bf16[16,4224]{1,0:T(8,128)(2,1)S(1)} %shard_map.65), channel_id=1, source_target_pairs={{0,24},{4,28},{8,16},{12,20},{16,8},{20,12},{24,0},{28,4},{1,25},{... | collective-permute-start | bytes 405512 | tf_op jit(solution)/shard_map/ppermute | solution.py:28
  9.9 7.4 %collective-permute-start.2 = (bf16[16,4224]{1,0:T(8,128)(2,1)S(1)}, bf16[16,4224]{1,0:T(8,128)(2,1)S(1)}, u32[]{:S(2)}, u32[]{:S(2)}) collective-permute-start(bf16[16,4224]{1,0:T(8,128)(2,1)S(1)} %shard_map.65), channel_id=1, source_target_pairs={{0,16},{4,20},{8,24},{12,28},{16,0},{20,4},{24,8},{28,12},{1,17},{... | collective-permute-start | bytes 405512 | tf_op jit(solution)/shard_map/ppermute | solution.py:28
  10.4 6.9 %collective-permute-start.1 = (bf16[16,4224]{1,0:T(8,128)(2,1)S(1)}, bf16[16,4224]{1,0:T(8,128)(2,1)S(1)}, u32[]{:S(2)}, u32[]{:S(2)}) collective-permute-start(bf16[16,4224]{1,0:T(8,128)(2,1)S(1)} %shard_map.65), channel_id=1, source_target_pairs={{0,8},{4,12},{8,0},{12,4},{16,24},{20,28},{24,16},{28,20},{1,9},{5... | collective-permute-start | bytes 405512 | tf_op jit(solution)/shard_map/ppermute | solution.py:28
  13.8 9.4 %collective-permute-start.8 = (bf16[16,4224]{1,0:T(8,128)(2,1)S(1)}, bf16[16,4224]{1,0:T(8,128)(2,1)S(1)}, u32[]{:S(2)}, u32[]{:S(2)}) collective-permute-start(bf16[16,4224]{1,0:T(8,128)(2,1)S(1)} %get-tuple-element.40), channel_id=1, source_target_pairs={{0,24},{4,28},{8,16},{12,20},{16,8},{20,12},{24,0},{28,4},{1,25},{... | collective-permute-start | bytes 405512 | tf_op jit(solution)/shard_map/ppermute | solution.py:28
  16.3 6.9 %collective-permute-start.7 = (bf16[16,4224]{1,0:T(8,128)(2,1)S(1)}, bf16[16,4224]{1,0:T(8,128)(2,1)S(1)}, u32[]{:S(2)}, u32[]{:S(2)}) collective-permute-start(bf16[16,4224]{1,0:T(8,128)(2,1)S(1)} %get-tuple-element.40), channel_id=1, source_target_pairs={{0,16},{4,20},{8,24},{12,28},{16,0},{20,4},{24,8},{28,12},{1,17},{... | collective-permute-start | bytes 405512 | tf_op jit(solution)/shard_map/ppermute | solution.py:28
  16.8 6.4 %collective-permute-start.6 = (bf16[16,4224]{1,0:T(8,128)(2,1)S(1)}, bf16[16,4224]{1,0:T(8,128)(2,1)S(1)}, u32[]{:S(2)}, u32[]{:S(2)}) collective-permute-start(bf16[16,4224]{1,0:T(8,128)(2,1)S(1)} %get-tuple-element.40), channel_id=1, source_target_pairs={{0,8},{4,12},{8,0},{12,4},{16,24},{20,28},{24,16},{28,20},{1,9},{5... | collective-permute-start | bytes 405512 | tf_op jit(solution)/shard_map/ppermute | solution.py:28
  17.4 5.9 %collective-permute-start.9 = (bf16[64,4224]{1,0:T(8,128)(2,1)S(1)}, bf16[64,4224]{1,0:T(8,128)(2,1)S(1)}, u32[]{:S(2)}, u32[]{:S(2)}) collective-permute-start(bf16[64,4224]{1,0:T(8,128)(2,1)S(1)} %pad_maximum_fusion.refs_0_), channel_id=1, source_target_pairs={{0,4},{4,0},{8,12},{12,8},{16,20},{20,16},{24,28},{28,24},{1,5},{5... | collective-permute-start | bytes 1622024 | tf_op jit(solution)/shard_map/ppermute | solution.py:28
  23.3 2.0 %collective-permute-start.10 = (bf16[64,4224]{1,0:T(8,128)(2,1)S(1)}, bf16[64,4224]{1,0:T(8,128)(2,1)S(1)}, u32[]{:S(2)}, u32[]{:S(2)}) collective-permute-start(bf16[64,4224]{1,0:T(8,128)(2,1)S(1)} %constant_dynamic-update-slice_fusion.2.refs_1_), channel_id=1, source_target_pairs={{0,4},{4,0},{8,12},{12,8},{16,20},{20,16},{24,28},{28,24},{1,5},{5... | collective-permute-start | bytes 1622024 | tf_op jit(solution)/shard_map/ppermute | solution.py:28
  30.4 1.4 %collective-permute-start.12 = (bf16[16,4096]{1,0:T(8,128)(2,1)S(1)}, bf16[16,4096]{1,0:T(8,128)(2,1)S(1)}, u32[]{:S(2)}, u32[]{:S(2)}) collective-permute-start(bf16[16,4096]{1,0:T(8,128)(2,1)S(1)} %get-tuple-element.20), channel_id=1, source_target_pairs={{0,4},{4,0},{8,12},{12,8},{16,20},{20,16},{24,28},{28,24},{1,5},{5... | collective-permute-start | bytes 393224 | tf_op jit(solution)/shard_map/ppermute | solution.py:28
  30.6 3.0 %collective-permute-start.17 = (bf16[48,4096]{1,0:T(8,128)(2,1)S(1)}, bf16[48,4096]{1,0:T(8,128)(2,1)S(1)}, u32[]{:S(2)}, u32[]{:S(2)}) collective-permute-start(bf16[48,4096]{1,0:T(8,128)(2,1)S(1)} %get-tuple-element.26), channel_id=1, source_target_pairs={{0,4},{4,0},{8,12},{12,8},{16,20},{20,16},{24,28},{28,24},{1,5},{5... | collective-permute-start | bytes 1179656 | tf_op jit(solution)/shard_map/ppermute | solution.py:28
  31.0 4.6 %collective-permute-start.11 = (bf16[64,4096]{1,0:T(8,128)(2,1)S(1)}, bf16[64,4096]{1,0:T(8,128)(2,1)S(1)}, u32[]{:S(2)}, u32[]{:S(2)}) collective-permute-start(bf16[64,4096]{1,0:T(8,128)(2,1)S(1)} %get-tuple-element.18), channel_id=1, source_target_pairs={{0,4},{4,0},{8,12},{12,8},{16,20},{20,16},{24,28},{28,24},{1,5},{5... | collective-permute-start | bytes 1572872 | tf_op jit(solution)/shard_map/ppermute | solution.py:28
  31.9 7.3 %collective-permute-start.13 = (bf16[16,4096]{1,0:T(8,128)(2,1)S(1)}, bf16[16,4096]{1,0:T(8,128)(2,1)S(1)}, u32[]{:S(2)}, u32[]{:S(2)}) collective-permute-start(bf16[16,4096]{1,0:T(8,128)(2,1)S(1)} %add_convert_fusion), channel_id=1, source_target_pairs={{0,24},{4,28},{8,16},{12,20},{16,8},{20,12},{24,0},{28,4},{1,25},{... | collective-permute-start | bytes 393224 | tf_op jit(solution)/shard_map/ppermute | solution.py:28
  33.7 9.0 %collective-permute-start.18 = (bf16[16,4096]{1,0:T(8,128)(2,1)S(1)}, bf16[16,4096]{1,0:T(8,128)(2,1)S(1)}, u32[]{:S(2)}, u32[]{:S(2)}) collective-permute-start(bf16[16,4096]{1,0:T(8,128)(2,1)S(1)} %get-tuple-element.36), channel_id=1, source_target_pairs={{0,16},{4,20},{8,24},{12,28},{16,0},{20,4},{24,8},{28,12},{1,17},{... | collective-permute-start | bytes 393224 | tf_op jit(solution)/shard_map/ppermute | solution.py:28
  35.1 7.6 %collective-permute-start.19 = (bf16[16,4096]{1,0:T(8,128)(2,1)S(1)}, bf16[16,4096]{1,0:T(8,128)(2,1)S(1)}, u32[]{:S(2)}, u32[]{:S(2)}) collective-permute-start(bf16[16,4096]{1,0:T(8,128)(2,1)S(1)} %get-tuple-element.37), channel_id=1, source_target_pairs={{0,8},{4,12},{8,0},{12,4},{16,24},{20,28},{24,16},{28,20},{1,9},{5... | collective-permute-start | bytes 393224 | tf_op jit(solution)/shard_map/ppermute | solution.py:28
  39.2 6.6 %collective-permute-start.14 = (bf16[16,4096]{1,0:T(8,128)(2,1)S(1)}, bf16[16,4096]{1,0:T(8,128)(2,1)S(1)}, u32[]{:S(2)}, u32[]{:S(2)}) collective-permute-start(bf16[16,4096]{1,0:T(8,128)(2,1)S(1)} %get-tuple-element.22), channel_id=1, source_target_pairs={{0,24},{4,28},{8,16},{12,20},{16,8},{20,12},{24,0},{28,4},{1,25},{... | collective-permute-start | bytes 393224 | tf_op jit(solution)/shard_map/ppermute | solution.py:28
  40.8 6.0 %collective-permute-start.15 = (bf16[16,4096]{1,0:T(8,128)(2,1)S(1)}, bf16[16,4096]{1,0:T(8,128)(2,1)S(1)}, u32[]{:S(2)}, u32[]{:S(2)}) collective-permute-start(bf16[16,4096]{1,0:T(8,128)(2,1)S(1)} %get-tuple-element.23), channel_id=1, source_target_pairs={{0,16},{4,20},{8,24},{12,28},{16,0},{20,4},{24,8},{28,12},{1,17},{... | collective-permute-start | bytes 393224 | tf_op jit(solution)/shard_map/ppermute | solution.py:28
  42.2 5.0 %collective-permute-start.16 = (bf16[16,4096]{1,0:T(8,128)(2,1)S(1)}, bf16[16,4096]{1,0:T(8,128)(2,1)S(1)}, u32[]{:S(2)}, u32[]{:S(2)}) collective-permute-start(bf16[16,4096]{1,0:T(8,128)(2,1)S(1)} %get-tuple-element.24), channel_id=1, source_target_pairs={{0,8},{4,12},{8,0},{12,4},{16,24},{20,28},{24,16},{28,20},{1,9},{5... | collective-permute-start | bytes 393224 | tf_op jit(solution)/shard_map/ppermute | solution.py:28
  42.7 6.2 %collective-permute-start.20 = (bf16[8,4096]{1,0:T(8,128)(2,1)S(1)}, bf16[8,4096]{1,0:T(8,128)(2,1)S(1)}, u32[]{:S(2)}, u32[]{:S(2)}) collective-permute-start(bf16[8,4096]{1,0:T(8,128)(2,1)S(1)} %get-tuple-element.38), channel_id=1, source_target_pairs={{0,2},{1,3},{2,0},{3,1},{4,6},{5,7},{6,4},{7,5},{8,10},{9,11},{10,... | collective-permute-start | bytes 196616 | tf_op jit(solution)/shard_map/ppermute | solution.py:28
  44.3 6.1 %collective-permute-start.21 = (bf16[8,4096]{1,0:T(8,128)(2,1)S(1)}, bf16[8,4096]{1,0:T(8,128)(2,1)S(1)}, u32[]{:S(2)}, u32[]{:S(2)}) collective-permute-start(bf16[8,4096]{1,0:T(8,128)(2,1)S(1)} %get-tuple-element.39), channel_id=1, source_target_pairs={{0,3},{1,2},{2,1},{3,0},{4,7},{5,6},{6,5},{7,4},{8,11},{9,10},{10,... | collective-permute-start | bytes 196616 | tf_op jit(solution)/shard_map/ppermute | solution.py:28
  47.2 4.3 %collective-permute-start.22 = (bf16[8,4096]{1,0:T(8,128)(2,1)S(1)}, bf16[8,4096]{1,0:T(8,128)(2,1)S(1)}, u32[]{:S(2)}, u32[]{:S(2)}) collective-permute-start(bf16[8,4096]{1,0:T(8,128)(2,1)S(1)} %slice.81), channel_id=1, source_target_pairs={{0,1},{1,0},{2,3},{3,2},{4,5},{5,4},{6,7},{7,6},{8,9},{9,8},{10,11... | collective-permute-start | bytes 196616 | tf_op jit(solution)/shard_map/ppermute | solution.py:28

commit v10 on v9

--- a/solution.py
+++ b/solution.py
@@ -88,7 +88,7 @@
     near_here = [send(other, step) for other, step in zip(others, steps[::-1])]
     sums = [sum([wide(other) for other in here], far), sum([wide(other) for other in near_here], near)]
     far, (total, *near) = split(sums[0], depth // 2), split(sums[1], depth // 2)
-    far = [send(part, ("expert", mask + depth // 2)) for mask, part in enumerate(far)]
+    far = [send(part, ("expert", mask + depth // 2)) for mask, part in enumerate(far)][::-1]
     near = [send(part, ("expert", mask + 1)) for mask, part in enumerate(near)]
     far = sum(wide(part) for part in far)
     far, *near = lax.optimization_barrier((far, *near))

time: 52.3 us -> 52.4 us (level)
  no operation moved by 1% of the time
where the time goes in v10:
time: 52.4 us; the launch traced here: 52.2 us
  starting transfers between devices  23.1 us (44%)
  waiting for transfers between devices  21 us (40%)
  Pallas kernels  6.63 us (13%)
  other arithmetic  1.05 us (2%)
    ppermute x23, starting transfers between devices, swap(): return lax.ppermute(value, axis, [(i, i ^ mask) for i in range(count)])  23.1 us
    ppermute x23, waiting for transfers between devices, swap(): return lax.ppermute(value, axis, [(i, i ^ mask) for i in range(count)])  21 us
    pallas_call x1, Pallas kernels, run_experts(): pl.pallas_call(functools.partial(expert_kernel, exp_dev, expert_total, le...  5.07 us
    pallas_call x1, Pallas kernels, pack(): pl.pallas_call(pack_kernel, out_shape=pltpu.VMEM((rows, width + extra), t...  1.54 us
  transfers between devices with their start and end apart: 23, of which 11 were waited for; matrix products, arithmetic and copies ran while one was open for 1% of the time, Pallas kernels for 0%

profile of v10, /device:TPU:0, one launch (start us, length us, event | category | flops | bytes accessed | tf_op | source)
XLA Modules:
  0.0 52.2 jit_solution(2480169492250864025)
XLA Ops:
  0.0 0.0 slice-start
  0.0 0.0 slice-start.2
  0.0 1.5 %shard_map.64.refs_0_ = bf16[8,4224]{1,0:T(8,128)(2,1)S(1)} custom-call(bf16[8,4096]{1,0:T(8,128)(2,1)} %tokens_hbm.1, s32[8,8]{1,0:T(8,128)} %ids_hbm.1, bf16[16,4096]{1,0:T(8,128)(2,1)} %router_hbm.1), custom_call_target="tpu_custom_call" | custom-call | flops 1048576 | bytes 262144 | tf_op jit(solution)/shard_map/pallas_call | solution.py:133
  1.6 0.0 slice-start.1
  1.6 0.0 slice-start.3
  1.6 0.0 slice-start.5
  1.6 3.1 %collective-permute-start = (bf16[8,4224]{1,0:T(8,128)(2,1)S(1)}, bf16[8,4224]{1,0:T(8,128)(2,1)S(1)}, u32[]{:S(2)}, u32[]{:S(2)}) collective-permute-start(bf16[8,4224]{1,0:T(8,128)(2,1)S(1)} %shard_map.64.refs_0_), channel_id=1, source_target_pairs={{0,1},{1,0},{2,3},{3,2},{4,5},{5,4},{6,7},{7,6},{8,9},{9,8},{10,11... | collective-permute-start | bytes 202760 | tf_op jit(solution)/shard_map/ppermute | solution.py:28
  4.7 2.5 %collective-permute-start.5 = (bf16[8,4224]{1,0:T(8,128)(2,1)S(1)}, bf16[8,4224]{1,0:T(8,128)(2,1)S(1)}, u32[]{:S(2)}, u32[]{:S(2)}) collective-permute-start(bf16[8,4224]{1,0:T(8,128)(2,1)S(1)} %shard_map.64.refs_0_), channel_id=1, source_target_pairs={{0,3},{1,2},{2,1},{3,0},{4,7},{5,6},{6,5},{7,4},{8,11},{9,10},{10,... | collective-permute-start | bytes 202760 | tf_op jit(solution)/shard_map/ppermute | solution.py:28
  7.2 0.1 collective-permute-start.4
  7.3 0.0 collective-permute-done.refs_1_
  7.3 2.6 %collective-permute-start.3 = (bf16[16,4224]{1,0:T(8,128)(2,1)S(1)}, bf16[16,4224]{1,0:T(8,128)(2,1)S(1)}, u32[]{:S(2)}, u32[]{:S(2)}) collective-permute-start(bf16[16,4224]{1,0:T(8,128)(2,1)S(1)} %shard_map.65), channel_id=1, source_target_pairs={{0,24},{4,28},{8,16},{12,20},{16,8},{20,12},{24,0},{28,4},{1,25},{... | collective-permute-start | bytes 405512 | tf_op jit(solution)/shard_map/ppermute | solution.py:28
  9.9 0.5 collective-permute-start.2
  10.4 0.4 collective-permute-start.1
  10.9 2.9 %collective-permute-done.4 = bf16[8,4224]{1,0:T(8,128)(2,1)S(1)} collective-permute-done((bf16[8,4224]{1,0:T(8,128)(2,1)S(1)}, bf16[8,4224]{1,0:T(8,128)(2,1)S(1)}, u32[]{:S(2)}, u32[]{:S(2)}) %collective-permute-start.4) | collective-permute-done | bytes 67616 | tf_op jit(solution)/shard_map/ppermute | solution.py:28
  13.8 0.0 collective-permute-done.5
  13.8 2.5 %collective-permute-start.8 = (bf16[16,4224]{1,0:T(8,128)(2,1)S(1)}, bf16[16,4224]{1,0:T(8,128)(2,1)S(1)}, u32[]{:S(2)}, u32[]{:S(2)}) collective-permute-start(bf16[16,4224]{1,0:T(8,128)(2,1)S(1)} %get-tuple-element.40), channel_id=1, source_target_pairs={{0,24},{4,28},{8,16},{12,20},{16,8},{20,12},{24,0},{28,4},{1,25},{... | collective-permute-start | bytes 405512 | tf_op jit(solution)/shard_map/ppermute | solution.py:28
  16.3 0.5 collective-permute-start.7
  16.8 0.0 collective-permute-done.3
  16.8 0.5 %collective-permute-start.6 = (bf16[16,4224]{1,0:T(8,128)(2,1)S(1)}, bf16[16,4224]{1,0:T(8,128)(2,1)S(1)}, u32[]{:S(2)}, u32[]{:S(2)}) collective-permute-start(bf16[16,4224]{1,0:T(8,128)(2,1)S(1)} %get-tuple-element.40), channel_id=1, source_target_pairs={{0,8},{4,12},{8,0},{12,4},{16,24},{20,28},{24,16},{28,20},{1,9},{5... | collective-permute-start | bytes 405512 | tf_op jit(solution)/shard_map/ppermute | solution.py:28
  17.4 0.0 collective-permute-done.2
  17.4 0.0 collective-permute-done.1
  17.4 0.1 collective-permute-start.9
  17.5 5.7 %collective-permute-done.6 = bf16[16,4224]{1,0:T(8,128)(2,1)S(1)} collective-permute-done((bf16[16,4224]{1,0:T(8,128)(2,1)S(1)}, bf16[16,4224]{1,0:T(8,128)(2,1)S(1)}, u32[]{:S(2)}, u32[]{:S(2)}) %collective-permute-start.6) | collective-permute-done | bytes 135200 | tf_op jit(solution)/shard_map/ppermute | solution.py:28
  23.2 0.0 collective-permute-done.7
  23.2 0.0 collective-permute-done.8
  23.3 0.1 collective-permute-start.10
  23.3 0.0 collective-permute-done.9.refs_2_
  23.4 1.9 %collective-permute-done.10.refs_3_ = bf16[64,4224]{1,0:T(8,128)(2,1)S(1)} collective-permute-done((bf16[64,4224]{1,0:T(8,128)(2,1)S(1)}, bf16[64,4224]{1,0:T(8,128)(2,1)S(1)}, u32[]{:S(2)}, u32[]{:S(2)}) %collective-permute-start.10) | collective-permute-done | bytes 540704 | tf_op jit(solution)/shard_map/ppermute | solution.py:28
  25.3 0.0 slice-done
  25.3 0.0 slice-done.2
  25.3 0.0 slice-done.4
  25.3 0.0 slice-done.1
  25.3 0.0 slice-done.3
  25.3 0.0 slice-done.5
  25.3 5.1 %shard_map.66 = (f32[64,4096]{1,0:T(8,128)S(1)}, f32[48,4096]{1,0:T(8,128)S(1)}, f32[16,4096]{1,0:T(8,128)S(1)}, bf16[64,4096]{1,0:T(8,128)(2,1)S(1)}, bf16[48,4...) custom-call(bf16[64,4224]{1,0:T(8,128)(2,1)S(1)} %pad_maximum_fusion.refs_0_, ...), custom_call_target="tpu_custom_call" | custom-call | flops 4831838208 | bytes 5242880 | tf_op jit(solution)/shard_map/pallas_call | solution.py:204
  30.4 0.2 collective-permute-start.12
  30.6 0.4 collective-permute-start.17
  31.0 0.1 collective-permute-start.11
  31.1 0.7 %collective-permute-done.12 = bf16[16,4096]{1,0:T(8,128)(2,1)S(1)} collective-permute-done((bf16[16,4096]{1,0:T(8,128)(2,1)S(1)}, bf16[16,4096]{1,0:T(8,128)(2,1)S(1)}, u32[]{:S(2)}, u32[]{:S(2)}) %collective-permute-start.12) | collective-permute-done | bytes 131104 | tf_op jit(solution)/shard_map/ppermute | solution.py:28
  31.9 1.7 %collective-permute-start.13 = (bf16[16,4096]{1,0:T(8,128)(2,1)S(1)}, bf16[16,4096]{1,0:T(8,128)(2,1)S(1)}, u32[]{:S(2)}, u32[]{:S(2)}) collective-permute-start(bf16[16,4096]{1,0:T(8,128)(2,1)S(1)} %add_convert_fusion), channel_id=1, source_target_pairs={{0,24},{4,28},{8,16},{12,20},{16,8},{20,12},{24,0},{28,4},{1,25},{... | collective-permute-start | bytes 393224 | tf_op jit(solution)/shard_map/ppermute | solution.py:28
  33.6 0.0 collective-permute-done.17
  33.6 0.1 fusion.8
  33.7 1.4 %collective-permute-start.18 = (bf16[16,4096]{1,0:T(8,128)(2,1)S(1)}, bf16[16,4096]{1,0:T(8,128)(2,1)S(1)}, u32[]{:S(2)}, u32[]{:S(2)}) collective-permute-start(bf16[16,4096]{1,0:T(8,128)(2,1)S(1)} %get-tuple-element.36), channel_id=1, source_target_pairs={{0,16},{4,20},{8,24},{12,28},{16,0},{20,4},{24,8},{28,12},{1,17},{... | collective-permute-start | bytes 393224 | tf_op jit(solution)/shard_map/ppermute | solution.py:28
  35.1 0.5 collective-permute-start.19
  35.6 0.0 collective-permute-done.11
  35.6 0.1 fusion.7
  35.8 3.4 %collective-permute-done.13 = bf16[16,4096]{1,0:T(8,128)(2,1)S(1)} collective-permute-done((bf16[16,4096]{1,0:T(8,128)(2,1)S(1)}, bf16[16,4096]{1,0:T(8,128)(2,1)S(1)}, u32[]{:S(2)}, u32[]{:S(2)}) %collective-permute-start.13) | collective-permute-done | bytes 131104 | tf_op jit(solution)/shard_map/ppermute | solution.py:28
  39.2 1.7 %collective-permute-start.14 = (bf16[16,4096]{1,0:T(8,128)(2,1)S(1)}, bf16[16,4096]{1,0:T(8,128)(2,1)S(1)}, u32[]{:S(2)}, u32[]{:S(2)}) collective-permute-start(bf16[16,4096]{1,0:T(8,128)(2,1)S(1)} %get-tuple-element.22), channel_id=1, source_target_pairs={{0,24},{4,28},{8,16},{12,20},{16,8},{20,12},{24,0},{28,4},{1,25},{... | collective-permute-start | bytes 393224 | tf_op jit(solution)/shard_map/ppermute | solution.py:28
  40.8 1.3 %collective-permute-start.15 = (bf16[16,4096]{1,0:T(8,128)(2,1)S(1)}, bf16[16,4096]{1,0:T(8,128)(2,1)S(1)}, u32[]{:S(2)}, u32[]{:S(2)}) collective-permute-start(bf16[16,4096]{1,0:T(8,128)(2,1)S(1)} %get-tuple-element.23), channel_id=1, source_target_pairs={{0,16},{4,20},{8,24},{12,28},{16,0},{20,4},{24,8},{28,12},{1,17},{... | collective-permute-start | bytes 393224 | tf_op jit(solution)/shard_map/ppermute | solution.py:28
  42.2 0.5 collective-permute-start.16
  42.7 0.0 collective-permute-done.18
  42.7 0.0 collective-permute-done.19
  42.7 0.1 fusion.2
  42.7 2.1 %collective-permute-start.20 = (bf16[8,4096]{1,0:T(8,128)(2,1)S(1)}, bf16[8,4096]{1,0:T(8,128)(2,1)S(1)}, u32[]{:S(2)}, u32[]{:S(2)}) collective-permute-start(bf16[8,4096]{1,0:T(8,128)(2,1)S(1)} %get-tuple-element.38), channel_id=1, source_target_pairs={{0,3},{1,2},{2,1},{3,0},{4,7},{5,6},{6,5},{7,4},{8,11},{9,10},{10,... | collective-permute-start | bytes 196616 | tf_op jit(solution)/shard_map/ppermute | solution.py:28
  44.9 0.0 collective-permute-start.21
  44.9 0.9 %collective-permute-done.14 = bf16[16,4096]{1,0:T(8,128)(2,1)S(1)} collective-permute-done((bf16[16,4096]{1,0:T(8,128)(2,1)S(1)}, bf16[16,4096]{1,0:T(8,128)(2,1)S(1)}, u32[]{:S(2)}, u32[]{:S(2)}) %collective-permute-start.14) | collective-permute-done | bytes 131104 | tf_op jit(solution)/shard_map/ppermute | solution.py:28
  45.7 1.1 %collective-permute-done.15 = bf16[16,4096]{1,0:T(8,128)(2,1)S(1)} collective-permute-done((bf16[16,4096]{1,0:T(8,128)(2,1)S(1)}, bf16[16,4096]{1,0:T(8,128)(2,1)S(1)}, u32[]{:S(2)}, u32[]{:S(2)}) %collective-permute-start.15) | collective-permute-done | bytes 131104 | tf_op jit(solution)/shard_map/ppermute | solution.py:28
  46.8 0.3 collective-permute-done.16
  47.1 0.1 fusion.4
  47.2 0.2 collective-permute-start.22
  47.4 2.3 %collective-permute-done.20 = bf16[8,4096]{1,0:T(8,128)(2,1)S(1)} collective-permute-done((bf16[8,4096]{1,0:T(8,128)(2,1)S(1)}, bf16[8,4096]{1,0:T(8,128)(2,1)S(1)}, u32[]{:S(2)}, u32[]{:S(2)}) %collective-permute-start.20) | collective-permute-done | bytes 65568 | tf_op jit(solution)/shard_map/ppermute | solution.py:28
  49.7 1.2 %collective-permute-done.21 = bf16[8,4096]{1,0:T(8,128)(2,1)S(1)} collective-permute-done((bf16[8,4096]{1,0:T(8,128)(2,1)S(1)}, bf16[8,4096]{1,0:T(8,128)(2,1)S(1)}, u32[]{:S(2)}, u32[]{:S(2)}) %collective-permute-start.21) | collective-permute-done | bytes 65568 | tf_op jit(solution)/shard_map/ppermute | solution.py:28
  50.9 0.7 %collective-permute-done.22 = bf16[8,4096]{1,0:T(8,128)(2,1)S(1)} collective-permute-done((bf16[8,4096]{1,0:T(8,128)(2,1)S(1)}, bf16[8,4096]{1,0:T(8,128)(2,1)S(1)}, u32[]{:S(2)}, u32[]{:S(2)}) %collective-permute-start.22) | collective-permute-done | bytes 65568 | tf_op jit(solution)/shard_map/ppermute | solution.py:28
  51.6 0.6 %fusion.6 = bf16[8,4096]{1,0:T(8,128)(2,1)} fusion(f32[8,4096]{1,0:T(8,128)S(1)} %convert_add_fusion.2, f32[16,4096]{1,0:T(8,128)S(1)} %fusion.4, bf16[8,4096]{1,0:T(8,128)(2,1)S(1)} %collective-permute-done.22), kind=kLoop, calls=%fused_computation.14 | loop fusion | flops 131072 | bytes 393216 | tf_op jit(solution)/shard_map/convert_element_type | solution.py:95
  (17 shorter events, 0.2 us)
Async XLA Ops:
  0.0 25.3 %slice-start = ((s8[6291456]{0:T(1024)(128)(4,1)}), s8[4194304]{0:T(1024)(128)(4,1)S(1)}, s32[]{:S(2)}) async-start(s8[6291456]{0:T(1024)(128)(4,1)} %bitcast), calls=%async_computation | async-start | bytes 8388608
  0.0 25.3 %slice-start.2 = ((s8[6291456]{0:T(1024)(128)(4,1)}), s8[4194304]{0:T(1024)(128)(4,1)S(1)}, s32[]{:S(2)}) async-start(s8[6291456]{0:T(1024)(128)(4,1)} %bitcast.2), calls=%async_computation.2 | async-start | bytes 8388608
  0.0 25.3 %slice-start.4 = ((s8[6291456]{0:T(1024)(128)(4,1)}), s8[4194304]{0:T(1024)(128)(4,1)S(1)}, s32[]{:S(2)}) async-start(s8[6291456]{0:T(1024)(128)(4,1)} %bitcast.4), calls=%async_computation.4 | async-start | bytes 8388608
  1.6 23.7 %slice-start.1 = ((s8[6291456]{0:T(1024)(128)(4,1)}), s8[2097152]{0:T(1024)(128)(4,1)S(1)}, s32[]{:S(2)}) async-start(s8[6291456]{0:T(1024)(128)(4,1)} %bitcast), calls=%async_computation.1 | async-start | bytes 4194304
  1.6 23.7 %slice-start.3 = ((s8[6291456]{0:T(1024)(128)(4,1)}), s8[2097152]{0:T(1024)(128)(4,1)S(1)}, s32[]{:S(2)}) async-start(s8[6291456]{0:T(1024)(128)(4,1)} %bitcast.2), calls=%async_computation.3 | async-start | bytes 4194304
  1.6 23.7 %slice-start.5 = ((s8[6291456]{0:T(1024)(128)(4,1)}), s8[2097152]{0:T(1024)(128)(4,1)S(1)}, s32[]{:S(2)}) async-start(s8[6291456]{0:T(1024)(128)(4,1)} %bitcast.4), calls=%async_computation.5 | async-start | bytes 4194304
  1.6 5.7 %collective-permute-start = (bf16[8,4224]{1,0:T(8,128)(2,1)S(1)}, bf16[8,4224]{1,0:T(8,128)(2,1)S(1)}, u32[]{:S(2)}, u32[]{:S(2)}) collective-permute-start(bf16[8,4224]{1,0:T(8,128)(2,1)S(1)} %shard_map.64.refs_0_), channel_id=1, source_target_pairs={{0,1},{1,0},{2,3},{3,2},{4,5},{5,4},{6,7},{7,6},{8,9},{9,8},{10,11... | collective-permute-start | bytes 202760 | tf_op jit(solution)/shard_map/ppermute | solution.py:28
  4.7 9.1 %collective-permute-start.5 = (bf16[8,4224]{1,0:T(8,128)(2,1)S(1)}, bf16[8,4224]{1,0:T(8,128)(2,1)S(1)}, u32[]{:S(2)}, u32[]{:S(2)}) collective-permute-start(bf16[8,4224]{1,0:T(8,128)(2,1)S(1)} %shard_map.64.refs_0_), channel_id=1, source_target_pairs={{0,3},{1,2},{2,1},{3,0},{4,7},{5,6},{6,5},{7,4},{8,11},{9,10},{10,... | collective-permute-start | bytes 202760 | tf_op jit(solution)/shard_map/ppermute | solution.py:28
  7.2 6.6 %collective-permute-start.4 = (bf16[8,4224]{1,0:T(8,128)(2,1)S(1)}, bf16[8,4224]{1,0:T(8,128)(2,1)S(1)}, u32[]{:S(2)}, u32[]{:S(2)}) collective-permute-start(bf16[8,4224]{1,0:T(8,128)(2,1)S(1)} %shard_map.64.refs_0_), channel_id=1, source_target_pairs={{0,2},{1,3},{2,0},{3,1},{4,6},{5,7},{6,4},{7,5},{8,10},{9,11},{10,... | collective-permute-start | bytes 202760 | tf_op jit(solution)/shard_map/ppermute | solution.py:28
  7.3 9.5 %collective-permute-start.3 = (bf16[16,4224]{1,0:T(8,128)(2,1)S(1)}, bf16[16,4224]{1,0:T(8,128)(2,1)S(1)}, u32[]{:S(2)}, u32[]{:S(2)}) collective-permute-start(bf16[16,4224]{1,0:T(8,128)(2,1)S(1)} %shard_map.65), channel_id=1, source_target_pairs={{0,24},{4,28},{8,16},{12,20},{16,8},{20,12},{24,0},{28,4},{1,25},{... | collective-permute-start | bytes 405512 | tf_op jit(solution)/shard_map/ppermute | solution.py:28
  9.9 7.4 %collective-permute-start.2 = (bf16[16,4224]{1,0:T(8,128)(2,1)S(1)}, bf16[16,4224]{1,0:T(8,128)(2,1)S(1)}, u32[]{:S(2)}, u32[]{:S(2)}) collective-permute-start(bf16[16,4224]{1,0:T(8,128)(2,1)S(1)} %shard_map.65), channel_id=1, source_target_pairs={{0,16},{4,20},{8,24},{12,28},{16,0},{20,4},{24,8},{28,12},{1,17},{... | collective-permute-start | bytes 405512 | tf_op jit(solution)/shard_map/ppermute | solution.py:28
  10.4 6.9 %collective-permute-start.1 = (bf16[16,4224]{1,0:T(8,128)(2,1)S(1)}, bf16[16,4224]{1,0:T(8,128)(2,1)S(1)}, u32[]{:S(2)}, u32[]{:S(2)}) collective-permute-start(bf16[16,4224]{1,0:T(8,128)(2,1)S(1)} %shard_map.65), channel_id=1, source_target_pairs={{0,8},{4,12},{8,0},{12,4},{16,24},{20,28},{24,16},{28,20},{1,9},{5... | collective-permute-start | bytes 405512 | tf_op jit(solution)/shard_map/ppermute | solution.py:28
  13.8 9.4 %collective-permute-start.8 = (bf16[16,4224]{1,0:T(8,128)(2,1)S(1)}, bf16[16,4224]{1,0:T(8,128)(2,1)S(1)}, u32[]{:S(2)}, u32[]{:S(2)}) collective-permute-start(bf16[16,4224]{1,0:T(8,128)(2,1)S(1)} %get-tuple-element.40), channel_id=1, source_target_pairs={{0,24},{4,28},{8,16},{12,20},{16,8},{20,12},{24,0},{28,4},{1,25},{... | collective-permute-start | bytes 405512 | tf_op jit(solution)/shard_map/ppermute | solution.py:28
  16.3 6.9 %collective-permute-start.7 = (bf16[16,4224]{1,0:T(8,128)(2,1)S(1)}, bf16[16,4224]{1,0:T(8,128)(2,1)S(1)}, u32[]{:S(2)}, u32[]{:S(2)}) collective-permute-start(bf16[16,4224]{1,0:T(8,128)(2,1)S(1)} %get-tuple-element.40), channel_id=1, source_target_pairs={{0,16},{4,20},{8,24},{12,28},{16,0},{20,4},{24,8},{28,12},{1,17},{... | collective-permute-start | bytes 405512 | tf_op jit(solution)/shard_map/ppermute | solution.py:28
  16.8 6.4 %collective-permute-start.6 = (bf16[16,4224]{1,0:T(8,128)(2,1)S(1)}, bf16[16,4224]{1,0:T(8,128)(2,1)S(1)}, u32[]{:S(2)}, u32[]{:S(2)}) collective-permute-start(bf16[16,4224]{1,0:T(8,128)(2,1)S(1)} %get-tuple-element.40), channel_id=1, source_target_pairs={{0,8},{4,12},{8,0},{12,4},{16,24},{20,28},{24,16},{28,20},{1,9},{5... | collective-permute-start | bytes 405512 | tf_op jit(solution)/shard_map/ppermute | solution.py:28
  17.4 5.9 %collective-permute-start.9 = (bf16[64,4224]{1,0:T(8,128)(2,1)S(1)}, bf16[64,4224]{1,0:T(8,128)(2,1)S(1)}, u32[]{:S(2)}, u32[]{:S(2)}) collective-permute-start(bf16[64,4224]{1,0:T(8,128)(2,1)S(1)} %pad_maximum_fusion.refs_0_), channel_id=1, source_target_pairs={{0,4},{4,0},{8,12},{12,8},{16,20},{20,16},{24,28},{28,24},{1,5},{5... | collective-permute-start | bytes 1622024 | tf_op jit(solution)/shard_map/ppermute | solution.py:28
  23.3 2.0 %collective-permute-start.10 = (bf16[64,4224]{1,0:T(8,128)(2,1)S(1)}, bf16[64,4224]{1,0:T(8,128)(2,1)S(1)}, u32[]{:S(2)}, u32[]{:S(2)}) collective-permute-start(bf16[64,4224]{1,0:T(8,128)(2,1)S(1)} %constant_dynamic-update-slice_fusion.2.refs_1_), channel_id=1, source_target_pairs={{0,4},{4,0},{8,12},{12,8},{16,20},{20,16},{24,28},{28,24},{1,5},{5... | collective-permute-start | bytes 1622024 | tf_op jit(solution)/shard_map/ppermute | solution.py:28
  30.4 1.4 %collective-permute-start.12 = (bf16[16,4096]{1,0:T(8,128)(2,1)S(1)}, bf16[16,4096]{1,0:T(8,128)(2,1)S(1)}, u32[]{:S(2)}, u32[]{:S(2)}) collective-permute-start(bf16[16,4096]{1,0:T(8,128)(2,1)S(1)} %get-tuple-element.20), channel_id=1, source_target_pairs={{0,4},{4,0},{8,12},{12,8},{16,20},{20,16},{24,28},{28,24},{1,5},{5... | collective-permute-start | bytes 393224 | tf_op jit(solution)/shard_map/ppermute | solution.py:28
  30.6 3.0 %collective-permute-start.17 = (bf16[48,4096]{1,0:T(8,128)(2,1)S(1)}, bf16[48,4096]{1,0:T(8,128)(2,1)S(1)}, u32[]{:S(2)}, u32[]{:S(2)}) collective-permute-start(bf16[48,4096]{1,0:T(8,128)(2,1)S(1)} %get-tuple-element.26), channel_id=1, source_target_pairs={{0,4},{4,0},{8,12},{12,8},{16,20},{20,16},{24,28},{28,24},{1,5},{5... | collective-permute-start | bytes 1179656 | tf_op jit(solution)/shard_map/ppermute | solution.py:28
  31.0 4.6 %collective-permute-start.11 = (bf16[64,4096]{1,0:T(8,128)(2,1)S(1)}, bf16[64,4096]{1,0:T(8,128)(2,1)S(1)}, u32[]{:S(2)}, u32[]{:S(2)}) collective-permute-start(bf16[64,4096]{1,0:T(8,128)(2,1)S(1)} %get-tuple-element.18), channel_id=1, source_target_pairs={{0,4},{4,0},{8,12},{12,8},{16,20},{20,16},{24,28},{28,24},{1,5},{5... | collective-permute-start | bytes 1572872 | tf_op jit(solution)/shard_map/ppermute | solution.py:28
  31.9 7.3 %collective-permute-start.13 = (bf16[16,4096]{1,0:T(8,128)(2,1)S(1)}, bf16[16,4096]{1,0:T(8,128)(2,1)S(1)}, u32[]{:S(2)}, u32[]{:S(2)}) collective-permute-start(bf16[16,4096]{1,0:T(8,128)(2,1)S(1)} %add_convert_fusion), channel_id=1, source_target_pairs={{0,24},{4,28},{8,16},{12,20},{16,8},{20,12},{24,0},{28,4},{1,25},{... | collective-permute-start | bytes 393224 | tf_op jit(solution)/shard_map/ppermute | solution.py:28
  33.7 9.0 %collective-permute-start.18 = (bf16[16,4096]{1,0:T(8,128)(2,1)S(1)}, bf16[16,4096]{1,0:T(8,128)(2,1)S(1)}, u32[]{:S(2)}, u32[]{:S(2)}) collective-permute-start(bf16[16,4096]{1,0:T(8,128)(2,1)S(1)} %get-tuple-element.36), channel_id=1, source_target_pairs={{0,16},{4,20},{8,24},{12,28},{16,0},{20,4},{24,8},{28,12},{1,17},{... | collective-permute-start | bytes 393224 | tf_op jit(solution)/shard_map/ppermute | solution.py:28
  35.1 7.6 %collective-permute-start.19 = (bf16[16,4096]{1,0:T(8,128)(2,1)S(1)}, bf16[16,4096]{1,0:T(8,128)(2,1)S(1)}, u32[]{:S(2)}, u32[]{:S(2)}) collective-permute-start(bf16[16,4096]{1,0:T(8,128)(2,1)S(1)} %get-tuple-element.37), channel_id=1, source_target_pairs={{0,8},{4,12},{8,0},{12,4},{16,24},{20,28},{24,16},{28,20},{1,9},{5... | collective-permute-start | bytes 393224 | tf_op jit(solution)/shard_map/ppermute | solution.py:28
  39.2 6.6 %collective-permute-start.14 = (bf16[16,4096]{1,0:T(8,128)(2,1)S(1)}, bf16[16,4096]{1,0:T(8,128)(2,1)S(1)}, u32[]{:S(2)}, u32[]{:S(2)}) collective-permute-start(bf16[16,4096]{1,0:T(8,128)(2,1)S(1)} %get-tuple-element.22), channel_id=1, source_target_pairs={{0,24},{4,28},{8,16},{12,20},{16,8},{20,12},{24,0},{28,4},{1,25},{... | collective-permute-start | bytes 393224 | tf_op jit(solution)/shard_map/ppermute | solution.py:28
  40.8 6.0 %collective-permute-start.15 = (bf16[16,4096]{1,0:T(8,128)(2,1)S(1)}, bf16[16,4096]{1,0:T(8,128)(2,1)S(1)}, u32[]{:S(2)}, u32[]{:S(2)}) collective-permute-start(bf16[16,4096]{1,0:T(8,128)(2,1)S(1)} %get-tuple-element.23), channel_id=1, source_target_pairs={{0,16},{4,20},{8,24},{12,28},{16,0},{20,4},{24,8},{28,12},{1,17},{... | collective-permute-start | bytes 393224 | tf_op jit(solution)/shard_map/ppermute | solution.py:28
  42.2 5.0 %collective-permute-start.16 = (bf16[16,4096]{1,0:T(8,128)(2,1)S(1)}, bf16[16,4096]{1,0:T(8,128)(2,1)S(1)}, u32[]{:S(2)}, u32[]{:S(2)}) collective-permute-start(bf16[16,4096]{1,0:T(8,128)(2,1)S(1)} %get-tuple-element.24), channel_id=1, source_target_pairs={{0,8},{4,12},{8,0},{12,4},{16,24},{20,28},{24,16},{28,20},{1,9},{5... | collective-permute-start | bytes 393224 | tf_op jit(solution)/shard_map/ppermute | solution.py:28
  42.7 6.9 %collective-permute-start.20 = (bf16[8,4096]{1,0:T(8,128)(2,1)S(1)}, bf16[8,4096]{1,0:T(8,128)(2,1)S(1)}, u32[]{:S(2)}, u32[]{:S(2)}) collective-permute-start(bf16[8,4096]{1,0:T(8,128)(2,1)S(1)} %get-tuple-element.38), channel_id=1, source_target_pairs={{0,3},{1,2},{2,1},{3,0},{4,7},{5,6},{6,5},{7,4},{8,11},{9,10},{10,... | collective-permute-start | bytes 196616 | tf_op jit(solution)/shard_map/ppermute | solution.py:28
  44.9 6.0 %collective-permute-start.21 = (bf16[8,4096]{1,0:T(8,128)(2,1)S(1)}, bf16[8,4096]{1,0:T(8,128)(2,1)S(1)}, u32[]{:S(2)}, u32[]{:S(2)}) collective-permute-start(bf16[8,4096]{1,0:T(8,128)(2,1)S(1)} %get-tuple-element.39), channel_id=1, source_target_pairs={{0,2},{1,3},{2,0},{3,1},{4,6},{5,7},{6,4},{7,5},{8,10},{9,11},{10,... | collective-permute-start | bytes 196616 | tf_op jit(solution)/shard_map/ppermute | solution.py:28
  47.2 4.4 %collective-permute-start.22 = (bf16[8,4096]{1,0:T(8,128)(2,1)S(1)}, bf16[8,4096]{1,0:T(8,128)(2,1)S(1)}, u32[]{:S(2)}, u32[]{:S(2)}) collective-permute-start(bf16[8,4096]{1,0:T(8,128)(2,1)S(1)} %slice.81), channel_id=1, source_target_pairs={{0,1},{1,0},{2,3},{3,2},{4,5},{5,4},{6,7},{7,6},{8,9},{9,8},{10,11... | collective-permute-start | bytes 196616 | tf_op jit(solution)/shard_map/ppermute | solution.py:28
